TPU v7x, 256 devices: a whole 4x4x8 slice. The times are simulated.
256 devices in a mesh: dp: 32 (over x_hi, z, core), fsdp: 8 (over y, x_lo).
Axes of the slice: x: 4 (x_hi: 2, x_lo: 2; x = x_hi * 2 + x_lo), y: 4, z: 8, core: 2. Of those that a mesh axis runs over, the one named last changes fastest.
Arguments:
- tokens: bfloat16 [49152, 6144], P(('dp', 'fsdp')), may hold values from -6 to 6
- cotangent: bfloat16 [49152, 6144], P(('dp', 'fsdp')), may hold values from -24 to 24
- lengths: int32 [256, 3], P(('dp', 'fsdp')), may hold values from 0 to 80, as said below
- positions: int32 [2, 49152], P(None, ('dp', 'fsdp')), may hold values from 0 to 63, as said below
- weights: bfloat16 [4, 6144, 256], P(None, 'fsdp'), may hold values from -0.078125 to 0.078125
Outputs:
- grad_tokens: bfloat16 [49152, 6144], P(('dp', 'fsdp'))
- weight_grads: float32 [4, 6144, 256], P(None, 'fsdp')
Inputs may be any that keep to these rules, and one draw needn't show every extreme that they name: Devices pair up: dp indices i and i + 16 with the same fsdp index. In every pair exactly one device holds more than 112 live patches; its third image is not empty, its first two images together hold at most 112 patches, and its partner's live patches plus that third image are at most 112. No device holds more than 192 live patches; the first pair's heavy device holds exactly 192. Every non-empty image has at least 10 patches; lengths are 0 only in the light device's third slot. `positions`: each image is laid out row by row with a width w of 2 to 64 patches (exactly 64 for images of 80 patches): its patch number k has row k // w and column k % w; padding rows hold 0.
All inputs are finite; a program needn't handle non-finite values.
Results may differ from a plain program's by a relative error of at most 0.015.
Values may be sent and summed in bfloat16 or wider, within the bound.
No kernel may reach another device: no remote copies, remote signals or barrier semaphores. Data moves between devices by JAX's collectives and lax.ppermute only.
A program may use at most 128 MiB of HBM per device.

v0:
```python
import functools
import math

import jax
import jax.numpy as jnp
from jax import lax
from jax.experimental import pallas as pl
from jax.experimental.pallas import tpu as pltpu
from jax.sharding import PartitionSpec as P

HD = 128
HEADS = 2
ROPE_BASE = 100.0
EPS = 1e-6
NX, NY, NZ = 4, 4, 8
ORDER = [(0, 0), (0, 1), (1, 0), (1, 1), (3, 0), (2, 0), (3, 1), (2, 1)]
X_AT, X_LO, CORE, SIGN = 16, 17, 18, 19
BF16, F32 = jnp.bfloat16, jnp.float32


def flat_index(x, y, z, core):
    return ((x // 2) * 16 + z * 2 + core) * 8 + y * 2 + x % 2


DEVICES = [(x, y, z, core) for x in range(NX) for y in range(NY) for z in range(NZ) for core in range(2)]


def permute(values, target):
    pairs = []
    for x, y, z, core in DEVICES:
        tx, ty, tz, tcore = target(x, y, z, core)
        pairs.append((flat_index(x, y, z, core), flat_index(tx % NX, ty % NY, tz % NZ, tcore)))
    return lax.ppermute(values, ("dp", "fsdp"), pairs)


def shift(values, dx=0, dy=0, dc=0):
    def target(x, y, z, core):
        s = 1 - 2 * core
        return x + s * dx, y + s * dy, z, core ^ dc

    return permute(values, target)


def along(values, first=0, second=0):
    def target(x, y, z, core):
        dx, dy = (second, first) if core == 0 else (first, second)
        return x + dx, y + dy, z, core

    return permute(values, target)


def call(body, out_shapes, operands, scalars=0, scratch=(), flops=0, nbytes=0, name=None, after=()):
    count, last = len(operands), len(operands) + len(after)
    specs = [pl.BlockSpec(memory_space=pltpu.SMEM if i < scalars else pltpu.VMEM) for i in range(count)]
    specs += [pl.BlockSpec(memory_space=pl.ANY) for _ in after]
    kernel = (lambda *refs: body(*refs[:count], *refs[last:])) if after else body
    return pl.pallas_call(
        kernel,
        out_shape=out_shapes,
        in_specs=specs,
        out_specs=jax.tree.map(lambda _: pl.BlockSpec(memory_space=pltpu.VMEM), out_shapes),
        scratch_shapes=list(scratch),
        compiler_params=pltpu.CompilerParams(vmem_limit_bytes=56 * 1024 * 1024),
        cost_estimate=pl.CostEstimate(flops=flops, bytes_accessed=nbytes, transcendentals=0),
        name=name,
    )(*operands, *after)


def gate(value, after):
    return pl.pallas_call(
        lambda *refs: None,
        out_shape=shape(value.shape, value.dtype),
        in_specs=[pl.BlockSpec(memory_space=pl.ANY)] * (1 + len(after)),
        out_specs=pl.BlockSpec(memory_space=pl.ANY),
        input_output_aliases={0: 0},
        cost_estimate=pl.CostEstimate(flops=1, bytes_accessed=1, transcendentals=0),
        name="gate",
    )(value, *after)


def shape(dims, dtype=BF16):
    return jax.ShapeDtypeStruct(dims, dtype)


def prep_kernel(width, info, tokens, cot, own, send, normed):
    rows, model = tokens.shape
    step = 16

    def body(i, carry):
        at = pl.ds(pl.multiple_of(i * step, step), step)
        x = tokens[at, :].astype(F32)
        center = x - jnp.sum(x, axis=1, keepdims=True) / model
        var = jnp.sum(center * center, axis=1, keepdims=True) / model
        normed[at, :] = (center * lax.rsqrt(var + EPS)).astype(BF16)
        return carry

    lax.fori_loop(0, rows // step, body, 0)
    for j in range(8):
        to = slice(j * width, (j + 1) * width)
        for out, first in ((own, 0), (send, 8)):
            cols = pl.ds(pl.multiple_of(info[first + j], 128), width)
            out[0, :, to] = normed[:, cols]
            out[1, :, to] = cot[:, cols]


def flip_kernel(width, info, own, peer, out):
    half = width // 2
    quarter = half // 2
    core, sign, x_at = info[CORE], info[SIGN], info[X_AT]
    for j, (k, dx) in enumerate(ORDER):
        at = slice(j * width, (j + 1) * width)
        y_steps = lax.rem(4 - sign * k, 4)
        for i in range(2):
            turned = jnp.concatenate([own[i, :, at], peer[i, :, at]], axis=0).T
            for x_hi in range(2):
                x_to = 2 * x_hi + lax.rem(info[X_LO] + dx, 2)
                x_steps = lax.rem(x_to - x_at + 4, 4)
                first = jnp.where(core == 0, y_steps, x_steps)
                second = jnp.where(core == 0, x_steps, y_steps)
                for side in range(2):
                    steps = first if side == 0 else lax.rem(4 - first, 4)
                    start = x_hi * half + side * quarter
                    out[side, steps, i, second] = turned[start : start + quarter]


def linear_kernel(width, first, pairs, own, peer, *refs):
    shards, rest = refs[: 2 * pairs], refs[2 * pairs :]
    before, outs = rest[:-2], rest[-2:]
    cols = shards[0].shape[2]
    for m in range(4):
        to = slice(m * cols, (m + 1) * cols)
        rights = [jnp.concatenate([shards[2 * p][m], shards[2 * p + 1][m]], axis=0) for p in range(pairs)]
        for side, left in enumerate((own, peer)):
            total = before[side][:, to] if before else None
            for p, right in enumerate(rights):
                at = slice(2 * (first + p) * width, 2 * (first + p + 1) * width)
                term = jnp.dot(left[m // 3, :, at], right, preferred_element_type=F32)
                total = term if total is None else total + term
            outs[side][:, to] = total


def swap_quarters(x):
    lane = lax.broadcasted_iota(jnp.int32, x.shape, 1)
    quarter = HD // 4
    up = pltpu.roll(x, HD - quarter, 1)
    down = pltpu.roll(x, quarter, 1)
    return jnp.where(lane % (2 * quarter) < quarter, up, down)


def mean_of(x):
    return jnp.sum(x, axis=1, keepdims=True) * (1.0 / HD)


def norm_rows(x):
    center = x - mean_of(x)
    scale = lax.rsqrt(mean_of(center * center) + EPS)
    return center * scale, scale


def norm_rows_back(g, hat, scale):
    return scale * (g - mean_of(g) - hat * mean_of(g * hat))


def dot_t(a, b, dims):
    return lax.dot_general(a, b, ((dims[0], dims[1]), ((), ())), preferred_element_type=F32)


def attend_kernel(ends, mine, theirs, cos_t, sin_t, out):
    rows = mine.shape[0]
    cols = HEADS * HD
    row_id = lax.broadcasted_iota(jnp.int32, (rows, 1), 0)
    col_id = lax.broadcasted_iota(jnp.int32, (1, rows), 1)

    def slot(ids):
        count = jnp.zeros(ids.shape, jnp.int32)
        for k in range(3):
            count = count + (ids >= ends[k]).astype(jnp.int32)
        return count

    row_slot, col_slot = slot(row_id), slot(col_id)
    same = row_slot == col_slot
    live = row_slot < 3
    cosine, sine = cos_t[...], sin_t[...]
    score_scale = 1.0 / math.sqrt(HD)
    for h in range(HEADS):

        def part(m):
            at = slice(m * cols + h * HD, m * cols + (h + 1) * HD)
            return mine[:, at] + theirs[:, at]

        q_hat, q_scale = norm_rows(part(0))
        k_hat, k_scale = norm_rows(part(1))
        q = (q_hat * cosine + swap_quarters(q_hat) * sine).astype(BF16)
        k = (k_hat * cosine + swap_quarters(k_hat) * sine).astype(BF16)
        v = part(2).astype(BF16)
        ga = jnp.where(live, part(3), 0.0).astype(BF16)
        scores = dot_t(q, k, ((1,), (1,))) * score_scale
        e = jnp.where(same, jnp.exp(scores), 0.0)
        p32 = e / jnp.sum(e, axis=1, keepdims=True)
        p = p32.astype(BF16)
        att = jnp.dot(p, v, preferred_element_type=F32).astype(BF16)
        gv = dot_t(p, ga, ((0,), (0,)))
        gp = dot_t(ga, v, ((1,), (1,))).astype(BF16).astype(F32)
        gs = p32 * (gp - jnp.sum(gp * p32, axis=1, keepdims=True)) * score_scale
        gs = gs.astype(BF16)
        gq = jnp.dot(gs, k, preferred_element_type=F32).astype(BF16).astype(F32)
        gk = dot_t(gs, q, ((0,), (0,))).astype(BF16).astype(F32)
        gq = norm_rows_back(gq * cosine + swap_quarters(gq * sine), q_hat, q_scale)
        gk = norm_rows_back(gk * cosine + swap_quarters(gk * sine), k_hat, k_scale)
        at = lambda m: slice(m * cols + h * HD, m * cols + (h + 1) * HD)
        out[:, at(0)] = gq.astype(BF16)
        out[:, at(1)] = gk.astype(BF16)
        out[:, at(2)] = gv.astype(BF16)
        out[:, at(3)] = jnp.where(live, att.astype(F32), 0.0).astype(BF16)


def terms_kernel(steps, turned, y_own, y_peer, *outs):
    rows, depth = turned.shape[4:]
    y_all = jnp.concatenate([y_own[...], y_peer[...]], axis=0)
    proj = 3 * HEADS * HD
    for k, step in enumerate(steps):
        for side in range(2):
            for i, right in ((0, y_all[:, :proj]), (1, y_all[:, proj:])):
                left = turned[side, step, i].reshape(4 * rows, depth)
                value = jnp.dot(left, right, preferred_element_type=F32).astype(BF16)
                for n in range(right.shape[1] // 128):
                    for u in range(4):
                        block = value[u * rows : (u + 1) * rows, n * 128 : (n + 1) * 128]
                        outs[2 * k + side][u, 6 * i + n] = block


def add_up(refs, at):
    total = refs[0][at].astype(F32)
    for ref in refs[1:]:
        total = total + ref[at].astype(F32)
    return total.astype(BF16)


def join_kernel(*refs):
    for u in range(refs[0].shape[0]):
        for n in range(refs[0].shape[1]):
            refs[-1][u, n] = add_up(refs[:-1], (u, n))


def sides_kernel(*refs):
    for side in range(2):
        for u, out in enumerate(refs[6:]):
            for n in range(8):
                out[n, side] = add_up(refs[3 * side : 3 * side + 3], (u, n))


def seconds_kernel(*refs):
    for n in range(8):
        for side in range(2):
            refs[-1][n, side] = add_up(refs[:-1], (n, side))


def last_kernel(got, out):
    for side in range(2):
        total = got[0, side].astype(F32)
        for k in range(1, 8):
            total = total + got[k, side].astype(F32)
        for k in range(out.shape[0]):
            out[k, side] = total.astype(BF16)


def sum_call(body, name, outs, arrays, after=()):
    size = math.prod(arrays[0].shape)
    return call(
        body, outs, arrays, flops=len(arrays) * size, nbytes=2 * size * (len(arrays) + 2), name=name, after=after
    )


def normed_grad_kernel(width, y_own, y_peer, *refs):
    shards, (g_own, g_send) = refs[:-2], refs[-2:]
    rows = y_own.shape[0]
    proj = 3 * HEADS * HD
    left = jnp.concatenate([y_own[:, :proj], y_peer[:, :proj]], axis=0)
    for j in range(8):
        right = jnp.concatenate([shards[j][m] for m in range(3)], axis=1)
        total = dot_t(left, right, ((1,), (1,)))
        at = slice(j * width, (j + 1) * width)
        g_own[:, at] = total[:rows]
        g_send[:, at] = total[rows:]


def token_grad_kernel(width, info, tokens, g_own, g_peer, out, g):
    rows, model = tokens.shape
    for first, ref in ((0, g_own), (8, g_peer)):
        for j in range(8):
            to = pl.ds(pl.multiple_of(info[first + j], 128), width)
            g[:, to] = ref[:, j * width : (j + 1) * width]
    step = 16

    def body(i, carry):
        at = pl.ds(pl.multiple_of(i * step, step), step)
        x = tokens[at, :].astype(F32)
        center = x - jnp.sum(x, axis=1, keepdims=True) / model
        scale = lax.rsqrt(jnp.sum(center * center, axis=1, keepdims=True) / model + EPS)
        hat = center * scale
        grad = g[at, :]
        mean_g = jnp.sum(grad, axis=1, keepdims=True) / model
        mean_gh = jnp.sum(grad * hat, axis=1, keepdims=True) / model
        out[at, :] = (scale * (grad - mean_g - hat * mean_gh)).astype(BF16)
        return carry

    lax.fori_loop(0, rows // step, body, 0)


def place_kernel(info, own, other, out):
    rows = own.shape[3]
    for k, ref in enumerate((own, other)):
        c = info[CORE] if k == 0 else 1 - info[CORE]
        for h in range(2):
            for n in range(8):
                for side in range(2):
                    to = pl.ds(pl.multiple_of(c * 4 * rows + (2 * h + side) * rows, rows), rows)
                    out[n // 2, to, (n % 2) * 128 : (n % 2 + 1) * 128] = ref[h, n, side].astype(F32)


def swap_groups(with_x):
    if with_x:
        return [[x * 16 + z * 2 + core for x in range(2) for z in range(NZ)] for core in range(2)]
    return [[x * 16 + z * 2 + core for z in range(NZ)] for x in range(2) for core in range(2)]


def exchange(values, with_x):
    return lax.all_to_all(
        values, "dp", split_axis=0, concat_axis=0, axis_index_groups=swap_groups(with_x), tiled=True
    )


def per_device(tokens, cotangent, lengths, positions, weights):
    rows, model = tokens.shape
    shard_rows, cols = weights.shape[1], weights.shape[2]
    width = shard_rows // 2
    dp, fs = lax.axis_index("dp"), lax.axis_index("fsdp")
    core, x_hi = dp % 2, dp // 16
    y_at, x_lo = fs // 2, fs % 2
    sign = 1 - 2 * core
    offs = []
    for c, s in ((core, sign), (1 - core, -sign)):
        for k, dx in ORDER:
            shard = ((y_at - s * k + 4) % NY) * 2 + (x_lo + dx) % 2
            offs.append(shard * shard_rows + c * width)
    l0, l1, l2 = lengths[0, 0], lengths[0, 1], lengths[0, 2]
    ends = jnp.stack([l0, l0 + l1, l0 + l1 + l2]).astype(jnp.int32)
    info = jnp.stack(offs + [x_hi * 2 + x_lo, x_lo, core, sign]).astype(jnp.int32)
    half = width // 2

    pair_shape = shape((2, rows, model // 2))
    own, send = call(
        functools.partial(prep_kernel, width),
        [pair_shape] * 2,
        [info, tokens, cotangent],
        scalars=1,
        scratch=[pltpu.VMEM((rows, model), BF16)],
        flops=8 * rows * model,
        nbytes=8 * rows * model,
        name="prep",
    )
    w = {(0, 0): lax.dynamic_slice(weights, (0, core * width, 0), (4, width, cols))}
    w[0, 1] = shift(w[0, 0], dx=1)
    w[3, 0] = shift(w[0, 0], dy=-1)
    w[1, 0] = gate(shift(w[0, 0], dy=1), [own, w[0, 1]])
    w[2, 0] = shift(w[1, 0], dy=1)
    w[1, 1] = shift(w[1, 0], dx=1)
    w[3, 1] = shift(w[3, 0], dx=1)
    w[2, 1] = shift(w[1, 1], dy=1)
    shards = [w[place] for place in ORDER]

    peer = shift(gate(send, [w[1, 0], w[3, 0]]), dc=1)
    turned = call(
        functools.partial(flip_kernel, width),
        shape((2, 4, 2, 4, half // 2, 2 * rows)),
        [info, own, peer],
        scalars=1,
        nbytes=8 * rows * model,
        name="flip",
    )

    quarter = HD // 4
    frequency = ROPE_BASE ** (-jnp.arange(quarter, dtype=F32) / quarter)
    angle_r = positions[0].astype(F32)[:, None] * frequency[None, :]
    angle_c = positions[1].astype(F32)[:, None] * frequency[None, :]
    cos_r, sin_r, cos_c, sin_c = jnp.cos(angle_r), jnp.sin(angle_r), jnp.cos(angle_c), jnp.sin(angle_c)
    cos_t = jnp.concatenate([cos_r, cos_r, cos_c, cos_c], axis=1)
    sin_t = jnp.concatenate([-sin_r, sin_r, -sin_c, sin_c], axis=1)

    lin_shape = shape((rows, 4 * cols), F32)
    lin = []
    for first, pairs in ((0, 3), (3, 1)):
        lin = call(
            functools.partial(linear_kernel, width, first, pairs),
            [lin_shape] * 2,
            [own, peer] + shards[2 * first : 2 * (first + pairs)] + list(lin),
            flops=2 * 2 * rows * 2 * pairs * width * 4 * cols,
            nbytes=2 * pairs * width * 8 * cols + 8 * rows * 2 * pairs * width,
            name="linear",
            after=[] if first else [turned, cos_t, sin_t, ends],
        )
    lin_own, lin_send = lin
    lin_peer = shift(lin_send, dc=1)
    y_own = call(
        attend_kernel,
        shape((rows, 4 * cols)),
        [ends, lin_own, lin_peer, cos_t, sin_t],
        scalars=1,
        flops=HEADS * 10 * rows * rows * HD * 2,
        nbytes=10 * rows * 4 * cols,
        name="attend",
    )
    y_peer = shift(y_own, dc=1)

    quarter = half // 2
    piece = shape((4, 8, quarter, 128))

    def terms(steps):
        part = len(steps) / 4
        return call(
            functools.partial(terms_kernel, steps),
            [piece] * (2 * len(steps)),
            [turned, y_own, y_peer],
            flops=int(part * 2 * 2 * rows * (model // 2) * 4 * cols),
            nbytes=int(part * (4 * model * cols + 8 * rows * model)),
            name="terms",
        )

    far = terms([2])
    far = [along(far[0], first=1), along(far[1], first=-1)]
    back = terms([3])
    back = [along(back[0], first=-1), along(back[1], first=1)]
    near = terms([1, 0])

    g_own, g_send = call(
        functools.partial(normed_grad_kernel, width),
        [shape((rows, model // 2), F32)] * 2,
        [y_own, y_peer] + shards,
        flops=2 * rows * model * 3 * cols,
        nbytes=4 * model * cols + 4 * rows * model,
        name="normed_grad",
        after=[near[0]],
    )
    ahead = []
    for side in range(2):
        joined = sum_call(join_kernel, "join", piece, [near[side], far[side]], after=[g_send])
        ahead.append(along(joined, first=1 - 2 * side))
    halfway = sum_call(
        sides_kernel,
        "sides",
        [shape((8, 2, quarter, 128))] * 4,
        [near[2], back[0], ahead[0], near[3], back[1], ahead[1]],
    )
    g_peer = shift(gate(g_send, [halfway[0]]), dc=1)
    grad_tokens = call(
        functools.partial(token_grad_kernel, width),
        shape((rows, model)),
        [info, tokens, g_own, g_peer],
        scalars=1,
        scratch=[pltpu.VMEM((rows, model), F32)],
        flops=16 * rows * model,
        nbytes=8 * rows * model,
        name="token_grad",
    )

    rest = [along(halfway[d], second=d) for d in range(1, 4)]
    by_z = sum_call(seconds_kernel, "seconds", shape((8, 2, quarter, 128)), [halfway[0]] + rest, after=[grad_tokens])
    spread = sum_call(last_kernel, "last", shape((2 * NZ, 2, quarter, 128)), [exchange(by_z, False)])
    done = exchange(spread, True).reshape(2, NZ, 2, quarter, 128)
    weight_grads = call(
        place_kernel,
        shape((4, shard_rows, cols), F32),
        [info, done, shift(done, dc=1)],
        scalars=1,
        flops=4 * shard_rows * cols,
        nbytes=24 * shard_rows * cols,
        name="place",
    )
    return (grad_tokens, weight_grads)


def solution(mesh):
    return jax.shard_map(
        per_device,
        mesh=mesh,
        in_specs=(
            P(("dp", "fsdp"), None),
            P(("dp", "fsdp"), None),
            P(("dp", "fsdp"), None),
            P(None, ("dp", "fsdp")),
            P(None, "fsdp", None),
        ),
        out_specs=(P(("dp", "fsdp"), None), P(None, "fsdp", None)),
        check_vma=False,
    )
```

profile of v0, /device:TPU:1, one launch (start us, length us, event | category | flops | bytes accessed | tf_op | source)
XLA Modules:
  0.0 211.1 jit_solution(828399975959007378)
XLA Ops:
  3.0 3.3 %collective-permute-start.1 = (bf16[4,384,256]{2,1,0:T(8,128)(2,1)}, bf16[4,384,256]{2,1,0:T(8,128)(2,1)S(1)}, u32[]{:S(2)}, u32[]{:S(2)}) collective-permute-start(bf16[4,384,256]{2,1,0:T(8,128)(2,1)} %constant_dynamic-slice_fusion.refs_2_), channel_id=1, source_target_pairs={{0,1},{8,137},{16,17},{24,153},{32,33},{40,169},{48,49},{56,185},{... | collective-permute-start | bytes 2359304 | tf_op jit(solution)/shard_map/ppermute | solution.py:33
  6.3 2.7 %collective-permute-start = (bf16[4,384,256]{2,1,0:T(8,128)(2,1)}, bf16[4,384,256]{2,1,0:T(8,128)(2,1)S(1)}, u32[]{:S(2)}, u32[]{:S(2)}) collective-permute-start(bf16[4,384,256]{2,1,0:T(8,128)(2,1)} %constant_dynamic-slice_fusion.refs_2_), channel_id=1, source_target_pairs={{0,2},{8,14},{16,18},{24,30},{32,34},{40,46},{48,50},{56,62},{64,6... | collective-permute-start | bytes 2359304 | tf_op jit(solution)/shard_map/ppermute | solution.py:33
  9.7 8.6 %prep.1 = (bf16[2,192,3072]{2,1,0:T(8,128)(2,1)}, bf16[2,192,3072]{2,1,0:T(8,128)(2,1)}) custom-call(s32[20]{0:T(128)} %stack.92.info, bf16[192,6144]{1,0:T(8,128)(2,1)} %tokens.3, bf16[192,6144]{1,0:T(8,128)(2,1)} %cot.1), custom_call_target="tpu_custom_call" | custom-call | flops 9437184 | bytes 9437184 | tf_op jit(solution)/shard_map/prep/pallas_call | solution.py:57
  18.2 7.9 %collective-permute-done.refs_0_ = bf16[4,384,256]{2,1,0:T(8,128)(2,1)S(1)} collective-permute-done((bf16[4,384,256]{2,1,0:T(8,128)(2,1)}, bf16[4,384,256]{2,1,0:T(8,128)(2,1)S(1)}, u32[]{:S(2)}, u32[]{:S(2)}) %collective-permute-start) | collective-permute-done | bytes 786464 | tf_op jit(solution)/shard_map/ppermute | solution.py:33
  28.6 3.4 %collective-permute-start.5 = (bf16[4,384,256]{2,1,0:T(8,128)(2,1)S(1)}, bf16[4,384,256]{2,1,0:T(8,128)(2,1)S(1)}, u32[]{:S(2)}, u32[]{:S(2)}) collective-permute-start(bf16[4,384,256]{2,1,0:T(8,128)(2,1)S(1)} %copy-done.3), channel_id=1, source_target_pairs={{0,1},{8,137},{16,17},{24,153},{32,33},{40,169},{48,49},{56,185},{... | collective-permute-start | bytes 2359304 | tf_op jit(solution)/shard_map/ppermute | solution.py:33
  34.7 6.2 %collective-permute-done.5.refs_5_ = bf16[4,384,256]{2,1,0:T(8,128)(2,1)S(1)} collective-permute-done((bf16[4,384,256]{2,1,0:T(8,128)(2,1)S(1)}, bf16[4,384,256]{2,1,0:T(8,128)(2,1)S(1)}, u32[]{:S(2)}, u32[]{:S(2)}) %collective-permute-start.5) | collective-permute-done | bytes 786464 | tf_op jit(solution)/shard_map/ppermute | solution.py:33
  47.0 5.9 %flip.1.refs_8_.turned = bf16[2,4,2,4,96,384]{5,4,3,2,1,0:T(8,128)(2,1)} custom-call(s32[20]{0:T(128)} %stack.92.info, bf16[2,192,3072]{2,1,0:T(8,128)(2,1)} %get-tuple-element.22.refs_1_.own.refs_0_, bf16[2,192,3072]{2,1,0:T(8,128)(2,1)} %copy-done.1), custom_call_target="tpu_custom_call" | custom-call | bytes 9437184 | tf_op jit(solution)/shard_map/flip/pallas_call | solution.py:57
  53.8 6.8 %linear.2 = (f32[192,1024]{1,0:T(8,128)}, f32[192,1024]{1,0:T(8,128)}) custom-call(bf16[2,192,3072]{2,1,0:T(8,128)(2,1)} %get-tuple-element.22.refs_1_.own.refs_0_, bf16[2,192,3072]{2,1,0:T(8,128)(2,1)} %copy-done.1, bf16[4,384,256]{2,1,0:T(8,128)(2,1)} %constant_dynamic-slice_fusion.refs_2_, bf16[4,384,256]{2,1,0:T(8,128)(2,1)} %copy-done.4, ...), custom_call_target="tpu_custom_call" | custom-call | flops 1811939328 | bytes 8257536 | tf_op jit(solution)/shard_map/linear/pallas_call | solution.py:57
  61.8 5.2 %linear.3 = (f32[192,1024]{1,0:T(8,128)}, f32[192,1024]{1,0:T(8,128)}) custom-call(bf16[2,192,3072]{2,1,0:T(8,128)(2,1)} %get-tuple-element.22.refs_1_.own.refs_0_, bf16[2,192,3072]{2,1,0:T(8,128)(2,1)} %copy-done.1, bf16[4,384,256]{2,1,0:T(8,128)(2,1)} %copy-done.9, bf16[4,384,256]{2,1,0:T(8,128)(2,1)} %copy-done.10, ...), custom_call_target="tpu_custom_call" | custom-call | flops 603979776 | bytes 2752512 | tf_op jit(solution)/shard_map/linear/pallas_call | solution.py:57
  67.6 2.1 %collective-permute-done.8.theirs = f32[192,1024]{1,0:T(8,128)S(1)} collective-permute-done((f32[192,1024]{1,0:T(8,128)}, f32[192,1024]{1,0:T(8,128)S(1)}, u32[]{:S(2)}, u32[]{:S(2)}) %collective-permute-start.8) | collective-permute-done | bytes 786464 | tf_op jit(solution)/shard_map/ppermute | solution.py:33
  70.6 4.8 %attend.1.y_own.refs_0_ = bf16[192,1024]{1,0:T(8,128)(2,1)} custom-call(s32[3]{0:T(128)} %pad_add_fusion.refs_11_.ends, f32[192,1024]{1,0:T(8,128)} %get-tuple-element.26.mine, f32[192,1024]{1,0:T(8,128)} %copy-done.19, f32[192,128]{1,0:T(8,128)} %get-tuple-element.56.refs_9_.cos_t, f32[192,128]{1,0:T(8,128)} %get-tuple-element.57.refs_10_.sin_t), custom_call_target="tpu_custom_call" | custom-call | flops 188743680 | bytes 1966080 | tf_op jit(solution)/shard_map/attend/pallas_call | solution.py:57
  78.0 4.4 %terms.5 = (bf16[4,8,96,128]{3,2,1,0:T(8,128)(2,1)}, bf16[4,8,96,128]{3,2,1,0:T(8,128)(2,1)}) custom-call(bf16[2,4,2,4,96,384]{5,4,3,2,1,0:T(8,128)(2,1)} %flip.1.refs_8_.turned, bf16[192,1024]{1,0:T(8,128)(2,1)} %attend.1.y_own.refs_0_, bf16[192,1024]{1,0:T(8,128)(2,1)} %copy-done.5), custom_call_target="tpu_custom_call" | custom-call | flops 603979776 | bytes 3932160 | tf_op jit(solution)/shard_map/terms/pallas_call | solution.py:57
  84.2 4.4 %terms.4 = (bf16[4,8,96,128]{3,2,1,0:T(8,128)(2,1)}, bf16[4,8,96,128]{3,2,1,0:T(8,128)(2,1)}) custom-call(bf16[2,4,2,4,96,384]{5,4,3,2,1,0:T(8,128)(2,1)} %flip.1.refs_8_.turned, bf16[192,1024]{1,0:T(8,128)(2,1)} %attend.1.y_own.refs_0_, bf16[192,1024]{1,0:T(8,128)(2,1)} %copy-done.5), custom_call_target="tpu_custom_call" | custom-call | flops 603979776 | bytes 3932160 | tf_op jit(solution)/shard_map/terms/pallas_call | solution.py:57
  88.6 2.7 %collective-permute-start.10 = (bf16[4,8,96,128]{3,2,1,0:T(8,128)(2,1)}, bf16[4,8,96,128]{3,2,1,0:T(8,128)(2,1)S(1)}, u32[]{:S(2)}, u32[]{:S(2)}) collective-permute-start(bf16[4,8,96,128]{3,2,1,0:T(8,128)(2,1)} %get-tuple-element.32), channel_id=1, source_target_pairs={{0,6},{8,137},{16,22},{24,153},{32,38},{40,169},{48,54},{56,185},{... | collective-permute-start | bytes 2359304 | tf_op jit(solution)/shard_map/ppermute | solution.py:33
  91.3 5.2 %terms.3 = (bf16[4,8,96,128]{3,2,1,0:T(8,128)(2,1)}, bf16[4,8,96,128]{3,2,1,0:T(8,128)(2,1)}, bf16[4,8,96,128]{3,2,1,0:T(8,128)(2,1)}, bf16[4,8,96,128]{3,2,1,0:T(8,128)(2,1)}) custom-call(bf16[2,4,2,4,96,384]{5,4,3,2,1,0:T(8,128)(2,1)} %flip.1.refs_8_.turned, bf16[192,1024]{1,0:T(8,128)(2,1)} %attend.1.y_own.refs_0_, bf16[192,1024]{1,0:T(8,128)(2,1)} %copy-done.5), custom_call_target="tpu_custom_call" | custom-call | flops 1207959552 | bytes 7864320 | tf_op jit(solution)/shard_map/terms/pallas_call | solution.py:57
  96.5 7.8 %normed_grad.1 = (f32[192,3072]{1,0:T(8,128)}, f32[192,3072]{1,0:T(8,128)}) custom-call(bf16[192,1024]{1,0:T(8,128)(2,1)} %attend.1.y_own.refs_0_, bf16[192,1024]{1,0:T(8,128)(2,1)} %copy-done.5, bf16[4,384,256]{2,1,0:T(8,128)(2,1)} %constant_dynamic-slice_fusion.refs_2_, bf16[4,384,256]{2,1,0:T(8,128)(2,1)} %copy-done.4, ...), custom_call_target="tpu_custom_call" | custom-call | flops 1811939328 | bytes 11010048 | tf_op jit(solution)/shard_map/normed_grad/pallas_call | solution.py:57
  105.2 2.5 %join.3 = bf16[4,8,96,128]{3,2,1,0:T(8,128)(2,1)} custom-call(bf16[4,8,96,128]{3,2,1,0:T(8,128)(2,1)} %get-tuple-element.36.refs_0_, bf16[4,8,96,128]{3,2,1,0:T(8,128)(2,1)} %copy-done.15, f32[192,3072]{1,0:T(8,128)} %get-tuple-element.30.refs_2_.refs_0_), custom_call_target="tpu_custom_call" | custom-call | flops 786432 | bytes 3145728 | tf_op jit(solution)/shard_map/join/pallas_call | solution.py:57
  107.6 2.7 %collective-permute-start.15 = (bf16[4,8,96,128]{3,2,1,0:T(8,128)(2,1)}, bf16[4,8,96,128]{3,2,1,0:T(8,128)(2,1)S(1)}, u32[]{:S(2)}, u32[]{:S(2)}) collective-permute-start(bf16[4,8,96,128]{3,2,1,0:T(8,128)(2,1)} %join.3), channel_id=1, source_target_pairs={{0,6},{8,137},{16,22},{24,153},{32,38},{40,169},{48,54},{56,185},{... | collective-permute-start | bytes 2359304 | tf_op jit(solution)/shard_map/ppermute | solution.py:33
  111.2 2.4 %join.2 = bf16[4,8,96,128]{3,2,1,0:T(8,128)(2,1)} custom-call(bf16[4,8,96,128]{3,2,1,0:T(8,128)(2,1)} %get-tuple-element.28.refs_10_.refs_0_, bf16[4,8,96,128]{3,2,1,0:T(8,128)(2,1)} %copy-done.14, f32[192,3072]{1,0:T(8,128)} %get-tuple-element.30.refs_2_.refs_0_), custom_call_target="tpu_custom_call" | custom-call | flops 786432 | bytes 3145728 | tf_op jit(solution)/shard_map/join/pallas_call | solution.py:57
  113.6 5.9 %collective-permute-done.15.refs_5_ = bf16[4,8,96,128]{3,2,1,0:T(8,128)(2,1)S(1)} collective-permute-done((bf16[4,8,96,128]{3,2,1,0:T(8,128)(2,1)}, bf16[4,8,96,128]{3,2,1,0:T(8,128)(2,1)S(1)}, u32[]{:S(2)}, u32[]{:S(2)}) %collective-permute-start.15) | collective-permute-done | bytes 786464 | tf_op jit(solution)/shard_map/ppermute | solution.py:33
  119.5 6.6 %collective-permute-done.12.refs_2_ = bf16[4,8,96,128]{3,2,1,0:T(8,128)(2,1)S(1)} collective-permute-done((bf16[4,8,96,128]{3,2,1,0:T(8,128)(2,1)}, bf16[4,8,96,128]{3,2,1,0:T(8,128)(2,1)S(1)}, u32[]{:S(2)}, u32[]{:S(2)}) %collective-permute-start.12) | collective-permute-done | bytes 786464 | tf_op jit(solution)/shard_map/ppermute | solution.py:33
  127.1 3.8 %sides.1 = (bf16[8,2,96,128]{3,2,1,0:T(8,128)(2,1)}, bf16[8,2,96,128]{3,2,1,0:T(8,128)(2,1)}, bf16[8,2,96,128]{3,2,1,0:T(8,128)(2,1)}, bf16[8,2,96,128]{3,2,1,0:T(8,128)(2,1)}) custom-call(bf16[4,8,96,128]{3,2,1,0:T(8,128)(2,1)} %get-tuple-element.31.refs_0_, bf16[4,8,96,128]{3,2,1,0:T(8,128)(2,1)} %copy-done.12, bf16[4,8,96,128]{3,2,1,0:T(8,128)(2,1)} %copy-done.17, ...), custom_call_target="tpu_custom_call" | custom-call | flops 2359296 | bytes 6291456 | tf_op jit(solution)/shard_map/sides/pallas_call | solution.py:57
  130.8 3.9 %collective-permute-start.16 = (f32[192,3072]{1,0:T(8,128)}, f32[192,3072]{1,0:T(8,128)S(1)}, u32[]{:S(2)}, u32[]{:S(2)}) collective-permute-start(f32[192,3072]{1,0:T(8,128)} %gate.5), channel_id=1, source_target_pairs={{0,8},{8,0},{16,24},{24,16},{32,40},{40,32},{48,56},{56,48},{64,72... | collective-permute-start | bytes 7077896 | tf_op jit(solution)/shard_map/ppermute | solution.py:33
  135.3 2.2 %collective-permute-start.19 = (bf16[8,2,96,128]{3,2,1,0:T(8,128)(2,1)S(1)}, bf16[8,2,96,128]{3,2,1,0:T(8,128)(2,1)S(1)}, u32[]{:S(2)}, u32[]{:S(2)}) collective-permute-start(bf16[8,2,96,128]{3,2,1,0:T(8,128)(2,1)S(1)} %copy-done.25), channel_id=1, source_target_pairs={{0,129},{8,14},{16,145},{24,30},{32,161},{40,46},{48,177},{56,62},... | collective-permute-start | bytes 1179656 | tf_op jit(solution)/shard_map/ppermute | solution.py:33
  140.5 10.2 %token_grad.1.refs_4_ = bf16[192,6144]{1,0:T(8,128)(2,1)} custom-call(s32[20]{0:T(128)} %stack.92.info, bf16[192,6144]{1,0:T(8,128)(2,1)} %tokens.3, f32[192,3072]{1,0:T(8,128)} %get-tuple-element.29.g_own, f32[192,3072]{1,0:T(8,128)} %copy-done.11), custom_call_target="tpu_custom_call" | custom-call | flops 18874368 | bytes 9437184 | tf_op jit(solution)/shard_map/token_grad/pallas_call | solution.py:57
  152.4 2.3 %seconds.1 = bf16[8,2,96,128]{3,2,1,0:T(8,128)(2,1)} custom-call(bf16[8,2,96,128]{3,2,1,0:T(8,128)(2,1)} %get-tuple-element.38.refs_1_.refs_0_, bf16[8,2,96,128]{3,2,1,0:T(8,128)(2,1)} %copy-done.20, bf16[8,2,96,128]{3,2,1,0:T(8,128)(2,1)} %copy-done.21, bf16[8,2,96,128]{3,2,1,0:T(8,128)(2,1)} %copy-done.22, bf16[192,6144]{1,0:T(8,128)(2,1)} %token_grad.1.refs_4_), custom_call_target="tpu_custom_call" | custom-call | flops 786432 | bytes 2359296 | tf_op jit(solution)/shard_map/seconds/pallas_call | solution.py:57
  154.7 20.5 %all_to_all.10.got = bf16[8,2,96,128]{3,2,1,0:T(8,128)(2,1)} all-to-all(bf16[8,2,96,128]{3,2,1,0:T(8,128)(2,1)} %seconds.1), channel_id=1, replica_groups={{0,16,32,48,64,80,96,112},{8,24,40,56,72,88,104,120},{128,144,160,176,1..., dimensions={0} | all-to-all | bytes 786432 | tf_op jit(solution)/shard_map/all_to_all | solution.py:328
  175.2 2.0 last.1
  177.2 25.2 %all_to_all.11 = bf16[16,2,96,128]{3,2,1,0:T(8,128)(2,1)S(1)} all-to-all(bf16[16,2,96,128]{3,2,1,0:T(8,128)(2,1)} %last.1), channel_id=1, replica_groups={{0,16,32,48,64,80,96,112,128,144,160,176,192,208,224,240},{8,24,40,56,7..., dimensions={0} | all-to-all | bytes 1572864 | tf_op jit(solution)/shard_map/all_to_all | solution.py:328
  202.3 2.7 %collective-permute-start.20 = (bf16[2,8,2,96,128]{4,3,2,1,0:T(8,128)(2,1)S(1)}, bf16[2,8,2,96,128]{4,3,2,1,0:T(8,128)(2,1)S(1)}, u32[]{:S(2)}, u32[]{:S(2)}) collective-permute-start(bf16[2,8,2,96,128]{4,3,2,1,0:T(8,128)(2,1)S(1)} %bitcast.26), channel_id=1, source_target_pairs={{0,8},{8,0},{16,24},{24,16},{32,40},{40,32},{48,56},{56,48},{64,72... | collective-permute-start | bytes 2359304 | tf_op jit(solution)/shard_map/ppermute | solution.py:33
  205.1 1.9 collective-permute-done.20.other
  207.9 3.2 %place.1 = f32[4,768,256]{2,1,0:T(8,128)} custom-call(s32[20]{0:T(128)} %stack.92.info, bf16[2,8,2,96,128]{4,3,2,1,0:T(8,128)(2,1)} %bitcast.27, bf16[2,8,2,96,128]{4,3,2,1,0:T(8,128)(2,1)} %copy-done.18), custom_call_target="tpu_custom_call" | custom-call | flops 786432 | bytes 4718592 | tf_op jit(solution)/shard_map/place/pallas_call | solution.py:57
  (93 shorter events, 28.9 us)
Async XLA Ops:
  0.6 1.4 copy-start
  3.0 15.3 %collective-permute-start.1 = (bf16[4,384,256]{2,1,0:T(8,128)(2,1)}, bf16[4,384,256]{2,1,0:T(8,128)(2,1)S(1)}, u32[]{:S(2)}, u32[]{:S(2)}) collective-permute-start(bf16[4,384,256]{2,1,0:T(8,128)(2,1)} %constant_dynamic-slice_fusion.refs_2_), channel_id=1, source_target_pairs={{0,1},{8,137},{16,17},{24,153},{32,33},{40,169},{48,49},{56,185},{... | collective-permute-start | bytes 2359304 | tf_op jit(solution)/shard_map/ppermute | solution.py:33
  6.3 19.8 %collective-permute-start = (bf16[4,384,256]{2,1,0:T(8,128)(2,1)}, bf16[4,384,256]{2,1,0:T(8,128)(2,1)S(1)}, u32[]{:S(2)}, u32[]{:S(2)}) collective-permute-start(bf16[4,384,256]{2,1,0:T(8,128)(2,1)} %constant_dynamic-slice_fusion.refs_2_), channel_id=1, source_target_pairs={{0,2},{8,14},{16,18},{24,30},{32,34},{40,46},{48,50},{56,62},{64,6... | collective-permute-start | bytes 2359304 | tf_op jit(solution)/shard_map/ppermute | solution.py:33
  9.0 18.5 %collective-permute-start.2 = (bf16[4,384,256]{2,1,0:T(8,128)(2,1)}, bf16[4,384,256]{2,1,0:T(8,128)(2,1)}, u32[]{:S(2)}, u32[]{:S(2)}) collective-permute-start(bf16[4,384,256]{2,1,0:T(8,128)(2,1)} %constant_dynamic-slice_fusion.refs_2_), channel_id=1, source_target_pairs={{0,6},{8,10},{16,22},{24,26},{32,38},{40,42},{48,54},{56,58},{64,7... | collective-permute-start | bytes 2359304 | tf_op jit(solution)/shard_map/ppermute | solution.py:33
  18.2 7.9 %copy-start.4 = (bf16[4,384,256]{2,1,0:T(8,128)(2,1)}, bf16[4,384,256]{2,1,0:T(8,128)(2,1)S(1)}, u32[]{:S(2)}) copy-start(bf16[4,384,256]{2,1,0:T(8,128)(2,1)S(1)} %collective-permute-done.1.refs_2_.refs_3_) | copy-start | bytes 2359300
  27.5 4.5 %copy-start.23 = (s32[1,3]{1,0:T(1,128)S(1)}, s32[1,3]{1,0:T(1,128)}, u32[]{:S(2)}) copy-start(s32[1,3]{1,0:T(1,128)} %param.7) | copy-start | bytes 40
  27.5 16.5 %copy-start.24 = (s32[2,192]{1,0:T(2,128)S(1)}, s32[2,192]{1,0:T(2,128)}, u32[]{:S(2)}) copy-start(s32[2,192]{1,0:T(2,128)} %param.8) | copy-start | bytes 4612
  27.5 18.1 %collective-permute-start.3 = (bf16[2,192,3072]{2,1,0:T(8,128)(2,1)}, bf16[2,192,3072]{2,1,0:T(8,128)(2,1)S(1)}, u32[]{:S(2)}, u32[]{:S(2)}) collective-permute-start(bf16[2,192,3072]{2,1,0:T(8,128)(2,1)} %gate.4), channel_id=1, source_target_pairs={{0,8},{8,0},{16,24},{24,16},{32,40},{40,32},{48,56},{56,48},{64,72... | collective-permute-start | bytes 7077896 | tf_op jit(solution)/shard_map/ppermute | solution.py:33
  28.6 12.3 %collective-permute-start.5 = (bf16[4,384,256]{2,1,0:T(8,128)(2,1)S(1)}, bf16[4,384,256]{2,1,0:T(8,128)(2,1)S(1)}, u32[]{:S(2)}, u32[]{:S(2)}) collective-permute-start(bf16[4,384,256]{2,1,0:T(8,128)(2,1)S(1)} %copy-done.3), channel_id=1, source_target_pairs={{0,1},{8,137},{16,17},{24,153},{32,33},{40,169},{48,49},{56,185},{... | collective-permute-start | bytes 2359304 | tf_op jit(solution)/shard_map/ppermute | solution.py:33
  34.5 18.4 %collective-permute-start.7 = (bf16[4,384,256]{2,1,0:T(8,128)(2,1)S(1)}, bf16[4,384,256]{2,1,0:T(8,128)(2,1)S(1)}, u32[]{:S(2)}, u32[]{:S(2)}) collective-permute-start(bf16[4,384,256]{2,1,0:T(8,128)(2,1)S(1)} %copy-done.3), channel_id=1, source_target_pairs={{0,2},{8,14},{16,18},{24,30},{32,34},{40,46},{48,50},{56,62},{64,6... | collective-permute-start | bytes 2359304 | tf_op jit(solution)/shard_map/ppermute | solution.py:33
  34.6 26.0 %collective-permute-start.4 = (bf16[4,384,256]{2,1,0:T(8,128)(2,1)}, bf16[4,384,256]{2,1,0:T(8,128)(2,1)S(1)}, u32[]{:S(2)}, u32[]{:S(2)}) collective-permute-start(bf16[4,384,256]{2,1,0:T(8,128)(2,1)} %collective-permute-done.2.refs_2_.refs_6_), channel_id=1, source_target_pairs={{0,1},{8,137},{16,17},{24,153},{32,33},{40,169},{48,49},{56,185},{... | collective-permute-start | bytes 2359304 | tf_op jit(solution)/shard_map/ppermute | solution.py:33
  40.9 12.0 %copy-start.7 = (bf16[4,384,256]{2,1,0:T(8,128)(2,1)}, bf16[4,384,256]{2,1,0:T(8,128)(2,1)S(1)}, u32[]{:S(2)}) copy-start(bf16[4,384,256]{2,1,0:T(8,128)(2,1)S(1)} %collective-permute-done.5.refs_5_) | copy-start | bytes 2359300
  40.9 19.8 %collective-permute-start.6 = (bf16[4,384,256]{2,1,0:T(8,128)(2,1)S(1)}, bf16[4,384,256]{2,1,0:T(8,128)(2,1)S(1)}, u32[]{:S(2)}, u32[]{:S(2)}) collective-permute-start(bf16[4,384,256]{2,1,0:T(8,128)(2,1)S(1)} %collective-permute-done.5.refs_5_), channel_id=1, source_target_pairs={{0,2},{8,14},{16,18},{24,30},{32,34},{40,46},{48,50},{56,62},{64,6... | collective-permute-start | bytes 2359304 | tf_op jit(solution)/shard_map/ppermute | solution.py:33
  67.0 2.6 %collective-permute-start.8 = (f32[192,1024]{1,0:T(8,128)}, f32[192,1024]{1,0:T(8,128)S(1)}, u32[]{:S(2)}, u32[]{:S(2)}) collective-permute-start(f32[192,1024]{1,0:T(8,128)} %get-tuple-element.27), channel_id=1, source_target_pairs={{0,8},{8,0},{16,24},{24,16},{32,40},{40,32},{48,56},{56,48},{64,72... | collective-permute-start | bytes 2359304 | tf_op jit(solution)/shard_map/ppermute | solution.py:33
  75.3 1.9 collective-permute-start.9
  82.4 21.8 %collective-permute-start.14 = (bf16[4,8,96,128]{3,2,1,0:T(8,128)(2,1)}, bf16[4,8,96,128]{3,2,1,0:T(8,128)(2,1)S(1)}, u32[]{:S(2)}, u32[]{:S(2)}) collective-permute-start(bf16[4,8,96,128]{3,2,1,0:T(8,128)(2,1)} %get-tuple-element.37), channel_id=1, source_target_pairs={{0,6},{8,137},{16,22},{24,153},{32,38},{40,169},{48,54},{56,185},{... | collective-permute-start | bytes 2359304 | tf_op jit(solution)/shard_map/ppermute | solution.py:33
  84.2 26.1 %collective-permute-start.11 = (bf16[4,8,96,128]{3,2,1,0:T(8,128)(2,1)}, bf16[4,8,96,128]{3,2,1,0:T(8,128)(2,1)S(1)}, u32[]{:S(2)}, u32[]{:S(2)}) collective-permute-start(bf16[4,8,96,128]{3,2,1,0:T(8,128)(2,1)} %get-tuple-element.33), channel_id=1, source_target_pairs={{0,2},{8,9},{16,18},{24,25},{32,34},{40,41},{48,50},{56,57},{64,66... | collective-permute-start | bytes 2359304 | tf_op jit(solution)/shard_map/ppermute | solution.py:33
  88.6 25.0 %collective-permute-start.10 = (bf16[4,8,96,128]{3,2,1,0:T(8,128)(2,1)}, bf16[4,8,96,128]{3,2,1,0:T(8,128)(2,1)S(1)}, u32[]{:S(2)}, u32[]{:S(2)}) collective-permute-start(bf16[4,8,96,128]{3,2,1,0:T(8,128)(2,1)} %get-tuple-element.32), channel_id=1, source_target_pairs={{0,6},{8,137},{16,22},{24,153},{32,38},{40,169},{48,54},{56,185},{... | collective-permute-start | bytes 2359304 | tf_op jit(solution)/shard_map/ppermute | solution.py:33
  91.3 22.3 %collective-permute-start.13 = (bf16[4,8,96,128]{3,2,1,0:T(8,128)(2,1)}, bf16[4,8,96,128]{3,2,1,0:T(8,128)(2,1)S(1)}, u32[]{:S(2)}, u32[]{:S(2)}) collective-permute-start(bf16[4,8,96,128]{3,2,1,0:T(8,128)(2,1)} %get-tuple-element.35), channel_id=1, source_target_pairs={{0,2},{8,9},{16,18},{24,25},{32,34},{40,41},{48,50},{56,57},{64,66... | collective-permute-start | bytes 2359304 | tf_op jit(solution)/shard_map/ppermute | solution.py:33
  107.6 11.9 %collective-permute-start.15 = (bf16[4,8,96,128]{3,2,1,0:T(8,128)(2,1)}, bf16[4,8,96,128]{3,2,1,0:T(8,128)(2,1)S(1)}, u32[]{:S(2)}, u32[]{:S(2)}) collective-permute-start(bf16[4,8,96,128]{3,2,1,0:T(8,128)(2,1)} %join.3), channel_id=1, source_target_pairs={{0,6},{8,137},{16,22},{24,153},{32,38},{40,169},{48,54},{56,185},{... | collective-permute-start | bytes 2359304 | tf_op jit(solution)/shard_map/ppermute | solution.py:33
  113.6 12.6 %collective-permute-start.12 = (bf16[4,8,96,128]{3,2,1,0:T(8,128)(2,1)}, bf16[4,8,96,128]{3,2,1,0:T(8,128)(2,1)S(1)}, u32[]{:S(2)}, u32[]{:S(2)}) collective-permute-start(bf16[4,8,96,128]{3,2,1,0:T(8,128)(2,1)} %join.2), channel_id=1, source_target_pairs={{0,2},{8,9},{16,18},{24,25},{32,34},{40,41},{48,50},{56,57},{64,66... | collective-permute-start | bytes 2359304 | tf_op jit(solution)/shard_map/ppermute | solution.py:33
  113.6 12.6 %copy-start.12 = (bf16[4,8,96,128]{3,2,1,0:T(8,128)(2,1)}, bf16[4,8,96,128]{3,2,1,0:T(8,128)(2,1)S(1)}, u32[]{:S(2)}) copy-start(bf16[4,8,96,128]{3,2,1,0:T(8,128)(2,1)S(1)} %collective-permute-done.10.refs_1_) | copy-start | bytes 2359300
  113.6 12.5 %copy-start.13 = (bf16[4,8,96,128]{3,2,1,0:T(8,128)(2,1)}, bf16[4,8,96,128]{3,2,1,0:T(8,128)(2,1)S(1)}, u32[]{:S(2)}) copy-start(bf16[4,8,96,128]{3,2,1,0:T(8,128)(2,1)S(1)} %collective-permute-done.13.refs_4_) | copy-start | bytes 2359300
  119.5 6.6 %copy-start.16 = (bf16[4,8,96,128]{3,2,1,0:T(8,128)(2,1)}, bf16[4,8,96,128]{3,2,1,0:T(8,128)(2,1)S(1)}, u32[]{:S(2)}) copy-start(bf16[4,8,96,128]{3,2,1,0:T(8,128)(2,1)S(1)} %collective-permute-done.15.refs_5_) | copy-start | bytes 2359300
  130.8 3.9 %copy-start.26 = (bf16[8,2,96,128]{3,2,1,0:T(8,128)(2,1)S(1)}, bf16[8,2,96,128]{3,2,1,0:T(8,128)(2,1)}, u32[]{:S(2)}) copy-start(bf16[8,2,96,128]{3,2,1,0:T(8,128)(2,1)} %get-tuple-element.40) | copy-start | bytes 1179652
  130.8 4.5 %copy-start.25 = (bf16[8,2,96,128]{3,2,1,0:T(8,128)(2,1)S(1)}, bf16[8,2,96,128]{3,2,1,0:T(8,128)(2,1)}, u32[]{:S(2)}) copy-start(bf16[8,2,96,128]{3,2,1,0:T(8,128)(2,1)} %get-tuple-element.41) | copy-start | bytes 1179652
  130.8 8.3 %collective-permute-start.16 = (f32[192,3072]{1,0:T(8,128)}, f32[192,3072]{1,0:T(8,128)S(1)}, u32[]{:S(2)}, u32[]{:S(2)}) collective-permute-start(f32[192,3072]{1,0:T(8,128)} %gate.5), channel_id=1, source_target_pairs={{0,8},{8,0},{16,24},{24,16},{32,40},{40,32},{48,56},{56,48},{64,72... | collective-permute-start | bytes 7077896 | tf_op jit(solution)/shard_map/ppermute | solution.py:33
  134.7 16.0 %collective-permute-start.17 = (bf16[8,2,96,128]{3,2,1,0:T(8,128)(2,1)}, bf16[8,2,96,128]{3,2,1,0:T(8,128)(2,1)S(1)}, u32[]{:S(2)}, u32[]{:S(2)}) collective-permute-start(bf16[8,2,96,128]{3,2,1,0:T(8,128)(2,1)} %get-tuple-element.39), channel_id=1, source_target_pairs={{0,1},{8,10},{16,17},{24,26},{32,33},{40,42},{48,49},{56,58},{64,6... | collective-permute-start | bytes 1179656 | tf_op jit(solution)/shard_map/ppermute | solution.py:33
  134.8 16.0 %collective-permute-start.18 = (bf16[8,2,96,128]{3,2,1,0:T(8,128)(2,1)S(1)}, bf16[8,2,96,128]{3,2,1,0:T(8,128)(2,1)S(1)}, u32[]{:S(2)}, u32[]{:S(2)}) collective-permute-start(bf16[8,2,96,128]{3,2,1,0:T(8,128)(2,1)S(1)} %copy-done.26), channel_id=1, source_target_pairs={{0,128},{8,12},{16,144},{24,28},{32,160},{40,44},{48,176},{56,60},... | collective-permute-start | bytes 1179656 | tf_op jit(solution)/shard_map/ppermute | solution.py:33
  135.3 15.5 %collective-permute-start.19 = (bf16[8,2,96,128]{3,2,1,0:T(8,128)(2,1)S(1)}, bf16[8,2,96,128]{3,2,1,0:T(8,128)(2,1)S(1)}, u32[]{:S(2)}, u32[]{:S(2)}) collective-permute-start(bf16[8,2,96,128]{3,2,1,0:T(8,128)(2,1)S(1)} %copy-done.25), channel_id=1, source_target_pairs={{0,129},{8,14},{16,145},{24,30},{32,161},{40,46},{48,177},{56,62},... | collective-permute-start | bytes 1179656 | tf_op jit(solution)/shard_map/ppermute | solution.py:33
  202.3 4.7 %copy-start.6 = (bf16[16,2,96,128]{3,2,1,0:T(8,128)(2,1)}, bf16[16,2,96,128]{3,2,1,0:T(8,128)(2,1)S(1)}, u32[]{:S(2)}) copy-start(bf16[16,2,96,128]{3,2,1,0:T(8,128)(2,1)S(1)} %all_to_all.11) | copy-start | bytes 2359300
  202.3 4.7 %collective-permute-start.20 = (bf16[2,8,2,96,128]{4,3,2,1,0:T(8,128)(2,1)S(1)}, bf16[2,8,2,96,128]{4,3,2,1,0:T(8,128)(2,1)S(1)}, u32[]{:S(2)}, u32[]{:S(2)}) collective-permute-start(bf16[2,8,2,96,128]{4,3,2,1,0:T(8,128)(2,1)S(1)} %bitcast.26), channel_id=1, source_target_pairs={{0,8},{8,0},{16,24},{24,16},{32,40},{40,32},{48,56},{56,48},{64,72... | collective-permute-start | bytes 2359304 | tf_op jit(solution)/shard_map/ppermute | solution.py:33
  (16 other events, 15.3 us)
where the time goes:
time: 212 us; the launch traced here: 211 us
  Pallas kernels  79.5 us (38%)
  blocking collectives  45.7 us (22%)
  waiting for transfers between devices  34.3 us (16%)
  starting transfers between devices  28.9 us (14%)
  local copies, waits for them, and re-layouts  17.1 us (8%)
  other arithmetic  2.9 us (1%)
  between operations  2.74 us (1%)
    pallas_call x16, Pallas kernels, call(): pl.pallas_call(kernel, out_shape=out_shapes, in_specs=specs, out_specs=ja...  79.5 us
    all_to_all x2, blocking collectives, exchange(): lax.all_to_all(values, 'dp', split_axis=0, concat_axis=0, axis_index_grou...  45.7 us
    ppermute x21, waiting for transfers between devices, permute(): return lax.ppermute(values, ('dp', 'fsdp'), pairs)  34.3 us
    ppermute x21, starting transfers between devices, permute(): return lax.ppermute(values, ('dp', 'fsdp'), pairs)  28.9 us
    unnamed x54, local copies, waits for them, and re-layouts  14.9 us
  transfers between devices with their start and end apart: 21, of which 9 were waited for; matrix products, arithmetic and copies ran while one was open for 2% of the time, Pallas kernels for 26%

commit v1 on v0

--- a/solution.py
+++ b/solution.py
@@ -49,21 +49,36 @@
     return permute(values, target)
 
 
-def call(body, out_shapes, operands, scalars=0, scratch=(), flops=0, nbytes=0, name=None, after=()):
+def call(body, outs, operands, grid=(), scalars=0, scratch=(), flops=0, nbytes=0, name=None, after=()):
     count, last = len(operands), len(operands) + len(after)
-    specs = [pl.BlockSpec(memory_space=pltpu.SMEM if i < scalars else pltpu.VMEM) for i in range(count)]
-    specs += [pl.BlockSpec(memory_space=pl.ANY) for _ in after]
+    held = 0
+    arrays, in_specs, out_shapes, out_specs = [], [], [], []
+    for k, item in enumerate(list(operands) + list(outs)):
+        value, *place = item if isinstance(item, tuple) else (item,)
+        if k < scalars:
+            spec = pl.BlockSpec(memory_space=pltpu.SMEM)
+        elif place:
+            spec = pl.BlockSpec(place[0], place[1])
+            held += 2 * math.prod(place[0]) * value.dtype.itemsize
+        else:
+            spec = pl.BlockSpec(memory_space=pltpu.VMEM)
+            held += math.prod(value.shape) * value.dtype.itemsize
+        (arrays if k < count else out_shapes).append(value)
+        (in_specs if k < count else out_specs).append(spec)
+    held += sum(math.prod(ref.shape) * ref.dtype.itemsize for ref in scratch)
+    in_specs += [pl.BlockSpec(memory_space=pl.ANY) for _ in after]
     kernel = (lambda *refs: body(*refs[:count], *refs[last:])) if after else body
     return pl.pallas_call(
         kernel,
+        grid=grid or (1,),
         out_shape=out_shapes,
-        in_specs=specs,
-        out_specs=jax.tree.map(lambda _: pl.BlockSpec(memory_space=pltpu.VMEM), out_shapes),
+        in_specs=in_specs,
+        out_specs=out_specs,
         scratch_shapes=list(scratch),
-        compiler_params=pltpu.CompilerParams(vmem_limit_bytes=56 * 1024 * 1024),
+        compiler_params=pltpu.CompilerParams(vmem_limit_bytes=held + 8 * 1024 * 1024),
         cost_estimate=pl.CostEstimate(flops=flops, bytes_accessed=nbytes, transcendentals=0),
         name=name,
-    )(*operands, *after)
+    )(*arrays, *after)
 
 
 def gate(value, after):
@@ -85,16 +100,12 @@
 def prep_kernel(width, info, tokens, cot, own, send, normed):
     rows, model = tokens.shape
     step = 16
-
-    def body(i, carry):
-        at = pl.ds(pl.multiple_of(i * step, step), step)
+    for i in range(rows // step):
+        at = slice(i * step, (i + 1) * step)
         x = tokens[at, :].astype(F32)
         center = x - jnp.sum(x, axis=1, keepdims=True) / model
         var = jnp.sum(center * center, axis=1, keepdims=True) / model
         normed[at, :] = (center * lax.rsqrt(var + EPS)).astype(BF16)
-        return carry
-
-    lax.fori_loop(0, rows // step, body, 0)
     for j in range(8):
         to = slice(j * width, (j + 1) * width)
         for out, first in ((own, 0), (send, 8)):
@@ -110,33 +121,29 @@
     for j, (k, dx) in enumerate(ORDER):
         at = slice(j * width, (j + 1) * width)
         y_steps = lax.rem(4 - sign * k, 4)
-        for i in range(2):
-            turned = jnp.concatenate([own[i, :, at], peer[i, :, at]], axis=0).T
-            for x_hi in range(2):
-                x_to = 2 * x_hi + lax.rem(info[X_LO] + dx, 2)
-                x_steps = lax.rem(x_to - x_at + 4, 4)
-                first = jnp.where(core == 0, y_steps, x_steps)
-                second = jnp.where(core == 0, x_steps, y_steps)
-                for side in range(2):
-                    steps = first if side == 0 else lax.rem(4 - first, 4)
-                    start = x_hi * half + side * quarter
-                    out[side, steps, i, second] = turned[start : start + quarter]
-
-
-def linear_kernel(width, first, pairs, own, peer, *refs):
+        turned = jnp.concatenate([own[0, :, at], peer[0, :, at]], axis=0).T
+        for x_hi in range(2):
+            x_to = 2 * x_hi + lax.rem(info[X_LO] + dx, 2)
+            x_steps = lax.rem(x_to - x_at + 4, 4)
+            first = jnp.where(core == 0, y_steps, x_steps)
+            second = jnp.where(core == 0, x_steps, y_steps)
+            for side in range(2):
+                steps = first if side == 0 else lax.rem(4 - first, 4)
+                start = x_hi * half + side * quarter
+                out[side, steps, 0, second] = turned[start : start + quarter]
+
+
+def linear_kernel(pairs, own, peer, *refs):
     shards, rest = refs[: 2 * pairs], refs[2 * pairs :]
     before, outs = rest[:-2], rest[-2:]
-    cols = shards[0].shape[2]
-    for m in range(4):
-        to = slice(m * cols, (m + 1) * cols)
-        rights = [jnp.concatenate([shards[2 * p][m], shards[2 * p + 1][m]], axis=0) for p in range(pairs)]
-        for side, left in enumerate((own, peer)):
-            total = before[side][:, to] if before else None
-            for p, right in enumerate(rights):
-                at = slice(2 * (first + p) * width, 2 * (first + p + 1) * width)
-                term = jnp.dot(left[m // 3, :, at], right, preferred_element_type=F32)
-                total = term if total is None else total + term
-            outs[side][:, to] = total
+    depth = own.shape[2] // pairs
+    rights = [jnp.concatenate([shards[2 * p][0], shards[2 * p + 1][0]], axis=0) for p in range(pairs)]
+    for side, left in enumerate((own, peer)):
+        total = before[side][...] if before else None
+        for p, right in enumerate(rights):
+            term = jnp.dot(left[0, :, p * depth : (p + 1) * depth], right, preferred_element_type=F32)
+            total = term if total is None else total + term
+        outs[side][...] = total
 
 
 def swap_quarters(x):
@@ -214,14 +221,15 @@
         out[:, at(3)] = jnp.where(live, att.astype(F32), 0.0).astype(BF16)
 
 
-def terms_kernel(steps, turned, y_own, y_peer, *outs):
-    rows, depth = turned.shape[4:]
+def terms_kernel(count, *refs):
+    turned, (y_own, y_peer), outs = refs[:count], refs[count : count + 2], refs[count + 2 :]
+    rows, depth = turned[0].shape[4:]
     y_all = jnp.concatenate([y_own[...], y_peer[...]], axis=0)
     proj = 3 * HEADS * HD
-    for k, step in enumerate(steps):
+    for k, ref in enumerate(turned):
         for side in range(2):
             for i, right in ((0, y_all[:, :proj]), (1, y_all[:, proj:])):
-                left = turned[side, step, i].reshape(4 * rows, depth)
+                left = ref[side, 0, i].reshape(4 * rows, depth)
                 value = jnp.dot(left, right, preferred_element_type=F32).astype(BF16)
                 for n in range(right.shape[1] // 128):
                     for u in range(4):
@@ -236,21 +244,21 @@
     return total.astype(BF16)
 
 
-def join_kernel(*refs):
-    for u in range(refs[0].shape[0]):
-        for n in range(refs[0].shape[1]):
-            refs[-1][u, n] = add_up(refs[:-1], (u, n))
+def join_kernel(near_0, far_0, near_1, far_1, out_0, out_1):
+    for n in range(8):
+        out_0[0, n] = add_up((near_0, far_0), (0, n))
+        out_1[0, n] = add_up((near_1, far_1), (0, n))
 
 
 def sides_kernel(*refs):
     for side in range(2):
         for u, out in enumerate(refs[6:]):
-            for n in range(8):
+            for n in range(out.shape[0]):
                 out[n, side] = add_up(refs[3 * side : 3 * side + 3], (u, n))
 
 
 def seconds_kernel(*refs):
-    for n in range(8):
+    for n in range(refs[0].shape[0]):
         for side in range(2):
             refs[-1][n, side] = add_up(refs[:-1], (n, side))
 
@@ -264,10 +272,18 @@
             out[k, side] = total.astype(BF16)
 
 
-def sum_call(body, name, outs, arrays, after=()):
-    size = math.prod(arrays[0].shape)
+def sum_call(body, name, outs, operands, grid=(), after=()):
+    value = operands[0][0] if isinstance(operands[0], tuple) else operands[0]
+    size = math.prod(value.shape)
     return call(
-        body, outs, arrays, flops=len(arrays) * size, nbytes=2 * size * (len(arrays) + 2), name=name, after=after
+        body,
+        outs,
+        operands,
+        grid=grid,
+        flops=len(operands) * size,
+        nbytes=2 * size * (len(operands) + 2),
+        name=name,
+        after=after,
     )
 
 
@@ -291,9 +307,8 @@
             to = pl.ds(pl.multiple_of(info[first + j], 128), width)
             g[:, to] = ref[:, j * width : (j + 1) * width]
     step = 16
-
-    def body(i, carry):
-        at = pl.ds(pl.multiple_of(i * step, step), step)
+    for i in range(rows // step):
+        at = slice(i * step, (i + 1) * step)
         x = tokens[at, :].astype(F32)
         center = x - jnp.sum(x, axis=1, keepdims=True) / model
         scale = lax.rsqrt(jnp.sum(center * center, axis=1, keepdims=True) / model + EPS)
@@ -302,9 +317,6 @@
         mean_g = jnp.sum(grad, axis=1, keepdims=True) / model
         mean_gh = jnp.sum(grad * hat, axis=1, keepdims=True) / model
         out[at, :] = (scale * (grad - mean_g - hat * mean_gh)).astype(BF16)
-        return carry
-
-    lax.fori_loop(0, rows // step, body, 0)
 
 
 def place_kernel(info, own, other, out):
@@ -312,10 +324,10 @@
     for k, ref in enumerate((own, other)):
         c = info[CORE] if k == 0 else 1 - info[CORE]
         for h in range(2):
-            for n in range(8):
+            for n in range(2):
                 for side in range(2):
                     to = pl.ds(pl.multiple_of(c * 4 * rows + (2 * h + side) * rows, rows), rows)
-                    out[n // 2, to, (n % 2) * 128 : (n % 2 + 1) * 128] = ref[h, n, side].astype(F32)
+                    out[0, to, n * 128 : (n + 1) * 128] = ref[h, n, side].astype(F32)
 
 
 def swap_groups(with_x):
@@ -348,17 +360,20 @@
     info = jnp.stack(offs + [x_hi * 2 + x_lo, x_lo, core, sign]).astype(jnp.int32)
     half = width // 2
 
-    pair_shape = shape((2, rows, model // 2))
+    pair = shape((2, rows, model // 2))
+    some = rows // 4
     own, send = call(
         functools.partial(prep_kernel, width),
-        [pair_shape] * 2,
-        [info, tokens, cotangent],
+        [(pair, (2, some, model // 2), lambda i: (0, i, 0))] * 2,
+        [info, (tokens, (some, model), lambda i: (i, 0)), (cotangent, (some, model), lambda i: (i, 0))],
+        grid=(4,),
         scalars=1,
-        scratch=[pltpu.VMEM((rows, model), BF16)],
+        scratch=[pltpu.VMEM((some, model), BF16)],
         flops=8 * rows * model,
         nbytes=8 * rows * model,
         name="prep",
     )
+
     w = {(0, 0): lax.dynamic_slice(weights, (0, core * width, 0), (4, width, cols))}
     w[0, 1] = shift(w[0, 0], dx=1)
     w[3, 0] = shift(w[0, 0], dy=-1)
@@ -369,11 +384,13 @@
     w[2, 1] = shift(w[1, 1], dy=1)
     shards = [w[place] for place in ORDER]
 
-    peer = shift(gate(send, [w[1, 0], w[3, 0]]), dc=1)
-    turned = call(
+    peer = shift(gate(send, [w[1, 0]]), dc=1)
+    one = (1, rows, model // 2)
+    (turned,) = call(
         functools.partial(flip_kernel, width),
-        shape((2, 4, 2, 4, half // 2, 2 * rows)),
-        [info, own, peer],
+        [(shape((2, 4, 2, 4, half // 2, 2 * rows)), (2, 4, 1, 4, half // 2, 2 * rows), lambda i: (0, 0, i, 0, 0, 0))],
+        [info, (own, one, lambda i: (i, 0, 0)), (peer, one, lambda i: (i, 0, 0))],
+        grid=(2,),
         scalars=1,
         nbytes=8 * rows * model,
         name="flip",
@@ -390,10 +407,16 @@
     lin_shape = shape((rows, 4 * cols), F32)
     lin = []
     for first, pairs in ((0, 3), (3, 1)):
+        span = 2 * pairs * width
+        columns = functools.partial(lambda c, m: (m // 3, 0, c), first // pairs)
+        acc = ((rows, cols), lambda m: (0, m))
         lin = call(
-            functools.partial(linear_kernel, width, first, pairs),
-            [lin_shape] * 2,
-            [own, peer] + shards[2 * first : 2 * (first + pairs)] + list(lin),
+            functools.partial(linear_kernel, pairs),
+            [(lin_shape, *acc)] * 2,
+            [(own, (1, rows, span), columns), (peer, (1, rows, span), columns)]
+            + [(w_j, (1, width, cols), lambda m: (m, 0, 0)) for w_j in shards[2 * first : 2 * (first + pairs)]]
+            + [(value, *acc) for value in lin],
+            grid=(4,),
             flops=2 * 2 * rows * 2 * pairs * width * 4 * cols,
             nbytes=2 * pairs * width * 8 * cols + 8 * rows * 2 * pairs * width,
             name="linear",
@@ -401,9 +424,9 @@
         )
     lin_own, lin_send = lin
     lin_peer = shift(lin_send, dc=1)
-    y_own = call(
+    (y_own,) = call(
         attend_kernel,
-        shape((rows, 4 * cols)),
+        [shape((rows, 4 * cols))],
         [ends, lin_own, lin_peer, cos_t, sin_t],
         scalars=1,
         flops=HEADS * 10 * rows * rows * HD * 2,
@@ -417,10 +440,11 @@
 
     def terms(steps):
         part = len(steps) / 4
+        picks = [functools.partial(lambda step, _: (0, step, 0, 0, 0, 0), step) for step in steps]
         return call(
-            functools.partial(terms_kernel, steps),
+            functools.partial(terms_kernel, len(steps)),
             [piece] * (2 * len(steps)),
-            [turned, y_own, y_peer],
+            [(turned, (2, 1, 2, 4, quarter, 2 * rows), pick) for pick in picks] + [y_own, y_peer],
             flops=int(part * 2 * 2 * rows * (model // 2) * 4 * cols),
             nbytes=int(part * (4 * model * cols + 8 * rows * model)),
             name="terms",
@@ -432,45 +456,69 @@
     back = [along(back[0], first=-1), along(back[1], first=1)]
     near = terms([1, 0])
 
+    per_u = ((1, 8, quarter, 128), lambda u: (u, 0, 0, 0))
+    joined = sum_call(
+        join_kernel,
+        "join",
+        [(piece, *per_u)] * 2,
+        [(near[0], *per_u), (far[0], *per_u), (near[1], *per_u), (far[1], *per_u)],
+        grid=(4,),
+    )
+    ahead = [along(joined[0], first=1), along(joined[1], first=-1)]
+
+    most = ((3, width, cols), lambda _: (0, 0, 0))
     g_own, g_send = call(
         functools.partial(normed_grad_kernel, width),
         [shape((rows, model // 2), F32)] * 2,
-        [y_own, y_peer] + shards,
+        [y_own, y_peer] + [(w_j, *most) for w_j in shards],
         flops=2 * rows * model * 3 * cols,
         nbytes=4 * model * cols + 4 * rows * model,
         name="normed_grad",
-        after=[near[0]],
-    )
-    ahead = []
-    for side in range(2):
-        joined = sum_call(join_kernel, "join", piece, [near[side], far[side]], after=[g_send])
-        ahead.append(along(joined, first=1 - 2 * side))
+        after=[joined[0]],
+    )
+
+    per_n = ((4, 2, quarter, 128), lambda n: (0, n, 0, 0))
+    mixed = shape((8, 2, quarter, 128))
+    out_n = ((2, 2, quarter, 128), lambda n: (n, 0, 0, 0))
     halfway = sum_call(
         sides_kernel,
         "sides",
-        [shape((8, 2, quarter, 128))] * 4,
-        [near[2], back[0], ahead[0], near[3], back[1], ahead[1]],
+        [(mixed, *out_n)] * 4,
+        [(value, *per_n) for value in (near[2], back[0], ahead[0], near[3], back[1], ahead[1])],
+        grid=(4,),
+        after=[g_send],
     )
     g_peer = shift(gate(g_send, [halfway[0]]), dc=1)
-    grad_tokens = call(
+    g_rows = ((some, model // 2), lambda i: (i, 0))
+    (grad_tokens,) = call(
         functools.partial(token_grad_kernel, width),
-        shape((rows, model)),
-        [info, tokens, g_own, g_peer],
+        [(shape((rows, model)), (some, model), lambda i: (i, 0))],
+        [info, (tokens, (some, model), lambda i: (i, 0)), (g_own, *g_rows), (g_peer, *g_rows)],
+        grid=(4,),
         scalars=1,
-        scratch=[pltpu.VMEM((rows, model), F32)],
+        scratch=[pltpu.VMEM((some, model), F32)],
         flops=16 * rows * model,
         nbytes=8 * rows * model,
         name="token_grad",
     )
 
     rest = [along(halfway[d], second=d) for d in range(1, 4)]
-    by_z = sum_call(seconds_kernel, "seconds", shape((8, 2, quarter, 128)), [halfway[0]] + rest, after=[grad_tokens])
-    spread = sum_call(last_kernel, "last", shape((2 * NZ, 2, quarter, 128)), [exchange(by_z, False)])
+    (by_z,) = sum_call(
+        seconds_kernel,
+        "seconds",
+        [(mixed, *out_n)],
+        [(value, *out_n) for value in [halfway[0]] + rest],
+        grid=(4,),
+        after=[grad_tokens],
+    )
+    (spread,) = sum_call(last_kernel, "last", [shape((2 * NZ, 2, quarter, 128))], [exchange(by_z, False)])
     done = exchange(spread, True).reshape(2, NZ, 2, quarter, 128)
-    weight_grads = call(
+    per_m = ((2, 2, 2, quarter, 128), lambda m: (0, m, 0, 0, 0))
+    (weight_grads,) = call(
         place_kernel,
-        shape((4, shard_rows, cols), F32),
-        [info, done, shift(done, dc=1)],
+        [(shape((4, shard_rows, cols), F32), (1, shard_rows, cols), lambda m: (m, 0, 0))],
+        [info, (done, *per_m), (shift(done, dc=1), *per_m)],
+        grid=(4,),
         scalars=1,
         flops=4 * shard_rows * cols,
         nbytes=24 * shard_rows * cols,

time: 212 us -> 165 us (0.78)
  Pallas kernels: 79.5 us -> 31.7 us
  starting transfers between devices: 28.9 us -> 33.4 us
  waiting for transfers between devices: 34.3 us -> 31.4 us
    pallas_call x16 -> x15, Pallas kernels: 79.5 us -> 31.7 us  [call(): pl.pallas_call(kernel, grid=grid or (1,), out_shape=out_shapes, in_specs=...]
    ppermute x21, starting transfers between devices: 28.9 us -> 33.4 us  [permute(): return lax.ppermute(values, ('dp', 'fsdp'), pairs)]
    ppermute x21, waiting for transfers between devices: 34.3 us -> 31.4 us  [permute(): return lax.ppermute(values, ('dp', 'fsdp'), pairs)]
    unnamed x54 -> x40, local copies, waits for them, and re-layouts: 14.9 us -> 16.1 us
  transfers between devices with their start and end apart: 21 -> 21, of which waited for: 9 -> 11; matrix products, arithmetic and copies ran while one was open for 2% -> 1% of each run, Pallas kernels for 26% -> 13%
where the time goes in v1:
time: 165 us; the launch traced here: 164 us
  blocking collectives  45.2 us (27%)
  starting transfers between devices  33.4 us (20%)
  Pallas kernels  31.7 us (19%)
  waiting for transfers between devices  31.4 us (19%)
  local copies, waits for them, and re-layouts  17.8 us (11%)
  between operations  2.87 us (2%)
  other arithmetic  1.7 us (1%)
    all_to_all x2, blocking collectives, exchange(): lax.all_to_all(values, 'dp', split_axis=0, concat_axis=0, axis_index_grou...  45.2 us
    ppermute x21, starting transfers between devices, permute(): return lax.ppermute(values, ('dp', 'fsdp'), pairs)  33.4 us
    pallas_call x15, Pallas kernels, call(): pl.pallas_call(kernel, grid=grid or (1,), out_shape=out_shapes, in_specs=...  31.7 us
    ppermute x21, waiting for transfers between devices, permute(): return lax.ppermute(values, ('dp', 'fsdp'), pairs)  31.4 us
    unnamed x40, local copies, waits for them, and re-layouts  16.1 us
  transfers between devices with their start and end apart: 21, of which 11 were waited for; matrix products, arithmetic and copies ran while one was open for 1% of the time, Pallas kernels for 13%

profile of v1, /device:TPU:1, one launch (start us, length us, event | category | flops | bytes accessed | tf_op | source)
XLA Modules:
  0.0 164.0 jit_solution(7944226173777064172)
XLA Ops:
  3.0 3.3 %collective-permute-start.1 = (bf16[4,384,256]{2,1,0:T(8,128)(2,1)}, bf16[4,384,256]{2,1,0:T(8,128)(2,1)S(1)}, u32[]{:S(2)}, u32[]{:S(2)}) collective-permute-start(bf16[4,384,256]{2,1,0:T(8,128)(2,1)} %constant_dynamic-slice_fusion.refs_2_), channel_id=1, source_target_pairs={{0,1},{8,137},{16,17},{24,153},{32,33},{40,169},{48,49},{56,185},{... | collective-permute-start | bytes 2359304 | tf_op jit(solution)/shard_map/ppermute | solution.py:33
  6.3 2.7 %collective-permute-start = (bf16[4,384,256]{2,1,0:T(8,128)(2,1)}, bf16[4,384,256]{2,1,0:T(8,128)(2,1)S(1)}, u32[]{:S(2)}, u32[]{:S(2)}) collective-permute-start(bf16[4,384,256]{2,1,0:T(8,128)(2,1)} %constant_dynamic-slice_fusion.refs_2_), channel_id=1, source_target_pairs={{0,2},{8,14},{16,18},{24,30},{32,34},{40,46},{48,50},{56,62},{64,6... | collective-permute-start | bytes 2359304 | tf_op jit(solution)/shard_map/ppermute | solution.py:33
  9.1 1.7 %copy-done.7 = bf16[192,6144]{1,0:T(8,128)(2,1)S(1)} copy-done((bf16[192,6144]{1,0:T(8,128)(2,1)S(1)}, bf16[192,6144]{1,0:T(8,128)(2,1)}, u32[]{:S(2)}) %copy-start.7) | copy-done | bytes 2359320
  10.8 1.7 %copy-done.12 = bf16[192,6144]{1,0:T(8,128)(2,1)S(1)} copy-done((bf16[192,6144]{1,0:T(8,128)(2,1)S(1)}, bf16[192,6144]{1,0:T(8,128)(2,1)}, u32[]{:S(2)}) %copy-start.12) | copy-done | bytes 2359320
  12.5 3.0 %prep.1 = (bf16[2,192,3072]{2,1,0:T(8,128)(2,1)S(1)}, bf16[2,192,3072]{2,1,0:T(8,128)(2,1)S(1)}) custom-call(s32[20]{0:T(128)S(1)} %stack.92.info, bf16[192,6144]{1,0:T(8,128)(2,1)S(1)} %copy-done.7, bf16[192,6144]{1,0:T(8,128)(2,1)S(1)} %copy-done.12), custom_call_target="tpu_custom_call" | custom-call | flops 9437184 | bytes 9437184 | tf_op jit(solution)/shard_map/prep/pallas_call | solution.py:71
  20.9 2.7 %collective-permute-start.5 = (bf16[4,384,256]{2,1,0:T(8,128)(2,1)S(1)}, bf16[4,384,256]{2,1,0:T(8,128)(2,1)S(1)}, u32[]{:S(2)}, u32[]{:S(2)}) collective-permute-start(bf16[4,384,256]{2,1,0:T(8,128)(2,1)S(1)} %copy-done.5), channel_id=1, source_target_pairs={{0,1},{8,137},{16,17},{24,153},{32,33},{40,169},{48,49},{56,185},{... | collective-permute-start | bytes 2359304 | tf_op jit(solution)/shard_map/ppermute | solution.py:33
  26.2 2.8 %collective-permute-start.7 = (bf16[4,384,256]{2,1,0:T(8,128)(2,1)S(1)}, bf16[4,384,256]{2,1,0:T(8,128)(2,1)S(1)}, u32[]{:S(2)}, u32[]{:S(2)}) collective-permute-start(bf16[4,384,256]{2,1,0:T(8,128)(2,1)S(1)} %copy-done.5), channel_id=1, source_target_pairs={{0,2},{8,14},{16,18},{24,30},{32,34},{40,46},{48,50},{56,62},{64,6... | collective-permute-start | bytes 2359304 | tf_op jit(solution)/shard_map/ppermute | solution.py:33
  29.0 7.0 %collective-permute-done.3.refs_6_ = bf16[4,384,256]{2,1,0:T(8,128)(2,1)S(1)} collective-permute-done((bf16[4,384,256]{2,1,0:T(8,128)(2,1)}, bf16[4,384,256]{2,1,0:T(8,128)(2,1)S(1)}, u32[]{:S(2)}, u32[]{:S(2)}) %collective-permute-start.3) | collective-permute-done | bytes 786464 | tf_op jit(solution)/shard_map/ppermute | solution.py:33
  36.0 3.1 %collective-permute-start.4 = (bf16[4,384,256]{2,1,0:T(8,128)(2,1)S(1)}, bf16[4,384,256]{2,1,0:T(8,128)(2,1)S(1)}, u32[]{:S(2)}, u32[]{:S(2)}) collective-permute-start(bf16[4,384,256]{2,1,0:T(8,128)(2,1)S(1)} %collective-permute-done.3.refs_6_), channel_id=1, source_target_pairs={{0,1},{8,137},{16,17},{24,153},{32,33},{40,169},{48,49},{56,185},{... | collective-permute-start | bytes 2359304 | tf_op jit(solution)/shard_map/ppermute | solution.py:33
  42.5 2.4 %flip.1.refs_8_.refs_0_.refs_1_ = bf16[2,4,2,4,96,384]{5,4,3,2,1,0:T(8,128)(2,1)S(1)} custom-call(s32[20]{0:T(128)S(1)} %stack.92.info, bf16[2,192,3072]{2,1,0:T(8,128)(2,1)S(1)} %copy-done.2, bf16[2,192,3072]{2,1,0:T(8,128)(2,1)S(1)} %collective-permute-done.2.peer.refs_1_), custom_call_target="tpu_custom_call" | custom-call | bytes 9437184 | tf_op jit(solution)/shard_map/flip/pallas_call | solution.py:71
  45.0 4.2 %linear.2 = (f32[192,1024]{1,0:T(8,128)S(1)}, f32[192,1024]{1,0:T(8,128)S(1)}) custom-call(bf16[2,192,3072]{2,1,0:T(8,128)(2,1)S(1)} %copy-done.3, bf16[2,192,3072]{2,1,0:T(8,128)(2,1)S(1)} %collective-permute-done.2.peer.refs_1_, bf16[4,384,256]{2,1,0:T(8,128)(2,1)} %constant_dynamic-slice_fusion.refs_2_, bf16[4,384,256]{2,1,0:T(8,128)(2,1)S(1)} %copy-done.11, ...), custom_call_target="tpu_custom_call" | custom-call | flops 1811939328 | bytes 8257536 | tf_op jit(solution)/shard_map/linear/pallas_call | solution.py:71
  50.3 1.8 %linear.3 = (f32[192,1024]{1,0:T(8,128)S(1)}, f32[192,1024]{1,0:T(8,128)S(1)}) custom-call(bf16[2,192,3072]{2,1,0:T(8,128)(2,1)S(1)} %copy-done.3, bf16[2,192,3072]{2,1,0:T(8,128)(2,1)S(1)} %collective-permute-done.2.peer.refs_1_, bf16[4,384,256]{2,1,0:T(8,128)(2,1)S(1)} %collective-permute-done.4.refs_0_.refs_8_, ...), custom_call_target="tpu_custom_call" | custom-call | flops 603979776 | bytes 2752512 | tf_op jit(solution)/shard_map/linear/pallas_call | solution.py:71
  52.0 3.0 %collective-permute-start.8 = (f32[192,1024]{1,0:T(8,128)S(1)}, f32[192,1024]{1,0:T(8,128)S(1)}, u32[]{:S(2)}, u32[]{:S(2)}) collective-permute-start(f32[192,1024]{1,0:T(8,128)S(1)} %get-tuple-element.29), channel_id=1, source_target_pairs={{0,8},{8,0},{16,24},{24,16},{32,40},{40,32},{48,56},{56,48},{64,72... | collective-permute-start | bytes 2359304 | tf_op jit(solution)/shard_map/ppermute | solution.py:33
  55.1 1.9 %collective-permute-done.8.theirs = f32[192,1024]{1,0:T(8,128)S(1)} collective-permute-done((f32[192,1024]{1,0:T(8,128)S(1)}, f32[192,1024]{1,0:T(8,128)S(1)}, u32[]{:S(2)}, u32[]{:S(2)}) %collective-permute-start.8) | collective-permute-done | bytes 786464 | tf_op jit(solution)/shard_map/ppermute | solution.py:33
  57.0 3.2 %attend.1.refs_2_.refs_1_.refs_0_ = bf16[192,1024]{1,0:T(8,128)(2,1)S(1)} custom-call(s32[3]{0:T(128)S(1)} %pad_add_fusion.refs_11_.ends, f32[192,1024]{1,0:T(8,128)S(1)} %get-tuple-element.28.mine, f32[192,1024]{1,0:T(8,128)S(1)} %collective-permute-done.8.theirs, f32[192,128]{1,0:T(8,128)S(1)} %get-tuple-element.60.refs_9_.cos_t, ...), custom_call_target="tpu_custom_call" | custom-call | flops 188743680 | bytes 1966080 | tf_op jit(solution)/shard_map/attend/pallas_call | solution.py:71
  66.7 1.7 %collective-permute-start.12 = (bf16[4,8,96,128]{3,2,1,0:T(8,128)(2,1)S(1)}, bf16[4,8,96,128]{3,2,1,0:T(8,128)(2,1)S(1)}, u32[]{:S(2)}, u32[]{:S(2)}) collective-permute-start(bf16[4,8,96,128]{3,2,1,0:T(8,128)(2,1)S(1)} %get-tuple-element.38), channel_id=1, source_target_pairs={{0,6},{8,137},{16,22},{24,153},{32,38},{40,169},{48,54},{56,185},{... | collective-permute-start | bytes 2359304 | tf_op jit(solution)/shard_map/ppermute | solution.py:33
  68.4 1.8 %terms.3 = (bf16[4,8,96,128]{3,2,1,0:T(8,128)(2,1)S(1)}, bf16[4,8,96,128]{3,2,1,0:T(8,128)(2,1)S(1)}, bf16[4,8,96,128]{3,2,1,0:T(8,128)(2,1)S(1)}, bf16[4,8,96,128]{3,2,1,0:T(8,128)(2,1)S(1)}) custom-call(bf16[2,4,2,4,96,384]{5,4,3,2,1,0:T(8,128)(2,1)S(1)} %flip.1.refs_8_.refs_0_.refs_1_, bf16[2,4,2,4,96,384]{5,4,3,2,1,0:T(8,128)(2,1)S(1)} %flip.1.refs_8_.refs_0_.refs_1_, ...), custom_call_target="tpu_custom_call" | custom-call | flops 1207959552 | bytes 7864320 | tf_op jit(solution)/shard_map/terms/pallas_call | solution.py:71
  70.2 5.2 %collective-permute-done.10.far_0 = bf16[4,8,96,128]{3,2,1,0:T(8,128)(2,1)S(1)} collective-permute-done((bf16[4,8,96,128]{3,2,1,0:T(8,128)(2,1)S(1)}, bf16[4,8,96,128]{3,2,1,0:T(8,128)(2,1)S(1)}, u32[]{:S(2)}, u32[]{:S(2)}) %collective-permute-start.10) | collective-permute-done | bytes 786464 | tf_op jit(solution)/shard_map/ppermute | solution.py:33
  76.7 1.8 %collective-permute-start.15 = (bf16[4,8,96,128]{3,2,1,0:T(8,128)(2,1)S(1)}, bf16[4,8,96,128]{3,2,1,0:T(8,128)(2,1)S(1)}, u32[]{:S(2)}, u32[]{:S(2)}) collective-permute-start(bf16[4,8,96,128]{3,2,1,0:T(8,128)(2,1)S(1)} %get-tuple-element.41), channel_id=1, source_target_pairs={{0,6},{8,137},{16,22},{24,153},{32,38},{40,169},{48,54},{56,185},{... | collective-permute-start | bytes 2359304 | tf_op jit(solution)/shard_map/ppermute | solution.py:33
  78.6 3.7 %normed_grad.1 = (f32[192,3072]{1,0:T(8,128)S(1)}, f32[192,3072]{1,0:T(8,128)S(1)}) custom-call(bf16[192,1024]{1,0:T(8,128)(2,1)S(1)} %attend.1.refs_2_.refs_1_.refs_0_, bf16[192,1024]{1,0:T(8,128)(2,1)S(1)} %collective-permute-done.9.refs_3_.refs_2_.refs_1_, bf16[4,384,256]{2,1,0:T(8,128)(2,1)} %constant_dynamic-slice_fusion.refs_2_, ...), custom_call_target="tpu_custom_call" | custom-call | flops 1811939328 | bytes 11010048 | tf_op jit(solution)/shard_map/normed_grad/pallas_call | solution.py:71
  82.3 2.4 %collective-permute-done.12.refs_1_ = bf16[4,8,96,128]{3,2,1,0:T(8,128)(2,1)S(1)} collective-permute-done((bf16[4,8,96,128]{3,2,1,0:T(8,128)(2,1)S(1)}, bf16[4,8,96,128]{3,2,1,0:T(8,128)(2,1)S(1)}, u32[]{:S(2)}, u32[]{:S(2)}) %collective-permute-start.12) | collective-permute-done | bytes 786464 | tf_op jit(solution)/shard_map/ppermute | solution.py:33
  84.7 8.4 %collective-permute-done.15.refs_5_ = bf16[4,8,96,128]{3,2,1,0:T(8,128)(2,1)S(1)} collective-permute-done((bf16[4,8,96,128]{3,2,1,0:T(8,128)(2,1)S(1)}, bf16[4,8,96,128]{3,2,1,0:T(8,128)(2,1)S(1)}, u32[]{:S(2)}, u32[]{:S(2)}) %collective-permute-start.15) | collective-permute-done | bytes 786464 | tf_op jit(solution)/shard_map/ppermute | solution.py:33
  95.3 4.1 %collective-permute-start.18 = (bf16[8,2,96,128]{3,2,1,0:T(8,128)(2,1)S(1)}, bf16[8,2,96,128]{3,2,1,0:T(8,128)(2,1)S(1)}, u32[]{:S(2)}, u32[]{:S(2)}) collective-permute-start(bf16[8,2,96,128]{3,2,1,0:T(8,128)(2,1)S(1)} %get-tuple-element.44), channel_id=1, source_target_pairs={{0,128},{8,12},{16,144},{24,28},{32,160},{40,44},{48,176},{56,60},... | collective-permute-start | bytes 1179656 | tf_op jit(solution)/shard_map/ppermute | solution.py:33
  99.7 1.7 %copy-done.8 = bf16[192,6144]{1,0:T(8,128)(2,1)S(1)} copy-done((bf16[192,6144]{1,0:T(8,128)(2,1)S(1)}, bf16[192,6144]{1,0:T(8,128)(2,1)}, u32[]{:S(2)}) %copy-start.8) | copy-done | bytes 2359320
  101.3 1.7 %copy-done.14 = f32[192,3072]{1,0:T(8,128)S(1)} copy-done((f32[192,3072]{1,0:T(8,128)S(1)}, f32[192,3072]{1,0:T(8,128)}, u32[]{:S(2)}) %copy-start.14) | copy-done | bytes 2359320
  103.0 5.1 %token_grad.1.refs_4_ = bf16[192,6144]{1,0:T(8,128)(2,1)} custom-call(s32[20]{0:T(128)S(1)} %stack.92.info, bf16[192,6144]{1,0:T(8,128)(2,1)S(1)} %copy-done.8, f32[192,3072]{1,0:T(8,128)S(1)} %copy-done.14, f32[192,3072]{1,0:T(8,128)S(1)} %collective-permute-done.16.g_peer), custom_call_target="tpu_custom_call" | custom-call | flops 18874368 | bytes 9437184 | tf_op jit(solution)/shard_map/token_grad/pallas_call | solution.py:71
  109.0 1.7 %copy-done.9 = bf16[192,6144]{1,0:T(8,128)(2,1)S(1)} copy-done((bf16[192,6144]{1,0:T(8,128)(2,1)S(1)}, bf16[192,6144]{1,0:T(8,128)(2,1)}, u32[]{:S(2)}) %copy-start.9) | copy-done | bytes 2359320
  111.0 21.5 %all_to_all.10.got = bf16[8,2,96,128]{3,2,1,0:T(8,128)(2,1)S(1)} all-to-all(bf16[8,2,96,128]{3,2,1,0:T(8,128)(2,1)S(1)} %seconds.1), channel_id=1, replica_groups={{0,16,32,48,64,80,96,112},{8,24,40,56,72,88,104,120},{128,144,160,176,1..., dimensions={0} | all-to-all | bytes 786432 | tf_op jit(solution)/shard_map/all_to_all | solution.py:340
  132.6 23.7 %all_to_all.11 = bf16[16,2,96,128]{3,2,1,0:T(8,128)(2,1)S(1)} all-to-all(bf16[16,2,96,128]{3,2,1,0:T(8,128)(2,1)S(1)} %last.1), channel_id=1, replica_groups={{0,16,32,48,64,80,96,112,128,144,160,176,192,208,224,240},{8,24,40,56,7..., dimensions={0} | all-to-all | bytes 1572864 | tf_op jit(solution)/shard_map/all_to_all | solution.py:340
  156.3 3.1 %collective-permute-start.20 = (bf16[2,8,2,96,128]{4,3,2,1,0:T(8,128)(2,1)S(1)}, bf16[2,8,2,96,128]{4,3,2,1,0:T(8,128)(2,1)S(1)}, u32[]{:S(2)}, u32[]{:S(2)}) collective-permute-start(bf16[2,8,2,96,128]{4,3,2,1,0:T(8,128)(2,1)S(1)} %bitcast.26), channel_id=1, source_target_pairs={{0,8},{8,0},{16,24},{24,16},{32,40},{40,32},{48,56},{56,48},{64,72... | collective-permute-start | bytes 2359304 | tf_op jit(solution)/shard_map/ppermute | solution.py:33
  159.3 1.9 %collective-permute-done.20.other = bf16[2,8,2,96,128]{4,3,2,1,0:T(8,128)(2,1)S(1)} collective-permute-done((bf16[2,8,2,96,128]{4,3,2,1,0:T(8,128)(2,1)S(1)}, bf16[2,8,2,96,128]{4,3,2,1,0:T(8,128)(2,1)S(1)}, u32[]{:S(2)}, u32[]{:S(2)}) %collective-permute-start.20) | collective-permute-done | bytes 786464 | tf_op jit(solution)/shard_map/ppermute | solution.py:33
  161.3 2.7 %place.1 = f32[4,768,256]{2,1,0:T(8,128)} custom-call(s32[20]{0:T(128)S(1)} %stack.92.info, bf16[2,8,2,96,128]{4,3,2,1,0:T(8,128)(2,1)S(1)} %bitcast.27, bf16[2,8,2,96,128]{4,3,2,1,0:T(8,128)(2,1)S(1)} %collective-permute-done.20.other), custom_call_target="tpu_custom_call" | custom-call | flops 786432 | bytes 4718592 | tf_op jit(solution)/shard_map/place/pallas_call | solution.py:71
  (78 shorter events, 24.5 us)
Async XLA Ops:
  3.0 15.3 %collective-permute-start.1 = (bf16[4,384,256]{2,1,0:T(8,128)(2,1)}, bf16[4,384,256]{2,1,0:T(8,128)(2,1)S(1)}, u32[]{:S(2)}, u32[]{:S(2)}) collective-permute-start(bf16[4,384,256]{2,1,0:T(8,128)(2,1)} %constant_dynamic-slice_fusion.refs_2_), channel_id=1, source_target_pairs={{0,1},{8,137},{16,17},{24,153},{32,33},{40,169},{48,49},{56,185},{... | collective-permute-start | bytes 2359304 | tf_op jit(solution)/shard_map/ppermute | solution.py:33
  6.3 12.0 %collective-permute-start = (bf16[4,384,256]{2,1,0:T(8,128)(2,1)}, bf16[4,384,256]{2,1,0:T(8,128)(2,1)S(1)}, u32[]{:S(2)}, u32[]{:S(2)}) collective-permute-start(bf16[4,384,256]{2,1,0:T(8,128)(2,1)} %constant_dynamic-slice_fusion.refs_2_), channel_id=1, source_target_pairs={{0,2},{8,14},{16,18},{24,30},{32,34},{40,46},{48,50},{56,62},{64,6... | collective-permute-start | bytes 2359304 | tf_op jit(solution)/shard_map/ppermute | solution.py:33
  9.1 1.7 %copy-start.7 = (bf16[192,6144]{1,0:T(8,128)(2,1)S(1)}, bf16[192,6144]{1,0:T(8,128)(2,1)}, u32[]{:S(2)}) copy-start(bf16[192,6144]{1,0:T(8,128)(2,1)} %tokens.3) | copy-start | bytes 7077892
  19.5 4.1 %copy-start.18 = (s32[1,3]{1,0:T(1,128)S(1)}, s32[1,3]{1,0:T(1,128)}, u32[]{:S(2)}) copy-start(s32[1,3]{1,0:T(1,128)} %param.7) | copy-start | bytes 40
  19.5 20.3 %copy-start.19 = (s32[2,192]{1,0:T(2,128)S(1)}, s32[2,192]{1,0:T(2,128)}, u32[]{:S(2)}) copy-start(s32[2,192]{1,0:T(2,128)} %param.8) | copy-start | bytes 4612
  19.5 21.3 %collective-permute-start.2 = (bf16[2,192,3072]{2,1,0:T(8,128)(2,1)}, bf16[2,192,3072]{2,1,0:T(8,128)(2,1)S(1)}, u32[]{:S(2)}, u32[]{:S(2)}) collective-permute-start(bf16[2,192,3072]{2,1,0:T(8,128)(2,1)} %gate.4), channel_id=1, source_target_pairs={{0,8},{8,0},{16,24},{24,16},{32,40},{40,32},{48,56},{56,48},{64,72... | collective-permute-start | bytes 7077896 | tf_op jit(solution)/shard_map/ppermute | solution.py:33
  20.9 15.1 %collective-permute-start.3 = (bf16[4,384,256]{2,1,0:T(8,128)(2,1)}, bf16[4,384,256]{2,1,0:T(8,128)(2,1)S(1)}, u32[]{:S(2)}, u32[]{:S(2)}) collective-permute-start(bf16[4,384,256]{2,1,0:T(8,128)(2,1)} %constant_dynamic-slice_fusion.refs_2_), channel_id=1, source_target_pairs={{0,6},{8,10},{16,22},{24,26},{32,38},{40,42},{48,54},{56,58},{64,7... | collective-permute-start | bytes 2359304 | tf_op jit(solution)/shard_map/ppermute | solution.py:33
  20.9 18.2 %collective-permute-start.5 = (bf16[4,384,256]{2,1,0:T(8,128)(2,1)S(1)}, bf16[4,384,256]{2,1,0:T(8,128)(2,1)S(1)}, u32[]{:S(2)}, u32[]{:S(2)}) collective-permute-start(bf16[4,384,256]{2,1,0:T(8,128)(2,1)S(1)} %copy-done.5), channel_id=1, source_target_pairs={{0,1},{8,137},{16,17},{24,153},{32,33},{40,169},{48,49},{56,185},{... | collective-permute-start | bytes 2359304 | tf_op jit(solution)/shard_map/ppermute | solution.py:33
  26.2 18.8 %collective-permute-start.7 = (bf16[4,384,256]{2,1,0:T(8,128)(2,1)S(1)}, bf16[4,384,256]{2,1,0:T(8,128)(2,1)S(1)}, u32[]{:S(2)}, u32[]{:S(2)}) collective-permute-start(bf16[4,384,256]{2,1,0:T(8,128)(2,1)S(1)} %copy-done.5), channel_id=1, source_target_pairs={{0,2},{8,14},{16,18},{24,30},{32,34},{40,46},{48,50},{56,62},{64,6... | collective-permute-start | bytes 2359304 | tf_op jit(solution)/shard_map/ppermute | solution.py:33
  36.0 13.2 %collective-permute-start.4 = (bf16[4,384,256]{2,1,0:T(8,128)(2,1)S(1)}, bf16[4,384,256]{2,1,0:T(8,128)(2,1)S(1)}, u32[]{:S(2)}, u32[]{:S(2)}) collective-permute-start(bf16[4,384,256]{2,1,0:T(8,128)(2,1)S(1)} %collective-permute-done.3.refs_6_), channel_id=1, source_target_pairs={{0,1},{8,137},{16,17},{24,153},{32,33},{40,169},{48,49},{56,185},{... | collective-permute-start | bytes 2359304 | tf_op jit(solution)/shard_map/ppermute | solution.py:33
  39.1 11.1 %collective-permute-start.6 = (bf16[4,384,256]{2,1,0:T(8,128)(2,1)S(1)}, bf16[4,384,256]{2,1,0:T(8,128)(2,1)S(1)}, u32[]{:S(2)}, u32[]{:S(2)}) collective-permute-start(bf16[4,384,256]{2,1,0:T(8,128)(2,1)S(1)} %collective-permute-done.5.refs_5_), channel_id=1, source_target_pairs={{0,2},{8,14},{16,18},{24,30},{32,34},{40,46},{48,50},{56,62},{64,6... | collective-permute-start | bytes 2359304 | tf_op jit(solution)/shard_map/ppermute | solution.py:33
  40.8 1.7 %copy-start.2 = (bf16[2,192,3072]{2,1,0:T(8,128)(2,1)S(1)}, bf16[2,192,3072]{2,1,0:T(8,128)(2,1)}, u32[]{:S(2)}) copy-start(bf16[2,192,3072]{2,1,0:T(8,128)(2,1)} %copy-done.1) | copy-start | bytes 7077892
  42.5 2.5 %copy-start.3 = (bf16[2,192,3072]{2,1,0:T(8,128)(2,1)S(1)}, bf16[2,192,3072]{2,1,0:T(8,128)(2,1)}, u32[]{:S(2)}) copy-start(bf16[2,192,3072]{2,1,0:T(8,128)(2,1)} %copy-done.1) | copy-start | bytes 7077892
  42.5 2.5 %copy-start.11 = (bf16[4,384,256]{2,1,0:T(8,128)(2,1)S(1)}, bf16[4,384,256]{2,1,0:T(8,128)(2,1)}, u32[]{:S(2)}) copy-start(bf16[4,384,256]{2,1,0:T(8,128)(2,1)} %copy-done.10) | copy-start | bytes 2359300
  52.0 4.9 %collective-permute-start.8 = (f32[192,1024]{1,0:T(8,128)S(1)}, f32[192,1024]{1,0:T(8,128)S(1)}, u32[]{:S(2)}, u32[]{:S(2)}) collective-permute-start(f32[192,1024]{1,0:T(8,128)S(1)} %get-tuple-element.29), channel_id=1, source_target_pairs={{0,8},{8,0},{16,24},{24,16},{32,40},{40,32},{48,56},{56,48},{64,72... | collective-permute-start | bytes 2359304 | tf_op jit(solution)/shard_map/ppermute | solution.py:33
  60.1 1.8 %collective-permute-start.9 = (bf16[192,1024]{1,0:T(8,128)(2,1)S(1)}, bf16[192,1024]{1,0:T(8,128)(2,1)S(1)}, u32[]{:S(2)}, u32[]{:S(2)}) collective-permute-start(bf16[192,1024]{1,0:T(8,128)(2,1)S(1)} %attend.1.refs_2_.refs_1_.refs_0_), channel_id=1, source_target_pairs={{0,8},{8,0},{16,24},{24,16},{32,40},{40,32},{48,56},{56,48},{64,72... | collective-permute-start | bytes 1179656 | tf_op jit(solution)/shard_map/ppermute | solution.py:33
  62.9 12.4 %collective-permute-start.10 = (bf16[4,8,96,128]{3,2,1,0:T(8,128)(2,1)S(1)}, bf16[4,8,96,128]{3,2,1,0:T(8,128)(2,1)S(1)}, u32[]{:S(2)}, u32[]{:S(2)}) collective-permute-start(bf16[4,8,96,128]{3,2,1,0:T(8,128)(2,1)S(1)} %get-tuple-element.31), channel_id=1, source_target_pairs={{0,2},{8,9},{16,18},{24,25},{32,34},{40,41},{48,50},{56,57},{64,66... | collective-permute-start | bytes 2359304 | tf_op jit(solution)/shard_map/ppermute | solution.py:33
  64.1 12.2 %collective-permute-start.11 = (bf16[4,8,96,128]{3,2,1,0:T(8,128)(2,1)S(1)}, bf16[4,8,96,128]{3,2,1,0:T(8,128)(2,1)S(1)}, u32[]{:S(2)}, u32[]{:S(2)}) collective-permute-start(bf16[4,8,96,128]{3,2,1,0:T(8,128)(2,1)S(1)} %get-tuple-element.33), channel_id=1, source_target_pairs={{0,6},{8,137},{16,22},{24,153},{32,38},{40,169},{48,54},{56,185},{... | collective-permute-start | bytes 2359304 | tf_op jit(solution)/shard_map/ppermute | solution.py:33
  66.7 18.0 %collective-permute-start.12 = (bf16[4,8,96,128]{3,2,1,0:T(8,128)(2,1)S(1)}, bf16[4,8,96,128]{3,2,1,0:T(8,128)(2,1)S(1)}, u32[]{:S(2)}, u32[]{:S(2)}) collective-permute-start(bf16[4,8,96,128]{3,2,1,0:T(8,128)(2,1)S(1)} %get-tuple-element.38), channel_id=1, source_target_pairs={{0,6},{8,137},{16,22},{24,153},{32,38},{40,169},{48,54},{56,185},{... | collective-permute-start | bytes 2359304 | tf_op jit(solution)/shard_map/ppermute | solution.py:33
  68.4 16.3 %collective-permute-start.14 = (bf16[4,8,96,128]{3,2,1,0:T(8,128)(2,1)S(1)}, bf16[4,8,96,128]{3,2,1,0:T(8,128)(2,1)S(1)}, u32[]{:S(2)}, u32[]{:S(2)}) collective-permute-start(bf16[4,8,96,128]{3,2,1,0:T(8,128)(2,1)S(1)} %get-tuple-element.40), channel_id=1, source_target_pairs={{0,2},{8,9},{16,18},{24,25},{32,34},{40,41},{48,50},{56,57},{64,66... | collective-permute-start | bytes 2359304 | tf_op jit(solution)/shard_map/ppermute | solution.py:33
  76.7 16.4 %collective-permute-start.15 = (bf16[4,8,96,128]{3,2,1,0:T(8,128)(2,1)S(1)}, bf16[4,8,96,128]{3,2,1,0:T(8,128)(2,1)S(1)}, u32[]{:S(2)}, u32[]{:S(2)}) collective-permute-start(bf16[4,8,96,128]{3,2,1,0:T(8,128)(2,1)S(1)} %get-tuple-element.41), channel_id=1, source_target_pairs={{0,6},{8,137},{16,22},{24,153},{32,38},{40,169},{48,54},{56,185},{... | collective-permute-start | bytes 2359304 | tf_op jit(solution)/shard_map/ppermute | solution.py:33
  78.5 14.6 %collective-permute-start.13 = (bf16[4,8,96,128]{3,2,1,0:T(8,128)(2,1)S(1)}, bf16[4,8,96,128]{3,2,1,0:T(8,128)(2,1)S(1)}, u32[]{:S(2)}, u32[]{:S(2)}) collective-permute-start(bf16[4,8,96,128]{3,2,1,0:T(8,128)(2,1)S(1)} %get-tuple-element.34.refs_10_), channel_id=1, source_target_pairs={{0,2},{8,9},{16,18},{24,25},{32,34},{40,41},{48,50},{56,57},{64,66... | collective-permute-start | bytes 2359304 | tf_op jit(solution)/shard_map/ppermute | solution.py:33
  82.2 11.9 %copy-start.6 = (f32[192,3072]{1,0:T(8,128)}, f32[192,3072]{1,0:T(8,128)S(1)}, u32[]{:S(2)}) copy-start(f32[192,3072]{1,0:T(8,128)S(1)} %get-tuple-element.36.refs_6_.refs_0_) | copy-start | bytes 7077892
  82.2 11.9 %copy-start.13 = (f32[192,3072]{1,0:T(8,128)}, f32[192,3072]{1,0:T(8,128)S(1)}, u32[]{:S(2)}) copy-start(f32[192,3072]{1,0:T(8,128)S(1)} %get-tuple-element.35.g_own) | copy-start | bytes 7077892
  94.9 4.8 %collective-permute-start.16 = (f32[192,3072]{1,0:T(8,128)}, f32[192,3072]{1,0:T(8,128)S(1)}, u32[]{:S(2)}, u32[]{:S(2)}) collective-permute-start(f32[192,3072]{1,0:T(8,128)} %gate.5), channel_id=1, source_target_pairs={{0,8},{8,0},{16,24},{24,16},{32,40},{40,32},{48,56},{56,48},{64,72... | collective-permute-start | bytes 7077896 | tf_op jit(solution)/shard_map/ppermute | solution.py:33
  95.3 12.8 %collective-permute-start.17 = (bf16[8,2,96,128]{3,2,1,0:T(8,128)(2,1)S(1)}, bf16[8,2,96,128]{3,2,1,0:T(8,128)(2,1)S(1)}, u32[]{:S(2)}, u32[]{:S(2)}) collective-permute-start(bf16[8,2,96,128]{3,2,1,0:T(8,128)(2,1)S(1)} %get-tuple-element.43), channel_id=1, source_target_pairs={{0,1},{8,10},{16,17},{24,26},{32,33},{40,42},{48,49},{56,58},{64,6... | collective-permute-start | bytes 1179656 | tf_op jit(solution)/shard_map/ppermute | solution.py:33
  95.3 13.7 %collective-permute-start.18 = (bf16[8,2,96,128]{3,2,1,0:T(8,128)(2,1)S(1)}, bf16[8,2,96,128]{3,2,1,0:T(8,128)(2,1)S(1)}, u32[]{:S(2)}, u32[]{:S(2)}) collective-permute-start(bf16[8,2,96,128]{3,2,1,0:T(8,128)(2,1)S(1)} %get-tuple-element.44), channel_id=1, source_target_pairs={{0,128},{8,12},{16,144},{24,28},{32,160},{40,44},{48,176},{56,60},... | collective-permute-start | bytes 1179656 | tf_op jit(solution)/shard_map/ppermute | solution.py:33
  99.4 9.7 %collective-permute-start.19 = (bf16[8,2,96,128]{3,2,1,0:T(8,128)(2,1)S(1)}, bf16[8,2,96,128]{3,2,1,0:T(8,128)(2,1)S(1)}, u32[]{:S(2)}, u32[]{:S(2)}) collective-permute-start(bf16[8,2,96,128]{3,2,1,0:T(8,128)(2,1)S(1)} %get-tuple-element.45), channel_id=1, source_target_pairs={{0,129},{8,14},{16,145},{24,30},{32,161},{40,46},{48,177},{56,62},... | collective-permute-start | bytes 1179656 | tf_op jit(solution)/shard_map/ppermute | solution.py:33
  99.7 1.7 %copy-start.8 = (bf16[192,6144]{1,0:T(8,128)(2,1)S(1)}, bf16[192,6144]{1,0:T(8,128)(2,1)}, u32[]{:S(2)}) copy-start(bf16[192,6144]{1,0:T(8,128)(2,1)} %tokens.3) | copy-start | bytes 7077892
  103.0 6.0 %copy-start.17 = (bf16[8,2,96,128]{3,2,1,0:T(8,128)(2,1)S(1)}, bf16[8,2,96,128]{3,2,1,0:T(8,128)(2,1)}, u32[]{:S(2)}) copy-start(bf16[8,2,96,128]{3,2,1,0:T(8,128)(2,1)} %copy-done.16) | copy-start | bytes 1179652
  109.0 1.7 %copy-start.9 = (bf16[192,6144]{1,0:T(8,128)(2,1)S(1)}, bf16[192,6144]{1,0:T(8,128)(2,1)}, u32[]{:S(2)}) copy-start(bf16[192,6144]{1,0:T(8,128)(2,1)} %token_grad.1.refs_4_) | copy-start | bytes 7077892
  156.3 5.0 %collective-permute-start.20 = (bf16[2,8,2,96,128]{4,3,2,1,0:T(8,128)(2,1)S(1)}, bf16[2,8,2,96,128]{4,3,2,1,0:T(8,128)(2,1)S(1)}, u32[]{:S(2)}, u32[]{:S(2)}) collective-permute-start(bf16[2,8,2,96,128]{4,3,2,1,0:T(8,128)(2,1)S(1)} %bitcast.26), channel_id=1, source_target_pairs={{0,8},{8,0},{16,24},{24,16},{32,40},{40,32},{48,56},{56,48},{64,72... | collective-permute-start | bytes 2359304 | tf_op jit(solution)/shard_map/ppermute | solution.py:33
  (9 other events, 11.8 us)

commit v2 on v1

--- a/solution.py
+++ b/solution.py
@@ -97,7 +97,8 @@
     return jax.ShapeDtypeStruct(dims, dtype)
 
 
-def prep_kernel(width, info, tokens, cot, own, send, normed):
+def prep_kernel(width, info, tokens, cot, *refs):
+    passed, out, normed = refs[:-2], refs[-2], refs[-1]
     rows, model = tokens.shape
     step = 16
     for i in range(rows // step):
@@ -108,10 +109,11 @@
         normed[at, :] = (center * lax.rsqrt(var + EPS)).astype(BF16)
     for j in range(8):
         to = slice(j * width, (j + 1) * width)
-        for out, first in ((own, 0), (send, 8)):
-            cols = pl.ds(pl.multiple_of(info[first + j], 128), width)
-            out[0, :, to] = normed[:, cols]
-            out[1, :, to] = cot[:, cols]
+        cols = pl.ds(pl.multiple_of(info[j], 128), width)
+        out[0, :, to] = normed[:, cols]
+        out[1, :, to] = cot[:, cols]
+    if passed:
+        passed[1][...] = passed[0][...]
 
 
 def flip_kernel(width, info, own, peer, out):
@@ -300,7 +302,8 @@
         g_send[:, at] = total[rows:]
 
 
-def token_grad_kernel(width, info, tokens, g_own, g_peer, out, g):
+def token_grad_kernel(width, info, tokens, g_own, g_peer, out, mark, g):
+    mark[...] = jnp.zeros_like(mark)
     rows, model = tokens.shape
     for first, ref in ((0, g_own), (8, g_peer)):
         for j in range(8):
@@ -319,15 +322,31 @@
         out[at, :] = (scale * (grad - mean_g - hat * mean_gh)).astype(BF16)
 
 
-def place_kernel(info, own, other, out):
-    rows = own.shape[3]
-    for k, ref in enumerate((own, other)):
-        c = info[CORE] if k == 0 else 1 - info[CORE]
-        for h in range(2):
-            for n in range(2):
-                for side in range(2):
-                    to = pl.ds(pl.multiple_of(c * 4 * rows + (2 * h + side) * rows, rows), rows)
-                    out[0, to, n * 128 : (n + 1) * 128] = ref[h, n, side].astype(F32)
+def place_kernel(at, blocks, *refs):
+    out, rows = refs[-1], blocks.shape[3]
+    for h in range(2):
+        for n in range(2):
+            for side in range(2):
+                to = slice((2 * h + side) * rows, (2 * h + side + 1) * rows)
+                out[0, to, n * 128 : (n + 1) * 128] = blocks[h, n, side].astype(F32)
+
+
+def place(at, blocks, dims, before=()):
+    return pl.pallas_call(
+        place_kernel,
+        grid_spec=pltpu.PrefetchScalarGridSpec(
+            num_scalar_prefetch=1,
+            grid=(4,),
+            in_specs=[pl.BlockSpec((2, 2) + blocks.shape[2:], lambda m, at: (0, m, 0, 0, 0))]
+            + [pl.BlockSpec(memory_space=pl.ANY) for _ in before],
+            out_specs=pl.BlockSpec((1, dims[1] // 2, dims[2]), lambda m, at: (m, at[0], 0)),
+        ),
+        out_shape=shape(dims, F32),
+        input_output_aliases={2: 0} if before else {},
+        compiler_params=pltpu.CompilerParams(vmem_limit_bytes=12 * 1024 * 1024),
+        cost_estimate=pl.CostEstimate(flops=1, bytes_accessed=8 * math.prod(dims), transcendentals=0),
+        name="place",
+    )(at, blocks, *before)
 
 
 def swap_groups(with_x):
@@ -362,29 +381,26 @@
 
     pair = shape((2, rows, model // 2))
     some = rows // 4
-    own, send = call(
-        functools.partial(prep_kernel, width),
-        [(pair, (2, some, model // 2), lambda i: (0, i, 0))] * 2,
-        [info, (tokens, (some, model), lambda i: (i, 0)), (cotangent, (some, model), lambda i: (i, 0))],
-        grid=(4,),
-        scalars=1,
-        scratch=[pltpu.VMEM((some, model), BF16)],
-        flops=8 * rows * model,
-        nbytes=8 * rows * model,
-        name="prep",
-    )
+    row_block = ((some, model), lambda i: (i, 0))
+
+    def prep(tokens, cotangent, passed=()):
+        passed = [(value, (1,) + value.shape[1:], lambda i: (i, 0, 0)) for value in passed]
+        return call(
+            functools.partial(prep_kernel, width),
+            [(shape(item[0].shape), *item[1:]) for item in passed]
+            + [(pair, (2, some, model // 2), lambda i: (0, i, 0))],
+            [info, (tokens, *row_block), (cotangent, *row_block)] + passed,
+            grid=(4,),
+            scalars=1,
+            scratch=[pltpu.VMEM((some, model), BF16)],
+            flops=8 * rows * model,
+            nbytes=8 * rows * model,
+            name="prep",
+        )
 
     w = {(0, 0): lax.dynamic_slice(weights, (0, core * width, 0), (4, width, cols))}
-    w[0, 1] = shift(w[0, 0], dx=1)
-    w[3, 0] = shift(w[0, 0], dy=-1)
-    w[1, 0] = gate(shift(w[0, 0], dy=1), [own, w[0, 1]])
-    w[2, 0] = shift(w[1, 0], dy=1)
-    w[1, 1] = shift(w[1, 0], dx=1)
-    w[3, 1] = shift(w[3, 0], dx=1)
-    w[2, 1] = shift(w[1, 1], dy=1)
-    shards = [w[place] for place in ORDER]
-
-    peer = shift(gate(send, [w[1, 0]]), dc=1)
+    later, own = prep(tokens, cotangent, [w[0, 0]])
+    (peer,) = prep(shift(tokens, dc=1), shift(cotangent, dc=1))
     one = (1, rows, model // 2)
     (turned,) = call(
         functools.partial(flip_kernel, width),
@@ -395,6 +411,14 @@
         nbytes=8 * rows * model,
         name="flip",
     )
+    w[0, 1] = shift(w[0, 0], dx=1)
+    w[1, 0] = gate(shift(w[0, 0], dy=1), [own, w[0, 1]])
+    w[3, 0] = gate(shift(later, dy=-1), [peer])
+    w[2, 0] = shift(w[1, 0], dy=1)
+    w[1, 1] = gate(shift(w[1, 0], dx=1), [turned])
+    w[3, 1] = shift(w[3, 0], dx=1)
+    w[2, 1] = shift(w[1, 1], dy=1)
+    shards = [w[place] for place in ORDER]
 
     quarter = HD // 4
     frequency = ROPE_BASE ** (-jnp.arange(quarter, dtype=F32) / quarter)
@@ -490,10 +514,10 @@
     )
     g_peer = shift(gate(g_send, [halfway[0]]), dc=1)
     g_rows = ((some, model // 2), lambda i: (i, 0))
-    (grad_tokens,) = call(
+    grad_tokens, mark = call(
         functools.partial(token_grad_kernel, width),
-        [(shape((rows, model)), (some, model), lambda i: (i, 0))],
-        [info, (tokens, (some, model), lambda i: (i, 0)), (g_own, *g_rows), (g_peer, *g_rows)],
+        [(shape((rows, model)), *row_block), (shape((8, 128), F32), (8, 128), lambda i: (0, 0))],
+        [info, (tokens, *row_block), (g_own, *g_rows), (g_peer, *g_rows)],
         grid=(4,),
         scalars=1,
         scratch=[pltpu.VMEM((some, model), F32)],
@@ -509,21 +533,13 @@
         [(mixed, *out_n)],
         [(value, *out_n) for value in [halfway[0]] + rest],
         grid=(4,),
-        after=[grad_tokens],
+        after=[mark],
     )
     (spread,) = sum_call(last_kernel, "last", [shape((2 * NZ, 2, quarter, 128))], [exchange(by_z, False)])
     done = exchange(spread, True).reshape(2, NZ, 2, quarter, 128)
-    per_m = ((2, 2, 2, quarter, 128), lambda m: (0, m, 0, 0, 0))
-    (weight_grads,) = call(
-        place_kernel,
-        [(shape((4, shard_rows, cols), F32), (1, shard_rows, cols), lambda m: (m, 0, 0))],
-        [info, (done, *per_m), (shift(done, dc=1), *per_m)],
-        grid=(4,),
-        scalars=1,
-        flops=4 * shard_rows * cols,
-        nbytes=24 * shard_rows * cols,
-        name="place",
-    )
+    dims = (4, shard_rows, cols)
+    weight_grads = place(jnp.stack([core]).astype(jnp.int32), done, dims)
+    weight_grads = place(jnp.stack([1 - core]).astype(jnp.int32), shift(done, dc=1), dims, [weight_grads])
     return (grad_tokens, weight_grads)
 
 

time: 165 us -> 166 us (level)
  waiting for transfers between devices: 31.4 us -> 22.1 us
  Pallas kernels: 31.7 us -> 39.6 us
  local copies, waits for them, and re-layouts: 17.8 us -> 22.3 us
  starting transfers between devices: 33.4 us -> 30.2 us
    ppermute x21 -> x22, waiting for transfers between devices: 31.4 us -> 22.1 us  [permute(): return lax.ppermute(values, ('dp', 'fsdp'), pairs)]
    unnamed x40 -> x50, local copies, waits for them, and re-layouts: 16.1 us -> 21.6 us
    pallas_call x15, Pallas kernels: 31.7 us -> 36.2 us  [call(): pl.pallas_call(kernel, grid=grid or (1,), out_shape=out_shapes, in_specs=...]
    pallas_call x0 -> x2, Pallas kernels: none -> 3.47 us  [place(): pl.pallas_call(place_kernel, grid_spec=pltpu.PrefetchScalarGridSpec(num_s...]
    ppermute x21 -> x22, starting transfers between devices: 33.4 us -> 30.2 us  [permute(): return lax.ppermute(values, ('dp', 'fsdp'), pairs)]
  transfers between devices with their start and end apart: 21 -> 22, of which waited for: 11 -> 11; matrix products, arithmetic and copies ran while one was open for 1% -> 1% of each run, Pallas kernels for 13% -> 18%
where the time goes in v2:
time: 166 us; the launch traced here: 165 us
  blocking collectives  46.6 us (28%)
  Pallas kernels  39.6 us (24%)
  starting transfers between devices  30.2 us (18%)
  local copies, waits for them, and re-layouts  22.3 us (13%)
  waiting for transfers between devices  22.1 us (13%)
  between operations  2.71 us (2%)
  other arithmetic  1.7 us (1%)
    all_to_all x2, blocking collectives, exchange(): lax.all_to_all(values, 'dp', split_axis=0, concat_axis=0, axis_index_grou...  46.6 us
    pallas_call x15, Pallas kernels, call(): pl.pallas_call(kernel, grid=grid or (1,), out_shape=out_shapes, in_specs=...  36.2 us
    ppermute x22, starting transfers between devices, permute(): return lax.ppermute(values, ('dp', 'fsdp'), pairs)  30.2 us
    ppermute x22, waiting for transfers between devices, permute(): return lax.ppermute(values, ('dp', 'fsdp'), pairs)  22.1 us
    unnamed x50, local copies, waits for them, and re-layouts  21.6 us
    pallas_call x2, Pallas kernels, place(): pl.pallas_call(place_kernel, grid_spec=pltpu.PrefetchScalarGridSpec(num_s...  3.47 us
  transfers between devices with their start and end apart: 22, of which 11 were waited for; matrix products, arithmetic and copies ran while one was open for 1% of the time, Pallas kernels for 18%

profile of v2, /device:TPU:1, one launch (start us, length us, event | category | flops | bytes accessed | tf_op | source)
XLA Modules:
  0.0 165.3 jit_solution(17787274708055991127)
XLA Ops:
  0.6 3.3 %collective-permute-start.1 = (bf16[192,6144]{1,0:T(8,128)(2,1)}, bf16[192,6144]{1,0:T(8,128)(2,1)}, u32[]{:S(2)}, u32[]{:S(2)}) collective-permute-start(bf16[192,6144]{1,0:T(8,128)(2,1)} %cot.1), channel_id=1, source_target_pairs={{0,8},{8,0},{16,24},{24,16},{32,40},{40,32},{48,56},{56,48},{64,72... | collective-permute-start | bytes 7077896 | tf_op jit(solution)/shard_map/ppermute | solution.py:33
  5.5 2.7 %collective-permute-start.4 = (bf16[4,384,256]{2,1,0:T(8,128)(2,1)S(1)}, bf16[4,384,256]{2,1,0:T(8,128)(2,1)}, u32[]{:S(2)}, u32[]{:S(2)}) collective-permute-start(bf16[4,384,256]{2,1,0:T(8,128)(2,1)S(1)} %constant_dynamic-slice_fusion.refs_0_.refs_2_), channel_id=1, source_target_pairs={{0,2},{8,14},{16,18},{24,30},{32,34},{40,46},{48,50},{56,62},{64,6... | collective-permute-start | bytes 2359304 | tf_op jit(solution)/shard_map/ppermute | solution.py:33
  10.0 1.7 %copy-done.18 = bf16[192,6144]{1,0:T(8,128)(2,1)S(1)} copy-done((bf16[192,6144]{1,0:T(8,128)(2,1)S(1)}, bf16[192,6144]{1,0:T(8,128)(2,1)}, u32[]{:S(2)}) %copy-start.18) | copy-done | bytes 2359320
  11.7 3.3 %prep.2 = (bf16[4,384,256]{2,1,0:T(8,128)(2,1)}, bf16[2,192,3072]{2,1,0:T(8,128)(2,1)S(1)}) custom-call(s32[20]{0:T(128)S(1)} %stack.96.info, bf16[192,6144]{1,0:T(8,128)(2,1)S(1)} %copy-done.11, bf16[192,6144]{1,0:T(8,128)(2,1)S(1)} %copy-done.18, bf16[4,384,256]{2,1,0:T(8,128)(2,1)S(1)} %constant_dynamic-slice_fusion.refs_0_.refs_2_), custom_call_target="tpu_custom_call" | custom-call | flops 9437184 | bytes 9437184 | tf_op jit(solution)/shard_map/prep/pallas_call | solution.py:71
  21.2 2.4 %collective-permute-start.8 = (bf16[4,384,256]{2,1,0:T(8,128)(2,1)}, bf16[4,384,256]{2,1,0:T(8,128)(2,1)}, u32[]{:S(2)}, u32[]{:S(2)}) collective-permute-start(bf16[4,384,256]{2,1,0:T(8,128)(2,1)} %gate.5.refs_4_), channel_id=1, source_target_pairs={{0,2},{8,14},{16,18},{24,30},{32,34},{40,46},{48,50},{56,62},{64,6... | collective-permute-start | bytes 2359304 | tf_op jit(solution)/shard_map/ppermute | solution.py:33
  23.6 4.2 %prep.3.refs_1_.peer = bf16[2,192,3072]{2,1,0:T(8,128)(2,1)S(1)} custom-call(s32[20]{0:T(128)S(1)} %stack.96.info, bf16[192,6144]{1,0:T(8,128)(2,1)} %collective-permute-done.tokens, bf16[192,6144]{1,0:T(8,128)(2,1)} %collective-permute-done.1.cot), custom_call_target="tpu_custom_call" | custom-call | flops 9437184 | bytes 9437184 | tf_op jit(solution)/shard_map/prep/pallas_call | solution.py:71
  30.5 1.7 %copy-done.4 = bf16[2,192,3072]{2,1,0:T(8,128)(2,1)S(1)} copy-done((bf16[2,192,3072]{2,1,0:T(8,128)(2,1)S(1)}, bf16[2,192,3072]{2,1,0:T(8,128)(2,1)}, u32[]{:S(2)}) %copy-start.4) | copy-done | bytes 2359320
  32.2 1.7 %copy-done.8 = bf16[2,192,3072]{2,1,0:T(8,128)(2,1)S(1)} copy-done((bf16[2,192,3072]{2,1,0:T(8,128)(2,1)S(1)}, bf16[2,192,3072]{2,1,0:T(8,128)(2,1)}, u32[]{:S(2)}) %copy-start.8) | copy-done | bytes 2359320
  33.8 2.4 %flip.1.refs_1_.refs_8_.refs_0_ = bf16[2,4,2,4,96,384]{5,4,3,2,1,0:T(8,128)(2,1)S(1)} custom-call(s32[20]{0:T(128)S(1)} %stack.96.info, bf16[2,192,3072]{2,1,0:T(8,128)(2,1)S(1)} %copy-done.8, bf16[2,192,3072]{2,1,0:T(8,128)(2,1)S(1)} %copy-done.4), custom_call_target="tpu_custom_call" | custom-call | bytes 9437184 | tf_op jit(solution)/shard_map/flip/pallas_call | solution.py:71
  36.3 2.2 %copy-done.1 = bf16[2,4,2,4,96,384]{5,4,3,2,1,0:T(8,128)(2,1)} copy-done((bf16[2,4,2,4,96,384]{5,4,3,2,1,0:T(8,128)(2,1)}, bf16[2,4,2,4,96,384]{5,4,3,2,1,0:T(8,128)(2,1)S(1)}, u32[]{:S(2)}) %copy-start.1) | copy-done | bytes 4718616
  40.3 2.3 %copy-done.2 = bf16[2,4,2,4,96,384]{5,4,3,2,1,0:T(8,128)(2,1)S(1)} copy-done((bf16[2,4,2,4,96,384]{5,4,3,2,1,0:T(8,128)(2,1)S(1)}, bf16[2,4,2,4,96,384]{5,4,3,2,1,0:T(8,128)(2,1)}, u32[]{:S(2)}) %copy-start.2) | copy-done | bytes 4718616
  42.6 1.7 %copy-done.5 = bf16[2,192,3072]{2,1,0:T(8,128)(2,1)S(1)} copy-done((bf16[2,192,3072]{2,1,0:T(8,128)(2,1)S(1)}, bf16[2,192,3072]{2,1,0:T(8,128)(2,1)}, u32[]{:S(2)}) %copy-start.5) | copy-done | bytes 2359320
  45.9 4.9 %linear.2 = (f32[192,1024]{1,0:T(8,128)S(1)}, f32[192,1024]{1,0:T(8,128)S(1)}) custom-call(bf16[2,192,3072]{2,1,0:T(8,128)(2,1)S(1)} %copy-done.9, bf16[2,192,3072]{2,1,0:T(8,128)(2,1)S(1)} %copy-done.5, bf16[4,384,256]{2,1,0:T(8,128)(2,1)S(1)} %constant_dynamic-slice_fusion.refs_0_.refs_2_, bf16[4,384,256]{2,1,0:T(8,128)(2,1)S(1)} %copy-done.15, ...), custom_call_target="tpu_custom_call" | custom-call | flops 1811939328 | bytes 8257536 | tf_op jit(solution)/shard_map/linear/pallas_call | solution.py:71
  50.9 3.1 %linear.3 = (f32[192,1024]{1,0:T(8,128)S(1)}, f32[192,1024]{1,0:T(8,128)S(1)}) custom-call(bf16[2,192,3072]{2,1,0:T(8,128)(2,1)S(1)} %copy-done.10, bf16[2,192,3072]{2,1,0:T(8,128)(2,1)S(1)} %copy-done.6, bf16[4,384,256]{2,1,0:T(8,128)(2,1)} %collective-permute-done.3.refs_0_.refs_8_, bf16[4,384,256]{2,1,0:T(8,128)(2,1)S(1)} %collective-permute-done.7.refs_1_.refs_9_, ...), custom_call_target="tpu_custom_call" | custom-call | flops 603979776 | bytes 2752512 | tf_op jit(solution)/shard_map/linear/pallas_call | solution.py:71
  54.0 4.2 %collective-permute-start.9 = (f32[192,1024]{1,0:T(8,128)S(1)}, f32[192,1024]{1,0:T(8,128)S(1)}, u32[]{:S(2)}, u32[]{:S(2)}) collective-permute-start(f32[192,1024]{1,0:T(8,128)S(1)} %get-tuple-element.31), channel_id=1, source_target_pairs={{0,8},{8,0},{16,24},{24,16},{32,40},{40,32},{48,56},{56,48},{64,72... | collective-permute-start | bytes 2359304 | tf_op jit(solution)/shard_map/ppermute | solution.py:33
  58.2 1.9 %collective-permute-done.9.theirs = f32[192,1024]{1,0:T(8,128)S(1)} collective-permute-done((f32[192,1024]{1,0:T(8,128)S(1)}, f32[192,1024]{1,0:T(8,128)S(1)}, u32[]{:S(2)}, u32[]{:S(2)}) %collective-permute-start.9) | collective-permute-done | bytes 786464 | tf_op jit(solution)/shard_map/ppermute | solution.py:33
  60.1 3.2 %attend.1.refs_2_.refs_1_.refs_0_ = bf16[192,1024]{1,0:T(8,128)(2,1)S(1)} custom-call(s32[3]{0:T(128)S(1)} %pad_add_fusion.refs_11_.ends, f32[192,1024]{1,0:T(8,128)S(1)} %get-tuple-element.30.mine, f32[192,1024]{1,0:T(8,128)S(1)} %collective-permute-done.9.theirs, f32[192,128]{1,0:T(8,128)S(1)} %get-tuple-element.64.refs_9_.cos_t, ...), custom_call_target="tpu_custom_call" | custom-call | flops 188743680 | bytes 1966080 | tf_op jit(solution)/shard_map/attend/pallas_call | solution.py:71
  66.1 1.9 %collective-permute-start.11 = (bf16[4,8,96,128]{3,2,1,0:T(8,128)(2,1)S(1)}, bf16[4,8,96,128]{3,2,1,0:T(8,128)(2,1)S(1)}, u32[]{:S(2)}, u32[]{:S(2)}) collective-permute-start(bf16[4,8,96,128]{3,2,1,0:T(8,128)(2,1)S(1)} %get-tuple-element.33), channel_id=1, source_target_pairs={{0,2},{8,9},{16,18},{24,25},{32,34},{40,41},{48,50},{56,57},{64,66... | collective-permute-start | bytes 2359304 | tf_op jit(solution)/shard_map/ppermute | solution.py:33
  71.4 1.8 %terms.3 = (bf16[4,8,96,128]{3,2,1,0:T(8,128)(2,1)S(1)}, bf16[4,8,96,128]{3,2,1,0:T(8,128)(2,1)S(1)}, bf16[4,8,96,128]{3,2,1,0:T(8,128)(2,1)S(1)}, bf16[4,8,96,128]{3,2,1,0:T(8,128)(2,1)S(1)}) custom-call(bf16[2,4,2,4,96,384]{5,4,3,2,1,0:T(8,128)(2,1)S(1)} %bitcast.28, bf16[2,4,2,4,96,384]{5,4,3,2,1,0:T(8,128)(2,1)S(1)} %bitcast.28, ...), custom_call_target="tpu_custom_call" | custom-call | flops 1207959552 | bytes 7864320 | tf_op jit(solution)/shard_map/terms/pallas_call | solution.py:71
  73.2 5.3 %collective-permute-done.11.far_0 = bf16[4,8,96,128]{3,2,1,0:T(8,128)(2,1)S(1)} collective-permute-done((bf16[4,8,96,128]{3,2,1,0:T(8,128)(2,1)S(1)}, bf16[4,8,96,128]{3,2,1,0:T(8,128)(2,1)S(1)}, u32[]{:S(2)}, u32[]{:S(2)}) %collective-permute-start.11) | collective-permute-done | bytes 786464 | tf_op jit(solution)/shard_map/ppermute | solution.py:33
  79.5 2.2 %collective-permute-start.16 = (bf16[4,8,96,128]{3,2,1,0:T(8,128)(2,1)S(1)}, bf16[4,8,96,128]{3,2,1,0:T(8,128)(2,1)S(1)}, u32[]{:S(2)}, u32[]{:S(2)}) collective-permute-start(bf16[4,8,96,128]{3,2,1,0:T(8,128)(2,1)S(1)} %get-tuple-element.43), channel_id=1, source_target_pairs={{0,6},{8,137},{16,22},{24,153},{32,38},{40,169},{48,54},{56,185},{... | collective-permute-start | bytes 2359304 | tf_op jit(solution)/shard_map/ppermute | solution.py:33
  81.7 4.4 %normed_grad.1 = (f32[192,3072]{1,0:T(8,128)S(1)}, f32[192,3072]{1,0:T(8,128)S(1)}) custom-call(bf16[192,1024]{1,0:T(8,128)(2,1)S(1)} %attend.1.refs_2_.refs_1_.refs_0_, bf16[192,1024]{1,0:T(8,128)(2,1)S(1)} %collective-permute-done.10.refs_3_.refs_2_.refs_1_, bf16[4,384,256]{2,1,0:T(8,128)(2,1)S(1)} %constant_dynamic-slice_fusion.refs_0_.refs_2_, ...), custom_call_target="tpu_custom_call" | custom-call | flops 1811939328 | bytes 11010048 | tf_op jit(solution)/shard_map/normed_grad/pallas_call | solution.py:71
  87.5 8.4 %collective-permute-done.16.refs_5_ = bf16[4,8,96,128]{3,2,1,0:T(8,128)(2,1)S(1)} collective-permute-done((bf16[4,8,96,128]{3,2,1,0:T(8,128)(2,1)S(1)}, bf16[4,8,96,128]{3,2,1,0:T(8,128)(2,1)S(1)}, u32[]{:S(2)}, u32[]{:S(2)}) %collective-permute-start.16) | collective-permute-done | bytes 786464 | tf_op jit(solution)/shard_map/ppermute | solution.py:33
  98.5 4.1 %collective-permute-start.19 = (bf16[8,2,96,128]{3,2,1,0:T(8,128)(2,1)S(1)}, bf16[8,2,96,128]{3,2,1,0:T(8,128)(2,1)S(1)}, u32[]{:S(2)}, u32[]{:S(2)}) collective-permute-start(bf16[8,2,96,128]{3,2,1,0:T(8,128)(2,1)S(1)} %get-tuple-element.47), channel_id=1, source_target_pairs={{0,128},{8,12},{16,144},{24,28},{32,160},{40,44},{48,176},{56,60},... | collective-permute-start | bytes 1179656 | tf_op jit(solution)/shard_map/ppermute | solution.py:33
  102.8 1.7 %copy-done.12 = bf16[192,6144]{1,0:T(8,128)(2,1)S(1)} copy-done((bf16[192,6144]{1,0:T(8,128)(2,1)S(1)}, bf16[192,6144]{1,0:T(8,128)(2,1)}, u32[]{:S(2)}) %copy-start.12) | copy-done | bytes 2359320
  104.5 1.7 %copy-done.17 = f32[192,3072]{1,0:T(8,128)S(1)} copy-done((f32[192,3072]{1,0:T(8,128)S(1)}, f32[192,3072]{1,0:T(8,128)}, u32[]{:S(2)}) %copy-start.17) | copy-done | bytes 2359320
  106.2 5.2 %token_grad.1 = (bf16[192,6144]{1,0:T(8,128)(2,1)}, f32[8,128]{1,0:T(8,128)S(1)}) custom-call(s32[20]{0:T(128)S(1)} %stack.96.info, bf16[192,6144]{1,0:T(8,128)(2,1)S(1)} %copy-done.12, f32[192,3072]{1,0:T(8,128)S(1)} %copy-done.17, f32[192,3072]{1,0:T(8,128)S(1)} %collective-permute-done.17.g_peer), custom_call_target="tpu_custom_call" | custom-call | flops 18874368 | bytes 9437184 | tf_op jit(solution)/shard_map/token_grad/pallas_call | solution.py:71
  112.2 21.5 %all_to_all.10.got = bf16[8,2,96,128]{3,2,1,0:T(8,128)(2,1)S(1)} all-to-all(bf16[8,2,96,128]{3,2,1,0:T(8,128)(2,1)S(1)} %seconds.1), channel_id=1, replica_groups={{0,16,32,48,64,80,96,112},{8,24,40,56,72,88,104,120},{128,144,160,176,1..., dimensions={0} | all-to-all | bytes 786432 | tf_op jit(solution)/shard_map/all_to_all | solution.py:359
  133.8 25.1 %all_to_all.11 = bf16[16,2,96,128]{3,2,1,0:T(8,128)(2,1)S(1)} all-to-all(bf16[16,2,96,128]{3,2,1,0:T(8,128)(2,1)S(1)} %last.1), channel_id=1, replica_groups={{0,16,32,48,64,80,96,112,128,144,160,176,192,208,224,240},{8,24,40,56,7..., dimensions={0} | all-to-all | bytes 1572864 | tf_op jit(solution)/shard_map/all_to_all | solution.py:359
  158.9 2.8 %collective-permute-start.21 = (bf16[2,8,2,96,128]{4,3,2,1,0:T(8,128)(2,1)S(1)}, bf16[2,8,2,96,128]{4,3,2,1,0:T(8,128)(2,1)S(1)}, u32[]{:S(2)}, u32[]{:S(2)}) collective-permute-start(bf16[2,8,2,96,128]{4,3,2,1,0:T(8,128)(2,1)S(1)} %bitcast.29), channel_id=1, source_target_pairs={{0,8},{8,0},{16,24},{24,16},{32,40},{40,32},{48,56},{56,48},{64,72... | collective-permute-start | bytes 2359304 | tf_op jit(solution)/shard_map/ppermute | solution.py:33
  161.7 1.7 %place.2.refs_0_ = f32[4,768,256]{2,1,0:T(8,128)} custom-call(s32[1]{0:T(128)} %bitcast.18.at, bf16[2,8,2,96,128]{4,3,2,1,0:T(8,128)(2,1)S(1)} %bitcast.30), custom_call_target="tpu_custom_call" | custom-call | flops 1 | bytes 6291456 | tf_op jit(solution)/shard_map/place/pallas_call | solution.py:335
  163.6 1.7 %place.3 = f32[4,768,256]{2,1,0:T(8,128)} custom-call(s32[1]{0:T(128)} %bitcast.25.at, bf16[2,8,2,96,128]{4,3,2,1,0:T(8,128)(2,1)S(1)} %collective-permute-done.21.blocks, f32[4,768,256]{2,1,0:T(8,128)} %place.2.refs_0_), custom_call_target="tpu_custom_call", output_to_operand_aliasing={{}: (2, {})} | custom-call | flops 1 | bytes 6291456 | tf_op jit(solution)/shard_map/place/pallas_call | solution.py:335
  (94 shorter events, 26.4 us)
Async XLA Ops:
  0.6 3.4 %copy-start = (bf16[4,768,256]{2,1,0:T(8,128)(2,1)S(1)}, bf16[4,768,256]{2,1,0:T(8,128)(2,1)}, u32[]{:S(2)}) copy-start(bf16[4,768,256]{2,1,0:T(8,128)(2,1)} %param.9) | copy-start | bytes 4718596
  0.6 23.0 %collective-permute-start.1 = (bf16[192,6144]{1,0:T(8,128)(2,1)}, bf16[192,6144]{1,0:T(8,128)(2,1)}, u32[]{:S(2)}, u32[]{:S(2)}) collective-permute-start(bf16[192,6144]{1,0:T(8,128)(2,1)} %cot.1), channel_id=1, source_target_pairs={{0,8},{8,0},{16,24},{24,16},{32,40},{40,32},{48,56},{56,48},{64,72... | collective-permute-start | bytes 7077896 | tf_op jit(solution)/shard_map/ppermute | solution.py:33
  4.0 19.6 %collective-permute-start = (bf16[192,6144]{1,0:T(8,128)(2,1)}, bf16[192,6144]{1,0:T(8,128)(2,1)}, u32[]{:S(2)}, u32[]{:S(2)}) collective-permute-start(bf16[192,6144]{1,0:T(8,128)(2,1)} %tokens.3), channel_id=1, source_target_pairs={{0,8},{8,0},{16,24},{24,16},{32,40},{40,32},{48,56},{56,48},{64,72... | collective-permute-start | bytes 7077896 | tf_op jit(solution)/shard_map/ppermute | solution.py:33
  4.1 12.3 %collective-permute-start.5 = (bf16[4,384,256]{2,1,0:T(8,128)(2,1)S(1)}, bf16[4,384,256]{2,1,0:T(8,128)(2,1)S(1)}, u32[]{:S(2)}, u32[]{:S(2)}) collective-permute-start(bf16[4,384,256]{2,1,0:T(8,128)(2,1)S(1)} %constant_dynamic-slice_fusion.refs_0_.refs_2_), channel_id=1, source_target_pairs={{0,1},{8,137},{16,17},{24,153},{32,33},{40,169},{48,49},{56,185},{... | collective-permute-start | bytes 2359304 | tf_op jit(solution)/shard_map/ppermute | solution.py:33
  5.5 11.7 %collective-permute-start.4 = (bf16[4,384,256]{2,1,0:T(8,128)(2,1)S(1)}, bf16[4,384,256]{2,1,0:T(8,128)(2,1)}, u32[]{:S(2)}, u32[]{:S(2)}) collective-permute-start(bf16[4,384,256]{2,1,0:T(8,128)(2,1)S(1)} %constant_dynamic-slice_fusion.refs_0_.refs_2_), channel_id=1, source_target_pairs={{0,2},{8,14},{16,18},{24,30},{32,34},{40,46},{48,50},{56,62},{64,6... | collective-permute-start | bytes 2359304 | tf_op jit(solution)/shard_map/ppermute | solution.py:33
  16.4 14.1 %collective-permute-start.2 = (bf16[4,384,256]{2,1,0:T(8,128)(2,1)}, bf16[4,384,256]{2,1,0:T(8,128)(2,1)}, u32[]{:S(2)}, u32[]{:S(2)}) collective-permute-start(bf16[4,384,256]{2,1,0:T(8,128)(2,1)} %get-tuple-element.27), channel_id=1, source_target_pairs={{0,6},{8,10},{16,22},{24,26},{32,38},{40,42},{48,54},{56,58},{64,7... | collective-permute-start | bytes 2359304 | tf_op jit(solution)/shard_map/ppermute | solution.py:33
  17.3 21.1 %collective-permute-start.6 = (bf16[4,384,256]{2,1,0:T(8,128)(2,1)}, bf16[4,384,256]{2,1,0:T(8,128)(2,1)}, u32[]{:S(2)}, u32[]{:S(2)}) collective-permute-start(bf16[4,384,256]{2,1,0:T(8,128)(2,1)} %gate.5.refs_4_), channel_id=1, source_target_pairs={{0,1},{8,137},{16,17},{24,153},{32,33},{40,169},{48,49},{56,185},{... | collective-permute-start | bytes 2359304 | tf_op jit(solution)/shard_map/ppermute | solution.py:33
  21.2 19.1 %collective-permute-start.8 = (bf16[4,384,256]{2,1,0:T(8,128)(2,1)}, bf16[4,384,256]{2,1,0:T(8,128)(2,1)}, u32[]{:S(2)}, u32[]{:S(2)}) collective-permute-start(bf16[4,384,256]{2,1,0:T(8,128)(2,1)} %gate.5.refs_4_), channel_id=1, source_target_pairs={{0,2},{8,14},{16,18},{24,30},{32,34},{40,46},{48,50},{56,62},{64,6... | collective-permute-start | bytes 2359304 | tf_op jit(solution)/shard_map/ppermute | solution.py:33
  36.3 2.2 %copy-start.1 = (bf16[2,4,2,4,96,384]{5,4,3,2,1,0:T(8,128)(2,1)}, bf16[2,4,2,4,96,384]{5,4,3,2,1,0:T(8,128)(2,1)S(1)}, u32[]{:S(2)}) copy-start(bf16[2,4,2,4,96,384]{5,4,3,2,1,0:T(8,128)(2,1)S(1)} %flip.1.refs_1_.refs_8_.refs_0_) | copy-start | bytes 14155780
  38.4 12.4 %collective-permute-start.3 = (bf16[4,384,256]{2,1,0:T(8,128)(2,1)}, bf16[4,384,256]{2,1,0:T(8,128)(2,1)}, u32[]{:S(2)}, u32[]{:S(2)}) collective-permute-start(bf16[4,384,256]{2,1,0:T(8,128)(2,1)} %gate.4.refs_6_), channel_id=1, source_target_pairs={{0,1},{8,137},{16,17},{24,153},{32,33},{40,169},{48,49},{56,185},{... | collective-permute-start | bytes 2359304 | tf_op jit(solution)/shard_map/ppermute | solution.py:33
  38.5 12.4 %collective-permute-start.7 = (bf16[4,384,256]{2,1,0:T(8,128)(2,1)}, bf16[4,384,256]{2,1,0:T(8,128)(2,1)S(1)}, u32[]{:S(2)}, u32[]{:S(2)}) collective-permute-start(bf16[4,384,256]{2,1,0:T(8,128)(2,1)} %gate.6.refs_5_), channel_id=1, source_target_pairs={{0,2},{8,14},{16,18},{24,30},{32,34},{40,46},{48,50},{56,62},{64,6... | collective-permute-start | bytes 2359304 | tf_op jit(solution)/shard_map/ppermute | solution.py:33
  40.3 2.3 %copy-start.2 = (bf16[2,4,2,4,96,384]{5,4,3,2,1,0:T(8,128)(2,1)S(1)}, bf16[2,4,2,4,96,384]{5,4,3,2,1,0:T(8,128)(2,1)}, u32[]{:S(2)}) copy-start(bf16[2,4,2,4,96,384]{5,4,3,2,1,0:T(8,128)(2,1)} %copy-done.1) | copy-start | bytes 14155780
  45.9 4.9 %copy-start.6 = (bf16[2,192,3072]{2,1,0:T(8,128)(2,1)S(1)}, bf16[2,192,3072]{2,1,0:T(8,128)(2,1)}, u32[]{:S(2)}) copy-start(bf16[2,192,3072]{2,1,0:T(8,128)(2,1)} %copy-done.3) | copy-start | bytes 7077892
  45.9 4.9 %copy-start.10 = (bf16[2,192,3072]{2,1,0:T(8,128)(2,1)S(1)}, bf16[2,192,3072]{2,1,0:T(8,128)(2,1)}, u32[]{:S(2)}) copy-start(bf16[2,192,3072]{2,1,0:T(8,128)(2,1)} %copy-done.7) | copy-start | bytes 7077892
  54.0 6.1 %collective-permute-start.9 = (f32[192,1024]{1,0:T(8,128)S(1)}, f32[192,1024]{1,0:T(8,128)S(1)}, u32[]{:S(2)}, u32[]{:S(2)}) collective-permute-start(f32[192,1024]{1,0:T(8,128)S(1)} %get-tuple-element.31), channel_id=1, source_target_pairs={{0,8},{8,0},{16,24},{24,16},{32,40},{40,32},{48,56},{56,48},{64,72... | collective-permute-start | bytes 2359304 | tf_op jit(solution)/shard_map/ppermute | solution.py:33
  60.1 11.3 %slice-start = ((s8[4718592]{0:T(1024)(128)(4,1)}), s8[4194304]{0:T(1024)(128)(4,1)S(1)}, s32[]{:S(2)}) async-start(s8[4718592]{0:T(1024)(128)(4,1)} %bitcast.27), calls=%async_computation.2 | async-start | bytes 8388608
  63.3 8.1 %slice-start.1 = ((s8[4718592]{0:T(1024)(128)(4,1)}), s8[524288]{0:T(1024)(128)(4,1)S(1)}, s32[]{:S(2)}) async-start(s8[4718592]{0:T(1024)(128)(4,1)} %bitcast.27), calls=%async_computation.3 | async-start | bytes 1048576
  63.3 1.8 %collective-permute-start.10 = (bf16[192,1024]{1,0:T(8,128)(2,1)S(1)}, bf16[192,1024]{1,0:T(8,128)(2,1)S(1)}, u32[]{:S(2)}, u32[]{:S(2)}) collective-permute-start(bf16[192,1024]{1,0:T(8,128)(2,1)S(1)} %attend.1.refs_2_.refs_1_.refs_0_), channel_id=1, source_target_pairs={{0,8},{8,0},{16,24},{24,16},{32,40},{40,32},{48,56},{56,48},{64,72... | collective-permute-start | bytes 1179656 | tf_op jit(solution)/shard_map/ppermute | solution.py:33
  66.1 12.4 %collective-permute-start.11 = (bf16[4,8,96,128]{3,2,1,0:T(8,128)(2,1)S(1)}, bf16[4,8,96,128]{3,2,1,0:T(8,128)(2,1)S(1)}, u32[]{:S(2)}, u32[]{:S(2)}) collective-permute-start(bf16[4,8,96,128]{3,2,1,0:T(8,128)(2,1)S(1)} %get-tuple-element.33), channel_id=1, source_target_pairs={{0,2},{8,9},{16,18},{24,25},{32,34},{40,41},{48,50},{56,57},{64,66... | collective-permute-start | bytes 2359304 | tf_op jit(solution)/shard_map/ppermute | solution.py:33
  68.0 11.1 %collective-permute-start.12 = (bf16[4,8,96,128]{3,2,1,0:T(8,128)(2,1)S(1)}, bf16[4,8,96,128]{3,2,1,0:T(8,128)(2,1)S(1)}, u32[]{:S(2)}, u32[]{:S(2)}) collective-permute-start(bf16[4,8,96,128]{3,2,1,0:T(8,128)(2,1)S(1)} %get-tuple-element.35), channel_id=1, source_target_pairs={{0,6},{8,137},{16,22},{24,153},{32,38},{40,169},{48,54},{56,185},{... | collective-permute-start | bytes 2359304 | tf_op jit(solution)/shard_map/ppermute | solution.py:33
  69.8 17.7 %collective-permute-start.13 = (bf16[4,8,96,128]{3,2,1,0:T(8,128)(2,1)S(1)}, bf16[4,8,96,128]{3,2,1,0:T(8,128)(2,1)S(1)}, u32[]{:S(2)}, u32[]{:S(2)}) collective-permute-start(bf16[4,8,96,128]{3,2,1,0:T(8,128)(2,1)S(1)} %get-tuple-element.40), channel_id=1, source_target_pairs={{0,6},{8,137},{16,22},{24,153},{32,38},{40,169},{48,54},{56,185},{... | collective-permute-start | bytes 2359304 | tf_op jit(solution)/shard_map/ppermute | solution.py:33
  69.9 17.6 %collective-permute-start.15 = (bf16[4,8,96,128]{3,2,1,0:T(8,128)(2,1)S(1)}, bf16[4,8,96,128]{3,2,1,0:T(8,128)(2,1)S(1)}, u32[]{:S(2)}, u32[]{:S(2)}) collective-permute-start(bf16[4,8,96,128]{3,2,1,0:T(8,128)(2,1)S(1)} %get-tuple-element.42), channel_id=1, source_target_pairs={{0,2},{8,9},{16,18},{24,25},{32,34},{40,41},{48,50},{56,57},{64,66... | collective-permute-start | bytes 2359304 | tf_op jit(solution)/shard_map/ppermute | solution.py:33
  79.5 16.4 %collective-permute-start.16 = (bf16[4,8,96,128]{3,2,1,0:T(8,128)(2,1)S(1)}, bf16[4,8,96,128]{3,2,1,0:T(8,128)(2,1)S(1)}, u32[]{:S(2)}, u32[]{:S(2)}) collective-permute-start(bf16[4,8,96,128]{3,2,1,0:T(8,128)(2,1)S(1)} %get-tuple-element.43), channel_id=1, source_target_pairs={{0,6},{8,137},{16,22},{24,153},{32,38},{40,169},{48,54},{56,185},{... | collective-permute-start | bytes 2359304 | tf_op jit(solution)/shard_map/ppermute | solution.py:33
  81.7 14.3 %collective-permute-start.14 = (bf16[4,8,96,128]{3,2,1,0:T(8,128)(2,1)S(1)}, bf16[4,8,96,128]{3,2,1,0:T(8,128)(2,1)S(1)}, u32[]{:S(2)}, u32[]{:S(2)}) collective-permute-start(bf16[4,8,96,128]{3,2,1,0:T(8,128)(2,1)S(1)} %get-tuple-element.36.refs_10_), channel_id=1, source_target_pairs={{0,2},{8,9},{16,18},{24,25},{32,34},{40,41},{48,50},{56,57},{64,66... | collective-permute-start | bytes 2359304 | tf_op jit(solution)/shard_map/ppermute | solution.py:33
  86.1 10.9 %copy-start.13 = (f32[192,3072]{1,0:T(8,128)}, f32[192,3072]{1,0:T(8,128)S(1)}, u32[]{:S(2)}) copy-start(f32[192,3072]{1,0:T(8,128)S(1)} %get-tuple-element.38.refs_6_.refs_0_) | copy-start | bytes 7077892
  86.1 10.9 %copy-start.16 = (f32[192,3072]{1,0:T(8,128)}, f32[192,3072]{1,0:T(8,128)S(1)}, u32[]{:S(2)}) copy-start(f32[192,3072]{1,0:T(8,128)S(1)} %get-tuple-element.37.g_own) | copy-start | bytes 7077892
  97.8 5.1 %collective-permute-start.17 = (f32[192,3072]{1,0:T(8,128)}, f32[192,3072]{1,0:T(8,128)S(1)}, u32[]{:S(2)}, u32[]{:S(2)}) collective-permute-start(f32[192,3072]{1,0:T(8,128)} %gate.7), channel_id=1, source_target_pairs={{0,8},{8,0},{16,24},{24,16},{32,40},{40,32},{48,56},{56,48},{64,72... | collective-permute-start | bytes 7077896 | tf_op jit(solution)/shard_map/ppermute | solution.py:33
  98.5 12.9 %collective-permute-start.18 = (bf16[8,2,96,128]{3,2,1,0:T(8,128)(2,1)S(1)}, bf16[8,2,96,128]{3,2,1,0:T(8,128)(2,1)S(1)}, u32[]{:S(2)}, u32[]{:S(2)}) collective-permute-start(bf16[8,2,96,128]{3,2,1,0:T(8,128)(2,1)S(1)} %get-tuple-element.46), channel_id=1, source_target_pairs={{0,1},{8,10},{16,17},{24,26},{32,33},{40,42},{48,49},{56,58},{64,6... | collective-permute-start | bytes 1179656 | tf_op jit(solution)/shard_map/ppermute | solution.py:33
  98.5 13.4 %collective-permute-start.19 = (bf16[8,2,96,128]{3,2,1,0:T(8,128)(2,1)S(1)}, bf16[8,2,96,128]{3,2,1,0:T(8,128)(2,1)S(1)}, u32[]{:S(2)}, u32[]{:S(2)}) collective-permute-start(bf16[8,2,96,128]{3,2,1,0:T(8,128)(2,1)S(1)} %get-tuple-element.47), channel_id=1, source_target_pairs={{0,128},{8,12},{16,144},{24,28},{32,160},{40,44},{48,176},{56,60},... | collective-permute-start | bytes 1179656 | tf_op jit(solution)/shard_map/ppermute | solution.py:33
  102.5 9.4 %collective-permute-start.20 = (bf16[8,2,96,128]{3,2,1,0:T(8,128)(2,1)S(1)}, bf16[8,2,96,128]{3,2,1,0:T(8,128)(2,1)S(1)}, u32[]{:S(2)}, u32[]{:S(2)}) collective-permute-start(bf16[8,2,96,128]{3,2,1,0:T(8,128)(2,1)S(1)} %get-tuple-element.48), channel_id=1, source_target_pairs={{0,129},{8,14},{16,145},{24,30},{32,161},{40,46},{48,177},{56,62},... | collective-permute-start | bytes 1179656 | tf_op jit(solution)/shard_map/ppermute | solution.py:33
  106.2 5.7 %copy-start.20 = (bf16[8,2,96,128]{3,2,1,0:T(8,128)(2,1)S(1)}, bf16[8,2,96,128]{3,2,1,0:T(8,128)(2,1)}, u32[]{:S(2)}) copy-start(bf16[8,2,96,128]{3,2,1,0:T(8,128)(2,1)} %copy-done.19) | copy-start | bytes 1179652
  158.9 4.7 %collective-permute-start.21 = (bf16[2,8,2,96,128]{4,3,2,1,0:T(8,128)(2,1)S(1)}, bf16[2,8,2,96,128]{4,3,2,1,0:T(8,128)(2,1)S(1)}, u32[]{:S(2)}, u32[]{:S(2)}) collective-permute-start(bf16[2,8,2,96,128]{4,3,2,1,0:T(8,128)(2,1)S(1)} %bitcast.29), channel_id=1, source_target_pairs={{0,8},{8,0},{16,24},{24,16},{32,40},{40,32},{48,56},{56,48},{64,72... | collective-permute-start | bytes 2359304 | tf_op jit(solution)/shard_map/ppermute | solution.py:33
  (15 other events, 22.0 us)

commit v3 on v2

--- a/solution.py
+++ b/solution.py
@@ -12,6 +12,7 @@
 HEADS = 2
 ROPE_BASE = 100.0
 EPS = 1e-6
+MOST_VMEM = 56 * 1024 * 1024
 NX, NY, NZ = 4, 4, 8
 ORDER = [(0, 0), (0, 1), (1, 0), (1, 1), (3, 0), (2, 0), (3, 1), (2, 1)]
 X_AT, X_LO, CORE, SIGN = 16, 17, 18, 19
@@ -49,8 +50,9 @@
     return permute(values, target)
 
 
-def call(body, outs, operands, grid=(), scalars=0, scratch=(), flops=0, nbytes=0, name=None, after=()):
+def call(body, outs, operands, grid=(), scalars=0, scratch=(), flops=0, nbytes=0, name=None, after=(), room=0):
     count, last = len(operands), len(operands) + len(after)
+    marked = last + len(outs)
     held = 0
     arrays, in_specs, out_shapes, out_specs = [], [], [], []
     for k, item in enumerate(list(operands) + list(outs)):
@@ -67,18 +69,23 @@
         (in_specs if k < count else out_specs).append(spec)
     held += sum(math.prod(ref.shape) * ref.dtype.itemsize for ref in scratch)
     in_specs += [pl.BlockSpec(memory_space=pl.ANY) for _ in after]
-    kernel = (lambda *refs: body(*refs[:count], *refs[last:])) if after else body
-    return pl.pallas_call(
+
+    def kernel(*refs):
+        refs[marked][...] = jnp.zeros((8, 128), F32)
+        body(*refs[:count], *refs[last:marked], *refs[marked + 1 :])
+
+    *results, mark = pl.pallas_call(
         kernel,
         grid=grid or (1,),
-        out_shape=out_shapes,
+        out_shape=out_shapes + [shape((8, 128), F32)],
         in_specs=in_specs,
-        out_specs=out_specs,
+        out_specs=out_specs + [pl.BlockSpec((8, 128), lambda i: (0, 0))],
         scratch_shapes=list(scratch),
-        compiler_params=pltpu.CompilerParams(vmem_limit_bytes=held + 8 * 1024 * 1024),
+        compiler_params=pltpu.CompilerParams(vmem_limit_bytes=room or held + 8 * 1024 * 1024),
         cost_estimate=pl.CostEstimate(flops=flops, bytes_accessed=nbytes, transcendentals=0),
         name=name,
     )(*arrays, *after)
+    return results, mark
 
 
 def gate(value, after):
@@ -302,8 +309,7 @@
         g_send[:, at] = total[rows:]
 
 
-def token_grad_kernel(width, info, tokens, g_own, g_peer, out, mark, g):
-    mark[...] = jnp.zeros_like(mark)
+def token_grad_kernel(width, info, tokens, g_own, g_peer, out, g):
     rows, model = tokens.shape
     for first, ref in ((0, g_own), (8, g_peer)):
         for j in range(8):
@@ -383,7 +389,7 @@
     some = rows // 4
     row_block = ((some, model), lambda i: (i, 0))
 
-    def prep(tokens, cotangent, passed=()):
+    def prep(tokens, cotangent, passed=(), room=0):
         passed = [(value, (1,) + value.shape[1:], lambda i: (i, 0, 0)) for value in passed]
         return call(
             functools.partial(prep_kernel, width),
@@ -396,13 +402,14 @@
             flops=8 * rows * model,
             nbytes=8 * rows * model,
             name="prep",
+            room=room,
         )
 
     w = {(0, 0): lax.dynamic_slice(weights, (0, core * width, 0), (4, width, cols))}
-    later, own = prep(tokens, cotangent, [w[0, 0]])
-    (peer,) = prep(shift(tokens, dc=1), shift(cotangent, dc=1))
+    (later, own), own_mark = prep(tokens, cotangent, [w[0, 0]], room=MOST_VMEM)
+    (peer,), peer_mark = prep(shift(tokens, dc=1), shift(cotangent, dc=1))
     one = (1, rows, model // 2)
-    (turned,) = call(
+    (turned,), turned_mark = call(
         functools.partial(flip_kernel, width),
         [(shape((2, 4, 2, 4, half // 2, 2 * rows)), (2, 4, 1, 4, half // 2, 2 * rows), lambda i: (0, 0, i, 0, 0, 0))],
         [info, (own, one, lambda i: (i, 0, 0)), (peer, one, lambda i: (i, 0, 0))],
@@ -412,10 +419,10 @@
         name="flip",
     )
     w[0, 1] = shift(w[0, 0], dx=1)
-    w[1, 0] = gate(shift(w[0, 0], dy=1), [own, w[0, 1]])
-    w[3, 0] = gate(shift(later, dy=-1), [peer])
+    w[1, 0] = gate(shift(w[0, 0], dy=1), [own_mark, w[0, 1]])
+    w[3, 0] = gate(shift(later, dy=-1), [peer_mark])
     w[2, 0] = shift(w[1, 0], dy=1)
-    w[1, 1] = gate(shift(w[1, 0], dx=1), [turned])
+    w[1, 1] = gate(shift(w[1, 0], dx=1), [turned_mark])
     w[3, 1] = shift(w[3, 0], dx=1)
     w[2, 1] = shift(w[1, 1], dy=1)
     shards = [w[place] for place in ORDER]
@@ -434,7 +441,7 @@
         span = 2 * pairs * width
         columns = functools.partial(lambda c, m: (m // 3, 0, c), first // pairs)
         acc = ((rows, cols), lambda m: (0, m))
-        lin = call(
+        lin, _ = call(
             functools.partial(linear_kernel, pairs),
             [(lin_shape, *acc)] * 2,
             [(own, (1, rows, span), columns), (peer, (1, rows, span), columns)]
@@ -444,11 +451,11 @@
             flops=2 * 2 * rows * 2 * pairs * width * 4 * cols,
             nbytes=2 * pairs * width * 8 * cols + 8 * rows * 2 * pairs * width,
             name="linear",
-            after=[] if first else [turned, cos_t, sin_t, ends],
+            after=[] if first else [turned_mark, cos_t, sin_t],
         )
     lin_own, lin_send = lin
     lin_peer = shift(lin_send, dc=1)
-    (y_own,) = call(
+    (y_own,), _ = call(
         attend_kernel,
         [shape((rows, 4 * cols))],
         [ends, lin_own, lin_peer, cos_t, sin_t],
@@ -472,7 +479,7 @@
             flops=int(part * 2 * 2 * rows * (model // 2) * 4 * cols),
             nbytes=int(part * (4 * model * cols + 8 * rows * model)),
             name="terms",
-        )
+        )[0]
 
     far = terms([2])
     far = [along(far[0], first=1), along(far[1], first=-1)]
@@ -481,7 +488,7 @@
     near = terms([1, 0])
 
     per_u = ((1, 8, quarter, 128), lambda u: (u, 0, 0, 0))
-    joined = sum_call(
+    joined, join_mark = sum_call(
         join_kernel,
         "join",
         [(piece, *per_u)] * 2,
@@ -491,32 +498,32 @@
     ahead = [along(joined[0], first=1), along(joined[1], first=-1)]
 
     most = ((3, width, cols), lambda _: (0, 0, 0))
-    g_own, g_send = call(
+    (g_own, g_send), g_mark = call(
         functools.partial(normed_grad_kernel, width),
         [shape((rows, model // 2), F32)] * 2,
         [y_own, y_peer] + [(w_j, *most) for w_j in shards],
         flops=2 * rows * model * 3 * cols,
         nbytes=4 * model * cols + 4 * rows * model,
         name="normed_grad",
-        after=[joined[0]],
+        after=[join_mark],
     )
 
     per_n = ((4, 2, quarter, 128), lambda n: (0, n, 0, 0))
     mixed = shape((8, 2, quarter, 128))
     out_n = ((2, 2, quarter, 128), lambda n: (n, 0, 0, 0))
-    halfway = sum_call(
+    halfway, halfway_mark = sum_call(
         sides_kernel,
         "sides",
         [(mixed, *out_n)] * 4,
         [(value, *per_n) for value in (near[2], back[0], ahead[0], near[3], back[1], ahead[1])],
         grid=(4,),
-        after=[g_send],
-    )
-    g_peer = shift(gate(g_send, [halfway[0]]), dc=1)
+        after=[g_mark],
+    )
+    g_peer = shift(gate(g_send, [halfway_mark]), dc=1)
     g_rows = ((some, model // 2), lambda i: (i, 0))
-    grad_tokens, mark = call(
+    (grad_tokens,), mark = call(
         functools.partial(token_grad_kernel, width),
-        [(shape((rows, model)), *row_block), (shape((8, 128), F32), (8, 128), lambda i: (0, 0))],
+        [(shape((rows, model)), *row_block)],
         [info, (tokens, *row_block), (g_own, *g_rows), (g_peer, *g_rows)],
         grid=(4,),
         scalars=1,
@@ -524,10 +531,11 @@
         flops=16 * rows * model,
         nbytes=8 * rows * model,
         name="token_grad",
+        room=MOST_VMEM,
     )
 
     rest = [along(halfway[d], second=d) for d in range(1, 4)]
-    (by_z,) = sum_call(
+    (by_z,), _ = sum_call(
         seconds_kernel,
         "seconds",
         [(mixed, *out_n)],
@@ -535,7 +543,7 @@
         grid=(4,),
         after=[mark],
     )
-    (spread,) = sum_call(last_kernel, "last", [shape((2 * NZ, 2, quarter, 128))], [exchange(by_z, False)])
+    (spread,), _ = sum_call(last_kernel, "last", [shape((2 * NZ, 2, quarter, 128))], [exchange(by_z, False)])
     done = exchange(spread, True).reshape(2, NZ, 2, quarter, 128)
     dims = (4, shard_rows, cols)
     weight_grads = place(jnp.stack([core]).astype(jnp.int32), done, dims)

time: 166 us -> 172 us (1.036)
  Pallas kernels: 39.6 us -> 48.1 us
  local copies, waits for them, and re-layouts: 22.3 us -> 16.7 us
  waiting for transfers between devices: 22.1 us -> 25.4 us
    pallas_call x15, Pallas kernels: 36.2 us -> 44.6 us  [call(): pl.pallas_call(kernel, grid=grid or (1,), out_shape=out_shapes + [shape((...]
    unnamed x50 -> x64, local copies, waits for them, and re-layouts: 21.6 us -> 15.4 us
    ppermute x22, waiting for transfers between devices: 22.1 us -> 25.4 us  [permute(): return lax.ppermute(values, ('dp', 'fsdp'), pairs)]
  transfers between devices with their start and end apart: 22 -> 22, of which waited for: 11 -> 11; matrix products, arithmetic and copies ran while one was open for 1% -> 2% of each run, Pallas kernels for 18% -> 20%
where the time goes in v3:
time: 172 us
  Pallas kernels  48.1 us (28%)
  blocking collectives  46.2 us (27%)
  starting transfers between devices  30.7 us (18%)
  waiting for transfers between devices  25.4 us (15%)
  local copies, waits for them, and re-layouts  16.7 us (10%)
  between operations  2.81 us (2%)
  other arithmetic  1.72 us (1%)
    all_to_all x2, blocking collectives, exchange(): lax.all_to_all(values, 'dp', split_axis=0, concat_axis=0, axis_index_grou...  46.2 us
    pallas_call x15, Pallas kernels, call(): pl.pallas_call(kernel, grid=grid or (1,), out_shape=out_shapes + [shape((...  44.6 us
    ppermute x22, starting transfers between devices, permute(): return lax.ppermute(values, ('dp', 'fsdp'), pairs)  30.7 us
    ppermute x22, waiting for transfers between devices, permute(): return lax.ppermute(values, ('dp', 'fsdp'), pairs)  25.4 us
    unnamed x64, local copies, waits for them, and re-layouts  15.4 us
    pallas_call x2, Pallas kernels, place(): pl.pallas_call(place_kernel, grid_spec=pltpu.PrefetchScalarGridSpec(num_s...  3.47 us
  transfers between devices with their start and end apart: 22, of which 11 were waited for; matrix products, arithmetic and copies ran while one was open for 2% of the time, Pallas kernels for 20%

profile of v3, /device:TPU:1, one launch (start us, length us, event | category | flops | bytes accessed | tf_op | source)
XLA Modules:
  0.0 171.6 jit_solution(4643137070643896259)
XLA Ops:
  0.6 3.3 %collective-permute-start = (bf16[192,6144]{1,0:T(8,128)(2,1)}, bf16[192,6144]{1,0:T(8,128)(2,1)}, u32[]{:S(2)}, u32[]{:S(2)}) collective-permute-start(bf16[192,6144]{1,0:T(8,128)(2,1)} %refs_1_.3), channel_id=1, source_target_pairs={{0,8},{8,0},{16,24},{24,16},{32,40},{40,32},{48,56},{56,48},{64,72... | collective-permute-start | bytes 7077896 | tf_op jit(solution)/shard_map/ppermute | solution.py:34
  4.1 1.6 collective-permute-start.4
  5.8 2.5 %collective-permute-start.5 = (bf16[4,384,256]{2,1,0:T(8,128)(2,1)S(1)}, bf16[4,384,256]{2,1,0:T(8,128)(2,1)S(1)}, u32[]{:S(2)}, u32[]{:S(2)}) collective-permute-start(bf16[4,384,256]{2,1,0:T(8,128)(2,1)S(1)} %constant_dynamic-slice_fusion.refs_3_.refs_2_), channel_id=1, source_target_pairs={{0,1},{8,137},{16,17},{24,153},{32,33},{40,169},{48,49},{56,185},{... | collective-permute-start | bytes 2359304 | tf_op jit(solution)/shard_map/ppermute | solution.py:34
  8.8 5.4 %prep.2 = (bf16[4,384,256]{2,1,0:T(8,128)(2,1)}, bf16[2,192,3072]{2,1,0:T(8,128)(2,1)}, f32[8,128]{1,0:T(8,128)}) custom-call(s32[20]{0:T(128)} %stack.96.refs_0_, bf16[192,6144]{1,0:T(8,128)(2,1)} %refs_1_.3, bf16[192,6144]{1,0:T(8,128)(2,1)} %refs_2_.1, bf16[4,384,256]{2,1,0:T(8,128)(2,1)} %copy-done.8), custom_call_target="tpu_custom_call" | custom-call | flops 9437184 | bytes 9437184 | tf_op jit(solution)/shard_map/prep/pallas_call | solution.py:77
  15.5 1.7 collective-permute-done.5.refs_2_.refs_3_
  18.1 3.1 %collective-permute-start.6 = (bf16[4,384,256]{2,1,0:T(8,128)(2,1)}, bf16[4,384,256]{2,1,0:T(8,128)(2,1)S(1)}, u32[]{:S(2)}, u32[]{:S(2)}) collective-permute-start(bf16[4,384,256]{2,1,0:T(8,128)(2,1)} %gate.5.refs_4_), channel_id=1, source_target_pairs={{0,1},{8,137},{16,17},{24,153},{32,33},{40,169},{48,49},{56,185},{... | collective-permute-start | bytes 2359304 | tf_op jit(solution)/shard_map/ppermute | solution.py:34
  21.2 2.7 %collective-permute-start.8 = (bf16[4,384,256]{2,1,0:T(8,128)(2,1)}, bf16[4,384,256]{2,1,0:T(8,128)(2,1)}, u32[]{:S(2)}, u32[]{:S(2)}) collective-permute-start(bf16[4,384,256]{2,1,0:T(8,128)(2,1)} %gate.5.refs_4_), channel_id=1, source_target_pairs={{0,2},{8,14},{16,18},{24,30},{32,34},{40,46},{48,50},{56,62},{64,6... | collective-permute-start | bytes 2359304 | tf_op jit(solution)/shard_map/ppermute | solution.py:34
  23.9 4.2 %prep.3 = (bf16[2,192,3072]{2,1,0:T(8,128)(2,1)S(1)}, f32[8,128]{1,0:T(8,128)S(1)}) custom-call(s32[20]{0:T(128)S(1)} %copy-done.23, bf16[192,6144]{1,0:T(8,128)(2,1)} %collective-permute-done.refs_1_, bf16[192,6144]{1,0:T(8,128)(2,1)} %collective-permute-done.1.refs_2_), custom_call_target="tpu_custom_call" | custom-call | flops 9437184 | bytes 9437184 | tf_op jit(solution)/shard_map/prep/pallas_call | solution.py:77
  28.6 2.4 %flip.1 = (bf16[2,4,2,4,96,384]{5,4,3,2,1,0:T(8,128)(2,1)S(1)}, f32[8,128]{1,0:T(8,128)S(1)}) custom-call(s32[20]{0:T(128)S(1)} %copy-done.23, bf16[2,192,3072]{2,1,0:T(8,128)(2,1)S(1)} %copy-done.2, bf16[2,192,3072]{2,1,0:T(8,128)(2,1)S(1)} %get-tuple-element.38.refs_2_.refs_1_), custom_call_target="tpu_custom_call" | custom-call | bytes 9437184 | tf_op jit(solution)/shard_map/flip/pallas_call | solution.py:77
  31.1 2.2 %copy-done.1 = bf16[2,4,2,4,96,384]{5,4,3,2,1,0:T(8,128)(2,1)} copy-done((bf16[2,4,2,4,96,384]{5,4,3,2,1,0:T(8,128)(2,1)}, bf16[2,4,2,4,96,384]{5,4,3,2,1,0:T(8,128)(2,1)S(1)}, u32[]{:S(2)}) %copy-start.1) | copy-done | bytes 4718616
  34.8 5.4 %collective-permute-done.2.refs_0_ = bf16[4,384,256]{2,1,0:T(8,128)(2,1)S(1)} collective-permute-done((bf16[4,384,256]{2,1,0:T(8,128)(2,1)}, bf16[4,384,256]{2,1,0:T(8,128)(2,1)S(1)}, u32[]{:S(2)}, u32[]{:S(2)}) %collective-permute-start.2) | collective-permute-done | bytes 786464 | tf_op jit(solution)/shard_map/ppermute | solution.py:34
  42.1 1.7 copy-done.3
  43.8 1.7 copy-done.6
  48.8 5.1 %linear.2 = (f32[192,1024]{1,0:T(8,128)S(1)}, f32[192,1024]{1,0:T(8,128)S(1)}, f32[8,128]{1,0:T(8,128)}) custom-call(bf16[2,192,3072]{2,1,0:T(8,128)(2,1)S(1)} %copy-done.3, bf16[2,192,3072]{2,1,0:T(8,128)(2,1)S(1)} %copy-done.6, bf16[4,384,256]{2,1,0:T(8,128)(2,1)S(1)} %copy-done.9, bf16[4,384,256]{2,1,0:T(8,128)(2,1)S(1)} %copy-done.17, ...), custom_call_target="tpu_custom_call" | custom-call | flops 1811939328 | bytes 8257536 | tf_op jit(solution)/shard_map/linear/pallas_call | solution.py:77
  54.0 3.9 %linear.3 = (f32[192,1024]{1,0:T(8,128)S(1)}, f32[192,1024]{1,0:T(8,128)S(1)}, f32[8,128]{1,0:T(8,128)}) custom-call(bf16[2,192,3072]{2,1,0:T(8,128)(2,1)S(1)} %copy-done.4, bf16[2,192,3072]{2,1,0:T(8,128)(2,1)S(1)} %copy-done.7, bf16[4,384,256]{2,1,0:T(8,128)(2,1)S(1)} %collective-permute-done.3.refs_2_.refs_8_, ...), custom_call_target="tpu_custom_call" | custom-call | flops 603979776 | bytes 2752512 | tf_op jit(solution)/shard_map/linear/pallas_call | solution.py:77
  57.9 1.7 collective-permute-start.9
  62.8 3.7 %attend.1 = (bf16[192,1024]{1,0:T(8,128)(2,1)S(1)}, f32[8,128]{1,0:T(8,128)}) custom-call(s32[3]{0:T(128)S(1)} %pad_add_fusion.refs_0_, f32[192,1024]{1,0:T(8,128)S(1)} %get-tuple-element.45.refs_1_, f32[192,1024]{1,0:T(8,128)S(1)} %collective-permute-done.9.refs_2_, f32[192,128]{1,0:T(8,128)S(1)} %get-tuple-element.86.refs_9_.refs_3_, ...), custom_call_target="tpu_custom_call" | custom-call | flops 188743680 | bytes 1966080 | tf_op jit(solution)/shard_map/attend/pallas_call | solution.py:77
  66.5 1.7 %collective-permute-done.10.refs_3_.refs_2_.refs_1_ = bf16[192,1024]{1,0:T(8,128)(2,1)S(1)} collective-permute-done((bf16[192,1024]{1,0:T(8,128)(2,1)S(1)}, bf16[192,1024]{1,0:T(8,128)(2,1)S(1)}, u32[]{:S(2)}, u32[]{:S(2)}) %collective-permute-start.10) | collective-permute-done | bytes 393248 | tf_op jit(solution)/shard_map/ppermute | solution.py:34
  70.7 1.8 %collective-permute-start.12 = (bf16[4,8,96,128]{3,2,1,0:T(8,128)(2,1)S(1)}, bf16[4,8,96,128]{3,2,1,0:T(8,128)(2,1)S(1)}, u32[]{:S(2)}, u32[]{:S(2)}) collective-permute-start(bf16[4,8,96,128]{3,2,1,0:T(8,128)(2,1)S(1)} %get-tuple-element.52), channel_id=1, source_target_pairs={{0,6},{8,137},{16,22},{24,153},{32,38},{40,169},{48,54},{56,185},{... | collective-permute-start | bytes 2359304 | tf_op jit(solution)/shard_map/ppermute | solution.py:34
  75.4 2.3 %terms.3 = (bf16[4,8,96,128]{3,2,1,0:T(8,128)(2,1)S(1)}, bf16[4,8,96,128]{3,2,1,0:T(8,128)(2,1)S(1)}, bf16[4,8,96,128]{3,2,1,0:T(8,128)(2,1)S(1)}, bf16[4,8,96,128]{3,2,1,0:T(8,128)(2,1)S(1)}, f32[8,128]{1,0:T(8,128)}) custom-call(bf16[2,4,2,4,96,384]{5,4,3,2,1,0:T(8,128)(2,1)S(1)} %bitcast.28, bf16[2,4,2,4,96,384]{5,4,3,2,1,0:T(8,128)(2,1)S(1)} %bitcast.28, ...), custom_call_target="tpu_custom_call" | custom-call | flops 1207959552 | bytes 7864320 | tf_op jit(solution)/shard_map/terms/pallas_call | solution.py:77
  77.7 4.4 %collective-permute-done.11.refs_1_ = bf16[4,8,96,128]{3,2,1,0:T(8,128)(2,1)S(1)} collective-permute-done((bf16[4,8,96,128]{3,2,1,0:T(8,128)(2,1)S(1)}, bf16[4,8,96,128]{3,2,1,0:T(8,128)(2,1)S(1)}, u32[]{:S(2)}, u32[]{:S(2)}) %collective-permute-start.11) | collective-permute-done | bytes 786464 | tf_op jit(solution)/shard_map/ppermute | solution.py:34
  83.2 1.5 collective-permute-start.14
  85.9 4.0 %normed_grad.1 = (f32[192,3072]{1,0:T(8,128)S(1)}, f32[192,3072]{1,0:T(8,128)S(1)}, f32[8,128]{1,0:T(8,128)S(1)}) custom-call(bf16[192,1024]{1,0:T(8,128)(2,1)S(1)} %get-tuple-element.47.refs_2_.refs_1_.refs_0_, bf16[192,1024]{1,0:T(8,128)(2,1)S(1)} %collective-permute-done.10.refs_3_.refs_2_.refs_1_, bf16[4,384,256]{2,1,0:T(8,128)(2,1)S(1)} %copy-done.9, ...), custom_call_target="tpu_custom_call" | custom-call | flops 1811939328 | bytes 11010048 | tf_op jit(solution)/shard_map/normed_grad/pallas_call | solution.py:77
  91.2 7.7 %collective-permute-done.14.refs_2_ = bf16[4,8,96,128]{3,2,1,0:T(8,128)(2,1)S(1)} collective-permute-done((bf16[4,8,96,128]{3,2,1,0:T(8,128)(2,1)S(1)}, bf16[4,8,96,128]{3,2,1,0:T(8,128)(2,1)S(1)}, u32[]{:S(2)}, u32[]{:S(2)}) %collective-permute-start.14) | collective-permute-done | bytes 786464 | tf_op jit(solution)/shard_map/ppermute | solution.py:34
  99.6 1.9 %sides.1 = (bf16[8,2,96,128]{3,2,1,0:T(8,128)(2,1)S(1)}, bf16[8,2,96,128]{3,2,1,0:T(8,128)(2,1)}, bf16[8,2,96,128]{3,2,1,0:T(8,128)(2,1)S(1)}, bf16[8,2,96,128]{3,2,1,0:T(8,128)(2,1)S(1)}, f32[8,128]{1,0:T(8,128)S(1)}) custom-call(bf16[4,8,96,128]{3,2,1,0:T(8,128)(2,1)S(1)} %get-tuple-element.56.refs_0_, ...), custom_call_target="tpu_custom_call" | custom-call | flops 2359296 | bytes 6291456 | tf_op jit(solution)/shard_map/sides/pallas_call | solution.py:77
  103.8 2.8 %collective-permute-start.19 = (bf16[8,2,96,128]{3,2,1,0:T(8,128)(2,1)S(1)}, bf16[8,2,96,128]{3,2,1,0:T(8,128)(2,1)S(1)}, u32[]{:S(2)}, u32[]{:S(2)}) collective-permute-start(bf16[8,2,96,128]{3,2,1,0:T(8,128)(2,1)S(1)} %get-tuple-element.67), channel_id=1, source_target_pairs={{0,128},{8,12},{16,144},{24,28},{32,160},{40,44},{48,176},{56,60},... | collective-permute-start | bytes 1179656 | tf_op jit(solution)/shard_map/ppermute | solution.py:34
  109.2 6.8 %token_grad.1 = (bf16[192,6144]{1,0:T(8,128)(2,1)}, f32[8,128]{1,0:T(8,128)}) custom-call(s32[20]{0:T(128)} %stack.96.refs_0_, bf16[192,6144]{1,0:T(8,128)(2,1)} %refs_1_.3, f32[192,3072]{1,0:T(8,128)} %copy-done.19, f32[192,3072]{1,0:T(8,128)} %copy-done.27), custom_call_target="tpu_custom_call" | custom-call | flops 18874368 | bytes 9437184 | tf_op jit(solution)/shard_map/token_grad/pallas_call | solution.py:77
  118.0 21.4 %all_to_all.10.refs_0_ = bf16[8,2,96,128]{3,2,1,0:T(8,128)(2,1)S(1)} all-to-all(bf16[8,2,96,128]{3,2,1,0:T(8,128)(2,1)S(1)} %get-tuple-element.70), channel_id=1, replica_groups={{0,16,32,48,64,80,96,112},{8,24,40,56,72,88,104,120},{128,144,160,176,1..., dimensions={0} | all-to-all | bytes 786432 | tf_op jit(solution)/shard_map/all_to_all | solution.py:365
  140.0 24.9 %all_to_all.11 = bf16[16,2,96,128]{3,2,1,0:T(8,128)(2,1)S(1)} all-to-all(bf16[16,2,96,128]{3,2,1,0:T(8,128)(2,1)S(1)} %get-tuple-element.71), channel_id=1, replica_groups={{0,16,32,48,64,80,96,112,128,144,160,176,192,208,224,240},{8,24,40,56,7..., dimensions={0} | all-to-all | bytes 1572864 | tf_op jit(solution)/shard_map/all_to_all | solution.py:365
  164.8 3.1 %collective-permute-start.21 = (bf16[2,8,2,96,128]{4,3,2,1,0:T(8,128)(2,1)S(1)}, bf16[2,8,2,96,128]{4,3,2,1,0:T(8,128)(2,1)S(1)}, u32[]{:S(2)}, u32[]{:S(2)}) collective-permute-start(bf16[2,8,2,96,128]{4,3,2,1,0:T(8,128)(2,1)S(1)} %bitcast.29), channel_id=1, source_target_pairs={{0,8},{8,0},{16,24},{24,16},{32,40},{40,32},{48,56},{56,48},{64,72... | collective-permute-start | bytes 2359304 | tf_op jit(solution)/shard_map/ppermute | solution.py:34
  168.0 1.7 %place.2.refs_0_ = f32[4,768,256]{2,1,0:T(8,128)} custom-call(s32[1]{0:T(128)} %bitcast.18.at, bf16[2,8,2,96,128]{4,3,2,1,0:T(8,128)(2,1)S(1)} %bitcast.30), custom_call_target="tpu_custom_call" | custom-call | flops 1 | bytes 6291456 | tf_op jit(solution)/shard_map/place/pallas_call | solution.py:341
  169.9 1.7 %place.3 = f32[4,768,256]{2,1,0:T(8,128)} custom-call(s32[1]{0:T(128)} %bitcast.25.at, bf16[2,8,2,96,128]{4,3,2,1,0:T(8,128)(2,1)S(1)} %collective-permute-done.21.blocks, f32[4,768,256]{2,1,0:T(8,128)} %place.2.refs_0_), custom_call_target="tpu_custom_call", output_to_operand_aliasing={{}: (2, {})} | custom-call | flops 1 | bytes 6291456 | tf_op jit(solution)/shard_map/place/pallas_call | solution.py:341
  (108 shorter events, 28.8 us)
Async XLA Ops:
  0.6 23.2 %collective-permute-start = (bf16[192,6144]{1,0:T(8,128)(2,1)}, bf16[192,6144]{1,0:T(8,128)(2,1)}, u32[]{:S(2)}, u32[]{:S(2)}) collective-permute-start(bf16[192,6144]{1,0:T(8,128)(2,1)} %refs_1_.3), channel_id=1, source_target_pairs={{0,8},{8,0},{16,24},{24,16},{32,40},{40,32},{48,56},{56,48},{64,72... | collective-permute-start | bytes 7077896 | tf_op jit(solution)/shard_map/ppermute | solution.py:34
  4.0 19.9 %collective-permute-start.1 = (bf16[192,6144]{1,0:T(8,128)(2,1)}, bf16[192,6144]{1,0:T(8,128)(2,1)}, u32[]{:S(2)}, u32[]{:S(2)}) collective-permute-start(bf16[192,6144]{1,0:T(8,128)(2,1)} %refs_2_.1), channel_id=1, source_target_pairs={{0,8},{8,0},{16,24},{24,16},{32,40},{40,32},{48,56},{56,48},{64,72... | collective-permute-start | bytes 7077896 | tf_op jit(solution)/shard_map/ppermute | solution.py:34
  4.1 11.3 %collective-permute-start.4 = (bf16[4,384,256]{2,1,0:T(8,128)(2,1)S(1)}, bf16[4,384,256]{2,1,0:T(8,128)(2,1)}, u32[]{:S(2)}, u32[]{:S(2)}) collective-permute-start(bf16[4,384,256]{2,1,0:T(8,128)(2,1)S(1)} %constant_dynamic-slice_fusion.refs_3_.refs_2_), channel_id=1, source_target_pairs={{0,2},{8,14},{16,18},{24,30},{32,34},{40,46},{48,50},{56,62},{64,6... | collective-permute-start | bytes 2359304 | tf_op jit(solution)/shard_map/ppermute | solution.py:34
  5.8 11.4 %collective-permute-start.5 = (bf16[4,384,256]{2,1,0:T(8,128)(2,1)S(1)}, bf16[4,384,256]{2,1,0:T(8,128)(2,1)S(1)}, u32[]{:S(2)}, u32[]{:S(2)}) collective-permute-start(bf16[4,384,256]{2,1,0:T(8,128)(2,1)S(1)} %constant_dynamic-slice_fusion.refs_3_.refs_2_), channel_id=1, source_target_pairs={{0,1},{8,137},{16,17},{24,153},{32,33},{40,169},{48,49},{56,185},{... | collective-permute-start | bytes 2359304 | tf_op jit(solution)/shard_map/ppermute | solution.py:34
  14.3 9.6 %copy-start.23 = (s32[20]{0:T(128)S(1)}, s32[20]{0:T(128)}, u32[]{:S(2)}) copy-start(s32[20]{0:T(128)} %stack.96.refs_0_) | copy-start | bytes 244
  18.1 15.8 %collective-permute-start.6 = (bf16[4,384,256]{2,1,0:T(8,128)(2,1)}, bf16[4,384,256]{2,1,0:T(8,128)(2,1)S(1)}, u32[]{:S(2)}, u32[]{:S(2)}) collective-permute-start(bf16[4,384,256]{2,1,0:T(8,128)(2,1)} %gate.5.refs_4_), channel_id=1, source_target_pairs={{0,1},{8,137},{16,17},{24,153},{32,33},{40,169},{48,49},{56,185},{... | collective-permute-start | bytes 2359304 | tf_op jit(solution)/shard_map/ppermute | solution.py:34
  21.2 7.5 %copy-start.2 = (bf16[2,192,3072]{2,1,0:T(8,128)(2,1)S(1)}, bf16[2,192,3072]{2,1,0:T(8,128)(2,1)}, u32[]{:S(2)}) copy-start(bf16[2,192,3072]{2,1,0:T(8,128)(2,1)} %get-tuple-element.37.refs_1_.refs_0_) | copy-start | bytes 7077892
  21.2 19.0 %collective-permute-start.2 = (bf16[4,384,256]{2,1,0:T(8,128)(2,1)}, bf16[4,384,256]{2,1,0:T(8,128)(2,1)S(1)}, u32[]{:S(2)}, u32[]{:S(2)}) collective-permute-start(bf16[4,384,256]{2,1,0:T(8,128)(2,1)} %get-tuple-element.39), channel_id=1, source_target_pairs={{0,6},{8,10},{16,22},{24,26},{32,38},{40,42},{48,54},{56,58},{64,7... | collective-permute-start | bytes 2359304 | tf_op jit(solution)/shard_map/ppermute | solution.py:34
  21.2 20.9 %collective-permute-start.8 = (bf16[4,384,256]{2,1,0:T(8,128)(2,1)}, bf16[4,384,256]{2,1,0:T(8,128)(2,1)}, u32[]{:S(2)}, u32[]{:S(2)}) collective-permute-start(bf16[4,384,256]{2,1,0:T(8,128)(2,1)} %gate.5.refs_4_), channel_id=1, source_target_pairs={{0,2},{8,14},{16,18},{24,30},{32,34},{40,46},{48,50},{56,62},{64,6... | collective-permute-start | bytes 2359304 | tf_op jit(solution)/shard_map/ppermute | solution.py:34
  33.9 8.2 %copy-start.9 = (bf16[4,384,256]{2,1,0:T(8,128)(2,1)S(1)}, bf16[4,384,256]{2,1,0:T(8,128)(2,1)}, u32[]{:S(2)}) copy-start(bf16[4,384,256]{2,1,0:T(8,128)(2,1)} %copy-done.8) | copy-start | bytes 2359300
  34.8 19.2 %collective-permute-start.7 = (bf16[4,384,256]{2,1,0:T(8,128)(2,1)}, bf16[4,384,256]{2,1,0:T(8,128)(2,1)}, u32[]{:S(2)}, u32[]{:S(2)}) collective-permute-start(bf16[4,384,256]{2,1,0:T(8,128)(2,1)} %gate.6.refs_5_), channel_id=1, source_target_pairs={{0,2},{8,14},{16,18},{24,30},{32,34},{40,46},{48,50},{56,62},{64,6... | collective-permute-start | bytes 2359304 | tf_op jit(solution)/shard_map/ppermute | solution.py:34
  41.0 12.9 %collective-permute-start.3 = (bf16[4,384,256]{2,1,0:T(8,128)(2,1)}, bf16[4,384,256]{2,1,0:T(8,128)(2,1)S(1)}, u32[]{:S(2)}, u32[]{:S(2)}) collective-permute-start(bf16[4,384,256]{2,1,0:T(8,128)(2,1)} %gate.4.refs_6_), channel_id=1, source_target_pairs={{0,1},{8,137},{16,17},{24,153},{32,33},{40,169},{48,49},{56,185},{... | collective-permute-start | bytes 2359304 | tf_op jit(solution)/shard_map/ppermute | solution.py:34
  53.9 14.3 %slice-start = ((s8[4718592]{0:T(1024)(128)(4,1)}), s8[4194304]{0:T(1024)(128)(4,1)S(1)}, s32[]{:S(2)}) async-start(s8[4718592]{0:T(1024)(128)(4,1)} %bitcast.27), calls=%async_computation.2 | async-start | bytes 8388608
  54.0 14.3 %slice-start.1 = ((s8[4718592]{0:T(1024)(128)(4,1)}), s8[524288]{0:T(1024)(128)(4,1)S(1)}, s32[]{:S(2)}) async-start(s8[4718592]{0:T(1024)(128)(4,1)} %bitcast.27), calls=%async_computation.3 | async-start | bytes 1048576
  57.9 4.9 %collective-permute-start.9 = (f32[192,1024]{1,0:T(8,128)S(1)}, f32[192,1024]{1,0:T(8,128)S(1)}, u32[]{:S(2)}, u32[]{:S(2)}) collective-permute-start(f32[192,1024]{1,0:T(8,128)S(1)} %get-tuple-element.46), channel_id=1, source_target_pairs={{0,8},{8,0},{16,24},{24,16},{32,40},{40,32},{48,56},{56,48},{64,72... | collective-permute-start | bytes 2359304 | tf_op jit(solution)/shard_map/ppermute | solution.py:34
  66.5 1.7 %collective-permute-start.10 = (bf16[192,1024]{1,0:T(8,128)(2,1)S(1)}, bf16[192,1024]{1,0:T(8,128)(2,1)S(1)}, u32[]{:S(2)}, u32[]{:S(2)}) collective-permute-start(bf16[192,1024]{1,0:T(8,128)(2,1)S(1)} %get-tuple-element.47.refs_2_.refs_1_.refs_0_), channel_id=1, source_target_pairs={{0,8},{8,0},{16,24},{24,16},{32,40},{40,32},{48,56},{56,48},{64,72... | collective-permute-start | bytes 1179656 | tf_op jit(solution)/shard_map/ppermute | solution.py:34
  69.7 12.3 %collective-permute-start.11 = (bf16[4,8,96,128]{3,2,1,0:T(8,128)(2,1)S(1)}, bf16[4,8,96,128]{3,2,1,0:T(8,128)(2,1)S(1)}, u32[]{:S(2)}, u32[]{:S(2)}) collective-permute-start(bf16[4,8,96,128]{3,2,1,0:T(8,128)(2,1)S(1)} %get-tuple-element.50), channel_id=1, source_target_pairs={{0,2},{8,9},{16,18},{24,25},{32,34},{40,41},{48,50},{56,57},{64,66... | collective-permute-start | bytes 2359304 | tf_op jit(solution)/shard_map/ppermute | solution.py:34
  70.7 12.1 %collective-permute-start.12 = (bf16[4,8,96,128]{3,2,1,0:T(8,128)(2,1)S(1)}, bf16[4,8,96,128]{3,2,1,0:T(8,128)(2,1)S(1)}, u32[]{:S(2)}, u32[]{:S(2)}) collective-permute-start(bf16[4,8,96,128]{3,2,1,0:T(8,128)(2,1)S(1)} %get-tuple-element.52), channel_id=1, source_target_pairs={{0,6},{8,137},{16,22},{24,153},{32,38},{40,169},{48,54},{56,185},{... | collective-permute-start | bytes 2359304 | tf_op jit(solution)/shard_map/ppermute | solution.py:34
  73.9 17.3 %collective-permute-start.13 = (bf16[4,8,96,128]{3,2,1,0:T(8,128)(2,1)S(1)}, bf16[4,8,96,128]{3,2,1,0:T(8,128)(2,1)S(1)}, u32[]{:S(2)}, u32[]{:S(2)}) collective-permute-start(bf16[4,8,96,128]{3,2,1,0:T(8,128)(2,1)S(1)} %get-tuple-element.57), channel_id=1, source_target_pairs={{0,6},{8,137},{16,22},{24,153},{32,38},{40,169},{48,54},{56,185},{... | collective-permute-start | bytes 2359304 | tf_op jit(solution)/shard_map/ppermute | solution.py:34
  75.2 16.0 %collective-permute-start.15 = (bf16[4,8,96,128]{3,2,1,0:T(8,128)(2,1)S(1)}, bf16[4,8,96,128]{3,2,1,0:T(8,128)(2,1)S(1)}, u32[]{:S(2)}, u32[]{:S(2)}) collective-permute-start(bf16[4,8,96,128]{3,2,1,0:T(8,128)(2,1)S(1)} %get-tuple-element.60), channel_id=1, source_target_pairs={{0,2},{8,9},{16,18},{24,25},{32,34},{40,41},{48,50},{56,57},{64,66... | collective-permute-start | bytes 2359304 | tf_op jit(solution)/shard_map/ppermute | solution.py:34
  77.7 8.3 %copy-start.12 = (bf16[4,384,256]{2,1,0:T(8,128)(2,1)S(1)}, bf16[4,384,256]{2,1,0:T(8,128)(2,1)}, u32[]{:S(2)}) copy-start(bf16[4,384,256]{2,1,0:T(8,128)(2,1)} %gate.4.refs_6_) | copy-start | bytes 2359300
  77.7 8.3 %copy-start.15 = (bf16[4,384,256]{2,1,0:T(8,128)(2,1)S(1)}, bf16[4,384,256]{2,1,0:T(8,128)(2,1)}, u32[]{:S(2)}) copy-start(bf16[4,384,256]{2,1,0:T(8,128)(2,1)} %gate.6.refs_5_) | copy-start | bytes 2359300
  77.7 8.3 %copy-start.18 = (bf16[4,384,256]{2,1,0:T(8,128)(2,1)S(1)}, bf16[4,384,256]{2,1,0:T(8,128)(2,1)}, u32[]{:S(2)}) copy-start(bf16[4,384,256]{2,1,0:T(8,128)(2,1)} %copy-done.16) | copy-start | bytes 2359300
  83.2 15.8 %collective-permute-start.14 = (bf16[4,8,96,128]{3,2,1,0:T(8,128)(2,1)S(1)}, bf16[4,8,96,128]{3,2,1,0:T(8,128)(2,1)S(1)}, u32[]{:S(2)}, u32[]{:S(2)}) collective-permute-start(bf16[4,8,96,128]{3,2,1,0:T(8,128)(2,1)S(1)} %get-tuple-element.58), channel_id=1, source_target_pairs={{0,2},{8,9},{16,18},{24,25},{32,34},{40,41},{48,50},{56,57},{64,66... | collective-permute-start | bytes 2359304 | tf_op jit(solution)/shard_map/ppermute | solution.py:34
  84.7 14.9 %collective-permute-start.16 = (bf16[4,8,96,128]{3,2,1,0:T(8,128)(2,1)S(1)}, bf16[4,8,96,128]{3,2,1,0:T(8,128)(2,1)S(1)}, u32[]{:S(2)}, u32[]{:S(2)}) collective-permute-start(bf16[4,8,96,128]{3,2,1,0:T(8,128)(2,1)S(1)} %get-tuple-element.61), channel_id=1, source_target_pairs={{0,6},{8,137},{16,22},{24,153},{32,38},{40,169},{48,54},{56,185},{... | collective-permute-start | bytes 2359304 | tf_op jit(solution)/shard_map/ppermute | solution.py:34
  90.0 11.5 %copy-start.19 = (f32[192,3072]{1,0:T(8,128)}, f32[192,3072]{1,0:T(8,128)S(1)}, u32[]{:S(2)}) copy-start(f32[192,3072]{1,0:T(8,128)S(1)} %get-tuple-element.54.refs_2_) | copy-start | bytes 7077892
  90.0 11.5 %copy-start.20 = (f32[192,3072]{1,0:T(8,128)}, f32[192,3072]{1,0:T(8,128)S(1)}, u32[]{:S(2)}) copy-start(f32[192,3072]{1,0:T(8,128)S(1)} %get-tuple-element.55.refs_0_) | copy-start | bytes 7077892
  102.1 5.7 %collective-permute-start.17 = (f32[192,3072]{1,0:T(8,128)}, f32[192,3072]{1,0:T(8,128)S(1)}, u32[]{:S(2)}, u32[]{:S(2)}) collective-permute-start(f32[192,3072]{1,0:T(8,128)} %gate.7), channel_id=1, source_target_pairs={{0,8},{8,0},{16,24},{24,16},{32,40},{40,32},{48,56},{56,48},{64,72... | collective-permute-start | bytes 7077896 | tf_op jit(solution)/shard_map/ppermute | solution.py:34
  102.8 13.2 %collective-permute-start.18 = (bf16[8,2,96,128]{3,2,1,0:T(8,128)(2,1)}, bf16[8,2,96,128]{3,2,1,0:T(8,128)(2,1)S(1)}, u32[]{:S(2)}, u32[]{:S(2)}) collective-permute-start(bf16[8,2,96,128]{3,2,1,0:T(8,128)(2,1)} %get-tuple-element.66), channel_id=1, source_target_pairs={{0,1},{8,10},{16,17},{24,26},{32,33},{40,42},{48,49},{56,58},{64,6... | collective-permute-start | bytes 1179656 | tf_op jit(solution)/shard_map/ppermute | solution.py:34
  103.8 12.7 %collective-permute-start.19 = (bf16[8,2,96,128]{3,2,1,0:T(8,128)(2,1)S(1)}, bf16[8,2,96,128]{3,2,1,0:T(8,128)(2,1)S(1)}, u32[]{:S(2)}, u32[]{:S(2)}) collective-permute-start(bf16[8,2,96,128]{3,2,1,0:T(8,128)(2,1)S(1)} %get-tuple-element.67), channel_id=1, source_target_pairs={{0,128},{8,12},{16,144},{24,28},{32,160},{40,44},{48,176},{56,60},... | collective-permute-start | bytes 1179656 | tf_op jit(solution)/shard_map/ppermute | solution.py:34
  106.6 9.9 %collective-permute-start.20 = (bf16[8,2,96,128]{3,2,1,0:T(8,128)(2,1)S(1)}, bf16[8,2,96,128]{3,2,1,0:T(8,128)(2,1)S(1)}, u32[]{:S(2)}, u32[]{:S(2)}) collective-permute-start(bf16[8,2,96,128]{3,2,1,0:T(8,128)(2,1)S(1)} %get-tuple-element.68), channel_id=1, source_target_pairs={{0,129},{8,14},{16,145},{24,30},{32,161},{40,46},{48,177},{56,62},... | collective-permute-start | bytes 1179656 | tf_op jit(solution)/shard_map/ppermute | solution.py:34
  164.8 5.1 %collective-permute-start.21 = (bf16[2,8,2,96,128]{4,3,2,1,0:T(8,128)(2,1)S(1)}, bf16[2,8,2,96,128]{4,3,2,1,0:T(8,128)(2,1)S(1)}, u32[]{:S(2)}, u32[]{:S(2)}) collective-permute-start(bf16[2,8,2,96,128]{4,3,2,1,0:T(8,128)(2,1)S(1)} %bitcast.29), channel_id=1, source_target_pairs={{0,8},{8,0},{16,24},{24,16},{32,40},{40,32},{48,56},{56,48},{64,72... | collective-permute-start | bytes 2359304 | tf_op jit(solution)/shard_map/ppermute | solution.py:34
  (22 other events, 56.4 us)

commit v4 on v1

--- a/solution.py
+++ b/solution.py
@@ -3,6 +3,7 @@
 
 import jax
 import jax.numpy as jnp
+import numpy as np
 from jax import lax
 from jax.experimental import pallas as pl
 from jax.experimental.pallas import tpu as pltpu
@@ -172,16 +173,17 @@
     return lax.dot_general(a, b, ((dims[0], dims[1]), ((), ())), preferred_element_type=F32)
 
 
-def attend_kernel(ends, mine, theirs, cos_t, sin_t, out):
+def attend_kernel(lengths, mine, theirs, cos_t, sin_t, out):
     rows = mine.shape[0]
     cols = HEADS * HD
     row_id = lax.broadcasted_iota(jnp.int32, (rows, 1), 0)
     col_id = lax.broadcasted_iota(jnp.int32, (1, rows), 1)
 
     def slot(ids):
-        count = jnp.zeros(ids.shape, jnp.int32)
+        count, end = jnp.zeros(ids.shape, jnp.int32), 0
         for k in range(3):
-            count = count + (ids >= ends[k]).astype(jnp.int32)
+            end = end + lengths[0, k]
+            count = count + (ids >= end).astype(jnp.int32)
         return count
 
     row_slot, col_slot = slot(row_id), slot(col_id)
@@ -300,7 +302,8 @@
         g_send[:, at] = total[rows:]
 
 
-def token_grad_kernel(width, info, tokens, g_own, g_peer, out, g):
+def token_grad_kernel(width, info, tokens, g_own, g_peer, out, mark, g):
+    mark[...] = jnp.zeros_like(mark)
     rows, model = tokens.shape
     for first, ref in ((0, g_own), (8, g_peer)):
         for j in range(8):
@@ -319,15 +322,31 @@
         out[at, :] = (scale * (grad - mean_g - hat * mean_gh)).astype(BF16)
 
 
-def place_kernel(info, own, other, out):
-    rows = own.shape[3]
-    for k, ref in enumerate((own, other)):
-        c = info[CORE] if k == 0 else 1 - info[CORE]
-        for h in range(2):
-            for n in range(2):
-                for side in range(2):
-                    to = pl.ds(pl.multiple_of(c * 4 * rows + (2 * h + side) * rows, rows), rows)
-                    out[0, to, n * 128 : (n + 1) * 128] = ref[h, n, side].astype(F32)
+def place_kernel(at, blocks, *refs):
+    out, rows = refs[-1], blocks.shape[3]
+    for h in range(2):
+        for n in range(2):
+            for side in range(2):
+                to = slice((2 * h + side) * rows, (2 * h + side + 1) * rows)
+                out[0, to, n * 128 : (n + 1) * 128] = blocks[h, n, side].astype(F32)
+
+
+def place(at, blocks, dims, before=()):
+    return pl.pallas_call(
+        place_kernel,
+        grid_spec=pltpu.PrefetchScalarGridSpec(
+            num_scalar_prefetch=1,
+            grid=(4,),
+            in_specs=[pl.BlockSpec((2, 2) + blocks.shape[2:], lambda m, at: (0, m, 0, 0, 0))]
+            + [pl.BlockSpec(memory_space=pl.ANY) for _ in before],
+            out_specs=pl.BlockSpec((1, dims[1] // 2, dims[2]), lambda m, at: (m, at[0], 0)),
+        ),
+        out_shape=shape(dims, F32),
+        input_output_aliases={2: 0} if before else {},
+        compiler_params=pltpu.CompilerParams(vmem_limit_bytes=12 * 1024 * 1024),
+        cost_estimate=pl.CostEstimate(flops=1, bytes_accessed=8 * math.prod(dims), transcendentals=0),
+        name="place",
+    )(at, blocks, *before)
 
 
 def swap_groups(with_x):
@@ -355,8 +374,6 @@
         for k, dx in ORDER:
             shard = ((y_at - s * k + 4) % NY) * 2 + (x_lo + dx) % 2
             offs.append(shard * shard_rows + c * width)
-    l0, l1, l2 = lengths[0, 0], lengths[0, 1], lengths[0, 2]
-    ends = jnp.stack([l0, l0 + l1, l0 + l1 + l2]).astype(jnp.int32)
     info = jnp.stack(offs + [x_hi * 2 + x_lo, x_lo, core, sign]).astype(jnp.int32)
     half = width // 2
 
@@ -377,14 +394,14 @@
     w = {(0, 0): lax.dynamic_slice(weights, (0, core * width, 0), (4, width, cols))}
     w[0, 1] = shift(w[0, 0], dx=1)
     w[3, 0] = shift(w[0, 0], dy=-1)
-    w[1, 0] = gate(shift(w[0, 0], dy=1), [own, w[0, 1]])
+    w[1, 0] = shift(w[0, 0], dy=1)
     w[2, 0] = shift(w[1, 0], dy=1)
     w[1, 1] = shift(w[1, 0], dx=1)
     w[3, 1] = shift(w[3, 0], dx=1)
     w[2, 1] = shift(w[1, 1], dy=1)
     shards = [w[place] for place in ORDER]
 
-    peer = shift(gate(send, [w[1, 0]]), dc=1)
+    peer = shift(gate(send, [w[1, 0], w[0, 1]]), dc=1)
     one = (1, rows, model // 2)
     (turned,) = call(
         functools.partial(flip_kernel, width),
@@ -397,7 +414,7 @@
     )
 
     quarter = HD // 4
-    frequency = ROPE_BASE ** (-jnp.arange(quarter, dtype=F32) / quarter)
+    frequency = (ROPE_BASE ** (-np.arange(quarter, dtype=np.float64) / quarter)).astype(np.float32)
     angle_r = positions[0].astype(F32)[:, None] * frequency[None, :]
     angle_c = positions[1].astype(F32)[:, None] * frequency[None, :]
     cos_r, sin_r, cos_c, sin_c = jnp.cos(angle_r), jnp.sin(angle_r), jnp.cos(angle_c), jnp.sin(angle_c)
@@ -420,14 +437,14 @@
             flops=2 * 2 * rows * 2 * pairs * width * 4 * cols,
             nbytes=2 * pairs * width * 8 * cols + 8 * rows * 2 * pairs * width,
             name="linear",
-            after=[] if first else [turned, cos_t, sin_t, ends],
+            after=[] if first else [turned, cos_t, sin_t],
         )
     lin_own, lin_send = lin
     lin_peer = shift(lin_send, dc=1)
     (y_own,) = call(
         attend_kernel,
         [shape((rows, 4 * cols))],
-        [ends, lin_own, lin_peer, cos_t, sin_t],
+        [lengths, lin_own, lin_peer, cos_t, sin_t],
         scalars=1,
         flops=HEADS * 10 * rows * rows * HD * 2,
         nbytes=10 * rows * 4 * cols,
@@ -490,9 +507,9 @@
     )
     g_peer = shift(gate(g_send, [halfway[0]]), dc=1)
     g_rows = ((some, model // 2), lambda i: (i, 0))
-    (grad_tokens,) = call(
+    grad_tokens, mark = call(
         functools.partial(token_grad_kernel, width),
-        [(shape((rows, model)), (some, model), lambda i: (i, 0))],
+        [(shape((rows, model)), (some, model), lambda i: (i, 0)), (shape((8, 128), F32), (8, 128), lambda i: (0, 0))],
         [info, (tokens, (some, model), lambda i: (i, 0)), (g_own, *g_rows), (g_peer, *g_rows)],
         grid=(4,),
         scalars=1,
@@ -509,21 +526,13 @@
         [(mixed, *out_n)],
         [(value, *out_n) for value in [halfway[0]] + rest],
         grid=(4,),
-        after=[grad_tokens],
+        after=[mark],
     )
     (spread,) = sum_call(last_kernel, "last", [shape((2 * NZ, 2, quarter, 128))], [exchange(by_z, False)])
     done = exchange(spread, True).reshape(2, NZ, 2, quarter, 128)
-    per_m = ((2, 2, 2, quarter, 128), lambda m: (0, m, 0, 0, 0))
-    (weight_grads,) = call(
-        place_kernel,
-        [(shape((4, shard_rows, cols), F32), (1, shard_rows, cols), lambda m: (m, 0, 0))],
-        [info, (done, *per_m), (shift(done, dc=1), *per_m)],
-        grid=(4,),
-        scalars=1,
-        flops=4 * shard_rows * cols,
-        nbytes=24 * shard_rows * cols,
-        name="place",
-    )
+    dims = (4, shard_rows, cols)
+    weight_grads = place(jnp.stack([core]).astype(jnp.int32), done, dims)
+    weight_grads = place(jnp.stack([1 - core]).astype(jnp.int32), shift(done, dc=1), dims, [weight_grads])
     return (grad_tokens, weight_grads)
 
 

time: 165 us -> 166 us (level)
  waiting for transfers between devices: 31.4 us -> 33.7 us
  local copies, waits for them, and re-layouts: 17.8 us -> 15.5 us
  between operations: 2.87 us -> 0.92 us
    pallas_call x0 -> x2, Pallas kernels: none -> 3.47 us  [place(): pl.pallas_call(place_kernel, grid_spec=pltpu.PrefetchScalarGridSpec(num_s...]
    ppermute x21, waiting for transfers between devices: 31.4 us -> 33.7 us  [permute(): return lax.ppermute(values, ('dp', 'fsdp'), pairs)]
    pallas_call x15 -> x14, Pallas kernels: 31.7 us -> 29.8 us  [call(): pl.pallas_call(kernel, grid=grid or (1,), out_shape=out_shapes, in_specs=...]
  transfers between devices with their start and end apart: 21 -> 21, of which waited for: 11 -> 12; matrix products, arithmetic and copies ran while one was open for 1% -> 1% of each run, Pallas kernels for 13% -> 14%
where the time goes in v4:
time: 166 us; the launch traced here: 165 us
  blocking collectives  45.8 us (28%)
  starting transfers between devices  34.6 us (21%)
  waiting for transfers between devices  33.7 us (20%)
  Pallas kernels  33.3 us (20%)
  local copies, waits for them, and re-layouts  15.5 us (9%)
    all_to_all x2, blocking collectives, exchange(): lax.all_to_all(values, 'dp', split_axis=0, concat_axis=0, axis_index_grou...  45.8 us
    ppermute x21, starting transfers between devices, permute(): return lax.ppermute(values, ('dp', 'fsdp'), pairs)  34.6 us
    ppermute x21, waiting for transfers between devices, permute(): return lax.ppermute(values, ('dp', 'fsdp'), pairs)  33.7 us
    pallas_call x14, Pallas kernels, call(): pl.pallas_call(kernel, grid=grid or (1,), out_shape=out_shapes, in_specs=...  29.8 us
    unnamed x40, local copies, waits for them, and re-layouts  14.4 us
    pallas_call x2, Pallas kernels, place(): pl.pallas_call(place_kernel, grid_spec=pltpu.PrefetchScalarGridSpec(num_s...  3.47 us
  transfers between devices with their start and end apart: 21, of which 12 were waited for; matrix products, arithmetic and copies ran while one was open for 1% of the time, Pallas kernels for 14%

profile of v4, /device:TPU:1, one launch (start us, length us, event | category | flops | bytes accessed | tf_op | source)
XLA Modules:
  0.0 164.8 jit_solution(2135031036258957900)
XLA Ops:
  3.0 3.3 %collective-permute-start.1 = (bf16[4,384,256]{2,1,0:T(8,128)(2,1)}, bf16[4,384,256]{2,1,0:T(8,128)(2,1)S(1)}, u32[]{:S(2)}, u32[]{:S(2)}) collective-permute-start(bf16[4,384,256]{2,1,0:T(8,128)(2,1)} %constant_dynamic-slice_fusion.refs_2_), channel_id=1, source_target_pairs={{0,1},{8,137},{16,17},{24,153},{32,33},{40,169},{48,49},{56,185},{... | collective-permute-start | bytes 2359304 | tf_op jit(solution)/shard_map/ppermute | solution.py:34
  6.3 2.7 %collective-permute-start = (bf16[4,384,256]{2,1,0:T(8,128)(2,1)}, bf16[4,384,256]{2,1,0:T(8,128)(2,1)S(1)}, u32[]{:S(2)}, u32[]{:S(2)}) collective-permute-start(bf16[4,384,256]{2,1,0:T(8,128)(2,1)} %constant_dynamic-slice_fusion.refs_2_), channel_id=1, source_target_pairs={{0,2},{8,14},{16,18},{24,30},{32,34},{40,46},{48,50},{56,62},{64,6... | collective-permute-start | bytes 2359304 | tf_op jit(solution)/shard_map/ppermute | solution.py:34
  9.1 1.7 %copy-done.4 = bf16[192,6144]{1,0:T(8,128)(2,1)S(1)} copy-done((bf16[192,6144]{1,0:T(8,128)(2,1)S(1)}, bf16[192,6144]{1,0:T(8,128)(2,1)}, u32[]{:S(2)}) %copy-start.4) | copy-done | bytes 2359320
  10.8 1.7 %copy-done.14 = bf16[192,6144]{1,0:T(8,128)(2,1)S(1)} copy-done((bf16[192,6144]{1,0:T(8,128)(2,1)S(1)}, bf16[192,6144]{1,0:T(8,128)(2,1)}, u32[]{:S(2)}) %copy-start.14) | copy-done | bytes 2359320
  12.5 3.0 %prep.1 = (bf16[2,192,3072]{2,1,0:T(8,128)(2,1)S(1)}, bf16[2,192,3072]{2,1,0:T(8,128)(2,1)S(1)}) custom-call(s32[20]{0:T(128)S(1)} %stack.87.info, bf16[192,6144]{1,0:T(8,128)(2,1)S(1)} %copy-done.4, bf16[192,6144]{1,0:T(8,128)(2,1)S(1)} %copy-done.14), custom_call_target="tpu_custom_call" | custom-call | flops 9437184 | bytes 9437184 | tf_op jit(solution)/shard_map/prep/pallas_call | solution.py:72
  20.8 2.7 %collective-permute-start.5 = (bf16[4,384,256]{2,1,0:T(8,128)(2,1)}, bf16[4,384,256]{2,1,0:T(8,128)(2,1)S(1)}, u32[]{:S(2)}, u32[]{:S(2)}) collective-permute-start(bf16[4,384,256]{2,1,0:T(8,128)(2,1)} %copy-done.9), channel_id=1, source_target_pairs={{0,1},{8,137},{16,17},{24,153},{32,33},{40,169},{48,49},{56,185},{... | collective-permute-start | bytes 2359304 | tf_op jit(solution)/shard_map/ppermute | solution.py:34
  23.5 2.7 %collective-permute-start.7 = (bf16[4,384,256]{2,1,0:T(8,128)(2,1)}, bf16[4,384,256]{2,1,0:T(8,128)(2,1)S(1)}, u32[]{:S(2)}, u32[]{:S(2)}) collective-permute-start(bf16[4,384,256]{2,1,0:T(8,128)(2,1)} %copy-done.9), channel_id=1, source_target_pairs={{0,2},{8,14},{16,18},{24,30},{32,34},{40,46},{48,50},{56,62},{64,6... | collective-permute-start | bytes 2359304 | tf_op jit(solution)/shard_map/ppermute | solution.py:34
  26.2 12.2 %collective-permute-done.3.refs_6_ = bf16[4,384,256]{2,1,0:T(8,128)(2,1)S(1)} collective-permute-done((bf16[4,384,256]{2,1,0:T(8,128)(2,1)}, bf16[4,384,256]{2,1,0:T(8,128)(2,1)S(1)}, u32[]{:S(2)}, u32[]{:S(2)}) %collective-permute-start.3) | collective-permute-done | bytes 786464 | tf_op jit(solution)/shard_map/ppermute | solution.py:34
  38.4 3.1 %collective-permute-start.4 = (bf16[4,384,256]{2,1,0:T(8,128)(2,1)S(1)}, bf16[4,384,256]{2,1,0:T(8,128)(2,1)S(1)}, u32[]{:S(2)}, u32[]{:S(2)}) collective-permute-start(bf16[4,384,256]{2,1,0:T(8,128)(2,1)S(1)} %collective-permute-done.3.refs_6_), channel_id=1, source_target_pairs={{0,1},{8,137},{16,17},{24,153},{32,33},{40,169},{48,49},{56,185},{... | collective-permute-start | bytes 2359304 | tf_op jit(solution)/shard_map/ppermute | solution.py:34
  42.6 1.7 %copy-done.2 = bf16[2,192,3072]{2,1,0:T(8,128)(2,1)S(1)} copy-done((bf16[2,192,3072]{2,1,0:T(8,128)(2,1)S(1)}, bf16[2,192,3072]{2,1,0:T(8,128)(2,1)}, u32[]{:S(2)}) %copy-start.2) | copy-done | bytes 2359320
  44.2 2.4 %flip.1.refs_8_.refs_0_.refs_1_ = bf16[2,4,2,4,96,384]{5,4,3,2,1,0:T(8,128)(2,1)S(1)} custom-call(s32[20]{0:T(128)S(1)} %stack.87.info, bf16[2,192,3072]{2,1,0:T(8,128)(2,1)S(1)} %copy-done.2, bf16[2,192,3072]{2,1,0:T(8,128)(2,1)S(1)} %collective-permute-done.2.peer.refs_1_), custom_call_target="tpu_custom_call" | custom-call | bytes 9437184 | tf_op jit(solution)/shard_map/flip/pallas_call | solution.py:72
  46.7 4.2 %linear.2 = (f32[192,1024]{1,0:T(8,128)S(1)}, f32[192,1024]{1,0:T(8,128)S(1)}) custom-call(bf16[2,192,3072]{2,1,0:T(8,128)(2,1)S(1)} %copy-done.3, bf16[2,192,3072]{2,1,0:T(8,128)(2,1)S(1)} %collective-permute-done.2.peer.refs_1_, bf16[4,384,256]{2,1,0:T(8,128)(2,1)} %constant_dynamic-slice_fusion.refs_2_, bf16[4,384,256]{2,1,0:T(8,128)(2,1)S(1)} %copy-done.8, ...), custom_call_target="tpu_custom_call" | custom-call | flops 1811939328 | bytes 8257536 | tf_op jit(solution)/shard_map/linear/pallas_call | solution.py:72
  51.0 1.7 %collective-permute-done.6.refs_1_.refs_9_ = bf16[4,384,256]{2,1,0:T(8,128)(2,1)S(1)} collective-permute-done((bf16[4,384,256]{2,1,0:T(8,128)(2,1)S(1)}, bf16[4,384,256]{2,1,0:T(8,128)(2,1)S(1)}, u32[]{:S(2)}, u32[]{:S(2)}) %collective-permute-start.6) | collective-permute-done | bytes 786464 | tf_op jit(solution)/shard_map/ppermute | solution.py:34
  52.7 1.8 %linear.3 = (f32[192,1024]{1,0:T(8,128)S(1)}, f32[192,1024]{1,0:T(8,128)S(1)}) custom-call(bf16[2,192,3072]{2,1,0:T(8,128)(2,1)S(1)} %copy-done.3, bf16[2,192,3072]{2,1,0:T(8,128)(2,1)S(1)} %collective-permute-done.2.peer.refs_1_, bf16[4,384,256]{2,1,0:T(8,128)(2,1)S(1)} %collective-permute-done.4.refs_0_.refs_8_, ...), custom_call_target="tpu_custom_call" | custom-call | flops 603979776 | bytes 2752512 | tf_op jit(solution)/shard_map/linear/pallas_call | solution.py:72
  54.4 3.1 %collective-permute-start.8 = (f32[192,1024]{1,0:T(8,128)S(1)}, f32[192,1024]{1,0:T(8,128)S(1)}, u32[]{:S(2)}, u32[]{:S(2)}) collective-permute-start(f32[192,1024]{1,0:T(8,128)S(1)} %get-tuple-element.31), channel_id=1, source_target_pairs={{0,8},{8,0},{16,24},{24,16},{32,40},{40,32},{48,56},{56,48},{64,72... | collective-permute-start | bytes 2359304 | tf_op jit(solution)/shard_map/ppermute | solution.py:34
  57.5 1.9 %collective-permute-done.8.theirs = f32[192,1024]{1,0:T(8,128)S(1)} collective-permute-done((f32[192,1024]{1,0:T(8,128)S(1)}, f32[192,1024]{1,0:T(8,128)S(1)}, u32[]{:S(2)}, u32[]{:S(2)}) %collective-permute-start.8) | collective-permute-done | bytes 786464 | tf_op jit(solution)/shard_map/ppermute | solution.py:34
  59.4 3.2 %attend.1.refs_2_.refs_1_.refs_0_ = bf16[192,1024]{1,0:T(8,128)(2,1)S(1)} custom-call(s32[1,3]{1,0:T(1,128)S(1)} %copy-done.17, f32[192,1024]{1,0:T(8,128)S(1)} %get-tuple-element.30.mine, f32[192,1024]{1,0:T(8,128)S(1)} %collective-permute-done.8.theirs, f32[192,128]{1,0:T(8,128)S(1)} %get-tuple-element.61.refs_9_.cos_t, ...), custom_call_target="tpu_custom_call" | custom-call | flops 188743680 | bytes 1966080 | tf_op jit(solution)/shard_map/attend/pallas_call | solution.py:72
  70.7 1.8 %terms.3 = (bf16[4,8,96,128]{3,2,1,0:T(8,128)(2,1)S(1)}, bf16[4,8,96,128]{3,2,1,0:T(8,128)(2,1)S(1)}, bf16[4,8,96,128]{3,2,1,0:T(8,128)(2,1)S(1)}, bf16[4,8,96,128]{3,2,1,0:T(8,128)(2,1)S(1)}) custom-call(bf16[2,4,2,4,96,384]{5,4,3,2,1,0:T(8,128)(2,1)S(1)} %flip.1.refs_8_.refs_0_.refs_1_, bf16[2,4,2,4,96,384]{5,4,3,2,1,0:T(8,128)(2,1)S(1)} %flip.1.refs_8_.refs_0_.refs_1_, ...), custom_call_target="tpu_custom_call" | custom-call | flops 1207959552 | bytes 7864320 | tf_op jit(solution)/shard_map/terms/pallas_call | solution.py:72
  72.5 5.3 %collective-permute-done.10.far_0 = bf16[4,8,96,128]{3,2,1,0:T(8,128)(2,1)S(1)} collective-permute-done((bf16[4,8,96,128]{3,2,1,0:T(8,128)(2,1)S(1)}, bf16[4,8,96,128]{3,2,1,0:T(8,128)(2,1)S(1)}, u32[]{:S(2)}, u32[]{:S(2)}) %collective-permute-start.10) | collective-permute-done | bytes 786464 | tf_op jit(solution)/shard_map/ppermute | solution.py:34
  78.2 2.8 %collective-permute-start.15 = (bf16[4,8,96,128]{3,2,1,0:T(8,128)(2,1)S(1)}, bf16[4,8,96,128]{3,2,1,0:T(8,128)(2,1)S(1)}, u32[]{:S(2)}, u32[]{:S(2)}) collective-permute-start(bf16[4,8,96,128]{3,2,1,0:T(8,128)(2,1)S(1)} %get-tuple-element.43), channel_id=1, source_target_pairs={{0,6},{8,137},{16,22},{24,153},{32,38},{40,169},{48,54},{56,185},{... | collective-permute-start | bytes 2359304 | tf_op jit(solution)/shard_map/ppermute | solution.py:34
  81.0 3.7 %normed_grad.1 = (f32[192,3072]{1,0:T(8,128)S(1)}, f32[192,3072]{1,0:T(8,128)S(1)}) custom-call(bf16[192,1024]{1,0:T(8,128)(2,1)S(1)} %attend.1.refs_2_.refs_1_.refs_0_, bf16[192,1024]{1,0:T(8,128)(2,1)S(1)} %collective-permute-done.9.refs_3_.refs_2_.refs_1_, bf16[4,384,256]{2,1,0:T(8,128)(2,1)} %constant_dynamic-slice_fusion.refs_2_, ...), custom_call_target="tpu_custom_call" | custom-call | flops 1811939328 | bytes 11010048 | tf_op jit(solution)/shard_map/normed_grad/pallas_call | solution.py:72
  86.2 8.3 %collective-permute-done.15.refs_5_ = bf16[4,8,96,128]{3,2,1,0:T(8,128)(2,1)S(1)} collective-permute-done((bf16[4,8,96,128]{3,2,1,0:T(8,128)(2,1)S(1)}, bf16[4,8,96,128]{3,2,1,0:T(8,128)(2,1)S(1)}, u32[]{:S(2)}, u32[]{:S(2)}) %collective-permute-start.15) | collective-permute-done | bytes 786464 | tf_op jit(solution)/shard_map/ppermute | solution.py:34
  94.7 1.9 %sides.1 = (bf16[8,2,96,128]{3,2,1,0:T(8,128)(2,1)S(1)}, bf16[8,2,96,128]{3,2,1,0:T(8,128)(2,1)}, bf16[8,2,96,128]{3,2,1,0:T(8,128)(2,1)S(1)}, bf16[8,2,96,128]{3,2,1,0:T(8,128)(2,1)S(1)}) custom-call(bf16[4,8,96,128]{3,2,1,0:T(8,128)(2,1)S(1)} %get-tuple-element.39.refs_0_, bf16[4,8,96,128]{3,2,1,0:T(8,128)(2,1)S(1)} %collective-permute-done.12.refs_1_, ...), custom_call_target="tpu_custom_call" | custom-call | flops 2359296 | bytes 6291456 | tf_op jit(solution)/shard_map/sides/pallas_call | solution.py:72
  98.6 4.1 %collective-permute-start.18 = (bf16[8,2,96,128]{3,2,1,0:T(8,128)(2,1)S(1)}, bf16[8,2,96,128]{3,2,1,0:T(8,128)(2,1)S(1)}, u32[]{:S(2)}, u32[]{:S(2)}) collective-permute-start(bf16[8,2,96,128]{3,2,1,0:T(8,128)(2,1)S(1)} %get-tuple-element.47), channel_id=1, source_target_pairs={{0,128},{8,12},{16,144},{24,28},{32,160},{40,44},{48,176},{56,60},... | collective-permute-start | bytes 1179656 | tf_op jit(solution)/shard_map/ppermute | solution.py:34
  103.0 1.7 %copy-done.5 = bf16[192,6144]{1,0:T(8,128)(2,1)S(1)} copy-done((bf16[192,6144]{1,0:T(8,128)(2,1)S(1)}, bf16[192,6144]{1,0:T(8,128)(2,1)}, u32[]{:S(2)}) %copy-start.5) | copy-done | bytes 2359320
  104.7 1.7 %copy-done.12 = f32[192,3072]{1,0:T(8,128)S(1)} copy-done((f32[192,3072]{1,0:T(8,128)S(1)}, f32[192,3072]{1,0:T(8,128)}, u32[]{:S(2)}) %copy-start.12) | copy-done | bytes 2359320
  106.3 5.2 %token_grad.1 = (bf16[192,6144]{1,0:T(8,128)(2,1)}, f32[8,128]{1,0:T(8,128)S(1)}) custom-call(s32[20]{0:T(128)S(1)} %stack.87.info, bf16[192,6144]{1,0:T(8,128)(2,1)S(1)} %copy-done.5, f32[192,3072]{1,0:T(8,128)S(1)} %copy-done.12, f32[192,3072]{1,0:T(8,128)S(1)} %collective-permute-done.16.g_peer), custom_call_target="tpu_custom_call" | custom-call | flops 18874368 | bytes 9437184 | tf_op jit(solution)/shard_map/token_grad/pallas_call | solution.py:72
  112.5 21.6 %all_to_all.10.got = bf16[8,2,96,128]{3,2,1,0:T(8,128)(2,1)S(1)} all-to-all(bf16[8,2,96,128]{3,2,1,0:T(8,128)(2,1)S(1)} %seconds.1), channel_id=1, replica_groups={{0,16,32,48,64,80,96,112},{8,24,40,56,72,88,104,120},{128,144,160,176,1..., dimensions={0} | all-to-all | bytes 786432 | tf_op jit(solution)/shard_map/all_to_all | solution.py:359
  134.2 24.3 %all_to_all.11 = bf16[16,2,96,128]{3,2,1,0:T(8,128)(2,1)S(1)} all-to-all(bf16[16,2,96,128]{3,2,1,0:T(8,128)(2,1)S(1)} %last.1), channel_id=1, replica_groups={{0,16,32,48,64,80,96,112,128,144,160,176,192,208,224,240},{8,24,40,56,7..., dimensions={0} | all-to-all | bytes 1572864 | tf_op jit(solution)/shard_map/all_to_all | solution.py:359
  158.4 2.8 %collective-permute-start.20 = (bf16[2,8,2,96,128]{4,3,2,1,0:T(8,128)(2,1)S(1)}, bf16[2,8,2,96,128]{4,3,2,1,0:T(8,128)(2,1)S(1)}, u32[]{:S(2)}, u32[]{:S(2)}) collective-permute-start(bf16[2,8,2,96,128]{4,3,2,1,0:T(8,128)(2,1)S(1)} %bitcast.24), channel_id=1, source_target_pairs={{0,8},{8,0},{16,24},{24,16},{32,40},{40,32},{48,56},{56,48},{64,72... | collective-permute-start | bytes 2359304 | tf_op jit(solution)/shard_map/ppermute | solution.py:34
  161.2 1.7 %place.2.refs_0_ = f32[4,768,256]{2,1,0:T(8,128)} custom-call(s32[1]{0:T(128)} %bitcast.18.at, bf16[2,8,2,96,128]{4,3,2,1,0:T(8,128)(2,1)S(1)} %bitcast.25), custom_call_target="tpu_custom_call" | custom-call | flops 1 | bytes 6291456 | tf_op jit(solution)/shard_map/place/pallas_call | solution.py:335
  163.1 1.7 %place.3 = f32[4,768,256]{2,1,0:T(8,128)} custom-call(s32[1]{0:T(128)} %bitcast.22.at, bf16[2,8,2,96,128]{4,3,2,1,0:T(8,128)(2,1)S(1)} %collective-permute-done.20.blocks, f32[4,768,256]{2,1,0:T(8,128)} %place.2.refs_0_), custom_call_target="tpu_custom_call", output_to_operand_aliasing={{}: (2, {})} | custom-call | flops 1 | bytes 6291456 | tf_op jit(solution)/shard_map/place/pallas_call | solution.py:335
  (75 shorter events, 22.6 us)
Async XLA Ops:
  3.0 15.3 %collective-permute-start.1 = (bf16[4,384,256]{2,1,0:T(8,128)(2,1)}, bf16[4,384,256]{2,1,0:T(8,128)(2,1)S(1)}, u32[]{:S(2)}, u32[]{:S(2)}) collective-permute-start(bf16[4,384,256]{2,1,0:T(8,128)(2,1)} %constant_dynamic-slice_fusion.refs_2_), channel_id=1, source_target_pairs={{0,1},{8,137},{16,17},{24,153},{32,33},{40,169},{48,49},{56,185},{... | collective-permute-start | bytes 2359304 | tf_op jit(solution)/shard_map/ppermute | solution.py:34
  6.3 12.0 %collective-permute-start = (bf16[4,384,256]{2,1,0:T(8,128)(2,1)}, bf16[4,384,256]{2,1,0:T(8,128)(2,1)S(1)}, u32[]{:S(2)}, u32[]{:S(2)}) collective-permute-start(bf16[4,384,256]{2,1,0:T(8,128)(2,1)} %constant_dynamic-slice_fusion.refs_2_), channel_id=1, source_target_pairs={{0,2},{8,14},{16,18},{24,30},{32,34},{40,46},{48,50},{56,62},{64,6... | collective-permute-start | bytes 2359304 | tf_op jit(solution)/shard_map/ppermute | solution.py:34
  9.1 1.7 %copy-start.4 = (bf16[192,6144]{1,0:T(8,128)(2,1)S(1)}, bf16[192,6144]{1,0:T(8,128)(2,1)}, u32[]{:S(2)}) copy-start(bf16[192,6144]{1,0:T(8,128)(2,1)} %tokens.3) | copy-start | bytes 7077892
  19.5 22.0 %copy-start.18 = (s32[2,192]{1,0:T(2,128)S(1)}, s32[2,192]{1,0:T(2,128)}, u32[]{:S(2)}) copy-start(s32[2,192]{1,0:T(2,128)} %param.10) | copy-start | bytes 4612
  19.5 22.0 %copy-start.19 = (f32[32]{0:T(128)S(1)}, f32[32]{0:T(128)}, u32[]{:S(2)}) copy-start(f32[32]{0:T(128)} %constant.149) | copy-start | bytes 388
  19.5 23.0 %collective-permute-start.2 = (bf16[2,192,3072]{2,1,0:T(8,128)(2,1)}, bf16[2,192,3072]{2,1,0:T(8,128)(2,1)S(1)}, u32[]{:S(2)}, u32[]{:S(2)}) collective-permute-start(bf16[2,192,3072]{2,1,0:T(8,128)(2,1)} %gate.2), channel_id=1, source_target_pairs={{0,8},{8,0},{16,24},{24,16},{32,40},{40,32},{48,56},{56,48},{64,72... | collective-permute-start | bytes 7077896 | tf_op jit(solution)/shard_map/ppermute | solution.py:34
  20.8 17.6 %collective-permute-start.3 = (bf16[4,384,256]{2,1,0:T(8,128)(2,1)}, bf16[4,384,256]{2,1,0:T(8,128)(2,1)S(1)}, u32[]{:S(2)}, u32[]{:S(2)}) collective-permute-start(bf16[4,384,256]{2,1,0:T(8,128)(2,1)} %constant_dynamic-slice_fusion.refs_2_), channel_id=1, source_target_pairs={{0,6},{8,10},{16,22},{24,26},{32,38},{40,42},{48,54},{56,58},{64,7... | collective-permute-start | bytes 2359304 | tf_op jit(solution)/shard_map/ppermute | solution.py:34
  20.8 20.7 %collective-permute-start.5 = (bf16[4,384,256]{2,1,0:T(8,128)(2,1)}, bf16[4,384,256]{2,1,0:T(8,128)(2,1)S(1)}, u32[]{:S(2)}, u32[]{:S(2)}) collective-permute-start(bf16[4,384,256]{2,1,0:T(8,128)(2,1)} %copy-done.9), channel_id=1, source_target_pairs={{0,1},{8,137},{16,17},{24,153},{32,33},{40,169},{48,49},{56,185},{... | collective-permute-start | bytes 2359304 | tf_op jit(solution)/shard_map/ppermute | solution.py:34
  23.5 23.2 %collective-permute-start.7 = (bf16[4,384,256]{2,1,0:T(8,128)(2,1)}, bf16[4,384,256]{2,1,0:T(8,128)(2,1)S(1)}, u32[]{:S(2)}, u32[]{:S(2)}) collective-permute-start(bf16[4,384,256]{2,1,0:T(8,128)(2,1)} %copy-done.9), channel_id=1, source_target_pairs={{0,2},{8,14},{16,18},{24,30},{32,34},{40,46},{48,50},{56,62},{64,6... | collective-permute-start | bytes 2359304 | tf_op jit(solution)/shard_map/ppermute | solution.py:34
  38.4 12.6 %collective-permute-start.4 = (bf16[4,384,256]{2,1,0:T(8,128)(2,1)S(1)}, bf16[4,384,256]{2,1,0:T(8,128)(2,1)S(1)}, u32[]{:S(2)}, u32[]{:S(2)}) collective-permute-start(bf16[4,384,256]{2,1,0:T(8,128)(2,1)S(1)} %collective-permute-done.3.refs_6_), channel_id=1, source_target_pairs={{0,1},{8,137},{16,17},{24,153},{32,33},{40,169},{48,49},{56,185},{... | collective-permute-start | bytes 2359304 | tf_op jit(solution)/shard_map/ppermute | solution.py:34
  41.5 11.1 %collective-permute-start.6 = (bf16[4,384,256]{2,1,0:T(8,128)(2,1)S(1)}, bf16[4,384,256]{2,1,0:T(8,128)(2,1)S(1)}, u32[]{:S(2)}, u32[]{:S(2)}) collective-permute-start(bf16[4,384,256]{2,1,0:T(8,128)(2,1)S(1)} %collective-permute-done.5.refs_5_), channel_id=1, source_target_pairs={{0,2},{8,14},{16,18},{24,30},{32,34},{40,46},{48,50},{56,62},{64,6... | collective-permute-start | bytes 2359304 | tf_op jit(solution)/shard_map/ppermute | solution.py:34
  42.6 1.7 %copy-start.2 = (bf16[2,192,3072]{2,1,0:T(8,128)(2,1)S(1)}, bf16[2,192,3072]{2,1,0:T(8,128)(2,1)}, u32[]{:S(2)}) copy-start(bf16[2,192,3072]{2,1,0:T(8,128)(2,1)} %copy-done.1) | copy-start | bytes 7077892
  44.2 2.5 %copy-start.3 = (bf16[2,192,3072]{2,1,0:T(8,128)(2,1)S(1)}, bf16[2,192,3072]{2,1,0:T(8,128)(2,1)}, u32[]{:S(2)}) copy-start(bf16[2,192,3072]{2,1,0:T(8,128)(2,1)} %copy-done.1) | copy-start | bytes 7077892
  44.2 2.5 %copy-start.8 = (bf16[4,384,256]{2,1,0:T(8,128)(2,1)S(1)}, bf16[4,384,256]{2,1,0:T(8,128)(2,1)}, u32[]{:S(2)}) copy-start(bf16[4,384,256]{2,1,0:T(8,128)(2,1)} %copy-done.7) | copy-start | bytes 2359300
  44.2 2.5 %copy-start.10 = (bf16[4,384,256]{2,1,0:T(8,128)(2,1)S(1)}, bf16[4,384,256]{2,1,0:T(8,128)(2,1)}, u32[]{:S(2)}) copy-start(bf16[4,384,256]{2,1,0:T(8,128)(2,1)} %copy-done.9) | copy-start | bytes 2359300
  52.7 6.8 %copy-start.17 = (s32[1,3]{1,0:T(1,128)S(1)}, s32[1,3]{1,0:T(1,128)}, u32[]{:S(2)}) copy-start(s32[1,3]{1,0:T(1,128)} %lengths.1) | copy-start | bytes 40
  54.4 5.0 %collective-permute-start.8 = (f32[192,1024]{1,0:T(8,128)S(1)}, f32[192,1024]{1,0:T(8,128)S(1)}, u32[]{:S(2)}, u32[]{:S(2)}) collective-permute-start(f32[192,1024]{1,0:T(8,128)S(1)} %get-tuple-element.31), channel_id=1, source_target_pairs={{0,8},{8,0},{16,24},{24,16},{32,40},{40,32},{48,56},{56,48},{64,72... | collective-permute-start | bytes 2359304 | tf_op jit(solution)/shard_map/ppermute | solution.py:34
  62.6 1.8 %collective-permute-start.9 = (bf16[192,1024]{1,0:T(8,128)(2,1)S(1)}, bf16[192,1024]{1,0:T(8,128)(2,1)S(1)}, u32[]{:S(2)}, u32[]{:S(2)}) collective-permute-start(bf16[192,1024]{1,0:T(8,128)(2,1)S(1)} %attend.1.refs_2_.refs_1_.refs_0_), channel_id=1, source_target_pairs={{0,8},{8,0},{16,24},{24,16},{32,40},{40,32},{48,56},{56,48},{64,72... | collective-permute-start | bytes 1179656 | tf_op jit(solution)/shard_map/ppermute | solution.py:34
  65.4 12.4 %collective-permute-start.10 = (bf16[4,8,96,128]{3,2,1,0:T(8,128)(2,1)S(1)}, bf16[4,8,96,128]{3,2,1,0:T(8,128)(2,1)S(1)}, u32[]{:S(2)}, u32[]{:S(2)}) collective-permute-start(bf16[4,8,96,128]{3,2,1,0:T(8,128)(2,1)S(1)} %get-tuple-element.33), channel_id=1, source_target_pairs={{0,2},{8,9},{16,18},{24,25},{32,34},{40,41},{48,50},{56,57},{64,66... | collective-permute-start | bytes 2359304 | tf_op jit(solution)/shard_map/ppermute | solution.py:34
  66.5 11.3 %collective-permute-start.11 = (bf16[4,8,96,128]{3,2,1,0:T(8,128)(2,1)S(1)}, bf16[4,8,96,128]{3,2,1,0:T(8,128)(2,1)S(1)}, u32[]{:S(2)}, u32[]{:S(2)}) collective-permute-start(bf16[4,8,96,128]{3,2,1,0:T(8,128)(2,1)S(1)} %get-tuple-element.35), channel_id=1, source_target_pairs={{0,6},{8,137},{16,22},{24,153},{32,38},{40,169},{48,54},{56,185},{... | collective-permute-start | bytes 2359304 | tf_op jit(solution)/shard_map/ppermute | solution.py:34
  69.1 17.0 %collective-permute-start.12 = (bf16[4,8,96,128]{3,2,1,0:T(8,128)(2,1)S(1)}, bf16[4,8,96,128]{3,2,1,0:T(8,128)(2,1)S(1)}, u32[]{:S(2)}, u32[]{:S(2)}) collective-permute-start(bf16[4,8,96,128]{3,2,1,0:T(8,128)(2,1)S(1)} %get-tuple-element.40), channel_id=1, source_target_pairs={{0,6},{8,137},{16,22},{24,153},{32,38},{40,169},{48,54},{56,185},{... | collective-permute-start | bytes 2359304 | tf_op jit(solution)/shard_map/ppermute | solution.py:34
  69.8 16.5 %collective-permute-start.14 = (bf16[4,8,96,128]{3,2,1,0:T(8,128)(2,1)S(1)}, bf16[4,8,96,128]{3,2,1,0:T(8,128)(2,1)S(1)}, u32[]{:S(2)}, u32[]{:S(2)}) collective-permute-start(bf16[4,8,96,128]{3,2,1,0:T(8,128)(2,1)S(1)} %get-tuple-element.42), channel_id=1, source_target_pairs={{0,2},{8,9},{16,18},{24,25},{32,34},{40,41},{48,50},{56,57},{64,66... | collective-permute-start | bytes 2359304 | tf_op jit(solution)/shard_map/ppermute | solution.py:34
  78.2 16.3 %collective-permute-start.15 = (bf16[4,8,96,128]{3,2,1,0:T(8,128)(2,1)S(1)}, bf16[4,8,96,128]{3,2,1,0:T(8,128)(2,1)S(1)}, u32[]{:S(2)}, u32[]{:S(2)}) collective-permute-start(bf16[4,8,96,128]{3,2,1,0:T(8,128)(2,1)S(1)} %get-tuple-element.43), channel_id=1, source_target_pairs={{0,6},{8,137},{16,22},{24,153},{32,38},{40,169},{48,54},{56,185},{... | collective-permute-start | bytes 2359304 | tf_op jit(solution)/shard_map/ppermute | solution.py:34
  81.0 13.7 %collective-permute-start.13 = (bf16[4,8,96,128]{3,2,1,0:T(8,128)(2,1)S(1)}, bf16[4,8,96,128]{3,2,1,0:T(8,128)(2,1)S(1)}, u32[]{:S(2)}, u32[]{:S(2)}) collective-permute-start(bf16[4,8,96,128]{3,2,1,0:T(8,128)(2,1)S(1)} %get-tuple-element.36.refs_10_), channel_id=1, source_target_pairs={{0,2},{8,9},{16,18},{24,25},{32,34},{40,41},{48,50},{56,57},{64,66... | collective-permute-start | bytes 2359304 | tf_op jit(solution)/shard_map/ppermute | solution.py:34
  84.7 11.9 %copy-start.6 = (f32[192,3072]{1,0:T(8,128)}, f32[192,3072]{1,0:T(8,128)S(1)}, u32[]{:S(2)}) copy-start(f32[192,3072]{1,0:T(8,128)S(1)} %get-tuple-element.38.refs_6_.refs_0_) | copy-start | bytes 7077892
  84.7 11.9 %copy-start.11 = (f32[192,3072]{1,0:T(8,128)}, f32[192,3072]{1,0:T(8,128)S(1)}, u32[]{:S(2)}) copy-start(f32[192,3072]{1,0:T(8,128)S(1)} %get-tuple-element.37.g_own) | copy-start | bytes 7077892
  97.3 5.7 %collective-permute-start.16 = (f32[192,3072]{1,0:T(8,128)}, f32[192,3072]{1,0:T(8,128)S(1)}, u32[]{:S(2)}, u32[]{:S(2)}) collective-permute-start(f32[192,3072]{1,0:T(8,128)} %gate.3), channel_id=1, source_target_pairs={{0,8},{8,0},{16,24},{24,16},{32,40},{40,32},{48,56},{56,48},{64,72... | collective-permute-start | bytes 7077896 | tf_op jit(solution)/shard_map/ppermute | solution.py:34
  98.6 12.9 %collective-permute-start.17 = (bf16[8,2,96,128]{3,2,1,0:T(8,128)(2,1)}, bf16[8,2,96,128]{3,2,1,0:T(8,128)(2,1)S(1)}, u32[]{:S(2)}, u32[]{:S(2)}) collective-permute-start(bf16[8,2,96,128]{3,2,1,0:T(8,128)(2,1)} %get-tuple-element.46), channel_id=1, source_target_pairs={{0,1},{8,10},{16,17},{24,26},{32,33},{40,42},{48,49},{56,58},{64,6... | collective-permute-start | bytes 1179656 | tf_op jit(solution)/shard_map/ppermute | solution.py:34
  98.6 13.6 %collective-permute-start.18 = (bf16[8,2,96,128]{3,2,1,0:T(8,128)(2,1)S(1)}, bf16[8,2,96,128]{3,2,1,0:T(8,128)(2,1)S(1)}, u32[]{:S(2)}, u32[]{:S(2)}) collective-permute-start(bf16[8,2,96,128]{3,2,1,0:T(8,128)(2,1)S(1)} %get-tuple-element.47), channel_id=1, source_target_pairs={{0,128},{8,12},{16,144},{24,28},{32,160},{40,44},{48,176},{56,60},... | collective-permute-start | bytes 1179656 | tf_op jit(solution)/shard_map/ppermute | solution.py:34
  102.7 9.6 %collective-permute-start.19 = (bf16[8,2,96,128]{3,2,1,0:T(8,128)(2,1)S(1)}, bf16[8,2,96,128]{3,2,1,0:T(8,128)(2,1)S(1)}, u32[]{:S(2)}, u32[]{:S(2)}) collective-permute-start(bf16[8,2,96,128]{3,2,1,0:T(8,128)(2,1)S(1)} %get-tuple-element.48), channel_id=1, source_target_pairs={{0,129},{8,14},{16,145},{24,30},{32,161},{40,46},{48,177},{56,62},... | collective-permute-start | bytes 1179656 | tf_op jit(solution)/shard_map/ppermute | solution.py:34
  106.3 6.0 %copy-start.16 = (bf16[8,2,96,128]{3,2,1,0:T(8,128)(2,1)S(1)}, bf16[8,2,96,128]{3,2,1,0:T(8,128)(2,1)}, u32[]{:S(2)}) copy-start(bf16[8,2,96,128]{3,2,1,0:T(8,128)(2,1)} %copy-done.15) | copy-start | bytes 1179652
  158.4 4.7 %collective-permute-start.20 = (bf16[2,8,2,96,128]{4,3,2,1,0:T(8,128)(2,1)S(1)}, bf16[2,8,2,96,128]{4,3,2,1,0:T(8,128)(2,1)S(1)}, u32[]{:S(2)}, u32[]{:S(2)}) collective-permute-start(bf16[2,8,2,96,128]{4,3,2,1,0:T(8,128)(2,1)S(1)} %bitcast.24), channel_id=1, source_target_pairs={{0,8},{8,0},{16,24},{24,16},{32,40},{40,32},{48,56},{56,48},{64,72... | collective-permute-start | bytes 2359304 | tf_op jit(solution)/shard_map/ppermute | solution.py:34
  (9 other events, 12.0 us)

commit v5 on v4

--- a/solution.py
+++ b/solution.py
@@ -134,9 +134,13 @@
                 out[side, steps, 0, second] = turned[start : start + quarter]
 
 
-def linear_kernel(pairs, own, peer, *refs):
-    shards, rest = refs[: 2 * pairs], refs[2 * pairs :]
-    before, outs = rest[:-2], rest[-2:]
+def linear_kernel(counts, own, peer, *refs):
+    pairs, shards, start = len(counts) // 2, [], 0
+    for count in counts:
+        got = refs[start : start + count]
+        start += count
+        shards.append(got[0][...] if count == 1 else jnp.where(pl.program_id(0) < 2, got[0][...], got[1][...]))
+    before, outs = refs[start:-2], refs[-2:]
     depth = own.shape[2] // pairs
     rights = [jnp.concatenate([shards[2 * p][0], shards[2 * p + 1][0]], axis=0) for p in range(pairs)]
     for side, left in enumerate((own, peer)):
@@ -289,17 +293,20 @@
     )
 
 
-def normed_grad_kernel(width, y_own, y_peer, *refs):
-    shards, (g_own, g_send) = refs[:-2], refs[-2:]
+def normed_grad_kernel(width, counts, y_own, y_peer, *refs):
+    shards, start, (g_own, g_send) = [], 0, refs[-2:]
+    for count in counts:
+        shards.append([ref[m] for ref in refs[start : start + count] for m in range(ref.shape[0])])
+        start += count
     rows = y_own.shape[0]
     proj = 3 * HEADS * HD
     left = jnp.concatenate([y_own[:, :proj], y_peer[:, :proj]], axis=0)
     for j in range(8):
-        right = jnp.concatenate([shards[j][m] for m in range(3)], axis=1)
+        right = jnp.concatenate(shards[j], axis=1)
         total = dot_t(left, right, ((1,), (1,)))
         at = slice(j * width, (j + 1) * width)
         g_own[:, at] = total[:rows]
-        g_send[:, at] = total[rows:]
+        g_send[:, at] = total[rows:].astype(BF16)
 
 
 def token_grad_kernel(width, info, tokens, g_own, g_peer, out, mark, g):
@@ -308,7 +315,7 @@
     for first, ref in ((0, g_own), (8, g_peer)):
         for j in range(8):
             to = pl.ds(pl.multiple_of(info[first + j], 128), width)
-            g[:, to] = ref[:, j * width : (j + 1) * width]
+            g[:, to] = ref[:, j * width : (j + 1) * width].astype(F32)
     step = 16
     for i in range(rows // step):
         at = slice(i * step, (i + 1) * step)
@@ -393,15 +400,16 @@
 
     w = {(0, 0): lax.dynamic_slice(weights, (0, core * width, 0), (4, width, cols))}
     w[0, 1] = shift(w[0, 0], dx=1)
-    w[3, 0] = shift(w[0, 0], dy=-1)
+    parts = [lax.dynamic_slice(weights, (m, core * width, 0), (2, width, cols)) for m in (0, 2)]
+    w[3, 0] = [shift(part, dy=-1) for part in parts]
     w[1, 0] = shift(w[0, 0], dy=1)
     w[2, 0] = shift(w[1, 0], dy=1)
     w[1, 1] = shift(w[1, 0], dx=1)
-    w[3, 1] = shift(w[3, 0], dx=1)
+    w[3, 1] = [shift(part, dx=1) for part in w[3, 0]]
     w[2, 1] = shift(w[1, 1], dy=1)
     shards = [w[place] for place in ORDER]
 
-    peer = shift(gate(send, [w[1, 0], w[0, 1]]), dc=1)
+    peer = shift(gate(send, [w[1, 0], w[0, 1], w[3, 0][0]]), dc=1)
     one = (1, rows, model // 2)
     (turned,) = call(
         functools.partial(flip_kernel, width),
@@ -422,16 +430,27 @@
     sin_t = jnp.concatenate([-sin_r, sin_r, -sin_c, sin_c], axis=1)
 
     lin_shape = shape((rows, 4 * cols), F32)
+    one_matrix = (1, width, cols)
+
+    def by_matrix(w_j):
+        if not isinstance(w_j, list):
+            return [(w_j, one_matrix, lambda m: (m, 0, 0))]
+        return [
+            (w_j[0], one_matrix, lambda m: (jnp.minimum(m, 1), 0, 0)),
+            (w_j[1], one_matrix, lambda m: (jnp.maximum(m - 2, 0), 0, 0)),
+        ]
+
     lin = []
     for first, pairs in ((0, 3), (3, 1)):
         span = 2 * pairs * width
+        group = shards[2 * first : 2 * (first + pairs)]
         columns = functools.partial(lambda c, m: (m // 3, 0, c), first // pairs)
         acc = ((rows, cols), lambda m: (0, m))
         lin = call(
-            functools.partial(linear_kernel, pairs),
+            functools.partial(linear_kernel, [len(w_j) if isinstance(w_j, list) else 1 for w_j in group]),
             [(lin_shape, *acc)] * 2,
             [(own, (1, rows, span), columns), (peer, (1, rows, span), columns)]
-            + [(w_j, (1, width, cols), lambda m: (m, 0, 0)) for w_j in shards[2 * first : 2 * (first + pairs)]]
+            + [item for w_j in group for item in by_matrix(w_j)]
             + [(value, *acc) for value in lin],
             grid=(4,),
             flops=2 * 2 * rows * 2 * pairs * width * 4 * cols,
@@ -483,11 +502,15 @@
     )
     ahead = [along(joined[0], first=1), along(joined[1], first=-1)]
 
-    most = ((3, width, cols), lambda _: (0, 0, 0))
+    def first_three(w_j):
+        if not isinstance(w_j, list):
+            return [(w_j, (3, width, cols), lambda _: (0, 0, 0))]
+        return [w_j[0], (w_j[1], one_matrix, lambda _: (0, 0, 0))]
+
     g_own, g_send = call(
-        functools.partial(normed_grad_kernel, width),
-        [shape((rows, model // 2), F32)] * 2,
-        [y_own, y_peer] + [(w_j, *most) for w_j in shards],
+        functools.partial(normed_grad_kernel, width, [len(first_three(w_j)) for w_j in shards]),
+        [shape((rows, model // 2), F32), shape((rows, model // 2))],
+        [y_own, y_peer] + [item for w_j in shards for item in first_three(w_j)],
         flops=2 * rows * model * 3 * cols,
         nbytes=4 * model * cols + 4 * rows * model,
         name="normed_grad",

time: 166 us -> 162 us (0.976)
  local copies, waits for them, and re-layouts: 15.5 us -> 12.4 us
    unnamed x40 -> x34, local copies, waits for them, and re-layouts: 14.4 us -> 8.19 us
    dynamic_slice x0 -> x1, local copies, waits for them, and re-layouts: none -> 2.06 us  [per_device(): lax.dynamic_slice(weights, (m, core * width, 0), (2, width, cols))]
    ppermute x21 -> x23, starting transfers between devices: 34.6 us -> 33.2 us  [permute(): return lax.ppermute(values, ('dp', 'fsdp'), pairs)]
    ppermute x21 -> x23, waiting for transfers between devices: 33.7 us -> 34.5 us  [permute(): return lax.ppermute(values, ('dp', 'fsdp'), pairs)]
  transfers between devices with their start and end apart: 21 -> 23, of which waited for: 12 -> 14; matrix products, arithmetic and copies ran while one was open for 1% -> 2% of each run, Pallas kernels for 14% -> 15%
where the time goes in v5:
time: 162 us; the launch traced here: 161 us
  blocking collectives  45.2 us (28%)
  waiting for transfers between devices  34.5 us (21%)
  Pallas kernels  33.9 us (21%)
  starting transfers between devices  33.2 us (20%)
  local copies, waits for them, and re-layouts  12.4 us (8%)
    all_to_all x2, blocking collectives, exchange(): lax.all_to_all(values, 'dp', split_axis=0, concat_axis=0, axis_index_grou...  45.2 us
    ppermute x23, waiting for transfers between devices, permute(): return lax.ppermute(values, ('dp', 'fsdp'), pairs)  34.5 us
    ppermute x23, starting transfers between devices, permute(): return lax.ppermute(values, ('dp', 'fsdp'), pairs)  33.2 us
    pallas_call x14, Pallas kernels, call(): pl.pallas_call(kernel, grid=grid or (1,), out_shape=out_shapes, in_specs=...  30.4 us
    unnamed x34, local copies, waits for them, and re-layouts  8.19 us
    pallas_call x2, Pallas kernels, place(): pl.pallas_call(place_kernel, grid_spec=pltpu.PrefetchScalarGridSpec(num_s...  3.47 us
  transfers between devices with their start and end apart: 23, of which 14 were waited for; matrix products, arithmetic and copies ran while one was open for 2% of the time, Pallas kernels for 15%

profile of v5, /device:TPU:1, one launch (start us, length us, event | category | flops | bytes accessed | tf_op | source)
XLA Modules:
  0.0 161.1 jit_solution(16496320752799648442)
XLA Ops:
  0.6 2.1 %constant_dynamic-slice_fusion.2.refs_2_ = bf16[4,384,256]{2,1,0:T(8,128)(2,1)} fusion(bf16[4,768,256]{2,1,0:T(8,128)(2,1)} %param.11, s32[]{:T(128)S(6)} %select_n.118), kind=kLoop, calls=%fused_computation.12 | loop fusion | bytes 1572868 | tf_op jit(solution)/shard_map/dynamic_slice | solution.py:401
  2.7 3.3 %collective-permute-start.1 = (bf16[4,384,256]{2,1,0:T(8,128)(2,1)}, bf16[4,384,256]{2,1,0:T(8,128)(2,1)S(1)}, u32[]{:S(2)}, u32[]{:S(2)}) collective-permute-start(bf16[4,384,256]{2,1,0:T(8,128)(2,1)} %constant_dynamic-slice_fusion.2.refs_2_), channel_id=1, source_target_pairs={{0,1},{8,137},{16,17},{24,153},{32,33},{40,169},{48,49},{56,185},{... | collective-permute-start | bytes 2359304 | tf_op jit(solution)/shard_map/ppermute | solution.py:34
  6.0 2.7 %collective-permute-start = (bf16[4,384,256]{2,1,0:T(8,128)(2,1)}, bf16[4,384,256]{2,1,0:T(8,128)(2,1)}, u32[]{:S(2)}, u32[]{:S(2)}) collective-permute-start(bf16[4,384,256]{2,1,0:T(8,128)(2,1)} %constant_dynamic-slice_fusion.2.refs_2_), channel_id=1, source_target_pairs={{0,2},{8,14},{16,18},{24,30},{32,34},{40,46},{48,50},{56,62},{64,6... | collective-permute-start | bytes 2359304 | tf_op jit(solution)/shard_map/ppermute | solution.py:34
  8.8 2.1 %constant_dynamic-slice_fusion = (bf16[2,384,256]{2,1,0:T(8,128)(2,1)}, bf16[2,384,256]{2,1,0:T(8,128)(2,1)}) fusion(bf16[4,768,256]{2,1,0:T(8,128)(2,1)} %param.11, s32[]{:T(128)S(6)} %select_n.118), kind=kLoop, calls=%fused_computation.10 | loop fusion | bytes 1572868 | tf_op jit(solution)/shard_map/dynamic_slice | solution.py:403
  12.6 1.7 %copy-done.10 = bf16[192,6144]{1,0:T(8,128)(2,1)S(1)} copy-done((bf16[192,6144]{1,0:T(8,128)(2,1)S(1)}, bf16[192,6144]{1,0:T(8,128)(2,1)}, u32[]{:S(2)}) %copy-start.10) | copy-done | bytes 2359320
  14.3 3.0 %prep.1 = (bf16[2,192,3072]{2,1,0:T(8,128)(2,1)S(1)}, bf16[2,192,3072]{2,1,0:T(8,128)(2,1)S(1)}) custom-call(s32[20]{0:T(128)S(1)} %stack.87.info, bf16[192,6144]{1,0:T(8,128)(2,1)S(1)} %copy-done, bf16[192,6144]{1,0:T(8,128)(2,1)S(1)} %copy-done.10), custom_call_target="tpu_custom_call" | custom-call | flops 9437184 | bytes 9437184 | tf_op jit(solution)/shard_map/prep/pallas_call | solution.py:72
  18.7 4.3 %collective-permute-done.2.refs_3_.refs_6_ = bf16[2,384,256]{2,1,0:T(8,128)(2,1)S(1)} collective-permute-done((bf16[2,384,256]{2,1,0:T(8,128)(2,1)}, bf16[2,384,256]{2,1,0:T(8,128)(2,1)S(1)}, u32[]{:S(2)}, u32[]{:S(2)}) %collective-permute-start.2) | collective-permute-done | bytes 393248 | tf_op jit(solution)/shard_map/ppermute | solution.py:34
  24.1 2.7 %collective-permute-start.7 = (bf16[4,384,256]{2,1,0:T(8,128)(2,1)}, bf16[4,384,256]{2,1,0:T(8,128)(2,1)S(1)}, u32[]{:S(2)}, u32[]{:S(2)}) collective-permute-start(bf16[4,384,256]{2,1,0:T(8,128)(2,1)} %collective-permute-done.refs_1_.refs_4_), channel_id=1, source_target_pairs={{0,1},{8,137},{16,17},{24,153},{32,33},{40,169},{48,49},{56,185},{... | collective-permute-start | bytes 2359304 | tf_op jit(solution)/shard_map/ppermute | solution.py:34
  28.2 7.8 %collective-permute-done.7.refs_5_ = bf16[4,384,256]{2,1,0:T(8,128)(2,1)S(1)} collective-permute-done((bf16[4,384,256]{2,1,0:T(8,128)(2,1)}, bf16[4,384,256]{2,1,0:T(8,128)(2,1)S(1)}, u32[]{:S(2)}, u32[]{:S(2)}) %collective-permute-start.7) | collective-permute-done | bytes 786464 | tf_op jit(solution)/shard_map/ppermute | solution.py:34
  36.9 3.2 %collective-permute-start.4 = (bf16[2,384,256]{2,1,0:T(8,128)(2,1)}, bf16[2,384,256]{2,1,0:T(8,128)(2,1)S(1)}, u32[]{:S(2)}, u32[]{:S(2)}) collective-permute-start(bf16[2,384,256]{2,1,0:T(8,128)(2,1)} %copy-done.5), channel_id=1, source_target_pairs={{0,1},{8,137},{16,17},{24,153},{32,33},{40,169},{48,49},{56,185},{... | collective-permute-start | bytes 1179656 | tf_op jit(solution)/shard_map/ppermute | solution.py:34
  41.2 2.5 %flip.1.refs_9_.refs_0_.refs_1_ = bf16[2,4,2,4,96,384]{5,4,3,2,1,0:T(8,128)(2,1)S(1)} custom-call(s32[20]{0:T(128)S(1)} %stack.87.info, bf16[2,192,3072]{2,1,0:T(8,128)(2,1)S(1)} %get-tuple-element.26.own.refs_0_, bf16[2,192,3072]{2,1,0:T(8,128)(2,1)S(1)} %collective-permute-done.3.peer.refs_1_), custom_call_target="tpu_custom_call" | custom-call | bytes 9437184 | tf_op jit(solution)/shard_map/flip/pallas_call | solution.py:72
  43.7 4.4 %linear.2 = (f32[192,1024]{1,0:T(8,128)S(1)}, f32[192,1024]{1,0:T(8,128)S(1)}) custom-call(bf16[2,192,3072]{2,1,0:T(8,128)(2,1)S(1)} %get-tuple-element.26.own.refs_0_, bf16[2,192,3072]{2,1,0:T(8,128)(2,1)S(1)} %collective-permute-done.3.peer.refs_1_, bf16[4,384,256]{2,1,0:T(8,128)(2,1)} %constant_dynamic-slice_fusion.2.refs_2_, ...), custom_call_target="tpu_custom_call" | custom-call | flops 1811939328 | bytes 8257536 | tf_op jit(solution)/shard_map/linear/pallas_call | solution.py:72
  50.0 1.8 %linear.3 = (f32[192,1024]{1,0:T(8,128)S(1)}, f32[192,1024]{1,0:T(8,128)S(1)}) custom-call(bf16[2,192,3072]{2,1,0:T(8,128)(2,1)S(1)} %get-tuple-element.26.own.refs_0_, bf16[2,192,3072]{2,1,0:T(8,128)(2,1)S(1)} %collective-permute-done.3.peer.refs_1_, bf16[2,384,256]{2,1,0:T(8,128)(2,1)S(1)} %collective-permute-done.4.refs_0_.refs_9_, ...), custom_call_target="tpu_custom_call" | custom-call | flops 603979776 | bytes 2752512 | tf_op jit(solution)/shard_map/linear/pallas_call | solution.py:72
  51.7 1.8 %collective-permute-start.10 = (f32[192,1024]{1,0:T(8,128)S(1)}, f32[192,1024]{1,0:T(8,128)S(1)}, u32[]{:S(2)}, u32[]{:S(2)}) collective-permute-start(f32[192,1024]{1,0:T(8,128)S(1)} %get-tuple-element.31), channel_id=1, source_target_pairs={{0,8},{8,0},{16,24},{24,16},{32,40},{40,32},{48,56},{56,48},{64,72... | collective-permute-start | bytes 2359304 | tf_op jit(solution)/shard_map/ppermute | solution.py:34
  53.6 1.9 %collective-permute-done.10.theirs = f32[192,1024]{1,0:T(8,128)S(1)} collective-permute-done((f32[192,1024]{1,0:T(8,128)S(1)}, f32[192,1024]{1,0:T(8,128)S(1)}, u32[]{:S(2)}, u32[]{:S(2)}) %collective-permute-start.10) | collective-permute-done | bytes 786464 | tf_op jit(solution)/shard_map/ppermute | solution.py:34
  55.5 3.2 %attend.1.refs_2_.refs_1_.refs_0_ = bf16[192,1024]{1,0:T(8,128)(2,1)S(1)} custom-call(s32[1,3]{1,0:T(1,128)S(1)} %copy-done.13, f32[192,1024]{1,0:T(8,128)S(1)} %get-tuple-element.30.mine, f32[192,1024]{1,0:T(8,128)S(1)} %collective-permute-done.10.theirs, f32[192,128]{1,0:T(8,128)S(1)} %get-tuple-element.63.refs_10_.cos_t, ...), custom_call_target="tpu_custom_call" | custom-call | flops 188743680 | bytes 1966080 | tf_op jit(solution)/shard_map/attend/pallas_call | solution.py:72
  62.1 2.1 %collective-permute-start.13 = (bf16[4,8,96,128]{3,2,1,0:T(8,128)(2,1)S(1)}, bf16[4,8,96,128]{3,2,1,0:T(8,128)(2,1)S(1)}, u32[]{:S(2)}, u32[]{:S(2)}) collective-permute-start(bf16[4,8,96,128]{3,2,1,0:T(8,128)(2,1)S(1)} %get-tuple-element.35), channel_id=1, source_target_pairs={{0,6},{8,137},{16,22},{24,153},{32,38},{40,169},{48,54},{56,185},{... | collective-permute-start | bytes 2359304 | tf_op jit(solution)/shard_map/ppermute | solution.py:34
  66.7 1.8 %terms.3 = (bf16[4,8,96,128]{3,2,1,0:T(8,128)(2,1)S(1)}, bf16[4,8,96,128]{3,2,1,0:T(8,128)(2,1)S(1)}, bf16[4,8,96,128]{3,2,1,0:T(8,128)(2,1)S(1)}, bf16[4,8,96,128]{3,2,1,0:T(8,128)(2,1)S(1)}) custom-call(bf16[2,4,2,4,96,384]{5,4,3,2,1,0:T(8,128)(2,1)S(1)} %flip.1.refs_9_.refs_0_.refs_1_, bf16[2,4,2,4,96,384]{5,4,3,2,1,0:T(8,128)(2,1)S(1)} %flip.1.refs_9_.refs_0_.refs_1_, ...), custom_call_target="tpu_custom_call" | custom-call | flops 1207959552 | bytes 7864320 | tf_op jit(solution)/shard_map/terms/pallas_call | solution.py:72
  68.5 5.3 %collective-permute-done.12.far_0 = bf16[4,8,96,128]{3,2,1,0:T(8,128)(2,1)S(1)} collective-permute-done((bf16[4,8,96,128]{3,2,1,0:T(8,128)(2,1)S(1)}, bf16[4,8,96,128]{3,2,1,0:T(8,128)(2,1)S(1)}, u32[]{:S(2)}, u32[]{:S(2)}) %collective-permute-start.12) | collective-permute-done | bytes 786464 | tf_op jit(solution)/shard_map/ppermute | solution.py:34
  74.3 2.8 %collective-permute-start.17 = (bf16[4,8,96,128]{3,2,1,0:T(8,128)(2,1)S(1)}, bf16[4,8,96,128]{3,2,1,0:T(8,128)(2,1)S(1)}, u32[]{:S(2)}, u32[]{:S(2)}) collective-permute-start(bf16[4,8,96,128]{3,2,1,0:T(8,128)(2,1)S(1)} %get-tuple-element.43), channel_id=1, source_target_pairs={{0,6},{8,137},{16,22},{24,153},{32,38},{40,169},{48,54},{56,185},{... | collective-permute-start | bytes 2359304 | tf_op jit(solution)/shard_map/ppermute | solution.py:34
  77.0 3.9 %normed_grad.1 = (f32[192,3072]{1,0:T(8,128)S(1)}, bf16[192,3072]{1,0:T(8,128)(2,1)S(1)}) custom-call(bf16[192,1024]{1,0:T(8,128)(2,1)S(1)} %attend.1.refs_2_.refs_1_.refs_0_, bf16[192,1024]{1,0:T(8,128)(2,1)S(1)} %collective-permute-done.11.refs_3_.refs_2_.refs_1_, bf16[4,384,256]{2,1,0:T(8,128)(2,1)} %constant_dynamic-slice_fusion.2.refs_2_, ...), custom_call_target="tpu_custom_call" | custom-call | flops 1811939328 | bytes 11010048 | tf_op jit(solution)/shard_map/normed_grad/pallas_call | solution.py:72
  82.3 7.8 %collective-permute-done.17.refs_5_ = bf16[4,8,96,128]{3,2,1,0:T(8,128)(2,1)S(1)} collective-permute-done((bf16[4,8,96,128]{3,2,1,0:T(8,128)(2,1)S(1)}, bf16[4,8,96,128]{3,2,1,0:T(8,128)(2,1)S(1)}, u32[]{:S(2)}, u32[]{:S(2)}) %collective-permute-start.17) | collective-permute-done | bytes 786464 | tf_op jit(solution)/shard_map/ppermute | solution.py:34
  90.7 2.0 %sides.1 = (bf16[8,2,96,128]{3,2,1,0:T(8,128)(2,1)S(1)}, bf16[8,2,96,128]{3,2,1,0:T(8,128)(2,1)}, bf16[8,2,96,128]{3,2,1,0:T(8,128)(2,1)}, bf16[8,2,96,128]{3,2,1,0:T(8,128)(2,1)S(1)}) custom-call(bf16[4,8,96,128]{3,2,1,0:T(8,128)(2,1)S(1)} %get-tuple-element.39.refs_0_, bf16[4,8,96,128]{3,2,1,0:T(8,128)(2,1)S(1)} %collective-permute-done.14.refs_1_, ...), custom_call_target="tpu_custom_call" | custom-call | flops 2359296 | bytes 6291456 | tf_op jit(solution)/shard_map/sides/pallas_call | solution.py:72
  96.2 2.6 %collective-permute-start.20 = (bf16[8,2,96,128]{3,2,1,0:T(8,128)(2,1)}, bf16[8,2,96,128]{3,2,1,0:T(8,128)(2,1)S(1)}, u32[]{:S(2)}, u32[]{:S(2)}) collective-permute-start(bf16[8,2,96,128]{3,2,1,0:T(8,128)(2,1)} %get-tuple-element.47), channel_id=1, source_target_pairs={{0,128},{8,12},{16,144},{24,28},{32,160},{40,44},{48,176},{56,60},... | collective-permute-start | bytes 1179656 | tf_op jit(solution)/shard_map/ppermute | solution.py:34
  99.9 1.7 %copy-done.8 = f32[192,3072]{1,0:T(8,128)S(1)} copy-done((f32[192,3072]{1,0:T(8,128)S(1)}, f32[192,3072]{1,0:T(8,128)}, u32[]{:S(2)}) %copy-start.8) | copy-done | bytes 2359320
  101.6 5.1 %token_grad.1 = (bf16[192,6144]{1,0:T(8,128)(2,1)}, f32[8,128]{1,0:T(8,128)S(1)}) custom-call(s32[20]{0:T(128)S(1)} %stack.87.info, bf16[192,6144]{1,0:T(8,128)(2,1)S(1)} %copy-done.1, f32[192,3072]{1,0:T(8,128)S(1)} %copy-done.8, bf16[192,3072]{1,0:T(8,128)(2,1)S(1)} %collective-permute-done.18.g_peer), custom_call_target="tpu_custom_call" | custom-call | flops 18874368 | bytes 9437184 | tf_op jit(solution)/shard_map/token_grad/pallas_call | solution.py:72
  106.7 2.0 %collective-permute-done.20.refs_2_ = bf16[8,2,96,128]{3,2,1,0:T(8,128)(2,1)S(1)} collective-permute-done((bf16[8,2,96,128]{3,2,1,0:T(8,128)(2,1)}, bf16[8,2,96,128]{3,2,1,0:T(8,128)(2,1)S(1)}, u32[]{:S(2)}, u32[]{:S(2)}) %collective-permute-start.20) | collective-permute-done | bytes 393248 | tf_op jit(solution)/shard_map/ppermute | solution.py:34
  109.0 20.9 %all_to_all.10.got = bf16[8,2,96,128]{3,2,1,0:T(8,128)(2,1)S(1)} all-to-all(bf16[8,2,96,128]{3,2,1,0:T(8,128)(2,1)S(1)} %seconds.1), channel_id=1, replica_groups={{0,16,32,48,64,80,96,112},{8,24,40,56,72,88,104,120},{128,144,160,176,1..., dimensions={0} | all-to-all | bytes 786432 | tf_op jit(solution)/shard_map/all_to_all | solution.py:366
  130.0 24.4 %all_to_all.11 = bf16[16,2,96,128]{3,2,1,0:T(8,128)(2,1)S(1)} all-to-all(bf16[16,2,96,128]{3,2,1,0:T(8,128)(2,1)S(1)} %last.1), channel_id=1, replica_groups={{0,16,32,48,64,80,96,112,128,144,160,176,192,208,224,240},{8,24,40,56,7..., dimensions={0} | all-to-all | bytes 1572864 | tf_op jit(solution)/shard_map/all_to_all | solution.py:366
  154.3 3.1 %collective-permute-start.22 = (bf16[2,8,2,96,128]{4,3,2,1,0:T(8,128)(2,1)S(1)}, bf16[2,8,2,96,128]{4,3,2,1,0:T(8,128)(2,1)S(1)}, u32[]{:S(2)}, u32[]{:S(2)}) collective-permute-start(bf16[2,8,2,96,128]{4,3,2,1,0:T(8,128)(2,1)S(1)} %bitcast.24), channel_id=1, source_target_pairs={{0,8},{8,0},{16,24},{24,16},{32,40},{40,32},{48,56},{56,48},{64,72... | collective-permute-start | bytes 2359304 | tf_op jit(solution)/shard_map/ppermute | solution.py:34
  157.5 1.7 %place.2.refs_0_ = f32[4,768,256]{2,1,0:T(8,128)} custom-call(s32[1]{0:T(128)} %bitcast.18.at, bf16[2,8,2,96,128]{4,3,2,1,0:T(8,128)(2,1)S(1)} %bitcast.25), custom_call_target="tpu_custom_call" | custom-call | flops 1 | bytes 6291456 | tf_op jit(solution)/shard_map/place/pallas_call | solution.py:342
  159.4 1.7 %place.3 = f32[4,768,256]{2,1,0:T(8,128)} custom-call(s32[1]{0:T(128)} %bitcast.22.at, bf16[2,8,2,96,128]{4,3,2,1,0:T(8,128)(2,1)S(1)} %collective-permute-done.22.blocks, f32[4,768,256]{2,1,0:T(8,128)} %place.2.refs_0_), custom_call_target="tpu_custom_call", output_to_operand_aliasing={{}: (2, {})} | custom-call | flops 1 | bytes 6291456 | tf_op jit(solution)/shard_map/place/pallas_call | solution.py:342
  (74 shorter events, 22.9 us)
Async XLA Ops:
  2.7 20.3 %collective-permute-start.1 = (bf16[4,384,256]{2,1,0:T(8,128)(2,1)}, bf16[4,384,256]{2,1,0:T(8,128)(2,1)S(1)}, u32[]{:S(2)}, u32[]{:S(2)}) collective-permute-start(bf16[4,384,256]{2,1,0:T(8,128)(2,1)} %constant_dynamic-slice_fusion.2.refs_2_), channel_id=1, source_target_pairs={{0,1},{8,137},{16,17},{24,153},{32,33},{40,169},{48,49},{56,185},{... | collective-permute-start | bytes 2359304 | tf_op jit(solution)/shard_map/ppermute | solution.py:34
  6.0 17.0 %collective-permute-start = (bf16[4,384,256]{2,1,0:T(8,128)(2,1)}, bf16[4,384,256]{2,1,0:T(8,128)(2,1)}, u32[]{:S(2)}, u32[]{:S(2)}) collective-permute-start(bf16[4,384,256]{2,1,0:T(8,128)(2,1)} %constant_dynamic-slice_fusion.2.refs_2_), channel_id=1, source_target_pairs={{0,2},{8,14},{16,18},{24,30},{32,34},{40,46},{48,50},{56,62},{64,6... | collective-permute-start | bytes 2359304 | tf_op jit(solution)/shard_map/ppermute | solution.py:34
  10.8 12.2 %collective-permute-start.2 = (bf16[2,384,256]{2,1,0:T(8,128)(2,1)}, bf16[2,384,256]{2,1,0:T(8,128)(2,1)S(1)}, u32[]{:S(2)}, u32[]{:S(2)}) collective-permute-start(bf16[2,384,256]{2,1,0:T(8,128)(2,1)} %get-tuple-element.51), channel_id=1, source_target_pairs={{0,6},{8,10},{16,22},{24,26},{32,38},{40,42},{48,54},{56,58},{64,7... | collective-permute-start | bytes 1179656 | tf_op jit(solution)/shard_map/ppermute | solution.py:34
  24.1 12.8 %copy-start.15 = (s32[2,192]{1,0:T(2,128)S(1)}, s32[2,192]{1,0:T(2,128)}, u32[]{:S(2)}) copy-start(s32[2,192]{1,0:T(2,128)} %param.10) | copy-start | bytes 4612
  24.1 16.1 %copy-start.16 = (f32[32]{0:T(128)S(1)}, f32[32]{0:T(128)}, u32[]{:S(2)}) copy-start(f32[32]{0:T(128)} %constant.149) | copy-start | bytes 388
  24.1 17.1 %collective-permute-start.3 = (bf16[2,192,3072]{2,1,0:T(8,128)(2,1)}, bf16[2,192,3072]{2,1,0:T(8,128)(2,1)S(1)}, u32[]{:S(2)}, u32[]{:S(2)}) collective-permute-start(bf16[2,192,3072]{2,1,0:T(8,128)(2,1)} %gate.2), channel_id=1, source_target_pairs={{0,8},{8,0},{16,24},{24,16},{32,40},{40,32},{48,56},{56,48},{64,72... | collective-permute-start | bytes 7077896 | tf_op jit(solution)/shard_map/ppermute | solution.py:34
  24.1 11.9 %collective-permute-start.7 = (bf16[4,384,256]{2,1,0:T(8,128)(2,1)}, bf16[4,384,256]{2,1,0:T(8,128)(2,1)S(1)}, u32[]{:S(2)}, u32[]{:S(2)}) collective-permute-start(bf16[4,384,256]{2,1,0:T(8,128)(2,1)} %collective-permute-done.refs_1_.refs_4_), channel_id=1, source_target_pairs={{0,1},{8,137},{16,17},{24,153},{32,33},{40,169},{48,49},{56,185},{... | collective-permute-start | bytes 2359304 | tf_op jit(solution)/shard_map/ppermute | solution.py:34
  26.8 16.9 %collective-permute-start.9 = (bf16[4,384,256]{2,1,0:T(8,128)(2,1)}, bf16[4,384,256]{2,1,0:T(8,128)(2,1)S(1)}, u32[]{:S(2)}, u32[]{:S(2)}) collective-permute-start(bf16[4,384,256]{2,1,0:T(8,128)(2,1)} %collective-permute-done.refs_1_.refs_4_), channel_id=1, source_target_pairs={{0,2},{8,14},{16,18},{24,30},{32,34},{40,46},{48,50},{56,62},{64,6... | collective-permute-start | bytes 2359304 | tf_op jit(solution)/shard_map/ppermute | solution.py:34
  27.5 12.6 %collective-permute-start.5 = (bf16[2,384,256]{2,1,0:T(8,128)(2,1)}, bf16[2,384,256]{2,1,0:T(8,128)(2,1)S(1)}, u32[]{:S(2)}, u32[]{:S(2)}) collective-permute-start(bf16[2,384,256]{2,1,0:T(8,128)(2,1)} %get-tuple-element.50), channel_id=1, source_target_pairs={{0,6},{8,10},{16,22},{24,26},{32,38},{40,42},{48,54},{56,58},{64,7... | collective-permute-start | bytes 1179656 | tf_op jit(solution)/shard_map/ppermute | solution.py:34
  36.0 13.9 %collective-permute-start.8 = (bf16[4,384,256]{2,1,0:T(8,128)(2,1)S(1)}, bf16[4,384,256]{2,1,0:T(8,128)(2,1)S(1)}, u32[]{:S(2)}, u32[]{:S(2)}) collective-permute-start(bf16[4,384,256]{2,1,0:T(8,128)(2,1)S(1)} %collective-permute-done.7.refs_5_), channel_id=1, source_target_pairs={{0,2},{8,14},{16,18},{24,30},{32,34},{40,46},{48,50},{56,62},{64,6... | collective-permute-start | bytes 2359304 | tf_op jit(solution)/shard_map/ppermute | solution.py:34
  36.9 12.3 %collective-permute-start.4 = (bf16[2,384,256]{2,1,0:T(8,128)(2,1)}, bf16[2,384,256]{2,1,0:T(8,128)(2,1)S(1)}, u32[]{:S(2)}, u32[]{:S(2)}) collective-permute-start(bf16[2,384,256]{2,1,0:T(8,128)(2,1)} %copy-done.5), channel_id=1, source_target_pairs={{0,1},{8,137},{16,17},{24,153},{32,33},{40,169},{48,49},{56,185},{... | collective-permute-start | bytes 1179656 | tf_op jit(solution)/shard_map/ppermute | solution.py:34
  40.1 9.1 %collective-permute-start.6 = (bf16[2,384,256]{2,1,0:T(8,128)(2,1)S(1)}, bf16[2,384,256]{2,1,0:T(8,128)(2,1)S(1)}, u32[]{:S(2)}, u32[]{:S(2)}) collective-permute-start(bf16[2,384,256]{2,1,0:T(8,128)(2,1)S(1)} %collective-permute-done.5.refs_7_), channel_id=1, source_target_pairs={{0,1},{8,137},{16,17},{24,153},{32,33},{40,169},{48,49},{56,185},{... | collective-permute-start | bytes 1179656 | tf_op jit(solution)/shard_map/ppermute | solution.py:34
  41.2 2.5 %copy-start.3 = (bf16[4,384,256]{2,1,0:T(8,128)(2,1)S(1)}, bf16[4,384,256]{2,1,0:T(8,128)(2,1)}, u32[]{:S(2)}) copy-start(bf16[4,384,256]{2,1,0:T(8,128)(2,1)} %copy-done.2) | copy-start | bytes 2359300
  41.2 2.5 %copy-start.6 = (bf16[2,384,256]{2,1,0:T(8,128)(2,1)S(1)}, bf16[2,384,256]{2,1,0:T(8,128)(2,1)}, u32[]{:S(2)}) copy-start(bf16[2,384,256]{2,1,0:T(8,128)(2,1)} %copy-done.5) | copy-start | bytes 1179652
  50.0 5.5 %copy-start.13 = (s32[1,3]{1,0:T(1,128)S(1)}, s32[1,3]{1,0:T(1,128)}, u32[]{:S(2)}) copy-start(s32[1,3]{1,0:T(1,128)} %lengths.1) | copy-start | bytes 40
  51.7 3.7 %collective-permute-start.10 = (f32[192,1024]{1,0:T(8,128)S(1)}, f32[192,1024]{1,0:T(8,128)S(1)}, u32[]{:S(2)}, u32[]{:S(2)}) collective-permute-start(f32[192,1024]{1,0:T(8,128)S(1)} %get-tuple-element.31), channel_id=1, source_target_pairs={{0,8},{8,0},{16,24},{24,16},{32,40},{40,32},{48,56},{56,48},{64,72... | collective-permute-start | bytes 2359304 | tf_op jit(solution)/shard_map/ppermute | solution.py:34
  58.6 1.8 %collective-permute-start.11 = (bf16[192,1024]{1,0:T(8,128)(2,1)S(1)}, bf16[192,1024]{1,0:T(8,128)(2,1)S(1)}, u32[]{:S(2)}, u32[]{:S(2)}) collective-permute-start(bf16[192,1024]{1,0:T(8,128)(2,1)S(1)} %attend.1.refs_2_.refs_1_.refs_0_), channel_id=1, source_target_pairs={{0,8},{8,0},{16,24},{24,16},{32,40},{40,32},{48,56},{56,48},{64,72... | collective-permute-start | bytes 1179656 | tf_op jit(solution)/shard_map/ppermute | solution.py:34
  61.4 12.4 %collective-permute-start.12 = (bf16[4,8,96,128]{3,2,1,0:T(8,128)(2,1)S(1)}, bf16[4,8,96,128]{3,2,1,0:T(8,128)(2,1)S(1)}, u32[]{:S(2)}, u32[]{:S(2)}) collective-permute-start(bf16[4,8,96,128]{3,2,1,0:T(8,128)(2,1)S(1)} %get-tuple-element.33), channel_id=1, source_target_pairs={{0,2},{8,9},{16,18},{24,25},{32,34},{40,41},{48,50},{56,57},{64,66... | collective-permute-start | bytes 2359304 | tf_op jit(solution)/shard_map/ppermute | solution.py:34
  62.1 11.8 %collective-permute-start.13 = (bf16[4,8,96,128]{3,2,1,0:T(8,128)(2,1)S(1)}, bf16[4,8,96,128]{3,2,1,0:T(8,128)(2,1)S(1)}, u32[]{:S(2)}, u32[]{:S(2)}) collective-permute-start(bf16[4,8,96,128]{3,2,1,0:T(8,128)(2,1)S(1)} %get-tuple-element.35), channel_id=1, source_target_pairs={{0,6},{8,137},{16,22},{24,153},{32,38},{40,169},{48,54},{56,185},{... | collective-permute-start | bytes 2359304 | tf_op jit(solution)/shard_map/ppermute | solution.py:34
  65.2 16.5 %collective-permute-start.14 = (bf16[4,8,96,128]{3,2,1,0:T(8,128)(2,1)S(1)}, bf16[4,8,96,128]{3,2,1,0:T(8,128)(2,1)S(1)}, u32[]{:S(2)}, u32[]{:S(2)}) collective-permute-start(bf16[4,8,96,128]{3,2,1,0:T(8,128)(2,1)S(1)} %get-tuple-element.40), channel_id=1, source_target_pairs={{0,6},{8,137},{16,22},{24,153},{32,38},{40,169},{48,54},{56,185},{... | collective-permute-start | bytes 2359304 | tf_op jit(solution)/shard_map/ppermute | solution.py:34
  65.9 16.4 %collective-permute-start.16 = (bf16[4,8,96,128]{3,2,1,0:T(8,128)(2,1)S(1)}, bf16[4,8,96,128]{3,2,1,0:T(8,128)(2,1)S(1)}, u32[]{:S(2)}, u32[]{:S(2)}) collective-permute-start(bf16[4,8,96,128]{3,2,1,0:T(8,128)(2,1)S(1)} %get-tuple-element.42), channel_id=1, source_target_pairs={{0,2},{8,9},{16,18},{24,25},{32,34},{40,41},{48,50},{56,57},{64,66... | collective-permute-start | bytes 2359304 | tf_op jit(solution)/shard_map/ppermute | solution.py:34
  74.3 15.8 %collective-permute-start.17 = (bf16[4,8,96,128]{3,2,1,0:T(8,128)(2,1)S(1)}, bf16[4,8,96,128]{3,2,1,0:T(8,128)(2,1)S(1)}, u32[]{:S(2)}, u32[]{:S(2)}) collective-permute-start(bf16[4,8,96,128]{3,2,1,0:T(8,128)(2,1)S(1)} %get-tuple-element.43), channel_id=1, source_target_pairs={{0,6},{8,137},{16,22},{24,153},{32,38},{40,169},{48,54},{56,185},{... | collective-permute-start | bytes 2359304 | tf_op jit(solution)/shard_map/ppermute | solution.py:34
  77.0 13.7 %collective-permute-start.15 = (bf16[4,8,96,128]{3,2,1,0:T(8,128)(2,1)S(1)}, bf16[4,8,96,128]{3,2,1,0:T(8,128)(2,1)S(1)}, u32[]{:S(2)}, u32[]{:S(2)}) collective-permute-start(bf16[4,8,96,128]{3,2,1,0:T(8,128)(2,1)S(1)} %get-tuple-element.36.refs_12_), channel_id=1, source_target_pairs={{0,2},{8,9},{16,18},{24,25},{32,34},{40,41},{48,50},{56,57},{64,66... | collective-permute-start | bytes 2359304 | tf_op jit(solution)/shard_map/ppermute | solution.py:34
  80.9 11.8 %copy-start.4 = (bf16[192,3072]{1,0:T(8,128)(2,1)}, bf16[192,3072]{1,0:T(8,128)(2,1)S(1)}, u32[]{:S(2)}) copy-start(bf16[192,3072]{1,0:T(8,128)(2,1)S(1)} %get-tuple-element.38.refs_6_.refs_0_) | copy-start | bytes 3538948
  80.9 11.8 %copy-start.7 = (f32[192,3072]{1,0:T(8,128)}, f32[192,3072]{1,0:T(8,128)S(1)}, u32[]{:S(2)}) copy-start(f32[192,3072]{1,0:T(8,128)S(1)} %get-tuple-element.37.g_own) | copy-start | bytes 7077892
  93.5 6.4 %copy-start.1 = (bf16[192,6144]{1,0:T(8,128)(2,1)S(1)}, bf16[192,6144]{1,0:T(8,128)(2,1)}, u32[]{:S(2)}) copy-start(bf16[192,6144]{1,0:T(8,128)(2,1)} %tokens.3) | copy-start | bytes 7077892
  93.5 6.4 %collective-permute-start.18 = (bf16[192,3072]{1,0:T(8,128)(2,1)}, bf16[192,3072]{1,0:T(8,128)(2,1)S(1)}, u32[]{:S(2)}, u32[]{:S(2)}) collective-permute-start(bf16[192,3072]{1,0:T(8,128)(2,1)} %gate.3), channel_id=1, source_target_pairs={{0,8},{8,0},{16,24},{24,16},{32,40},{40,32},{48,56},{56,48},{64,72... | collective-permute-start | bytes 3538952 | tf_op jit(solution)/shard_map/ppermute | solution.py:34
  94.8 11.9 %collective-permute-start.19 = (bf16[8,2,96,128]{3,2,1,0:T(8,128)(2,1)}, bf16[8,2,96,128]{3,2,1,0:T(8,128)(2,1)S(1)}, u32[]{:S(2)}, u32[]{:S(2)}) collective-permute-start(bf16[8,2,96,128]{3,2,1,0:T(8,128)(2,1)} %get-tuple-element.46), channel_id=1, source_target_pairs={{0,1},{8,10},{16,17},{24,26},{32,33},{40,42},{48,49},{56,58},{64,6... | collective-permute-start | bytes 1179656 | tf_op jit(solution)/shard_map/ppermute | solution.py:34
  96.2 12.5 %collective-permute-start.20 = (bf16[8,2,96,128]{3,2,1,0:T(8,128)(2,1)}, bf16[8,2,96,128]{3,2,1,0:T(8,128)(2,1)S(1)}, u32[]{:S(2)}, u32[]{:S(2)}) collective-permute-start(bf16[8,2,96,128]{3,2,1,0:T(8,128)(2,1)} %get-tuple-element.47), channel_id=1, source_target_pairs={{0,128},{8,12},{16,144},{24,28},{32,160},{40,44},{48,176},{56,60},... | collective-permute-start | bytes 1179656 | tf_op jit(solution)/shard_map/ppermute | solution.py:34
  98.9 9.9 %collective-permute-start.21 = (bf16[8,2,96,128]{3,2,1,0:T(8,128)(2,1)}, bf16[8,2,96,128]{3,2,1,0:T(8,128)(2,1)S(1)}, u32[]{:S(2)}, u32[]{:S(2)}) collective-permute-start(bf16[8,2,96,128]{3,2,1,0:T(8,128)(2,1)} %copy-done.14), channel_id=1, source_target_pairs={{0,129},{8,14},{16,145},{24,30},{32,161},{40,46},{48,177},{56,62},... | collective-permute-start | bytes 1179656 | tf_op jit(solution)/shard_map/ppermute | solution.py:34
  101.6 7.2 %copy-start.12 = (bf16[8,2,96,128]{3,2,1,0:T(8,128)(2,1)S(1)}, bf16[8,2,96,128]{3,2,1,0:T(8,128)(2,1)}, u32[]{:S(2)}) copy-start(bf16[8,2,96,128]{3,2,1,0:T(8,128)(2,1)} %copy-done.11) | copy-start | bytes 1179652
  154.3 5.1 %collective-permute-start.22 = (bf16[2,8,2,96,128]{4,3,2,1,0:T(8,128)(2,1)S(1)}, bf16[2,8,2,96,128]{4,3,2,1,0:T(8,128)(2,1)S(1)}, u32[]{:S(2)}, u32[]{:S(2)}) collective-permute-start(bf16[2,8,2,96,128]{4,3,2,1,0:T(8,128)(2,1)S(1)} %bitcast.24), channel_id=1, source_target_pairs={{0,8},{8,0},{16,24},{24,16},{32,40},{40,32},{48,56},{56,48},{64,72... | collective-permute-start | bytes 2359304 | tf_op jit(solution)/shard_map/ppermute | solution.py:34
  (8 other events, 10.3 us)

commit v6 on v5

--- a/solution.py
+++ b/solution.py
@@ -98,6 +98,33 @@
     return jax.ShapeDtypeStruct(dims, dtype)
 
 
+def half_kernel(weights, whole, *rest):
+    parts, sems = rest[:2], rest[2]
+    width = whole.shape[1]
+    rows = pl.ds(pl.multiple_of(lax.axis_index("dp") % 2 * width, width), width)
+    copies = [pltpu.make_async_copy(weights.at[:, rows], whole, sems.at[0])]
+    for k, part in enumerate(parts):
+        copies.append(pltpu.make_async_copy(weights.at[pl.ds(2 * k, 2), rows], part, sems.at[1 + k]))
+    for copy in copies:
+        copy.start()
+    for copy in copies:
+        copy.wait()
+
+
+def half_of(weights):
+    _, rows, cols = weights.shape
+    return pl.pallas_call(
+        half_kernel,
+        out_shape=[shape((count, rows // 2, cols)) for count in (4, 2, 2)],
+        in_specs=[pl.BlockSpec(memory_space=pl.ANY)],
+        out_specs=[pl.BlockSpec(memory_space=pl.ANY)] * 3,
+        scratch_shapes=[pltpu.SemaphoreType.DMA((3,))],
+        compiler_params=pltpu.CompilerParams(vmem_limit_bytes=56 * 1024 * 1024),
+        cost_estimate=pl.CostEstimate(flops=1, bytes_accessed=1, transcendentals=0),
+        name="half",
+    )(weights)
+
+
 def prep_kernel(width, info, tokens, cot, own, send, normed):
     rows, model = tokens.shape
     step = 16
@@ -398,9 +425,9 @@
         name="prep",
     )
 
-    w = {(0, 0): lax.dynamic_slice(weights, (0, core * width, 0), (4, width, cols))}
+    whole, *parts = half_of(weights)
+    w = {(0, 0): whole}
     w[0, 1] = shift(w[0, 0], dx=1)
-    parts = [lax.dynamic_slice(weights, (m, core * width, 0), (2, width, cols)) for m in (0, 2)]
     w[3, 0] = [shift(part, dy=-1) for part in parts]
     w[1, 0] = shift(w[0, 0], dy=1)
     w[2, 0] = shift(w[1, 0], dy=1)

time: 162 us -> 207 us (1.28)
  Pallas kernels: 33.9 us -> 82.3 us
  local copies, waits for them, and re-layouts: 12.4 us -> 7.57 us
    pallas_call x0 -> x1, Pallas kernels: none -> 48.8 us  [half_of(): pl.pallas_call(half_kernel, out_shape=[shape((count, rows // 2, cols)) fo...]
    dynamic_slice x2 -> x0, local copies, waits for them, and re-layouts: 4.14 us -> none  [the longest x1 2.07 us: per_device(): lax.dynamic_slice(weights, (0, core * width, 0), (4, width, cols))]
    unnamed x34 -> x36, local copies, waits for them, and re-layouts: 8.19 us -> 7.48 us
  transfers between devices with their start and end apart: 23 -> 23, of which waited for: 14 -> 14; matrix products, arithmetic and copies ran while one was open for 2% -> 1% of each run, Pallas kernels for 15% -> 11%
where the time goes in v6:
time: 207 us
  Pallas kernels  82.3 us (40%)
  blocking collectives  44.8 us (22%)
  waiting for transfers between devices  36.4 us (18%)
  starting transfers between devices  34 us (16%)
  local copies, waits for them, and re-layouts  7.57 us (4%)
    pallas_call x1, Pallas kernels, half_of(): pl.pallas_call(half_kernel, out_shape=[shape((count, rows // 2, cols)) fo...  48.8 us
    all_to_all x2, blocking collectives, exchange(): lax.all_to_all(values, 'dp', split_axis=0, concat_axis=0, axis_index_grou...  44.8 us
    ppermute x23, waiting for transfers between devices, permute(): return lax.ppermute(values, ('dp', 'fsdp'), pairs)  36.4 us
    ppermute x23, starting transfers between devices, permute(): return lax.ppermute(values, ('dp', 'fsdp'), pairs)  34 us
    pallas_call x14, Pallas kernels, call(): pl.pallas_call(kernel, grid=grid or (1,), out_shape=out_shapes, in_specs=...  30 us
    unnamed x36, local copies, waits for them, and re-layouts  7.48 us
  transfers between devices with their start and end apart: 23, of which 14 were waited for; matrix products, arithmetic and copies ran while one was open for 1% of the time, Pallas kernels for 11%

profile of v6, /device:TPU:1, one launch (start us, length us, event | category | flops | bytes accessed | tf_op | source)
XLA Modules:
  0.0 207.0 jit_solution(12722144532373251521)
XLA Ops:
  0.6 48.8 %half.1 = (bf16[4,384,256]{2,1,0:T(8,128)(2,1)}, bf16[2,384,256]{2,1,0:T(8,128)(2,1)}, bf16[2,384,256]{2,1,0:T(8,128)(2,1)}) custom-call(bf16[4,768,256]{2,1,0:T(8,128)(2,1)} %weights.1), custom_call_target="tpu_custom_call" | custom-call | flops 1 | bytes 1 | tf_op jit(solution)/shard_map/half/pallas_call | solution.py:116
  49.4 3.4 %collective-permute-start.1 = (bf16[4,384,256]{2,1,0:T(8,128)(2,1)}, bf16[4,384,256]{2,1,0:T(8,128)(2,1)S(1)}, u32[]{:S(2)}, u32[]{:S(2)}) collective-permute-start(bf16[4,384,256]{2,1,0:T(8,128)(2,1)} %get-tuple-element.31.refs_2_), channel_id=1, source_target_pairs={{0,1},{8,137},{16,17},{24,153},{32,33},{40,169},{48,49},{56,185},{... | collective-permute-start | bytes 2359304 | tf_op jit(solution)/shard_map/ppermute | solution.py:34
  52.8 2.7 %collective-permute-start = (bf16[4,384,256]{2,1,0:T(8,128)(2,1)}, bf16[4,384,256]{2,1,0:T(8,128)(2,1)}, u32[]{:S(2)}, u32[]{:S(2)}) collective-permute-start(bf16[4,384,256]{2,1,0:T(8,128)(2,1)} %get-tuple-element.31.refs_2_), channel_id=1, source_target_pairs={{0,2},{8,14},{16,18},{24,30},{32,34},{40,46},{48,50},{56,62},{64,6... | collective-permute-start | bytes 2359304 | tf_op jit(solution)/shard_map/ppermute | solution.py:34
  57.3 1.7 copy-done.11
  59.0 3.0 %prep.1 = (bf16[2,192,3072]{2,1,0:T(8,128)(2,1)S(1)}, bf16[2,192,3072]{2,1,0:T(8,128)(2,1)S(1)}) custom-call(s32[20]{0:T(128)S(1)} %stack.87.info, bf16[192,6144]{1,0:T(8,128)(2,1)S(1)} %copy-done, bf16[192,6144]{1,0:T(8,128)(2,1)S(1)} %copy-done.11), custom_call_target="tpu_custom_call" | custom-call | flops 9437184 | bytes 9437184 | tf_op jit(solution)/shard_map/prep/pallas_call | solution.py:72
  63.4 4.8 %collective-permute-done.2.refs_3_.refs_6_ = bf16[2,384,256]{2,1,0:T(8,128)(2,1)S(1)} collective-permute-done((bf16[2,384,256]{2,1,0:T(8,128)(2,1)}, bf16[2,384,256]{2,1,0:T(8,128)(2,1)S(1)}, u32[]{:S(2)}, u32[]{:S(2)}) %collective-permute-start.2) | collective-permute-done | bytes 393248 | tf_op jit(solution)/shard_map/ppermute | solution.py:34
  70.7 2.8 %collective-permute-start.7 = (bf16[4,384,256]{2,1,0:T(8,128)(2,1)}, bf16[4,384,256]{2,1,0:T(8,128)(2,1)S(1)}, u32[]{:S(2)}, u32[]{:S(2)}) collective-permute-start(bf16[4,384,256]{2,1,0:T(8,128)(2,1)} %collective-permute-done.refs_1_.refs_4_), channel_id=1, source_target_pairs={{0,1},{8,137},{16,17},{24,153},{32,33},{40,169},{48,49},{56,185},{... | collective-permute-start | bytes 2359304 | tf_op jit(solution)/shard_map/ppermute | solution.py:34
  74.9 7.8 %collective-permute-done.7.refs_5_ = bf16[4,384,256]{2,1,0:T(8,128)(2,1)S(1)} collective-permute-done((bf16[4,384,256]{2,1,0:T(8,128)(2,1)}, bf16[4,384,256]{2,1,0:T(8,128)(2,1)S(1)}, u32[]{:S(2)}, u32[]{:S(2)}) %collective-permute-start.7) | collective-permute-done | bytes 786464 | tf_op jit(solution)/shard_map/ppermute | solution.py:34
  83.7 2.4 %collective-permute-start.4 = (bf16[2,384,256]{2,1,0:T(8,128)(2,1)}, bf16[2,384,256]{2,1,0:T(8,128)(2,1)S(1)}, u32[]{:S(2)}, u32[]{:S(2)}) collective-permute-start(bf16[2,384,256]{2,1,0:T(8,128)(2,1)} %copy-done.5), channel_id=1, source_target_pairs={{0,1},{8,137},{16,17},{24,153},{32,33},{40,169},{48,49},{56,185},{... | collective-permute-start | bytes 1179656 | tf_op jit(solution)/shard_map/ppermute | solution.py:34
  87.3 2.5 %flip.1.refs_9_.refs_0_.refs_1_ = bf16[2,4,2,4,96,384]{5,4,3,2,1,0:T(8,128)(2,1)S(1)} custom-call(s32[20]{0:T(128)S(1)} %stack.87.info, bf16[2,192,3072]{2,1,0:T(8,128)(2,1)S(1)} %get-tuple-element.29.own.refs_0_, bf16[2,192,3072]{2,1,0:T(8,128)(2,1)S(1)} %collective-permute-done.3.peer.refs_1_), custom_call_target="tpu_custom_call" | custom-call | bytes 9437184 | tf_op jit(solution)/shard_map/flip/pallas_call | solution.py:72
  89.8 4.2 %linear.2 = (f32[192,1024]{1,0:T(8,128)S(1)}, f32[192,1024]{1,0:T(8,128)S(1)}) custom-call(bf16[2,192,3072]{2,1,0:T(8,128)(2,1)S(1)} %get-tuple-element.29.own.refs_0_, bf16[2,192,3072]{2,1,0:T(8,128)(2,1)S(1)} %collective-permute-done.3.peer.refs_1_, bf16[4,384,256]{2,1,0:T(8,128)(2,1)S(1)} %copy-done.7, bf16[4,384,256]{2,1,0:T(8,128)(2,1)S(1)} %copy-done.3, ...), custom_call_target="tpu_custom_call" | custom-call | flops 1811939328 | bytes 8257536 | tf_op jit(solution)/shard_map/linear/pallas_call | solution.py:72
  96.4 1.8 linear.3
  98.2 1.9 collective-permute-start.10
  100.0 1.9 collective-permute-done.10.theirs
  101.9 3.2 %attend.1.refs_2_.refs_1_.refs_0_ = bf16[192,1024]{1,0:T(8,128)(2,1)S(1)} custom-call(s32[1,3]{1,0:T(1,128)S(1)} %copy-done.14, f32[192,1024]{1,0:T(8,128)S(1)} %get-tuple-element.36.mine, f32[192,1024]{1,0:T(8,128)S(1)} %collective-permute-done.10.theirs, f32[192,128]{1,0:T(8,128)S(1)} %get-tuple-element.67.refs_10_.cos_t, ...), custom_call_target="tpu_custom_call" | custom-call | flops 188743680 | bytes 1966080 | tf_op jit(solution)/shard_map/attend/pallas_call | solution.py:72
  108.9 1.8 collective-permute-start.13
  113.2 1.8 terms.3
  115.0 5.3 %collective-permute-done.12.far_0 = bf16[4,8,96,128]{3,2,1,0:T(8,128)(2,1)S(1)} collective-permute-done((bf16[4,8,96,128]{3,2,1,0:T(8,128)(2,1)S(1)}, bf16[4,8,96,128]{3,2,1,0:T(8,128)(2,1)S(1)}, u32[]{:S(2)}, u32[]{:S(2)}) %collective-permute-start.12) | collective-permute-done | bytes 786464 | tf_op jit(solution)/shard_map/ppermute | solution.py:34
  120.7 2.8 %collective-permute-start.17 = (bf16[4,8,96,128]{3,2,1,0:T(8,128)(2,1)S(1)}, bf16[4,8,96,128]{3,2,1,0:T(8,128)(2,1)S(1)}, u32[]{:S(2)}, u32[]{:S(2)}) collective-permute-start(bf16[4,8,96,128]{3,2,1,0:T(8,128)(2,1)S(1)} %get-tuple-element.49), channel_id=1, source_target_pairs={{0,6},{8,137},{16,22},{24,153},{32,38},{40,169},{48,54},{56,185},{... | collective-permute-start | bytes 2359304 | tf_op jit(solution)/shard_map/ppermute | solution.py:34
  123.5 3.7 %normed_grad.1 = (f32[192,3072]{1,0:T(8,128)S(1)}, bf16[192,3072]{1,0:T(8,128)(2,1)S(1)}) custom-call(bf16[192,1024]{1,0:T(8,128)(2,1)S(1)} %attend.1.refs_2_.refs_1_.refs_0_, bf16[192,1024]{1,0:T(8,128)(2,1)S(1)} %collective-permute-done.11.refs_3_.refs_2_.refs_1_, bf16[4,384,256]{2,1,0:T(8,128)(2,1)S(1)} %copy-done.7, bf16[4,384,256]{2,1,0:T(8,128)(2,1)S(1)} %copy-done.3, ...), custom_call_target="tpu_custom_call" | custom-call | flops 1811939328 | bytes 11010048 | tf_op jit(solution)/shard_map/normed_grad/pallas_call | solution.py:72
  128.7 8.1 %collective-permute-done.17.refs_5_ = bf16[4,8,96,128]{3,2,1,0:T(8,128)(2,1)S(1)} collective-permute-done((bf16[4,8,96,128]{3,2,1,0:T(8,128)(2,1)S(1)}, bf16[4,8,96,128]{3,2,1,0:T(8,128)(2,1)S(1)}, u32[]{:S(2)}, u32[]{:S(2)}) %collective-permute-start.17) | collective-permute-done | bytes 786464 | tf_op jit(solution)/shard_map/ppermute | solution.py:34
  137.2 2.1 sides.1
  141.3 1.7 collective-permute-start.19
  143.1 2.3 %collective-permute-start.20 = (bf16[8,2,96,128]{3,2,1,0:T(8,128)(2,1)}, bf16[8,2,96,128]{3,2,1,0:T(8,128)(2,1)S(1)}, u32[]{:S(2)}, u32[]{:S(2)}) collective-permute-start(bf16[8,2,96,128]{3,2,1,0:T(8,128)(2,1)} %get-tuple-element.53), channel_id=1, source_target_pairs={{0,128},{8,12},{16,144},{24,28},{32,160},{40,44},{48,176},{56,60},... | collective-permute-start | bytes 1179656 | tf_op jit(solution)/shard_map/ppermute | solution.py:34
  146.2 1.7 copy-done.9
  147.8 5.1 %token_grad.1 = (bf16[192,6144]{1,0:T(8,128)(2,1)}, f32[8,128]{1,0:T(8,128)S(1)}) custom-call(s32[20]{0:T(128)S(1)} %stack.87.info, bf16[192,6144]{1,0:T(8,128)(2,1)S(1)} %copy-done.1, f32[192,3072]{1,0:T(8,128)S(1)} %copy-done.9, bf16[192,3072]{1,0:T(8,128)(2,1)S(1)} %collective-permute-done.18.g_peer), custom_call_target="tpu_custom_call" | custom-call | flops 18874368 | bytes 9437184 | tf_op jit(solution)/shard_map/token_grad/pallas_call | solution.py:72
  153.0 2.0 collective-permute-done.20.refs_2_
  155.2 20.5 %all_to_all.10.got = bf16[8,2,96,128]{3,2,1,0:T(8,128)(2,1)S(1)} all-to-all(bf16[8,2,96,128]{3,2,1,0:T(8,128)(2,1)S(1)} %seconds.1), channel_id=1, replica_groups={{0,16,32,48,64,80,96,112},{8,24,40,56,72,88,104,120},{128,144,160,176,1..., dimensions={0} | all-to-all | bytes 786432 | tf_op jit(solution)/shard_map/all_to_all | solution.py:393
  175.8 24.3 %all_to_all.11 = bf16[16,2,96,128]{3,2,1,0:T(8,128)(2,1)S(1)} all-to-all(bf16[16,2,96,128]{3,2,1,0:T(8,128)(2,1)S(1)} %last.1), channel_id=1, replica_groups={{0,16,32,48,64,80,96,112,128,144,160,176,192,208,224,240},{8,24,40,56,7..., dimensions={0} | all-to-all | bytes 1572864 | tf_op jit(solution)/shard_map/all_to_all | solution.py:393
  200.2 3.2 %collective-permute-start.22 = (bf16[2,8,2,96,128]{4,3,2,1,0:T(8,128)(2,1)S(1)}, bf16[2,8,2,96,128]{4,3,2,1,0:T(8,128)(2,1)S(1)}, u32[]{:S(2)}, u32[]{:S(2)}) collective-permute-start(bf16[2,8,2,96,128]{4,3,2,1,0:T(8,128)(2,1)S(1)} %bitcast.24), channel_id=1, source_target_pairs={{0,8},{8,0},{16,24},{24,16},{32,40},{40,32},{48,56},{56,48},{64,72... | collective-permute-start | bytes 2359304 | tf_op jit(solution)/shard_map/ppermute | solution.py:34
  203.3 1.7 place.2.refs_0_
  205.2 1.7 place.3
  (75 shorter events, 23.4 us)
Async XLA Ops:
  49.4 18.9 %collective-permute-start.1 = (bf16[4,384,256]{2,1,0:T(8,128)(2,1)}, bf16[4,384,256]{2,1,0:T(8,128)(2,1)S(1)}, u32[]{:S(2)}, u32[]{:S(2)}) collective-permute-start(bf16[4,384,256]{2,1,0:T(8,128)(2,1)} %get-tuple-element.31.refs_2_), channel_id=1, source_target_pairs={{0,1},{8,137},{16,17},{24,153},{32,33},{40,169},{48,49},{56,185},{... | collective-permute-start | bytes 2359304 | tf_op jit(solution)/shard_map/ppermute | solution.py:34
  52.8 16.2 %collective-permute-start = (bf16[4,384,256]{2,1,0:T(8,128)(2,1)}, bf16[4,384,256]{2,1,0:T(8,128)(2,1)}, u32[]{:S(2)}, u32[]{:S(2)}) collective-permute-start(bf16[4,384,256]{2,1,0:T(8,128)(2,1)} %get-tuple-element.31.refs_2_), channel_id=1, source_target_pairs={{0,2},{8,14},{16,18},{24,30},{32,34},{40,46},{48,50},{56,62},{64,6... | collective-permute-start | bytes 2359304 | tf_op jit(solution)/shard_map/ppermute | solution.py:34
  55.5 12.7 %collective-permute-start.2 = (bf16[2,384,256]{2,1,0:T(8,128)(2,1)}, bf16[2,384,256]{2,1,0:T(8,128)(2,1)S(1)}, u32[]{:S(2)}, u32[]{:S(2)}) collective-permute-start(bf16[2,384,256]{2,1,0:T(8,128)(2,1)} %get-tuple-element.32), channel_id=1, source_target_pairs={{0,6},{8,10},{16,22},{24,26},{32,38},{40,42},{48,54},{56,58},{64,7... | collective-permute-start | bytes 1179656 | tf_op jit(solution)/shard_map/ppermute | solution.py:34
  69.3 14.4 %copy-start.16 = (s32[2,192]{1,0:T(2,128)S(1)}, s32[2,192]{1,0:T(2,128)}, u32[]{:S(2)}) copy-start(s32[2,192]{1,0:T(2,128)} %param.10) | copy-start | bytes 4612
  69.3 16.9 %copy-start.17 = (f32[32]{0:T(128)S(1)}, f32[32]{0:T(128)}, u32[]{:S(2)}) copy-start(f32[32]{0:T(128)} %constant.148) | copy-start | bytes 388
  69.3 17.9 %collective-permute-start.3 = (bf16[2,192,3072]{2,1,0:T(8,128)(2,1)}, bf16[2,192,3072]{2,1,0:T(8,128)(2,1)S(1)}, u32[]{:S(2)}, u32[]{:S(2)}) collective-permute-start(bf16[2,192,3072]{2,1,0:T(8,128)(2,1)} %gate.2), channel_id=1, source_target_pairs={{0,8},{8,0},{16,24},{24,16},{32,40},{40,32},{48,56},{56,48},{64,72... | collective-permute-start | bytes 7077896 | tf_op jit(solution)/shard_map/ppermute | solution.py:34
  70.7 12.1 %collective-permute-start.7 = (bf16[4,384,256]{2,1,0:T(8,128)(2,1)}, bf16[4,384,256]{2,1,0:T(8,128)(2,1)S(1)}, u32[]{:S(2)}, u32[]{:S(2)}) collective-permute-start(bf16[4,384,256]{2,1,0:T(8,128)(2,1)} %collective-permute-done.refs_1_.refs_4_), channel_id=1, source_target_pairs={{0,1},{8,137},{16,17},{24,153},{32,33},{40,169},{48,49},{56,185},{... | collective-permute-start | bytes 2359304 | tf_op jit(solution)/shard_map/ppermute | solution.py:34
  73.5 16.3 %collective-permute-start.9 = (bf16[4,384,256]{2,1,0:T(8,128)(2,1)}, bf16[4,384,256]{2,1,0:T(8,128)(2,1)S(1)}, u32[]{:S(2)}, u32[]{:S(2)}) collective-permute-start(bf16[4,384,256]{2,1,0:T(8,128)(2,1)} %collective-permute-done.refs_1_.refs_4_), channel_id=1, source_target_pairs={{0,2},{8,14},{16,18},{24,30},{32,34},{40,46},{48,50},{56,62},{64,6... | collective-permute-start | bytes 2359304 | tf_op jit(solution)/shard_map/ppermute | solution.py:34
  73.5 12.6 %collective-permute-start.5 = (bf16[2,384,256]{2,1,0:T(8,128)(2,1)}, bf16[2,384,256]{2,1,0:T(8,128)(2,1)S(1)}, u32[]{:S(2)}, u32[]{:S(2)}) collective-permute-start(bf16[2,384,256]{2,1,0:T(8,128)(2,1)} %get-tuple-element.33), channel_id=1, source_target_pairs={{0,6},{8,10},{16,22},{24,26},{32,38},{40,42},{48,54},{56,58},{64,7... | collective-permute-start | bytes 1179656 | tf_op jit(solution)/shard_map/ppermute | solution.py:34
  82.7 13.6 %collective-permute-start.8 = (bf16[4,384,256]{2,1,0:T(8,128)(2,1)S(1)}, bf16[4,384,256]{2,1,0:T(8,128)(2,1)S(1)}, u32[]{:S(2)}, u32[]{:S(2)}) collective-permute-start(bf16[4,384,256]{2,1,0:T(8,128)(2,1)S(1)} %collective-permute-done.7.refs_5_), channel_id=1, source_target_pairs={{0,2},{8,14},{16,18},{24,30},{32,34},{40,46},{48,50},{56,62},{64,6... | collective-permute-start | bytes 2359304 | tf_op jit(solution)/shard_map/ppermute | solution.py:34
  83.7 10.3 %collective-permute-start.4 = (bf16[2,384,256]{2,1,0:T(8,128)(2,1)}, bf16[2,384,256]{2,1,0:T(8,128)(2,1)S(1)}, u32[]{:S(2)}, u32[]{:S(2)}) collective-permute-start(bf16[2,384,256]{2,1,0:T(8,128)(2,1)} %copy-done.5), channel_id=1, source_target_pairs={{0,1},{8,137},{16,17},{24,153},{32,33},{40,169},{48,49},{56,185},{... | collective-permute-start | bytes 1179656 | tf_op jit(solution)/shard_map/ppermute | solution.py:34
  86.1 9.1 %collective-permute-start.6 = (bf16[2,384,256]{2,1,0:T(8,128)(2,1)S(1)}, bf16[2,384,256]{2,1,0:T(8,128)(2,1)S(1)}, u32[]{:S(2)}, u32[]{:S(2)}) collective-permute-start(bf16[2,384,256]{2,1,0:T(8,128)(2,1)S(1)} %collective-permute-done.5.refs_7_), channel_id=1, source_target_pairs={{0,1},{8,137},{16,17},{24,153},{32,33},{40,169},{48,49},{56,185},{... | collective-permute-start | bytes 1179656 | tf_op jit(solution)/shard_map/ppermute | solution.py:34
  87.2 2.5 %copy-start.3 = (bf16[4,384,256]{2,1,0:T(8,128)(2,1)S(1)}, bf16[4,384,256]{2,1,0:T(8,128)(2,1)}, u32[]{:S(2)}) copy-start(bf16[4,384,256]{2,1,0:T(8,128)(2,1)} %copy-done.2) | copy-start | bytes 2359300
  87.2 2.5 %copy-start.6 = (bf16[2,384,256]{2,1,0:T(8,128)(2,1)S(1)}, bf16[2,384,256]{2,1,0:T(8,128)(2,1)}, u32[]{:S(2)}) copy-start(bf16[2,384,256]{2,1,0:T(8,128)(2,1)} %copy-done.5) | copy-start | bytes 1179652
  96.4 5.6 %copy-start.14 = (s32[1,3]{1,0:T(1,128)S(1)}, s32[1,3]{1,0:T(1,128)}, u32[]{:S(2)}) copy-start(s32[1,3]{1,0:T(1,128)} %lengths.1) | copy-start | bytes 40
  98.2 3.8 %collective-permute-start.10 = (f32[192,1024]{1,0:T(8,128)S(1)}, f32[192,1024]{1,0:T(8,128)S(1)}, u32[]{:S(2)}, u32[]{:S(2)}) collective-permute-start(f32[192,1024]{1,0:T(8,128)S(1)} %get-tuple-element.37), channel_id=1, source_target_pairs={{0,8},{8,0},{16,24},{24,16},{32,40},{40,32},{48,56},{56,48},{64,72... | collective-permute-start | bytes 2359304 | tf_op jit(solution)/shard_map/ppermute | solution.py:34
  105.1 1.8 collective-permute-start.11
  107.9 12.4 %collective-permute-start.12 = (bf16[4,8,96,128]{3,2,1,0:T(8,128)(2,1)S(1)}, bf16[4,8,96,128]{3,2,1,0:T(8,128)(2,1)S(1)}, u32[]{:S(2)}, u32[]{:S(2)}) collective-permute-start(bf16[4,8,96,128]{3,2,1,0:T(8,128)(2,1)S(1)} %get-tuple-element.39), channel_id=1, source_target_pairs={{0,2},{8,9},{16,18},{24,25},{32,34},{40,41},{48,50},{56,57},{64,66... | collective-permute-start | bytes 2359304 | tf_op jit(solution)/shard_map/ppermute | solution.py:34
  108.9 11.4 %collective-permute-start.13 = (bf16[4,8,96,128]{3,2,1,0:T(8,128)(2,1)S(1)}, bf16[4,8,96,128]{3,2,1,0:T(8,128)(2,1)S(1)}, u32[]{:S(2)}, u32[]{:S(2)}) collective-permute-start(bf16[4,8,96,128]{3,2,1,0:T(8,128)(2,1)S(1)} %get-tuple-element.41), channel_id=1, source_target_pairs={{0,6},{8,137},{16,22},{24,153},{32,38},{40,169},{48,54},{56,185},{... | collective-permute-start | bytes 2359304 | tf_op jit(solution)/shard_map/ppermute | solution.py:34
  111.6 16.8 %collective-permute-start.14 = (bf16[4,8,96,128]{3,2,1,0:T(8,128)(2,1)S(1)}, bf16[4,8,96,128]{3,2,1,0:T(8,128)(2,1)S(1)}, u32[]{:S(2)}, u32[]{:S(2)}) collective-permute-start(bf16[4,8,96,128]{3,2,1,0:T(8,128)(2,1)S(1)} %get-tuple-element.46), channel_id=1, source_target_pairs={{0,6},{8,137},{16,22},{24,153},{32,38},{40,169},{48,54},{56,185},{... | collective-permute-start | bytes 2359304 | tf_op jit(solution)/shard_map/ppermute | solution.py:34
  111.7 17.0 %collective-permute-start.16 = (bf16[4,8,96,128]{3,2,1,0:T(8,128)(2,1)S(1)}, bf16[4,8,96,128]{3,2,1,0:T(8,128)(2,1)S(1)}, u32[]{:S(2)}, u32[]{:S(2)}) collective-permute-start(bf16[4,8,96,128]{3,2,1,0:T(8,128)(2,1)S(1)} %get-tuple-element.48), channel_id=1, source_target_pairs={{0,2},{8,9},{16,18},{24,25},{32,34},{40,41},{48,50},{56,57},{64,66... | collective-permute-start | bytes 2359304 | tf_op jit(solution)/shard_map/ppermute | solution.py:34
  120.7 16.1 %collective-permute-start.17 = (bf16[4,8,96,128]{3,2,1,0:T(8,128)(2,1)S(1)}, bf16[4,8,96,128]{3,2,1,0:T(8,128)(2,1)S(1)}, u32[]{:S(2)}, u32[]{:S(2)}) collective-permute-start(bf16[4,8,96,128]{3,2,1,0:T(8,128)(2,1)S(1)} %get-tuple-element.49), channel_id=1, source_target_pairs={{0,6},{8,137},{16,22},{24,153},{32,38},{40,169},{48,54},{56,185},{... | collective-permute-start | bytes 2359304 | tf_op jit(solution)/shard_map/ppermute | solution.py:34
  123.5 13.7 %collective-permute-start.15 = (bf16[4,8,96,128]{3,2,1,0:T(8,128)(2,1)S(1)}, bf16[4,8,96,128]{3,2,1,0:T(8,128)(2,1)S(1)}, u32[]{:S(2)}, u32[]{:S(2)}) collective-permute-start(bf16[4,8,96,128]{3,2,1,0:T(8,128)(2,1)S(1)} %get-tuple-element.42.refs_12_), channel_id=1, source_target_pairs={{0,2},{8,9},{16,18},{24,25},{32,34},{40,41},{48,50},{56,57},{64,66... | collective-permute-start | bytes 2359304 | tf_op jit(solution)/shard_map/ppermute | solution.py:34
  127.2 12.1 %copy-start.4 = (bf16[192,3072]{1,0:T(8,128)(2,1)}, bf16[192,3072]{1,0:T(8,128)(2,1)S(1)}, u32[]{:S(2)}) copy-start(bf16[192,3072]{1,0:T(8,128)(2,1)S(1)} %get-tuple-element.44.refs_6_.refs_0_) | copy-start | bytes 3538948
  127.2 12.0 %copy-start.8 = (f32[192,3072]{1,0:T(8,128)}, f32[192,3072]{1,0:T(8,128)S(1)}, u32[]{:S(2)}) copy-start(f32[192,3072]{1,0:T(8,128)S(1)} %get-tuple-element.43.g_own) | copy-start | bytes 7077892
  140.0 6.2 %copy-start.1 = (bf16[192,6144]{1,0:T(8,128)(2,1)S(1)}, bf16[192,6144]{1,0:T(8,128)(2,1)}, u32[]{:S(2)}) copy-start(bf16[192,6144]{1,0:T(8,128)(2,1)} %tokens.3) | copy-start | bytes 7077892
  140.0 6.2 %collective-permute-start.18 = (bf16[192,3072]{1,0:T(8,128)(2,1)}, bf16[192,3072]{1,0:T(8,128)(2,1)S(1)}, u32[]{:S(2)}, u32[]{:S(2)}) collective-permute-start(bf16[192,3072]{1,0:T(8,128)(2,1)} %gate.3), channel_id=1, source_target_pairs={{0,8},{8,0},{16,24},{24,16},{32,40},{40,32},{48,56},{56,48},{64,72... | collective-permute-start | bytes 3538952 | tf_op jit(solution)/shard_map/ppermute | solution.py:34
  141.3 11.7 %collective-permute-start.19 = (bf16[8,2,96,128]{3,2,1,0:T(8,128)(2,1)}, bf16[8,2,96,128]{3,2,1,0:T(8,128)(2,1)S(1)}, u32[]{:S(2)}, u32[]{:S(2)}) collective-permute-start(bf16[8,2,96,128]{3,2,1,0:T(8,128)(2,1)} %get-tuple-element.52), channel_id=1, source_target_pairs={{0,1},{8,10},{16,17},{24,26},{32,33},{40,42},{48,49},{56,58},{64,6... | collective-permute-start | bytes 1179656 | tf_op jit(solution)/shard_map/ppermute | solution.py:34
  143.1 11.9 %collective-permute-start.20 = (bf16[8,2,96,128]{3,2,1,0:T(8,128)(2,1)}, bf16[8,2,96,128]{3,2,1,0:T(8,128)(2,1)S(1)}, u32[]{:S(2)}, u32[]{:S(2)}) collective-permute-start(bf16[8,2,96,128]{3,2,1,0:T(8,128)(2,1)} %get-tuple-element.53), channel_id=1, source_target_pairs={{0,128},{8,12},{16,144},{24,28},{32,160},{40,44},{48,176},{56,60},... | collective-permute-start | bytes 1179656 | tf_op jit(solution)/shard_map/ppermute | solution.py:34
  145.4 9.6 %collective-permute-start.21 = (bf16[8,2,96,128]{3,2,1,0:T(8,128)(2,1)}, bf16[8,2,96,128]{3,2,1,0:T(8,128)(2,1)S(1)}, u32[]{:S(2)}, u32[]{:S(2)}) collective-permute-start(bf16[8,2,96,128]{3,2,1,0:T(8,128)(2,1)} %copy-done.15), channel_id=1, source_target_pairs={{0,129},{8,14},{16,145},{24,30},{32,161},{40,46},{48,177},{56,62},... | collective-permute-start | bytes 1179656 | tf_op jit(solution)/shard_map/ppermute | solution.py:34
  147.8 7.1 %copy-start.13 = (bf16[8,2,96,128]{3,2,1,0:T(8,128)(2,1)S(1)}, bf16[8,2,96,128]{3,2,1,0:T(8,128)(2,1)}, u32[]{:S(2)}) copy-start(bf16[8,2,96,128]{3,2,1,0:T(8,128)(2,1)} %copy-done.12) | copy-start | bytes 1179652
  200.2 5.1 %collective-permute-start.22 = (bf16[2,8,2,96,128]{4,3,2,1,0:T(8,128)(2,1)S(1)}, bf16[2,8,2,96,128]{4,3,2,1,0:T(8,128)(2,1)S(1)}, u32[]{:S(2)}, u32[]{:S(2)}) collective-permute-start(bf16[2,8,2,96,128]{4,3,2,1,0:T(8,128)(2,1)S(1)} %bitcast.24), channel_id=1, source_target_pairs={{0,8},{8,0},{16,24},{24,16},{32,40},{40,32},{48,56},{56,48},{64,72... | collective-permute-start | bytes 2359304 | tf_op jit(solution)/shard_map/ppermute | solution.py:34
  (9 other events, 12.8 us)

commit v7 on v6

--- a/solution.py
+++ b/solution.py
@@ -117,7 +117,7 @@
         half_kernel,
         out_shape=[shape((count, rows // 2, cols)) for count in (4, 2, 2)],
         in_specs=[pl.BlockSpec(memory_space=pl.ANY)],
-        out_specs=[pl.BlockSpec(memory_space=pl.ANY)] * 3,
+        out_specs=[pl.BlockSpec(memory_space=pltpu.VMEM)] * 3,
         scratch_shapes=[pltpu.SemaphoreType.DMA((3,))],
         compiler_params=pltpu.CompilerParams(vmem_limit_bytes=56 * 1024 * 1024),
         cost_estimate=pl.CostEstimate(flops=1, bytes_accessed=1, transcendentals=0),

time: 207 us -> 161 us (0.78)
  Pallas kernels: 82.3 us -> 36 us
    pallas_call x1, Pallas kernels: 48.8 us -> 2.53 us  [half_of(): pl.pallas_call(half_kernel, out_shape=[shape((count, rows // 2, cols)) fo...]
  transfers between devices with their start and end apart: 23 -> 23, of which waited for: 14 -> 14; matrix products, arithmetic and copies ran while one was open for 1% -> 1% of each run, Pallas kernels for 11% -> 15%
where the time goes in v7:
time: 161 us
  blocking collectives  44.8 us (28%)
  waiting for transfers between devices  36.5 us (23%)
  Pallas kernels  36 us (22%)
  starting transfers between devices  33.9 us (21%)
  local copies, waits for them, and re-layouts  7.57 us (5%)
    all_to_all x2, blocking collectives, exchange(): lax.all_to_all(values, 'dp', split_axis=0, concat_axis=0, axis_index_grou...  44.8 us
    ppermute x23, waiting for transfers between devices, permute(): return lax.ppermute(values, ('dp', 'fsdp'), pairs)  36.5 us
    ppermute x23, starting transfers between devices, permute(): return lax.ppermute(values, ('dp', 'fsdp'), pairs)  33.9 us
    pallas_call x14, Pallas kernels, call(): pl.pallas_call(kernel, grid=grid or (1,), out_shape=out_shapes, in_specs=...  30 us
    unnamed x36, local copies, waits for them, and re-layouts  7.48 us
    pallas_call x2, Pallas kernels, place(): pl.pallas_call(place_kernel, grid_spec=pltpu.PrefetchScalarGridSpec(num_s...  3.47 us
  transfers between devices with their start and end apart: 23, of which 14 were waited for; matrix products, arithmetic and copies ran while one was open for 1% of the time, Pallas kernels for 15%

profile of v7, /device:TPU:1, one launch (start us, length us, event | category | flops | bytes accessed | tf_op | source)
XLA Modules:
  0.0 160.7 jit_solution(7990754937947702635)
XLA Ops:
  0.6 2.5 %half.1 = (bf16[4,384,256]{2,1,0:T(8,128)(2,1)}, bf16[2,384,256]{2,1,0:T(8,128)(2,1)}, bf16[2,384,256]{2,1,0:T(8,128)(2,1)}) custom-call(bf16[4,768,256]{2,1,0:T(8,128)(2,1)} %weights.1), custom_call_target="tpu_custom_call" | custom-call | flops 1 | bytes 1 | tf_op jit(solution)/shard_map/half/pallas_call | solution.py:116
  3.2 3.4 %collective-permute-start.1 = (bf16[4,384,256]{2,1,0:T(8,128)(2,1)}, bf16[4,384,256]{2,1,0:T(8,128)(2,1)S(1)}, u32[]{:S(2)}, u32[]{:S(2)}) collective-permute-start(bf16[4,384,256]{2,1,0:T(8,128)(2,1)} %get-tuple-element.31.refs_2_), channel_id=1, source_target_pairs={{0,1},{8,137},{16,17},{24,153},{32,33},{40,169},{48,49},{56,185},{... | collective-permute-start | bytes 2359304 | tf_op jit(solution)/shard_map/ppermute | solution.py:34
  6.5 2.7 %collective-permute-start = (bf16[4,384,256]{2,1,0:T(8,128)(2,1)}, bf16[4,384,256]{2,1,0:T(8,128)(2,1)}, u32[]{:S(2)}, u32[]{:S(2)}) collective-permute-start(bf16[4,384,256]{2,1,0:T(8,128)(2,1)} %get-tuple-element.31.refs_2_), channel_id=1, source_target_pairs={{0,2},{8,14},{16,18},{24,30},{32,34},{40,46},{48,50},{56,62},{64,6... | collective-permute-start | bytes 2359304 | tf_op jit(solution)/shard_map/ppermute | solution.py:34
  11.1 1.7 %copy-done.11 = bf16[192,6144]{1,0:T(8,128)(2,1)S(1)} copy-done((bf16[192,6144]{1,0:T(8,128)(2,1)S(1)}, bf16[192,6144]{1,0:T(8,128)(2,1)}, u32[]{:S(2)}) %copy-start.11) | copy-done | bytes 2359320
  12.7 3.0 %prep.1 = (bf16[2,192,3072]{2,1,0:T(8,128)(2,1)S(1)}, bf16[2,192,3072]{2,1,0:T(8,128)(2,1)S(1)}) custom-call(s32[20]{0:T(128)S(1)} %stack.87.info, bf16[192,6144]{1,0:T(8,128)(2,1)S(1)} %copy-done, bf16[192,6144]{1,0:T(8,128)(2,1)S(1)} %copy-done.11), custom_call_target="tpu_custom_call" | custom-call | flops 9437184 | bytes 9437184 | tf_op jit(solution)/shard_map/prep/pallas_call | solution.py:72
  17.2 4.8 %collective-permute-done.2.refs_3_.refs_6_ = bf16[2,384,256]{2,1,0:T(8,128)(2,1)S(1)} collective-permute-done((bf16[2,384,256]{2,1,0:T(8,128)(2,1)}, bf16[2,384,256]{2,1,0:T(8,128)(2,1)S(1)}, u32[]{:S(2)}, u32[]{:S(2)}) %collective-permute-start.2) | collective-permute-done | bytes 393248 | tf_op jit(solution)/shard_map/ppermute | solution.py:34
  24.4 2.8 %collective-permute-start.7 = (bf16[4,384,256]{2,1,0:T(8,128)(2,1)}, bf16[4,384,256]{2,1,0:T(8,128)(2,1)S(1)}, u32[]{:S(2)}, u32[]{:S(2)}) collective-permute-start(bf16[4,384,256]{2,1,0:T(8,128)(2,1)} %collective-permute-done.refs_1_.refs_4_), channel_id=1, source_target_pairs={{0,1},{8,137},{16,17},{24,153},{32,33},{40,169},{48,49},{56,185},{... | collective-permute-start | bytes 2359304 | tf_op jit(solution)/shard_map/ppermute | solution.py:34
  28.7 7.8 %collective-permute-done.7.refs_5_ = bf16[4,384,256]{2,1,0:T(8,128)(2,1)S(1)} collective-permute-done((bf16[4,384,256]{2,1,0:T(8,128)(2,1)}, bf16[4,384,256]{2,1,0:T(8,128)(2,1)S(1)}, u32[]{:S(2)}, u32[]{:S(2)}) %collective-permute-start.7) | collective-permute-done | bytes 786464 | tf_op jit(solution)/shard_map/ppermute | solution.py:34
  37.4 2.4 %collective-permute-start.4 = (bf16[2,384,256]{2,1,0:T(8,128)(2,1)}, bf16[2,384,256]{2,1,0:T(8,128)(2,1)S(1)}, u32[]{:S(2)}, u32[]{:S(2)}) collective-permute-start(bf16[2,384,256]{2,1,0:T(8,128)(2,1)} %copy-done.5), channel_id=1, source_target_pairs={{0,1},{8,137},{16,17},{24,153},{32,33},{40,169},{48,49},{56,185},{... | collective-permute-start | bytes 1179656 | tf_op jit(solution)/shard_map/ppermute | solution.py:34
  41.0 2.5 %flip.1.refs_9_.refs_0_.refs_1_ = bf16[2,4,2,4,96,384]{5,4,3,2,1,0:T(8,128)(2,1)S(1)} custom-call(s32[20]{0:T(128)S(1)} %stack.87.info, bf16[2,192,3072]{2,1,0:T(8,128)(2,1)S(1)} %get-tuple-element.29.own.refs_0_, bf16[2,192,3072]{2,1,0:T(8,128)(2,1)S(1)} %collective-permute-done.3.peer.refs_1_), custom_call_target="tpu_custom_call" | custom-call | bytes 9437184 | tf_op jit(solution)/shard_map/flip/pallas_call | solution.py:72
  43.5 4.2 %linear.2 = (f32[192,1024]{1,0:T(8,128)S(1)}, f32[192,1024]{1,0:T(8,128)S(1)}) custom-call(bf16[2,192,3072]{2,1,0:T(8,128)(2,1)S(1)} %get-tuple-element.29.own.refs_0_, bf16[2,192,3072]{2,1,0:T(8,128)(2,1)S(1)} %collective-permute-done.3.peer.refs_1_, bf16[4,384,256]{2,1,0:T(8,128)(2,1)S(1)} %copy-done.7, bf16[4,384,256]{2,1,0:T(8,128)(2,1)S(1)} %copy-done.3, ...), custom_call_target="tpu_custom_call" | custom-call | flops 1811939328 | bytes 8257536 | tf_op jit(solution)/shard_map/linear/pallas_call | solution.py:72
  50.1 1.8 %linear.3 = (f32[192,1024]{1,0:T(8,128)S(1)}, f32[192,1024]{1,0:T(8,128)S(1)}) custom-call(bf16[2,192,3072]{2,1,0:T(8,128)(2,1)S(1)} %get-tuple-element.29.own.refs_0_, bf16[2,192,3072]{2,1,0:T(8,128)(2,1)S(1)} %collective-permute-done.3.peer.refs_1_, bf16[2,384,256]{2,1,0:T(8,128)(2,1)S(1)} %collective-permute-done.4.refs_0_.refs_9_, ...), custom_call_target="tpu_custom_call" | custom-call | flops 603979776 | bytes 2752512 | tf_op jit(solution)/shard_map/linear/pallas_call | solution.py:72
  51.9 1.9 %collective-permute-start.10 = (f32[192,1024]{1,0:T(8,128)S(1)}, f32[192,1024]{1,0:T(8,128)S(1)}, u32[]{:S(2)}, u32[]{:S(2)}) collective-permute-start(f32[192,1024]{1,0:T(8,128)S(1)} %get-tuple-element.37), channel_id=1, source_target_pairs={{0,8},{8,0},{16,24},{24,16},{32,40},{40,32},{48,56},{56,48},{64,72... | collective-permute-start | bytes 2359304 | tf_op jit(solution)/shard_map/ppermute | solution.py:34
  53.8 1.9 %collective-permute-done.10.theirs = f32[192,1024]{1,0:T(8,128)S(1)} collective-permute-done((f32[192,1024]{1,0:T(8,128)S(1)}, f32[192,1024]{1,0:T(8,128)S(1)}, u32[]{:S(2)}, u32[]{:S(2)}) %collective-permute-start.10) | collective-permute-done | bytes 786464 | tf_op jit(solution)/shard_map/ppermute | solution.py:34
  55.7 3.2 %attend.1.refs_2_.refs_1_.refs_0_ = bf16[192,1024]{1,0:T(8,128)(2,1)S(1)} custom-call(s32[1,3]{1,0:T(1,128)S(1)} %copy-done.14, f32[192,1024]{1,0:T(8,128)S(1)} %get-tuple-element.36.mine, f32[192,1024]{1,0:T(8,128)S(1)} %collective-permute-done.10.theirs, f32[192,128]{1,0:T(8,128)S(1)} %get-tuple-element.67.refs_10_.cos_t, ...), custom_call_target="tpu_custom_call" | custom-call | flops 188743680 | bytes 1966080 | tf_op jit(solution)/shard_map/attend/pallas_call | solution.py:72
  62.6 1.8 %collective-permute-start.13 = (bf16[4,8,96,128]{3,2,1,0:T(8,128)(2,1)S(1)}, bf16[4,8,96,128]{3,2,1,0:T(8,128)(2,1)S(1)}, u32[]{:S(2)}, u32[]{:S(2)}) collective-permute-start(bf16[4,8,96,128]{3,2,1,0:T(8,128)(2,1)S(1)} %get-tuple-element.41), channel_id=1, source_target_pairs={{0,6},{8,137},{16,22},{24,153},{32,38},{40,169},{48,54},{56,185},{... | collective-permute-start | bytes 2359304 | tf_op jit(solution)/shard_map/ppermute | solution.py:34
  66.9 1.8 %terms.3 = (bf16[4,8,96,128]{3,2,1,0:T(8,128)(2,1)S(1)}, bf16[4,8,96,128]{3,2,1,0:T(8,128)(2,1)S(1)}, bf16[4,8,96,128]{3,2,1,0:T(8,128)(2,1)S(1)}, bf16[4,8,96,128]{3,2,1,0:T(8,128)(2,1)S(1)}) custom-call(bf16[2,4,2,4,96,384]{5,4,3,2,1,0:T(8,128)(2,1)S(1)} %flip.1.refs_9_.refs_0_.refs_1_, bf16[2,4,2,4,96,384]{5,4,3,2,1,0:T(8,128)(2,1)S(1)} %flip.1.refs_9_.refs_0_.refs_1_, ...), custom_call_target="tpu_custom_call" | custom-call | flops 1207959552 | bytes 7864320 | tf_op jit(solution)/shard_map/terms/pallas_call | solution.py:72
  68.7 5.3 %collective-permute-done.12.far_0 = bf16[4,8,96,128]{3,2,1,0:T(8,128)(2,1)S(1)} collective-permute-done((bf16[4,8,96,128]{3,2,1,0:T(8,128)(2,1)S(1)}, bf16[4,8,96,128]{3,2,1,0:T(8,128)(2,1)S(1)}, u32[]{:S(2)}, u32[]{:S(2)}) %collective-permute-start.12) | collective-permute-done | bytes 786464 | tf_op jit(solution)/shard_map/ppermute | solution.py:34
  74.5 2.8 %collective-permute-start.17 = (bf16[4,8,96,128]{3,2,1,0:T(8,128)(2,1)S(1)}, bf16[4,8,96,128]{3,2,1,0:T(8,128)(2,1)S(1)}, u32[]{:S(2)}, u32[]{:S(2)}) collective-permute-start(bf16[4,8,96,128]{3,2,1,0:T(8,128)(2,1)S(1)} %get-tuple-element.49), channel_id=1, source_target_pairs={{0,6},{8,137},{16,22},{24,153},{32,38},{40,169},{48,54},{56,185},{... | collective-permute-start | bytes 2359304 | tf_op jit(solution)/shard_map/ppermute | solution.py:34
  77.2 3.7 %normed_grad.1 = (f32[192,3072]{1,0:T(8,128)S(1)}, bf16[192,3072]{1,0:T(8,128)(2,1)S(1)}) custom-call(bf16[192,1024]{1,0:T(8,128)(2,1)S(1)} %attend.1.refs_2_.refs_1_.refs_0_, bf16[192,1024]{1,0:T(8,128)(2,1)S(1)} %collective-permute-done.11.refs_3_.refs_2_.refs_1_, bf16[4,384,256]{2,1,0:T(8,128)(2,1)S(1)} %copy-done.7, bf16[4,384,256]{2,1,0:T(8,128)(2,1)S(1)} %copy-done.3, ...), custom_call_target="tpu_custom_call" | custom-call | flops 1811939328 | bytes 11010048 | tf_op jit(solution)/shard_map/normed_grad/pallas_call | solution.py:72
  82.5 8.1 %collective-permute-done.17.refs_5_ = bf16[4,8,96,128]{3,2,1,0:T(8,128)(2,1)S(1)} collective-permute-done((bf16[4,8,96,128]{3,2,1,0:T(8,128)(2,1)S(1)}, bf16[4,8,96,128]{3,2,1,0:T(8,128)(2,1)S(1)}, u32[]{:S(2)}, u32[]{:S(2)}) %collective-permute-start.17) | collective-permute-done | bytes 786464 | tf_op jit(solution)/shard_map/ppermute | solution.py:34
  90.9 2.1 %sides.1 = (bf16[8,2,96,128]{3,2,1,0:T(8,128)(2,1)S(1)}, bf16[8,2,96,128]{3,2,1,0:T(8,128)(2,1)}, bf16[8,2,96,128]{3,2,1,0:T(8,128)(2,1)}, bf16[8,2,96,128]{3,2,1,0:T(8,128)(2,1)S(1)}) custom-call(bf16[4,8,96,128]{3,2,1,0:T(8,128)(2,1)S(1)} %get-tuple-element.45.refs_0_, bf16[4,8,96,128]{3,2,1,0:T(8,128)(2,1)S(1)} %collective-permute-done.14.refs_1_, ...), custom_call_target="tpu_custom_call" | custom-call | flops 2359296 | bytes 6291456 | tf_op jit(solution)/shard_map/sides/pallas_call | solution.py:72
  95.1 1.7 %collective-permute-start.19 = (bf16[8,2,96,128]{3,2,1,0:T(8,128)(2,1)}, bf16[8,2,96,128]{3,2,1,0:T(8,128)(2,1)S(1)}, u32[]{:S(2)}, u32[]{:S(2)}) collective-permute-start(bf16[8,2,96,128]{3,2,1,0:T(8,128)(2,1)} %get-tuple-element.52), channel_id=1, source_target_pairs={{0,1},{8,10},{16,17},{24,26},{32,33},{40,42},{48,49},{56,58},{64,6... | collective-permute-start | bytes 1179656 | tf_op jit(solution)/shard_map/ppermute | solution.py:34
  96.8 2.3 %collective-permute-start.20 = (bf16[8,2,96,128]{3,2,1,0:T(8,128)(2,1)}, bf16[8,2,96,128]{3,2,1,0:T(8,128)(2,1)S(1)}, u32[]{:S(2)}, u32[]{:S(2)}) collective-permute-start(bf16[8,2,96,128]{3,2,1,0:T(8,128)(2,1)} %get-tuple-element.53), channel_id=1, source_target_pairs={{0,128},{8,12},{16,144},{24,28},{32,160},{40,44},{48,176},{56,60},... | collective-permute-start | bytes 1179656 | tf_op jit(solution)/shard_map/ppermute | solution.py:34
  99.9 1.7 %copy-done.9 = f32[192,3072]{1,0:T(8,128)S(1)} copy-done((f32[192,3072]{1,0:T(8,128)S(1)}, f32[192,3072]{1,0:T(8,128)}, u32[]{:S(2)}) %copy-start.9) | copy-done | bytes 2359320
  101.6 5.1 %token_grad.1 = (bf16[192,6144]{1,0:T(8,128)(2,1)}, f32[8,128]{1,0:T(8,128)S(1)}) custom-call(s32[20]{0:T(128)S(1)} %stack.87.info, bf16[192,6144]{1,0:T(8,128)(2,1)S(1)} %copy-done.1, f32[192,3072]{1,0:T(8,128)S(1)} %copy-done.9, bf16[192,3072]{1,0:T(8,128)(2,1)S(1)} %collective-permute-done.18.g_peer), custom_call_target="tpu_custom_call" | custom-call | flops 18874368 | bytes 9437184 | tf_op jit(solution)/shard_map/token_grad/pallas_call | solution.py:72
  106.7 2.0 %collective-permute-done.20.refs_2_ = bf16[8,2,96,128]{3,2,1,0:T(8,128)(2,1)S(1)} collective-permute-done((bf16[8,2,96,128]{3,2,1,0:T(8,128)(2,1)}, bf16[8,2,96,128]{3,2,1,0:T(8,128)(2,1)S(1)}, u32[]{:S(2)}, u32[]{:S(2)}) %collective-permute-start.20) | collective-permute-done | bytes 393248 | tf_op jit(solution)/shard_map/ppermute | solution.py:34
  109.0 20.5 %all_to_all.10.got = bf16[8,2,96,128]{3,2,1,0:T(8,128)(2,1)S(1)} all-to-all(bf16[8,2,96,128]{3,2,1,0:T(8,128)(2,1)S(1)} %seconds.1), channel_id=1, replica_groups={{0,16,32,48,64,80,96,112},{8,24,40,56,72,88,104,120},{128,144,160,176,1..., dimensions={0} | all-to-all | bytes 786432 | tf_op jit(solution)/shard_map/all_to_all | solution.py:393
  129.6 24.3 %all_to_all.11 = bf16[16,2,96,128]{3,2,1,0:T(8,128)(2,1)S(1)} all-to-all(bf16[16,2,96,128]{3,2,1,0:T(8,128)(2,1)S(1)} %last.1), channel_id=1, replica_groups={{0,16,32,48,64,80,96,112,128,144,160,176,192,208,224,240},{8,24,40,56,7..., dimensions={0} | all-to-all | bytes 1572864 | tf_op jit(solution)/shard_map/all_to_all | solution.py:393
  153.9 3.2 %collective-permute-start.22 = (bf16[2,8,2,96,128]{4,3,2,1,0:T(8,128)(2,1)S(1)}, bf16[2,8,2,96,128]{4,3,2,1,0:T(8,128)(2,1)S(1)}, u32[]{:S(2)}, u32[]{:S(2)}) collective-permute-start(bf16[2,8,2,96,128]{4,3,2,1,0:T(8,128)(2,1)S(1)} %bitcast.24), channel_id=1, source_target_pairs={{0,8},{8,0},{16,24},{24,16},{32,40},{40,32},{48,56},{56,48},{64,72... | collective-permute-start | bytes 2359304 | tf_op jit(solution)/shard_map/ppermute | solution.py:34
  157.1 1.7 %place.2.refs_0_ = f32[4,768,256]{2,1,0:T(8,128)} custom-call(s32[1]{0:T(128)} %bitcast.18.at, bf16[2,8,2,96,128]{4,3,2,1,0:T(8,128)(2,1)S(1)} %bitcast.25), custom_call_target="tpu_custom_call" | custom-call | flops 1 | bytes 6291456 | tf_op jit(solution)/shard_map/place/pallas_call | solution.py:369
  159.0 1.7 %place.3 = f32[4,768,256]{2,1,0:T(8,128)} custom-call(s32[1]{0:T(128)} %bitcast.22.at, bf16[2,8,2,96,128]{4,3,2,1,0:T(8,128)(2,1)S(1)} %collective-permute-done.22.blocks, f32[4,768,256]{2,1,0:T(8,128)} %place.2.refs_0_), custom_call_target="tpu_custom_call", output_to_operand_aliasing={{}: (2, {})} | custom-call | flops 1 | bytes 6291456 | tf_op jit(solution)/shard_map/place/pallas_call | solution.py:369
  (75 shorter events, 23.4 us)
Async XLA Ops:
  3.2 18.9 %collective-permute-start.1 = (bf16[4,384,256]{2,1,0:T(8,128)(2,1)}, bf16[4,384,256]{2,1,0:T(8,128)(2,1)S(1)}, u32[]{:S(2)}, u32[]{:S(2)}) collective-permute-start(bf16[4,384,256]{2,1,0:T(8,128)(2,1)} %get-tuple-element.31.refs_2_), channel_id=1, source_target_pairs={{0,1},{8,137},{16,17},{24,153},{32,33},{40,169},{48,49},{56,185},{... | collective-permute-start | bytes 2359304 | tf_op jit(solution)/shard_map/ppermute | solution.py:34
  6.5 16.2 %collective-permute-start = (bf16[4,384,256]{2,1,0:T(8,128)(2,1)}, bf16[4,384,256]{2,1,0:T(8,128)(2,1)}, u32[]{:S(2)}, u32[]{:S(2)}) collective-permute-start(bf16[4,384,256]{2,1,0:T(8,128)(2,1)} %get-tuple-element.31.refs_2_), channel_id=1, source_target_pairs={{0,2},{8,14},{16,18},{24,30},{32,34},{40,46},{48,50},{56,62},{64,6... | collective-permute-start | bytes 2359304 | tf_op jit(solution)/shard_map/ppermute | solution.py:34
  9.3 12.7 %collective-permute-start.2 = (bf16[2,384,256]{2,1,0:T(8,128)(2,1)}, bf16[2,384,256]{2,1,0:T(8,128)(2,1)S(1)}, u32[]{:S(2)}, u32[]{:S(2)}) collective-permute-start(bf16[2,384,256]{2,1,0:T(8,128)(2,1)} %get-tuple-element.32), channel_id=1, source_target_pairs={{0,6},{8,10},{16,22},{24,26},{32,38},{40,42},{48,54},{56,58},{64,7... | collective-permute-start | bytes 1179656 | tf_op jit(solution)/shard_map/ppermute | solution.py:34
  23.0 14.4 %copy-start.16 = (s32[2,192]{1,0:T(2,128)S(1)}, s32[2,192]{1,0:T(2,128)}, u32[]{:S(2)}) copy-start(s32[2,192]{1,0:T(2,128)} %param.10) | copy-start | bytes 4612
  23.0 16.9 %copy-start.17 = (f32[32]{0:T(128)S(1)}, f32[32]{0:T(128)}, u32[]{:S(2)}) copy-start(f32[32]{0:T(128)} %constant.148) | copy-start | bytes 388
  23.0 17.9 %collective-permute-start.3 = (bf16[2,192,3072]{2,1,0:T(8,128)(2,1)}, bf16[2,192,3072]{2,1,0:T(8,128)(2,1)S(1)}, u32[]{:S(2)}, u32[]{:S(2)}) collective-permute-start(bf16[2,192,3072]{2,1,0:T(8,128)(2,1)} %gate.2), channel_id=1, source_target_pairs={{0,8},{8,0},{16,24},{24,16},{32,40},{40,32},{48,56},{56,48},{64,72... | collective-permute-start | bytes 7077896 | tf_op jit(solution)/shard_map/ppermute | solution.py:34
  24.4 12.0 %collective-permute-start.7 = (bf16[4,384,256]{2,1,0:T(8,128)(2,1)}, bf16[4,384,256]{2,1,0:T(8,128)(2,1)S(1)}, u32[]{:S(2)}, u32[]{:S(2)}) collective-permute-start(bf16[4,384,256]{2,1,0:T(8,128)(2,1)} %collective-permute-done.refs_1_.refs_4_), channel_id=1, source_target_pairs={{0,1},{8,137},{16,17},{24,153},{32,33},{40,169},{48,49},{56,185},{... | collective-permute-start | bytes 2359304 | tf_op jit(solution)/shard_map/ppermute | solution.py:34
  27.2 16.3 %collective-permute-start.9 = (bf16[4,384,256]{2,1,0:T(8,128)(2,1)}, bf16[4,384,256]{2,1,0:T(8,128)(2,1)S(1)}, u32[]{:S(2)}, u32[]{:S(2)}) collective-permute-start(bf16[4,384,256]{2,1,0:T(8,128)(2,1)} %collective-permute-done.refs_1_.refs_4_), channel_id=1, source_target_pairs={{0,2},{8,14},{16,18},{24,30},{32,34},{40,46},{48,50},{56,62},{64,6... | collective-permute-start | bytes 2359304 | tf_op jit(solution)/shard_map/ppermute | solution.py:34
  27.2 12.6 %collective-permute-start.5 = (bf16[2,384,256]{2,1,0:T(8,128)(2,1)}, bf16[2,384,256]{2,1,0:T(8,128)(2,1)S(1)}, u32[]{:S(2)}, u32[]{:S(2)}) collective-permute-start(bf16[2,384,256]{2,1,0:T(8,128)(2,1)} %get-tuple-element.33), channel_id=1, source_target_pairs={{0,6},{8,10},{16,22},{24,26},{32,38},{40,42},{48,54},{56,58},{64,7... | collective-permute-start | bytes 1179656 | tf_op jit(solution)/shard_map/ppermute | solution.py:34
  36.5 13.7 %collective-permute-start.8 = (bf16[4,384,256]{2,1,0:T(8,128)(2,1)S(1)}, bf16[4,384,256]{2,1,0:T(8,128)(2,1)S(1)}, u32[]{:S(2)}, u32[]{:S(2)}) collective-permute-start(bf16[4,384,256]{2,1,0:T(8,128)(2,1)S(1)} %collective-permute-done.7.refs_5_), channel_id=1, source_target_pairs={{0,2},{8,14},{16,18},{24,30},{32,34},{40,46},{48,50},{56,62},{64,6... | collective-permute-start | bytes 2359304 | tf_op jit(solution)/shard_map/ppermute | solution.py:34
  37.4 10.3 %collective-permute-start.4 = (bf16[2,384,256]{2,1,0:T(8,128)(2,1)}, bf16[2,384,256]{2,1,0:T(8,128)(2,1)S(1)}, u32[]{:S(2)}, u32[]{:S(2)}) collective-permute-start(bf16[2,384,256]{2,1,0:T(8,128)(2,1)} %copy-done.5), channel_id=1, source_target_pairs={{0,1},{8,137},{16,17},{24,153},{32,33},{40,169},{48,49},{56,185},{... | collective-permute-start | bytes 1179656 | tf_op jit(solution)/shard_map/ppermute | solution.py:34
  39.9 9.1 %collective-permute-start.6 = (bf16[2,384,256]{2,1,0:T(8,128)(2,1)S(1)}, bf16[2,384,256]{2,1,0:T(8,128)(2,1)S(1)}, u32[]{:S(2)}, u32[]{:S(2)}) collective-permute-start(bf16[2,384,256]{2,1,0:T(8,128)(2,1)S(1)} %collective-permute-done.5.refs_7_), channel_id=1, source_target_pairs={{0,1},{8,137},{16,17},{24,153},{32,33},{40,169},{48,49},{56,185},{... | collective-permute-start | bytes 1179656 | tf_op jit(solution)/shard_map/ppermute | solution.py:34
  41.0 2.5 %copy-start.3 = (bf16[4,384,256]{2,1,0:T(8,128)(2,1)S(1)}, bf16[4,384,256]{2,1,0:T(8,128)(2,1)}, u32[]{:S(2)}) copy-start(bf16[4,384,256]{2,1,0:T(8,128)(2,1)} %copy-done.2) | copy-start | bytes 2359300
  41.0 2.5 %copy-start.6 = (bf16[2,384,256]{2,1,0:T(8,128)(2,1)S(1)}, bf16[2,384,256]{2,1,0:T(8,128)(2,1)}, u32[]{:S(2)}) copy-start(bf16[2,384,256]{2,1,0:T(8,128)(2,1)} %copy-done.5) | copy-start | bytes 1179652
  50.1 5.6 %copy-start.14 = (s32[1,3]{1,0:T(1,128)S(1)}, s32[1,3]{1,0:T(1,128)}, u32[]{:S(2)}) copy-start(s32[1,3]{1,0:T(1,128)} %lengths.1) | copy-start | bytes 40
  51.9 3.8 %collective-permute-start.10 = (f32[192,1024]{1,0:T(8,128)S(1)}, f32[192,1024]{1,0:T(8,128)S(1)}, u32[]{:S(2)}, u32[]{:S(2)}) collective-permute-start(f32[192,1024]{1,0:T(8,128)S(1)} %get-tuple-element.37), channel_id=1, source_target_pairs={{0,8},{8,0},{16,24},{24,16},{32,40},{40,32},{48,56},{56,48},{64,72... | collective-permute-start | bytes 2359304 | tf_op jit(solution)/shard_map/ppermute | solution.py:34
  58.8 1.8 %collective-permute-start.11 = (bf16[192,1024]{1,0:T(8,128)(2,1)S(1)}, bf16[192,1024]{1,0:T(8,128)(2,1)S(1)}, u32[]{:S(2)}, u32[]{:S(2)}) collective-permute-start(bf16[192,1024]{1,0:T(8,128)(2,1)S(1)} %attend.1.refs_2_.refs_1_.refs_0_), channel_id=1, source_target_pairs={{0,8},{8,0},{16,24},{24,16},{32,40},{40,32},{48,56},{56,48},{64,72... | collective-permute-start | bytes 1179656 | tf_op jit(solution)/shard_map/ppermute | solution.py:34
  61.6 12.4 %collective-permute-start.12 = (bf16[4,8,96,128]{3,2,1,0:T(8,128)(2,1)S(1)}, bf16[4,8,96,128]{3,2,1,0:T(8,128)(2,1)S(1)}, u32[]{:S(2)}, u32[]{:S(2)}) collective-permute-start(bf16[4,8,96,128]{3,2,1,0:T(8,128)(2,1)S(1)} %get-tuple-element.39), channel_id=1, source_target_pairs={{0,2},{8,9},{16,18},{24,25},{32,34},{40,41},{48,50},{56,57},{64,66... | collective-permute-start | bytes 2359304 | tf_op jit(solution)/shard_map/ppermute | solution.py:34
  62.6 11.4 %collective-permute-start.13 = (bf16[4,8,96,128]{3,2,1,0:T(8,128)(2,1)S(1)}, bf16[4,8,96,128]{3,2,1,0:T(8,128)(2,1)S(1)}, u32[]{:S(2)}, u32[]{:S(2)}) collective-permute-start(bf16[4,8,96,128]{3,2,1,0:T(8,128)(2,1)S(1)} %get-tuple-element.41), channel_id=1, source_target_pairs={{0,6},{8,137},{16,22},{24,153},{32,38},{40,169},{48,54},{56,185},{... | collective-permute-start | bytes 2359304 | tf_op jit(solution)/shard_map/ppermute | solution.py:34
  65.4 16.8 %collective-permute-start.14 = (bf16[4,8,96,128]{3,2,1,0:T(8,128)(2,1)S(1)}, bf16[4,8,96,128]{3,2,1,0:T(8,128)(2,1)S(1)}, u32[]{:S(2)}, u32[]{:S(2)}) collective-permute-start(bf16[4,8,96,128]{3,2,1,0:T(8,128)(2,1)S(1)} %get-tuple-element.46), channel_id=1, source_target_pairs={{0,6},{8,137},{16,22},{24,153},{32,38},{40,169},{48,54},{56,185},{... | collective-permute-start | bytes 2359304 | tf_op jit(solution)/shard_map/ppermute | solution.py:34
  65.5 17.0 %collective-permute-start.16 = (bf16[4,8,96,128]{3,2,1,0:T(8,128)(2,1)S(1)}, bf16[4,8,96,128]{3,2,1,0:T(8,128)(2,1)S(1)}, u32[]{:S(2)}, u32[]{:S(2)}) collective-permute-start(bf16[4,8,96,128]{3,2,1,0:T(8,128)(2,1)S(1)} %get-tuple-element.48), channel_id=1, source_target_pairs={{0,2},{8,9},{16,18},{24,25},{32,34},{40,41},{48,50},{56,57},{64,66... | collective-permute-start | bytes 2359304 | tf_op jit(solution)/shard_map/ppermute | solution.py:34
  74.5 16.1 %collective-permute-start.17 = (bf16[4,8,96,128]{3,2,1,0:T(8,128)(2,1)S(1)}, bf16[4,8,96,128]{3,2,1,0:T(8,128)(2,1)S(1)}, u32[]{:S(2)}, u32[]{:S(2)}) collective-permute-start(bf16[4,8,96,128]{3,2,1,0:T(8,128)(2,1)S(1)} %get-tuple-element.49), channel_id=1, source_target_pairs={{0,6},{8,137},{16,22},{24,153},{32,38},{40,169},{48,54},{56,185},{... | collective-permute-start | bytes 2359304 | tf_op jit(solution)/shard_map/ppermute | solution.py:34
  77.2 13.7 %collective-permute-start.15 = (bf16[4,8,96,128]{3,2,1,0:T(8,128)(2,1)S(1)}, bf16[4,8,96,128]{3,2,1,0:T(8,128)(2,1)S(1)}, u32[]{:S(2)}, u32[]{:S(2)}) collective-permute-start(bf16[4,8,96,128]{3,2,1,0:T(8,128)(2,1)S(1)} %get-tuple-element.42.refs_12_), channel_id=1, source_target_pairs={{0,2},{8,9},{16,18},{24,25},{32,34},{40,41},{48,50},{56,57},{64,66... | collective-permute-start | bytes 2359304 | tf_op jit(solution)/shard_map/ppermute | solution.py:34
  80.9 12.1 %copy-start.4 = (bf16[192,3072]{1,0:T(8,128)(2,1)}, bf16[192,3072]{1,0:T(8,128)(2,1)S(1)}, u32[]{:S(2)}) copy-start(bf16[192,3072]{1,0:T(8,128)(2,1)S(1)} %get-tuple-element.44.refs_6_.refs_0_) | copy-start | bytes 3538948
  80.9 12.0 %copy-start.8 = (f32[192,3072]{1,0:T(8,128)}, f32[192,3072]{1,0:T(8,128)S(1)}, u32[]{:S(2)}) copy-start(f32[192,3072]{1,0:T(8,128)S(1)} %get-tuple-element.43.g_own) | copy-start | bytes 7077892
  93.7 6.2 %copy-start.1 = (bf16[192,6144]{1,0:T(8,128)(2,1)S(1)}, bf16[192,6144]{1,0:T(8,128)(2,1)}, u32[]{:S(2)}) copy-start(bf16[192,6144]{1,0:T(8,128)(2,1)} %tokens.3) | copy-start | bytes 7077892
  93.7 6.1 %collective-permute-start.18 = (bf16[192,3072]{1,0:T(8,128)(2,1)}, bf16[192,3072]{1,0:T(8,128)(2,1)S(1)}, u32[]{:S(2)}, u32[]{:S(2)}) collective-permute-start(bf16[192,3072]{1,0:T(8,128)(2,1)} %gate.3), channel_id=1, source_target_pairs={{0,8},{8,0},{16,24},{24,16},{32,40},{40,32},{48,56},{56,48},{64,72... | collective-permute-start | bytes 3538952 | tf_op jit(solution)/shard_map/ppermute | solution.py:34
  95.1 11.7 %collective-permute-start.19 = (bf16[8,2,96,128]{3,2,1,0:T(8,128)(2,1)}, bf16[8,2,96,128]{3,2,1,0:T(8,128)(2,1)S(1)}, u32[]{:S(2)}, u32[]{:S(2)}) collective-permute-start(bf16[8,2,96,128]{3,2,1,0:T(8,128)(2,1)} %get-tuple-element.52), channel_id=1, source_target_pairs={{0,1},{8,10},{16,17},{24,26},{32,33},{40,42},{48,49},{56,58},{64,6... | collective-permute-start | bytes 1179656 | tf_op jit(solution)/shard_map/ppermute | solution.py:34
  96.8 11.9 %collective-permute-start.20 = (bf16[8,2,96,128]{3,2,1,0:T(8,128)(2,1)}, bf16[8,2,96,128]{3,2,1,0:T(8,128)(2,1)S(1)}, u32[]{:S(2)}, u32[]{:S(2)}) collective-permute-start(bf16[8,2,96,128]{3,2,1,0:T(8,128)(2,1)} %get-tuple-element.53), channel_id=1, source_target_pairs={{0,128},{8,12},{16,144},{24,28},{32,160},{40,44},{48,176},{56,60},... | collective-permute-start | bytes 1179656 | tf_op jit(solution)/shard_map/ppermute | solution.py:34
  99.1 9.6 %collective-permute-start.21 = (bf16[8,2,96,128]{3,2,1,0:T(8,128)(2,1)}, bf16[8,2,96,128]{3,2,1,0:T(8,128)(2,1)S(1)}, u32[]{:S(2)}, u32[]{:S(2)}) collective-permute-start(bf16[8,2,96,128]{3,2,1,0:T(8,128)(2,1)} %copy-done.15), channel_id=1, source_target_pairs={{0,129},{8,14},{16,145},{24,30},{32,161},{40,46},{48,177},{56,62},... | collective-permute-start | bytes 1179656 | tf_op jit(solution)/shard_map/ppermute | solution.py:34
  101.6 7.1 %copy-start.13 = (bf16[8,2,96,128]{3,2,1,0:T(8,128)(2,1)S(1)}, bf16[8,2,96,128]{3,2,1,0:T(8,128)(2,1)}, u32[]{:S(2)}) copy-start(bf16[8,2,96,128]{3,2,1,0:T(8,128)(2,1)} %copy-done.12) | copy-start | bytes 1179652
  153.9 5.1 %collective-permute-start.22 = (bf16[2,8,2,96,128]{4,3,2,1,0:T(8,128)(2,1)S(1)}, bf16[2,8,2,96,128]{4,3,2,1,0:T(8,128)(2,1)S(1)}, u32[]{:S(2)}, u32[]{:S(2)}) collective-permute-start(bf16[2,8,2,96,128]{4,3,2,1,0:T(8,128)(2,1)S(1)} %bitcast.24), channel_id=1, source_target_pairs={{0,8},{8,0},{16,24},{24,16},{32,40},{40,32},{48,56},{56,48},{64,72... | collective-permute-start | bytes 2359304 | tf_op jit(solution)/shard_map/ppermute | solution.py:34
  (9 other events, 12.8 us)

commit v8 on v5

--- a/solution.py
+++ b/solution.py
@@ -330,12 +330,11 @@
 
 
 def place_kernel(at, blocks, *refs):
-    out, rows = refs[-1], blocks.shape[3]
-    for h in range(2):
-        for n in range(2):
-            for side in range(2):
-                to = slice((2 * h + side) * rows, (2 * h + side + 1) * rows)
-                out[0, to, n * 128 : (n + 1) * 128] = blocks[h, n, side].astype(F32)
+    out, rows = refs[-1], blocks.shape[2]
+    for n in range(2):
+        for side in range(2):
+            to = slice(side * rows, (side + 1) * rows)
+            out[0, to, n * 128 : (n + 1) * 128] = blocks[n, side].astype(F32)
 
 
 def place(at, blocks, dims, before=()):
@@ -344,28 +343,21 @@
         grid_spec=pltpu.PrefetchScalarGridSpec(
             num_scalar_prefetch=1,
             grid=(4,),
-            in_specs=[pl.BlockSpec((2, 2) + blocks.shape[2:], lambda m, at: (0, m, 0, 0, 0))]
+            in_specs=[pl.BlockSpec((2,) + blocks.shape[1:], lambda m, at: (m, 0, 0, 0))]
             + [pl.BlockSpec(memory_space=pl.ANY) for _ in before],
-            out_specs=pl.BlockSpec((1, dims[1] // 2, dims[2]), lambda m, at: (m, at[0], 0)),
+            out_specs=pl.BlockSpec((1, dims[1] // 4, dims[2]), lambda m, at: (m, at[0], 0)),
         ),
         out_shape=shape(dims, F32),
         input_output_aliases={2: 0} if before else {},
         compiler_params=pltpu.CompilerParams(vmem_limit_bytes=12 * 1024 * 1024),
-        cost_estimate=pl.CostEstimate(flops=1, bytes_accessed=8 * math.prod(dims), transcendentals=0),
+        cost_estimate=pl.CostEstimate(flops=1, bytes_accessed=4 * math.prod(dims), transcendentals=0),
         name="place",
     )(at, blocks, *before)
 
 
-def swap_groups(with_x):
-    if with_x:
-        return [[x * 16 + z * 2 + core for x in range(2) for z in range(NZ)] for core in range(2)]
-    return [[x * 16 + z * 2 + core for z in range(NZ)] for x in range(2) for core in range(2)]
-
-
-def exchange(values, with_x):
-    return lax.all_to_all(
-        values, "dp", split_axis=0, concat_axis=0, axis_index_groups=swap_groups(with_x), tiled=True
-    )
+def exchange(values):
+    groups = [[x * 16 + z * 2 + core for z in range(NZ)] for x in range(2) for core in range(2)]
+    return lax.all_to_all(values, "dp", split_axis=0, concat_axis=0, axis_index_groups=groups, tiled=True)
 
 
 def per_device(tokens, cotangent, lengths, positions, weights):
@@ -551,11 +543,16 @@
         grid=(4,),
         after=[mark],
     )
-    (spread,) = sum_call(last_kernel, "last", [shape((2 * NZ, 2, quarter, 128))], [exchange(by_z, False)])
-    done = exchange(spread, True).reshape(2, NZ, 2, quarter, 128)
+    (spread,) = sum_call(last_kernel, "last", [shape((NZ, 2, quarter, 128))], [exchange(by_z)])
+    here = exchange(spread)
+    there = permute(here, lambda x, y, z, core: (x + 2, y, z, core))
     dims = (4, shard_rows, cols)
-    weight_grads = place(jnp.stack([core]).astype(jnp.int32), done, dims)
-    weight_grads = place(jnp.stack([1 - core]).astype(jnp.int32), shift(done, dc=1), dims, [weight_grads])
+    weight_grads = []
+    for blocks, h in ((here, x_hi), (there, 1 - x_hi)):
+        blocks = gate(blocks, weight_grads) if weight_grads else blocks
+        for c, value in ((core, blocks), (1 - core, shift(blocks, dc=1))):
+            weight_grads = [place(jnp.stack([2 * c + h]).astype(jnp.int32), value, dims, weight_grads)]
+    (weight_grads,) = weight_grads
     return (grad_tokens, weight_grads)
 
 

time: 162 us -> 165 us (1.019)
  blocking collectives: 45.2 us -> 33.8 us
  waiting for transfers between devices: 34.5 us -> 41.1 us
  starting transfers between devices: 33.2 us -> 37.4 us
  Pallas kernels: 33.9 us -> 36 us
  local copies, waits for them, and re-layouts: 12.4 us -> 14.2 us
    all_to_all x2, blocking collectives: 45.2 us -> 33.8 us  [exchange(): lax.all_to_all(values, 'dp', split_axis=0, concat_axis=0, axis_index_grou...]
    ppermute x23 -> x25, waiting for transfers between devices: 34.5 us -> 41.1 us  [permute(): return lax.ppermute(values, ('dp', 'fsdp'), pairs)]
    ppermute x23 -> x25, starting transfers between devices: 33.2 us -> 37.4 us  [permute(): return lax.ppermute(values, ('dp', 'fsdp'), pairs)]
    pallas_call x2 -> x4, Pallas kernels: 3.47 us -> 5.78 us  [place(): pl.pallas_call(place_kernel, grid_spec=pltpu.PrefetchScalarGridSpec(num_s...]
    unnamed x34 -> x40, local copies, waits for them, and re-layouts: 8.19 us -> 9.95 us
  transfers between devices with their start and end apart: 23 -> 25, of which waited for: 14 -> 13; matrix products, arithmetic and copies ran while one was open for 2% -> 2% of each run, Pallas kernels for 15% -> 16%
where the time goes in v8:
time: 165 us; the launch traced here: 164 us
  waiting for transfers between devices  41.1 us (25%)
  starting transfers between devices  37.4 us (23%)
  Pallas kernels  36 us (22%)
  blocking collectives  33.8 us (20%)
  local copies, waits for them, and re-layouts  14.2 us (9%)
    ppermute x25, waiting for transfers between devices, permute(): return lax.ppermute(values, ('dp', 'fsdp'), pairs)  41.1 us
    ppermute x25, starting transfers between devices, permute(): return lax.ppermute(values, ('dp', 'fsdp'), pairs)  37.4 us
    all_to_all x2, blocking collectives, exchange(): lax.all_to_all(values, 'dp', split_axis=0, concat_axis=0, axis_index_grou...  33.8 us
    pallas_call x14, Pallas kernels, call(): pl.pallas_call(kernel, grid=grid or (1,), out_shape=out_shapes, in_specs=...  30.3 us
    unnamed x40, local copies, waits for them, and re-layouts  9.95 us
    pallas_call x4, Pallas kernels, place(): pl.pallas_call(place_kernel, grid_spec=pltpu.PrefetchScalarGridSpec(num_s...  5.78 us
  transfers between devices with their start and end apart: 25, of which 13 were waited for; matrix products, arithmetic and copies ran while one was open for 2% of the time, Pallas kernels for 16%

profile of v8, /device:TPU:1, one launch (start us, length us, event | category | flops | bytes accessed | tf_op | source)
XLA Modules:
  0.0 164.4 jit_solution(17333956809592038117)
XLA Ops:
  0.6 2.1 %constant_dynamic-slice_fusion.2.refs_2_ = bf16[4,384,256]{2,1,0:T(8,128)(2,1)} fusion(bf16[4,768,256]{2,1,0:T(8,128)(2,1)} %param.11, s32[]{:T(128)S(6)} %select_n.118), kind=kLoop, calls=%fused_computation.12 | loop fusion | bytes 1572868 | tf_op jit(solution)/shard_map/dynamic_slice | solution.py:393
  2.7 3.6 %collective-permute-start = (bf16[4,384,256]{2,1,0:T(8,128)(2,1)}, bf16[4,384,256]{2,1,0:T(8,128)(2,1)S(1)}, u32[]{:S(2)}, u32[]{:S(2)}) collective-permute-start(bf16[4,384,256]{2,1,0:T(8,128)(2,1)} %constant_dynamic-slice_fusion.2.refs_2_), channel_id=1, source_target_pairs={{0,2},{8,14},{16,18},{24,30},{32,34},{40,46},{48,50},{56,62},{64,6... | collective-permute-start | bytes 2359304 | tf_op jit(solution)/shard_map/ppermute | solution.py:34
  6.3 2.5 %collective-permute-start.1 = (bf16[4,384,256]{2,1,0:T(8,128)(2,1)}, bf16[4,384,256]{2,1,0:T(8,128)(2,1)}, u32[]{:S(2)}, u32[]{:S(2)}) collective-permute-start(bf16[4,384,256]{2,1,0:T(8,128)(2,1)} %constant_dynamic-slice_fusion.2.refs_2_), channel_id=1, source_target_pairs={{0,1},{8,137},{16,17},{24,153},{32,33},{40,169},{48,49},{56,185},{... | collective-permute-start | bytes 2359304 | tf_op jit(solution)/shard_map/ppermute | solution.py:34
  8.8 2.0 %constant_dynamic-slice_fusion = (bf16[2,384,256]{2,1,0:T(8,128)(2,1)}, bf16[2,384,256]{2,1,0:T(8,128)(2,1)}) fusion(bf16[4,768,256]{2,1,0:T(8,128)(2,1)} %param.11, s32[]{:T(128)S(6)} %select_n.118), kind=kLoop, calls=%fused_computation.10 | loop fusion | bytes 1572868 | tf_op jit(solution)/shard_map/dynamic_slice | solution.py:395
  12.6 1.7 %copy-done.10 = bf16[192,6144]{1,0:T(8,128)(2,1)S(1)} copy-done((bf16[192,6144]{1,0:T(8,128)(2,1)S(1)}, bf16[192,6144]{1,0:T(8,128)(2,1)}, u32[]{:S(2)}) %copy-start.10) | copy-done | bytes 2359320
  14.2 3.0 %prep.1 = (bf16[2,192,3072]{2,1,0:T(8,128)(2,1)S(1)}, bf16[2,192,3072]{2,1,0:T(8,128)(2,1)S(1)}) custom-call(s32[20]{0:T(128)S(1)} %stack.95.info, bf16[192,6144]{1,0:T(8,128)(2,1)S(1)} %copy-done, bf16[192,6144]{1,0:T(8,128)(2,1)S(1)} %copy-done.10), custom_call_target="tpu_custom_call" | custom-call | flops 9437184 | bytes 9437184 | tf_op jit(solution)/shard_map/prep/pallas_call | solution.py:72
  18.7 4.2 %collective-permute-done.2.refs_3_.refs_6_ = bf16[2,384,256]{2,1,0:T(8,128)(2,1)S(1)} collective-permute-done((bf16[2,384,256]{2,1,0:T(8,128)(2,1)}, bf16[2,384,256]{2,1,0:T(8,128)(2,1)S(1)}, u32[]{:S(2)}, u32[]{:S(2)}) %collective-permute-start.2) | collective-permute-done | bytes 393248 | tf_op jit(solution)/shard_map/ppermute | solution.py:34
  25.2 1.8 %collective-permute-start.9 = (bf16[4,384,256]{2,1,0:T(8,128)(2,1)}, bf16[4,384,256]{2,1,0:T(8,128)(2,1)S(1)}, u32[]{:S(2)}, u32[]{:S(2)}) collective-permute-start(bf16[4,384,256]{2,1,0:T(8,128)(2,1)} %copy-done.2), channel_id=1, source_target_pairs={{0,2},{8,14},{16,18},{24,30},{32,34},{40,46},{48,50},{56,62},{64,6... | collective-permute-start | bytes 2359304 | tf_op jit(solution)/shard_map/ppermute | solution.py:34
  26.9 8.6 %collective-permute-done.7.refs_5_ = bf16[4,384,256]{2,1,0:T(8,128)(2,1)S(1)} collective-permute-done((bf16[4,384,256]{2,1,0:T(8,128)(2,1)}, bf16[4,384,256]{2,1,0:T(8,128)(2,1)S(1)}, u32[]{:S(2)}, u32[]{:S(2)}) %collective-permute-start.7) | collective-permute-done | bytes 786464 | tf_op jit(solution)/shard_map/ppermute | solution.py:34
  36.2 3.3 %collective-permute-start.4 = (bf16[2,384,256]{2,1,0:T(8,128)(2,1)}, bf16[2,384,256]{2,1,0:T(8,128)(2,1)S(1)}, u32[]{:S(2)}, u32[]{:S(2)}) collective-permute-start(bf16[2,384,256]{2,1,0:T(8,128)(2,1)} %copy-done.5), channel_id=1, source_target_pairs={{0,1},{8,137},{16,17},{24,153},{32,33},{40,169},{48,49},{56,185},{... | collective-permute-start | bytes 1179656 | tf_op jit(solution)/shard_map/ppermute | solution.py:34
  40.8 2.5 %flip.1.refs_9_.refs_0_.refs_1_ = bf16[2,4,2,4,96,384]{5,4,3,2,1,0:T(8,128)(2,1)S(1)} custom-call(s32[20]{0:T(128)S(1)} %stack.95.info, bf16[2,192,3072]{2,1,0:T(8,128)(2,1)S(1)} %get-tuple-element.26.own.refs_0_, bf16[2,192,3072]{2,1,0:T(8,128)(2,1)S(1)} %collective-permute-done.3.peer.refs_1_), custom_call_target="tpu_custom_call" | custom-call | bytes 9437184 | tf_op jit(solution)/shard_map/flip/pallas_call | solution.py:72
  43.3 4.5 %linear.2 = (f32[192,1024]{1,0:T(8,128)S(1)}, f32[192,1024]{1,0:T(8,128)S(1)}) custom-call(bf16[2,192,3072]{2,1,0:T(8,128)(2,1)S(1)} %get-tuple-element.26.own.refs_0_, bf16[2,192,3072]{2,1,0:T(8,128)(2,1)S(1)} %collective-permute-done.3.peer.refs_1_, bf16[4,384,256]{2,1,0:T(8,128)(2,1)} %constant_dynamic-slice_fusion.2.refs_2_, ...), custom_call_target="tpu_custom_call" | custom-call | flops 1811939328 | bytes 8257536 | tf_op jit(solution)/shard_map/linear/pallas_call | solution.py:72
  49.1 1.8 %linear.3 = (f32[192,1024]{1,0:T(8,128)S(1)}, f32[192,1024]{1,0:T(8,128)S(1)}) custom-call(bf16[2,192,3072]{2,1,0:T(8,128)(2,1)S(1)} %get-tuple-element.26.own.refs_0_, bf16[2,192,3072]{2,1,0:T(8,128)(2,1)S(1)} %collective-permute-done.3.peer.refs_1_, bf16[2,384,256]{2,1,0:T(8,128)(2,1)S(1)} %collective-permute-done.4.refs_0_.refs_9_, ...), custom_call_target="tpu_custom_call" | custom-call | flops 603979776 | bytes 2752512 | tf_op jit(solution)/shard_map/linear/pallas_call | solution.py:72
  50.9 2.5 %collective-permute-start.10 = (f32[192,1024]{1,0:T(8,128)S(1)}, f32[192,1024]{1,0:T(8,128)S(1)}, u32[]{:S(2)}, u32[]{:S(2)}) collective-permute-start(f32[192,1024]{1,0:T(8,128)S(1)} %get-tuple-element.31), channel_id=1, source_target_pairs={{0,8},{8,0},{16,24},{24,16},{32,40},{40,32},{48,56},{56,48},{64,72... | collective-permute-start | bytes 2359304 | tf_op jit(solution)/shard_map/ppermute | solution.py:34
  53.4 1.9 %collective-permute-done.10.theirs = f32[192,1024]{1,0:T(8,128)S(1)} collective-permute-done((f32[192,1024]{1,0:T(8,128)S(1)}, f32[192,1024]{1,0:T(8,128)S(1)}, u32[]{:S(2)}, u32[]{:S(2)}) %collective-permute-start.10) | collective-permute-done | bytes 786464 | tf_op jit(solution)/shard_map/ppermute | solution.py:34
  55.4 3.2 %attend.1.refs_2_.refs_1_.refs_0_ = bf16[192,1024]{1,0:T(8,128)(2,1)S(1)} custom-call(s32[1,3]{1,0:T(1,128)S(1)} %copy-done.15, f32[192,1024]{1,0:T(8,128)S(1)} %get-tuple-element.30.mine, f32[192,1024]{1,0:T(8,128)S(1)} %collective-permute-done.10.theirs, f32[192,128]{1,0:T(8,128)S(1)} %get-tuple-element.63.refs_10_.cos_t, ...), custom_call_target="tpu_custom_call" | custom-call | flops 188743680 | bytes 1966080 | tf_op jit(solution)/shard_map/attend/pallas_call | solution.py:72
  61.5 2.6 %collective-permute-start.13 = (bf16[4,8,96,128]{3,2,1,0:T(8,128)(2,1)S(1)}, bf16[4,8,96,128]{3,2,1,0:T(8,128)(2,1)S(1)}, u32[]{:S(2)}, u32[]{:S(2)}) collective-permute-start(bf16[4,8,96,128]{3,2,1,0:T(8,128)(2,1)S(1)} %get-tuple-element.35), channel_id=1, source_target_pairs={{0,6},{8,137},{16,22},{24,153},{32,38},{40,169},{48,54},{56,185},{... | collective-permute-start | bytes 2359304 | tf_op jit(solution)/shard_map/ppermute | solution.py:34
  66.6 1.8 %terms.3 = (bf16[4,8,96,128]{3,2,1,0:T(8,128)(2,1)S(1)}, bf16[4,8,96,128]{3,2,1,0:T(8,128)(2,1)S(1)}, bf16[4,8,96,128]{3,2,1,0:T(8,128)(2,1)S(1)}, bf16[4,8,96,128]{3,2,1,0:T(8,128)(2,1)S(1)}) custom-call(bf16[2,4,2,4,96,384]{5,4,3,2,1,0:T(8,128)(2,1)S(1)} %flip.1.refs_9_.refs_0_.refs_1_, bf16[2,4,2,4,96,384]{5,4,3,2,1,0:T(8,128)(2,1)S(1)} %flip.1.refs_9_.refs_0_.refs_1_, ...), custom_call_target="tpu_custom_call" | custom-call | flops 1207959552 | bytes 7864320 | tf_op jit(solution)/shard_map/terms/pallas_call | solution.py:72
  68.4 5.3 %collective-permute-done.12.far_0 = bf16[4,8,96,128]{3,2,1,0:T(8,128)(2,1)S(1)} collective-permute-done((bf16[4,8,96,128]{3,2,1,0:T(8,128)(2,1)S(1)}, bf16[4,8,96,128]{3,2,1,0:T(8,128)(2,1)S(1)}, u32[]{:S(2)}, u32[]{:S(2)}) %collective-permute-start.12) | collective-permute-done | bytes 786464 | tf_op jit(solution)/shard_map/ppermute | solution.py:34
  74.3 3.0 %collective-permute-start.17 = (bf16[4,8,96,128]{3,2,1,0:T(8,128)(2,1)S(1)}, bf16[4,8,96,128]{3,2,1,0:T(8,128)(2,1)S(1)}, u32[]{:S(2)}, u32[]{:S(2)}) collective-permute-start(bf16[4,8,96,128]{3,2,1,0:T(8,128)(2,1)S(1)} %get-tuple-element.43), channel_id=1, source_target_pairs={{0,6},{8,137},{16,22},{24,153},{32,38},{40,169},{48,54},{56,185},{... | collective-permute-start | bytes 2359304 | tf_op jit(solution)/shard_map/ppermute | solution.py:34
  77.2 3.9 %normed_grad.1 = (f32[192,3072]{1,0:T(8,128)S(1)}, bf16[192,3072]{1,0:T(8,128)(2,1)S(1)}) custom-call(bf16[192,1024]{1,0:T(8,128)(2,1)S(1)} %attend.1.refs_2_.refs_1_.refs_0_, bf16[192,1024]{1,0:T(8,128)(2,1)S(1)} %collective-permute-done.11.refs_3_.refs_2_.refs_1_, bf16[4,384,256]{2,1,0:T(8,128)(2,1)} %constant_dynamic-slice_fusion.2.refs_2_, ...), custom_call_target="tpu_custom_call" | custom-call | flops 1811939328 | bytes 11010048 | tf_op jit(solution)/shard_map/normed_grad/pallas_call | solution.py:72
  82.2 8.4 %collective-permute-done.15.refs_2_ = bf16[4,8,96,128]{3,2,1,0:T(8,128)(2,1)S(1)} collective-permute-done((bf16[4,8,96,128]{3,2,1,0:T(8,128)(2,1)S(1)}, bf16[4,8,96,128]{3,2,1,0:T(8,128)(2,1)S(1)}, u32[]{:S(2)}, u32[]{:S(2)}) %collective-permute-start.15) | collective-permute-done | bytes 786464 | tf_op jit(solution)/shard_map/ppermute | solution.py:34
  90.6 1.9 %sides.1 = (bf16[8,2,96,128]{3,2,1,0:T(8,128)(2,1)S(1)}, bf16[8,2,96,128]{3,2,1,0:T(8,128)(2,1)}, bf16[8,2,96,128]{3,2,1,0:T(8,128)(2,1)S(1)}, bf16[8,2,96,128]{3,2,1,0:T(8,128)(2,1)S(1)}) custom-call(bf16[4,8,96,128]{3,2,1,0:T(8,128)(2,1)S(1)} %get-tuple-element.39.refs_0_, bf16[4,8,96,128]{3,2,1,0:T(8,128)(2,1)S(1)} %collective-permute-done.14.refs_1_, ...), custom_call_target="tpu_custom_call" | custom-call | flops 2359296 | bytes 6291456 | tf_op jit(solution)/shard_map/sides/pallas_call | solution.py:72
  95.6 3.1 %collective-permute-start.20 = (bf16[8,2,96,128]{3,2,1,0:T(8,128)(2,1)}, bf16[8,2,96,128]{3,2,1,0:T(8,128)(2,1)S(1)}, u32[]{:S(2)}, u32[]{:S(2)}) collective-permute-start(bf16[8,2,96,128]{3,2,1,0:T(8,128)(2,1)} %copy-done.17), channel_id=1, source_target_pairs={{0,128},{8,12},{16,144},{24,28},{32,160},{40,44},{48,176},{56,60},... | collective-permute-start | bytes 1179656 | tf_op jit(solution)/shard_map/ppermute | solution.py:34
  99.7 1.7 %copy-done.8 = f32[192,3072]{1,0:T(8,128)S(1)} copy-done((f32[192,3072]{1,0:T(8,128)S(1)}, f32[192,3072]{1,0:T(8,128)}, u32[]{:S(2)}) %copy-start.8) | copy-done | bytes 2359320
  101.4 5.1 %token_grad.1 = (bf16[192,6144]{1,0:T(8,128)(2,1)}, f32[8,128]{1,0:T(8,128)S(1)}) custom-call(s32[20]{0:T(128)S(1)} %stack.95.info, bf16[192,6144]{1,0:T(8,128)(2,1)S(1)} %copy-done.1, f32[192,3072]{1,0:T(8,128)S(1)} %copy-done.8, bf16[192,3072]{1,0:T(8,128)(2,1)S(1)} %collective-permute-done.18.g_peer), custom_call_target="tpu_custom_call" | custom-call | flops 18874368 | bytes 9437184 | tf_op jit(solution)/shard_map/token_grad/pallas_call | solution.py:72
  106.5 1.9 %collective-permute-done.20.refs_2_ = bf16[8,2,96,128]{3,2,1,0:T(8,128)(2,1)S(1)} collective-permute-done((bf16[8,2,96,128]{3,2,1,0:T(8,128)(2,1)}, bf16[8,2,96,128]{3,2,1,0:T(8,128)(2,1)S(1)}, u32[]{:S(2)}, u32[]{:S(2)}) %collective-permute-start.20) | collective-permute-done | bytes 393248 | tf_op jit(solution)/shard_map/ppermute | solution.py:34
  108.7 19.3 %all_to_all.10.got = bf16[8,2,96,128]{3,2,1,0:T(8,128)(2,1)S(1)} all-to-all(bf16[8,2,96,128]{3,2,1,0:T(8,128)(2,1)S(1)} %seconds.1), channel_id=1, replica_groups={{0,16,32,48,64,80,96,112},{8,24,40,56,72,88,104,120},{128,144,160,176,1..., dimensions={0} | all-to-all | bytes 786432 | tf_op jit(solution)/shard_map/all_to_all | solution.py:360
  128.1 14.5 %all_to_all.11.blocks = bf16[8,2,96,128]{3,2,1,0:T(8,128)(2,1)S(1)} all-to-all(bf16[8,2,96,128]{3,2,1,0:T(8,128)(2,1)S(1)} %last.1), channel_id=1, replica_groups={{0,16,32,48,64,80,96,112},{8,24,40,56,72,88,104,120},{128,144,160,176,1..., dimensions={0} | all-to-all | bytes 786432 | tf_op jit(solution)/shard_map/all_to_all | solution.py:360
  142.6 4.1 %collective-permute-start.23 = (bf16[8,2,96,128]{3,2,1,0:T(8,128)(2,1)S(1)}, bf16[8,2,96,128]{3,2,1,0:T(8,128)(2,1)S(1)}, u32[]{:S(2)}, u32[]{:S(2)}) collective-permute-start(bf16[8,2,96,128]{3,2,1,0:T(8,128)(2,1)S(1)} %all_to_all.11.blocks), channel_id=1, source_target_pairs={{0,8},{8,0},{16,24},{24,16},{32,40},{40,32},{48,56},{56,48},{64,72... | collective-permute-start | bytes 1179656 | tf_op jit(solution)/shard_map/ppermute | solution.py:34
  146.7 2.6 %collective-permute-start.22 = (bf16[8,2,96,128]{3,2,1,0:T(8,128)(2,1)S(1)}, bf16[8,2,96,128]{3,2,1,0:T(8,128)(2,1)S(1)}, u32[]{:S(2)}, u32[]{:S(2)}) collective-permute-start(bf16[8,2,96,128]{3,2,1,0:T(8,128)(2,1)S(1)} %all_to_all.11.blocks), channel_id=1, source_target_pairs={{0,128},{8,136},{16,144},{24,152},{32,160},{40,168},{48,176},{56,1... | collective-permute-start | bytes 1179656 | tf_op jit(solution)/shard_map/ppermute | solution.py:34
  152.1 6.8 %collective-permute-done.22.refs_0_ = bf16[8,2,96,128]{3,2,1,0:T(8,128)(2,1)S(1)} collective-permute-done((bf16[8,2,96,128]{3,2,1,0:T(8,128)(2,1)S(1)}, bf16[8,2,96,128]{3,2,1,0:T(8,128)(2,1)S(1)}, u32[]{:S(2)}, u32[]{:S(2)}) %collective-permute-start.22) | collective-permute-done | bytes 393248 | tf_op jit(solution)/shard_map/ppermute | solution.py:34
  (87 shorter events, 28.4 us)
Async XLA Ops:
  2.7 20.2 %collective-permute-start = (bf16[4,384,256]{2,1,0:T(8,128)(2,1)}, bf16[4,384,256]{2,1,0:T(8,128)(2,1)S(1)}, u32[]{:S(2)}, u32[]{:S(2)}) collective-permute-start(bf16[4,384,256]{2,1,0:T(8,128)(2,1)} %constant_dynamic-slice_fusion.2.refs_2_), channel_id=1, source_target_pairs={{0,2},{8,14},{16,18},{24,30},{32,34},{40,46},{48,50},{56,62},{64,6... | collective-permute-start | bytes 2359304 | tf_op jit(solution)/shard_map/ppermute | solution.py:34
  6.3 16.7 %collective-permute-start.1 = (bf16[4,384,256]{2,1,0:T(8,128)(2,1)}, bf16[4,384,256]{2,1,0:T(8,128)(2,1)}, u32[]{:S(2)}, u32[]{:S(2)}) collective-permute-start(bf16[4,384,256]{2,1,0:T(8,128)(2,1)} %constant_dynamic-slice_fusion.2.refs_2_), channel_id=1, source_target_pairs={{0,1},{8,137},{16,17},{24,153},{32,33},{40,169},{48,49},{56,185},{... | collective-permute-start | bytes 2359304 | tf_op jit(solution)/shard_map/ppermute | solution.py:34
  10.8 12.1 %collective-permute-start.2 = (bf16[2,384,256]{2,1,0:T(8,128)(2,1)}, bf16[2,384,256]{2,1,0:T(8,128)(2,1)S(1)}, u32[]{:S(2)}, u32[]{:S(2)}) collective-permute-start(bf16[2,384,256]{2,1,0:T(8,128)(2,1)} %get-tuple-element.51), channel_id=1, source_target_pairs={{0,6},{8,10},{16,22},{24,26},{32,38},{40,42},{48,54},{56,58},{64,7... | collective-permute-start | bytes 1179656 | tf_op jit(solution)/shard_map/ppermute | solution.py:34
  24.0 12.2 %copy-start.18 = (s32[2,192]{1,0:T(2,128)S(1)}, s32[2,192]{1,0:T(2,128)}, u32[]{:S(2)}) copy-start(s32[2,192]{1,0:T(2,128)} %param.10) | copy-start | bytes 4612
  24.0 15.8 %copy-start.19 = (f32[32]{0:T(128)S(1)}, f32[32]{0:T(128)}, u32[]{:S(2)}) copy-start(f32[32]{0:T(128)} %constant.149) | copy-start | bytes 388
  24.0 16.8 %collective-permute-start.3 = (bf16[2,192,3072]{2,1,0:T(8,128)(2,1)}, bf16[2,192,3072]{2,1,0:T(8,128)(2,1)S(1)}, u32[]{:S(2)}, u32[]{:S(2)}) collective-permute-start(bf16[2,192,3072]{2,1,0:T(8,128)(2,1)} %gate.3), channel_id=1, source_target_pairs={{0,8},{8,0},{16,24},{24,16},{32,40},{40,32},{48,56},{56,48},{64,72... | collective-permute-start | bytes 7077896 | tf_op jit(solution)/shard_map/ppermute | solution.py:34
  24.2 11.3 %collective-permute-start.7 = (bf16[4,384,256]{2,1,0:T(8,128)(2,1)}, bf16[4,384,256]{2,1,0:T(8,128)(2,1)S(1)}, u32[]{:S(2)}, u32[]{:S(2)}) collective-permute-start(bf16[4,384,256]{2,1,0:T(8,128)(2,1)} %copy-done.2), channel_id=1, source_target_pairs={{0,1},{8,137},{16,17},{24,153},{32,33},{40,169},{48,49},{56,185},{... | collective-permute-start | bytes 2359304 | tf_op jit(solution)/shard_map/ppermute | solution.py:34
  25.2 18.1 %collective-permute-start.9 = (bf16[4,384,256]{2,1,0:T(8,128)(2,1)}, bf16[4,384,256]{2,1,0:T(8,128)(2,1)S(1)}, u32[]{:S(2)}, u32[]{:S(2)}) collective-permute-start(bf16[4,384,256]{2,1,0:T(8,128)(2,1)} %copy-done.2), channel_id=1, source_target_pairs={{0,2},{8,14},{16,18},{24,30},{32,34},{40,46},{48,50},{56,62},{64,6... | collective-permute-start | bytes 2359304 | tf_op jit(solution)/shard_map/ppermute | solution.py:34
  26.9 12.6 %collective-permute-start.5 = (bf16[2,384,256]{2,1,0:T(8,128)(2,1)}, bf16[2,384,256]{2,1,0:T(8,128)(2,1)S(1)}, u32[]{:S(2)}, u32[]{:S(2)}) collective-permute-start(bf16[2,384,256]{2,1,0:T(8,128)(2,1)} %get-tuple-element.50), channel_id=1, source_target_pairs={{0,6},{8,10},{16,22},{24,26},{32,38},{40,42},{48,54},{56,58},{64,7... | collective-permute-start | bytes 1179656 | tf_op jit(solution)/shard_map/ppermute | solution.py:34
  35.6 13.5 %collective-permute-start.8 = (bf16[4,384,256]{2,1,0:T(8,128)(2,1)S(1)}, bf16[4,384,256]{2,1,0:T(8,128)(2,1)S(1)}, u32[]{:S(2)}, u32[]{:S(2)}) collective-permute-start(bf16[4,384,256]{2,1,0:T(8,128)(2,1)S(1)} %collective-permute-done.7.refs_5_), channel_id=1, source_target_pairs={{0,2},{8,14},{16,18},{24,30},{32,34},{40,46},{48,50},{56,62},{64,6... | collective-permute-start | bytes 2359304 | tf_op jit(solution)/shard_map/ppermute | solution.py:34
  36.2 11.5 %collective-permute-start.4 = (bf16[2,384,256]{2,1,0:T(8,128)(2,1)}, bf16[2,384,256]{2,1,0:T(8,128)(2,1)S(1)}, u32[]{:S(2)}, u32[]{:S(2)}) collective-permute-start(bf16[2,384,256]{2,1,0:T(8,128)(2,1)} %copy-done.5), channel_id=1, source_target_pairs={{0,1},{8,137},{16,17},{24,153},{32,33},{40,169},{48,49},{56,185},{... | collective-permute-start | bytes 1179656 | tf_op jit(solution)/shard_map/ppermute | solution.py:34
  39.6 9.1 %collective-permute-start.6 = (bf16[2,384,256]{2,1,0:T(8,128)(2,1)S(1)}, bf16[2,384,256]{2,1,0:T(8,128)(2,1)S(1)}, u32[]{:S(2)}, u32[]{:S(2)}) collective-permute-start(bf16[2,384,256]{2,1,0:T(8,128)(2,1)S(1)} %collective-permute-done.5.refs_7_), channel_id=1, source_target_pairs={{0,1},{8,137},{16,17},{24,153},{32,33},{40,169},{48,49},{56,185},{... | collective-permute-start | bytes 1179656 | tf_op jit(solution)/shard_map/ppermute | solution.py:34
  49.1 6.2 %copy-start.15 = (s32[1,3]{1,0:T(1,128)S(1)}, s32[1,3]{1,0:T(1,128)}, u32[]{:S(2)}) copy-start(s32[1,3]{1,0:T(1,128)} %lengths.1) | copy-start | bytes 40
  50.9 4.5 %collective-permute-start.10 = (f32[192,1024]{1,0:T(8,128)S(1)}, f32[192,1024]{1,0:T(8,128)S(1)}, u32[]{:S(2)}, u32[]{:S(2)}) collective-permute-start(f32[192,1024]{1,0:T(8,128)S(1)} %get-tuple-element.31), channel_id=1, source_target_pairs={{0,8},{8,0},{16,24},{24,16},{32,40},{40,32},{48,56},{56,48},{64,72... | collective-permute-start | bytes 2359304 | tf_op jit(solution)/shard_map/ppermute | solution.py:34
  58.5 1.8 %collective-permute-start.11 = (bf16[192,1024]{1,0:T(8,128)(2,1)S(1)}, bf16[192,1024]{1,0:T(8,128)(2,1)S(1)}, u32[]{:S(2)}, u32[]{:S(2)}) collective-permute-start(bf16[192,1024]{1,0:T(8,128)(2,1)S(1)} %attend.1.refs_2_.refs_1_.refs_0_), channel_id=1, source_target_pairs={{0,8},{8,0},{16,24},{24,16},{32,40},{40,32},{48,56},{56,48},{64,72... | collective-permute-start | bytes 1179656 | tf_op jit(solution)/shard_map/ppermute | solution.py:34
  61.3 12.4 %collective-permute-start.12 = (bf16[4,8,96,128]{3,2,1,0:T(8,128)(2,1)S(1)}, bf16[4,8,96,128]{3,2,1,0:T(8,128)(2,1)S(1)}, u32[]{:S(2)}, u32[]{:S(2)}) collective-permute-start(bf16[4,8,96,128]{3,2,1,0:T(8,128)(2,1)S(1)} %get-tuple-element.33), channel_id=1, source_target_pairs={{0,2},{8,9},{16,18},{24,25},{32,34},{40,41},{48,50},{56,57},{64,66... | collective-permute-start | bytes 2359304 | tf_op jit(solution)/shard_map/ppermute | solution.py:34
  61.5 12.2 %collective-permute-start.13 = (bf16[4,8,96,128]{3,2,1,0:T(8,128)(2,1)S(1)}, bf16[4,8,96,128]{3,2,1,0:T(8,128)(2,1)S(1)}, u32[]{:S(2)}, u32[]{:S(2)}) collective-permute-start(bf16[4,8,96,128]{3,2,1,0:T(8,128)(2,1)S(1)} %get-tuple-element.35), channel_id=1, source_target_pairs={{0,6},{8,137},{16,22},{24,153},{32,38},{40,169},{48,54},{56,185},{... | collective-permute-start | bytes 2359304 | tf_op jit(solution)/shard_map/ppermute | solution.py:34
  65.1 16.4 %collective-permute-start.14 = (bf16[4,8,96,128]{3,2,1,0:T(8,128)(2,1)S(1)}, bf16[4,8,96,128]{3,2,1,0:T(8,128)(2,1)S(1)}, u32[]{:S(2)}, u32[]{:S(2)}) collective-permute-start(bf16[4,8,96,128]{3,2,1,0:T(8,128)(2,1)S(1)} %get-tuple-element.40), channel_id=1, source_target_pairs={{0,6},{8,137},{16,22},{24,153},{32,38},{40,169},{48,54},{56,185},{... | collective-permute-start | bytes 2359304 | tf_op jit(solution)/shard_map/ppermute | solution.py:34
  65.6 16.6 %collective-permute-start.16 = (bf16[4,8,96,128]{3,2,1,0:T(8,128)(2,1)S(1)}, bf16[4,8,96,128]{3,2,1,0:T(8,128)(2,1)S(1)}, u32[]{:S(2)}, u32[]{:S(2)}) collective-permute-start(bf16[4,8,96,128]{3,2,1,0:T(8,128)(2,1)S(1)} %get-tuple-element.42), channel_id=1, source_target_pairs={{0,2},{8,9},{16,18},{24,25},{32,34},{40,41},{48,50},{56,57},{64,66... | collective-permute-start | bytes 2359304 | tf_op jit(solution)/shard_map/ppermute | solution.py:34
  74.2 16.4 %collective-permute-start.15 = (bf16[4,8,96,128]{3,2,1,0:T(8,128)(2,1)S(1)}, bf16[4,8,96,128]{3,2,1,0:T(8,128)(2,1)S(1)}, u32[]{:S(2)}, u32[]{:S(2)}) collective-permute-start(bf16[4,8,96,128]{3,2,1,0:T(8,128)(2,1)S(1)} %get-tuple-element.36.refs_12_), channel_id=1, source_target_pairs={{0,2},{8,9},{16,18},{24,25},{32,34},{40,41},{48,50},{56,57},{64,66... | collective-permute-start | bytes 2359304 | tf_op jit(solution)/shard_map/ppermute | solution.py:34
  74.3 16.3 %collective-permute-start.17 = (bf16[4,8,96,128]{3,2,1,0:T(8,128)(2,1)S(1)}, bf16[4,8,96,128]{3,2,1,0:T(8,128)(2,1)S(1)}, u32[]{:S(2)}, u32[]{:S(2)}) collective-permute-start(bf16[4,8,96,128]{3,2,1,0:T(8,128)(2,1)S(1)} %get-tuple-element.43), channel_id=1, source_target_pairs={{0,6},{8,137},{16,22},{24,153},{32,38},{40,169},{48,54},{56,185},{... | collective-permute-start | bytes 2359304 | tf_op jit(solution)/shard_map/ppermute | solution.py:34
  81.1 11.4 %copy-start.4 = (bf16[192,3072]{1,0:T(8,128)(2,1)}, bf16[192,3072]{1,0:T(8,128)(2,1)S(1)}, u32[]{:S(2)}) copy-start(bf16[192,3072]{1,0:T(8,128)(2,1)S(1)} %get-tuple-element.38.refs_6_.refs_0_) | copy-start | bytes 3538948
  81.1 11.4 %copy-start.7 = (f32[192,3072]{1,0:T(8,128)}, f32[192,3072]{1,0:T(8,128)S(1)}, u32[]{:S(2)}) copy-start(f32[192,3072]{1,0:T(8,128)S(1)} %get-tuple-element.37.g_own) | copy-start | bytes 7077892
  93.3 6.4 %copy-start.1 = (bf16[192,6144]{1,0:T(8,128)(2,1)S(1)}, bf16[192,6144]{1,0:T(8,128)(2,1)}, u32[]{:S(2)}) copy-start(bf16[192,6144]{1,0:T(8,128)(2,1)} %tokens.3) | copy-start | bytes 7077892
  93.3 6.4 %collective-permute-start.18 = (bf16[192,3072]{1,0:T(8,128)(2,1)}, bf16[192,3072]{1,0:T(8,128)(2,1)S(1)}, u32[]{:S(2)}, u32[]{:S(2)}) collective-permute-start(bf16[192,3072]{1,0:T(8,128)(2,1)} %gate.4), channel_id=1, source_target_pairs={{0,8},{8,0},{16,24},{24,16},{32,40},{40,32},{48,56},{56,48},{64,72... | collective-permute-start | bytes 3538952 | tf_op jit(solution)/shard_map/ppermute | solution.py:34
  94.5 12.0 %collective-permute-start.19 = (bf16[8,2,96,128]{3,2,1,0:T(8,128)(2,1)}, bf16[8,2,96,128]{3,2,1,0:T(8,128)(2,1)S(1)}, u32[]{:S(2)}, u32[]{:S(2)}) collective-permute-start(bf16[8,2,96,128]{3,2,1,0:T(8,128)(2,1)} %get-tuple-element.46), channel_id=1, source_target_pairs={{0,1},{8,10},{16,17},{24,26},{32,33},{40,42},{48,49},{56,58},{64,6... | collective-permute-start | bytes 1179656 | tf_op jit(solution)/shard_map/ppermute | solution.py:34
  95.6 12.9 %collective-permute-start.20 = (bf16[8,2,96,128]{3,2,1,0:T(8,128)(2,1)}, bf16[8,2,96,128]{3,2,1,0:T(8,128)(2,1)S(1)}, u32[]{:S(2)}, u32[]{:S(2)}) collective-permute-start(bf16[8,2,96,128]{3,2,1,0:T(8,128)(2,1)} %copy-done.17), channel_id=1, source_target_pairs={{0,128},{8,12},{16,144},{24,28},{32,160},{40,44},{48,176},{56,60},... | collective-permute-start | bytes 1179656 | tf_op jit(solution)/shard_map/ppermute | solution.py:34
  98.6 9.8 %collective-permute-start.21 = (bf16[8,2,96,128]{3,2,1,0:T(8,128)(2,1)}, bf16[8,2,96,128]{3,2,1,0:T(8,128)(2,1)S(1)}, u32[]{:S(2)}, u32[]{:S(2)}) collective-permute-start(bf16[8,2,96,128]{3,2,1,0:T(8,128)(2,1)} %copy-done.16), channel_id=1, source_target_pairs={{0,129},{8,14},{16,145},{24,30},{32,161},{40,46},{48,177},{56,62},... | collective-permute-start | bytes 1179656 | tf_op jit(solution)/shard_map/ppermute | solution.py:34
  101.4 7.1 %copy-start.12 = (bf16[8,2,96,128]{3,2,1,0:T(8,128)(2,1)S(1)}, bf16[8,2,96,128]{3,2,1,0:T(8,128)(2,1)}, u32[]{:S(2)}) copy-start(bf16[8,2,96,128]{3,2,1,0:T(8,128)(2,1)} %copy-done.11) | copy-start | bytes 1179652
  142.6 8.1 %collective-permute-start.23 = (bf16[8,2,96,128]{3,2,1,0:T(8,128)(2,1)S(1)}, bf16[8,2,96,128]{3,2,1,0:T(8,128)(2,1)S(1)}, u32[]{:S(2)}, u32[]{:S(2)}) collective-permute-start(bf16[8,2,96,128]{3,2,1,0:T(8,128)(2,1)S(1)} %all_to_all.11.blocks), channel_id=1, source_target_pairs={{0,8},{8,0},{16,24},{24,16},{32,40},{40,32},{48,56},{56,48},{64,72... | collective-permute-start | bytes 1179656 | tf_op jit(solution)/shard_map/ppermute | solution.py:34
  146.7 12.2 %collective-permute-start.22 = (bf16[8,2,96,128]{3,2,1,0:T(8,128)(2,1)S(1)}, bf16[8,2,96,128]{3,2,1,0:T(8,128)(2,1)S(1)}, u32[]{:S(2)}, u32[]{:S(2)}) collective-permute-start(bf16[8,2,96,128]{3,2,1,0:T(8,128)(2,1)S(1)} %all_to_all.11.blocks), channel_id=1, source_target_pairs={{0,128},{8,136},{16,144},{24,152},{32,160},{40,168},{48,176},{56,1... | collective-permute-start | bytes 1179656 | tf_op jit(solution)/shard_map/ppermute | solution.py:34
  159.7 3.2 %collective-permute-start.24 = (bf16[8,2,96,128]{3,2,1,0:T(8,128)(2,1)}, bf16[8,2,96,128]{3,2,1,0:T(8,128)(2,1)S(1)}, u32[]{:S(2)}, u32[]{:S(2)}) collective-permute-start(bf16[8,2,96,128]{3,2,1,0:T(8,128)(2,1)} %gate.5.blocks), channel_id=1, source_target_pairs={{0,8},{8,0},{16,24},{24,16},{32,40},{40,32},{48,56},{56,48},{64,72... | collective-permute-start | bytes 1179656 | tf_op jit(solution)/shard_map/ppermute | solution.py:34
  (13 other events, 19.2 us)
